TPU v7x, 32 devices: a whole 2x2x4 slice. The times are simulated.
32 devices in a mesh: seq: 8 (over z, core), dp: 4 (over y, x).
Axes of the slice: x: 2, y: 2, z: 4, core: 2. Of those that a mesh axis runs over, the one named last changes fastest.
Arguments:
- queries: bfloat16 [4, 1024, 1280], P('dp', 'seq'), may hold values from -43 to 43
- key_rows: bfloat16 [4, 1024, 1280], P('dp', 'seq'), may hold values from -7 to 7
- value_rows: bfloat16 [4, 1024, 1280], P('dp', 'seq'), may hold values from -6 to 6
- resid_in: bfloat16 [4, 1024, 1280], P('dp', 'seq'), may hold values from -6 to 6
- llm_grad: bfloat16 [4, 1536, 1280], P('dp', 'seq'), may hold values from -6 to 6
- vision_slot: int32 [4, 1536], P('dp', 'seq'), may hold values from -1 to 1023, as said below
- window_mask: int32 [4, 16, 2], P('dp', 'seq'), may hold values from 0 to 1, as said below
- w_up: bfloat16 [1280, 2560], P('dp'), may hold values from -0.15625 to 0.15625
- w_down: bfloat16 [2560, 1280], P('dp'), may hold values from -0.125 to 0.125
- norm_gain: bfloat16 [1280], P('dp'), may hold values from 0.25 to 1.75
Outputs:
- grad_query: bfloat16 [4, 1024, 1280], P('dp', 'seq')
- grad_key: bfloat16 [4, 1024, 1280], P('dp', 'seq')
- grad_value: bfloat16 [4, 1024, 1280], P('dp', 'seq')
- grad_resid: bfloat16 [4, 1024, 1280], P('dp', 'seq')
- grad_up: bfloat16 [1280, 2560], P('seq', 'dp')
- grad_down: bfloat16 [2560, 1280], P('seq', 'dp')
- grad_gain: float32 [1280], replicated
Inputs may be any that keep to these rules, and one draw needn't show every extreme that they name: `vision_slot`: -1 marks a text position; every vision token of a batch stands at exactly one position. Positions come in aligned runs of 16: each run is text or the 16 consecutive vision tokens of one tile, in order. Each language-model shard holds exactly 8 tiles, and at most 32 vision tokens of one owner; in every batch, for every owner, some shard holds exactly 32 of that owner's vision tokens. `window_mask`: each owner's 2 blocks are split into images of one or more consecutive blocks; a block attends to exactly the blocks of its own image, itself included (entry i % 2 of row i is 1).
All inputs are finite; a program needn't handle non-finite values.
Results may differ from a plain program's by a relative error of at most 0.023.
Values may be sent and summed in bfloat16 or wider, within the bound.
No kernel may reach another device: no remote copies, remote signals or barrier semaphores. Data moves between devices by JAX's collectives and lax.ppermute only.
A program may use at most 128 MiB of HBM per device.

v0:
```python
import math

import jax
import jax.numpy as jnp
from jax import lax
from jax.sharding import PartitionSpec as P

HEADS = 16
HDIM = 80
BLK = 64
PIECE = 16


def contract(left, right, left_dim, right_dim):
    return lax.dot_general(
        left, right, (((left_dim,), (right_dim,)), ((), ())), preferred_element_type=jnp.float32
    )


def per_device(
    queries,
    key_rows,
    value_rows,
    resid_in,
    llm_grad,
    vision_slot,
    window_mask,
    w_up,
    w_down,
    norm_gain,
):
    seq_count = lax.axis_size("seq")
    data_count = lax.axis_size("dp")
    query = queries[0]
    key_block = key_rows[0]
    value_block = value_rows[0]
    tokens, feat_dim = query.shape
    att_scale = 1.0 / math.sqrt(HDIM)
    up_full, down_full, gain_full = (
        lax.all_gather(w_up, "dp", axis=0, tiled=True),
        lax.all_gather(w_down, "dp", axis=0, tiled=True),
        lax.all_gather(norm_gain, "dp", axis=0, tiled=True),
    )
    slot_ids = vision_slot[0]
    piece_count = tokens // PIECE
    capacity = PIECE * (1 + (piece_count + seq_count - 2) // seq_count)
    owner_of = jnp.where(slot_ids >= 0, slot_ids // tokens, seq_count)
    onehot = (owner_of[:, None] == jnp.arange(seq_count)[None, :]).astype(jnp.int32)
    ranking = jnp.sum((jnp.cumsum(onehot, axis=0) - 1) * onehot, axis=1)
    target = jnp.where(slot_ids >= 0, owner_of * capacity + ranking, seq_count * capacity)
    send_rows = (
        jnp.zeros((seq_count * capacity, feat_dim), jnp.bfloat16)
        .at[target]
        .set(llm_grad[0], mode="drop")
    )
    send_ids = (
        jnp.full((seq_count * capacity,), -1, jnp.int32)
        .at[target]
        .set(jnp.where(slot_ids >= 0, slot_ids % tokens, -1), mode="drop")
    )
    recv_rows = lax.all_to_all(
        send_rows.reshape(seq_count, capacity, feat_dim),
        "seq",
        split_axis=0,
        concat_axis=0,
        tiled=True,
    )
    recv_ids = lax.all_to_all(
        send_ids.reshape(seq_count, capacity), "seq", split_axis=0, concat_axis=0, tiled=True
    )
    flat_ids = recv_ids.reshape(seq_count * capacity)
    landing = jnp.where(flat_ids >= 0, flat_ids, tokens)
    grad_rows = (
        jnp.zeros((tokens, feat_dim), jnp.bfloat16)
        .at[landing]
        .set(recv_rows.reshape(seq_count * capacity, feat_dim), mode="drop")
    )
    allowed = jnp.repeat(jnp.repeat(window_mask[0] > 0, BLK, axis=0), BLK, axis=1)
    q_heads = query.reshape(tokens, HEADS, HDIM)
    k_heads = key_block.reshape(tokens, HEADS, HDIM)
    v_heads = value_block.reshape(tokens, HEADS, HDIM)
    scores = (
        jnp.einsum("qhd,khd->hqk", q_heads, k_heads, preferred_element_type=jnp.float32) * att_scale
    )
    masked = jnp.where(allowed[None], scores, -jnp.inf)
    highest = jnp.max(masked, axis=2, keepdims=True)
    exp_terms = jnp.where(allowed[None], jnp.exp(masked - highest), 0.0)
    attn_probs = exp_terms / jnp.sum(exp_terms, axis=2, keepdims=True)
    probs_low = attn_probs.astype(jnp.bfloat16)
    attn_heads = jnp.einsum(
        "hqk,khd->qhd", probs_low, v_heads, preferred_element_type=jnp.float32
    ).astype(jnp.bfloat16)
    attn_out = attn_heads.reshape(tokens, feat_dim)
    hidden = resid_in[0].astype(jnp.float32) + attn_out.astype(jnp.float32)
    center = jnp.mean(hidden, axis=1, keepdims=True)
    variance = jnp.mean(jnp.square(hidden - center), axis=1, keepdims=True)
    inverse = lax.rsqrt(variance + 1e-06)
    normal_unit = (hidden - center) * inverse
    gain_wide = gain_full.astype(jnp.float32)
    normed = (normal_unit * gain_wide).astype(jnp.bfloat16)
    pre_act = jnp.dot(normed, up_full, preferred_element_type=jnp.float32)
    sig_gate = jax.nn.sigmoid(1.702 * pre_act)
    act_low = (pre_act * sig_gate).astype(jnp.bfloat16)
    down_term = contract(act_low, grad_rows, 0, 0)
    d_act = contract(grad_rows, down_full, 1, 1)
    d_pre = (d_act * (sig_gate + 1.702 * pre_act * sig_gate * (1.0 - sig_gate))).astype(
        jnp.bfloat16
    )
    d_normed = contract(d_pre, up_full, 1, 1)
    gain_term = jnp.sum(d_normed * normal_unit, axis=0)
    d_unit = d_normed * gain_wide
    d_hidden = inverse * (
        d_unit
        - jnp.mean(d_unit, axis=1, keepdims=True)
        - normal_unit * jnp.mean(d_unit * normal_unit, axis=1, keepdims=True)
    )
    grad_resid = (grad_rows.astype(jnp.float32) + d_hidden).astype(jnp.bfloat16)
    up_term = contract(normed, d_pre, 0, 0)
    grad_heads = grad_resid.reshape(tokens, HEADS, HDIM)
    grad_value = jnp.einsum(
        "hqk,qhd->khd", probs_low, grad_heads, preferred_element_type=jnp.float32
    ).astype(jnp.bfloat16)
    d_probs = jnp.einsum("qhd,khd->hqk", grad_heads, v_heads, preferred_element_type=jnp.float32)
    delta = jnp.einsum("qhd,qhd->hq", grad_heads, attn_heads, preferred_element_type=jnp.float32)
    d_scores = (attn_probs * (d_probs - delta[:, :, None]) * att_scale).astype(jnp.bfloat16)
    grad_query = jnp.einsum(
        "hqk,khd->qhd", d_scores, k_heads, preferred_element_type=jnp.float32
    ).astype(jnp.bfloat16)
    grad_key = jnp.einsum(
        "hqk,qhd->khd", d_scores, q_heads, preferred_element_type=jnp.float32
    ).astype(jnp.bfloat16)
    up_part, down_part = (
        lax.psum_scatter(
            up_term.astype(jnp.bfloat16), "seq", scatter_dimension=0, tiled=True
        ).astype(jnp.float32),
        lax.psum_scatter(
            down_term.astype(jnp.bfloat16), "seq", scatter_dimension=0, tiled=True
        ).astype(jnp.float32),
    )
    up_panel, down_panel = (
        lax.psum_scatter(
            up_part.astype(jnp.bfloat16), "dp", scatter_dimension=1, tiled=True
        ).astype(jnp.float32),
        lax.psum_scatter(
            down_part.astype(jnp.bfloat16), "dp", scatter_dimension=1, tiled=True
        ).astype(jnp.float32),
    )
    factor = 1.0 / math.sqrt(data_count * seq_count * tokens)
    gain_total = lax.psum(gain_term, ("seq", "dp"))
    return (
        grad_query.reshape(1, tokens, feat_dim),
        grad_key.reshape(1, tokens, feat_dim),
        grad_value.reshape(1, tokens, feat_dim),
        grad_resid[None],
        (up_panel * factor).astype(jnp.bfloat16),
        (down_panel * factor).astype(jnp.bfloat16),
        gain_total * factor,
    )


def solution(mesh):
    in_specs = (
        P("dp", "seq", None),
        P("dp", "seq", None),
        P("dp", "seq", None),
        P("dp", "seq", None),
        P("dp", "seq", None),
        P("dp", "seq"),
        P("dp", "seq", None),
        P("dp", None),
        P("dp", None),
        P("dp"),
    )
    out_specs = (
        P("dp", "seq", None),
        P("dp", "seq", None),
        P("dp", "seq", None),
        P("dp", "seq", None),
        P("seq", "dp"),
        P("seq", "dp"),
        P(),
    )
    return jax.shard_map(
        per_device, mesh=mesh, in_specs=in_specs, out_specs=out_specs, check_vma=False
    )
```

profile of v0, /device:TPU:0, one launch (start us, length us, event | category | flops | bytes accessed | tf_op | source)
XLA Modules:
  0.0 377.1 jit_solution(8138141014200120400)
XLA Ops:
  7.3 0.7 all-gather.5.cloned.1.call-update
  8.0 0.0 all-gather.3.cloned.1.call-start
  8.0 0.7 all-gather.3.cloned.1.call-update
  8.8 0.6 reduce-window.6
  9.4 0.2 slice_reduce_fusion
  9.6 0.1 add_bitcast_fusion
  9.7 1.2 scatter_custom_fusion
  10.9 0.7 all_to_all.9
  11.6 6.3 %all-to-all-start = ((s32[8,1,32]{2,1,0:T(1,128)}), s32[8,1,32]{2,1,0:T(1,128)S(1)}, u32[]{:S(2)}, u32[]{:S(2)}) async-start(s32[8,1,32]{2,1,0:T(1,128)} %all_to_all.9), calls=%async_computation | async-start | bytes 8192 | tf_op jit(solution)/shard_map/all_to_all | solution.py:68
  18.0 0.1 copy.49
  18.1 0.1 broadcast_in_dim.66
  18.1 0.1 reshape.229
  18.2 0.2 copy.50
  18.5 0.2 copy.51
  18.7 0.2 copy.52
  19.0 1.5 fusion.35
  20.5 1.7 convolution_convert_fusion.3
  22.2 2.3 scatter_custom_fusion.1
  24.6 5.2 %all-to-all-start.1 = ((bf16[8,32,1280]{2,1,0:T(8,128)(2,1)}), bf16[8,32,1280]{2,1,0:T(8,128)(2,1)S(1)}, u32[]{:S(2)}, u32[]{:S(2)}) async-start(bf16[8,32,1280]{2,1,0:T(8,128)(2,1)} %bitcast.15), calls=%async_computation.1 | async-start | bytes 1310720 | tf_op jit(solution)/shard_map/all_to_all | solution.py:61
  29.8 0.0 reduce-scatter.11.cloned.1.call-start
  29.8 0.1 bitcast_convert_fusion
  29.9 0.6 dynamic-slice
  31.2 0.3 dynamic-update-slice
  31.4 10.1 %all-reduce.1 = bf16[1280]{0:T(1024)(128)(2,1)S(1)} all-reduce(bf16[1280]{0:T(1024)(128)(2,1)S(1)} %dynamic-update-slice), channel_id=1, replica_groups=mesh['seq'=8,'dp'=4] {'dp'}, use_global_device_ids=true, to_apply=%add.1 | all-reduce | flops 1280 | bytes 5120
  41.6 0.2 copy.54
  41.8 0.1 fusion.34
  42.0 0.2 multiply_reduce_fusion.2
  42.2 0.5 broadcast.297
  42.7 0.7 reduce.7
  43.4 0.1 reshape.232
  43.5 4.5 %all-to-all-done.1 = bf16[8,32,1280]{2,1,0:T(8,128)(2,1)S(1)} async-done(((bf16[8,32,1280]{2,1,0:T(8,128)(2,1)}), bf16[8,32,1280]{2,1,0:T(8,128)(2,1)S(1)}, u32[]{:S(2)}, u32[]{:S(2)}) %all-to-all-start.1) | async-done | bytes 655392 | tf_op jit(solution)/shard_map/all_to_all | solution.py:61
  48.0 1.7 scatter_custom_fusion.2
  49.7 35.4 %all-gather.5.cloned.1.call-done = bf16[1280,2560]{1,0:T(8,128)(2,1)} async-done(((bf16[320,2560]{1,0:T(8,128)(2,1)}), bf16[1280,2560]{1,0:T(8,128)(2,1)}) %all-gather.5.cloned.1.call-update) | async-done | bytes 6553616 | tf_op jit(solution)/shard_map/all_gather | solution.py:40
  85.1 3.9 %fusion.31 = f32[128,2560]{1,0:T(8,128)S(1)} fusion(bf16[1280,2560]{1,0:T(8,128)(2,1)} %all-gather.5.cloned.1.call-done, f32[128,1280]{1,0:T(8,128)S(1)} %get-tuple-element.32, f32[1280]{0:T(1024)S(1)} %convert_element_type.92, f32[128]{0:T(128)S(1)} %add_rsqrt_fusion, f32[128]{0:T(128)S(1)} %broadcast_multiply_fusion.3), kind=kOutput, calls=%fused_computation.88 | convolution fusion | flops 839516160 | bytes 8525824 | tf_op jit(solution)/shard_map/dot_general | solution.py:101
  89.0 4.6 %convolution_convert_fusion = bf16[2560,1280]{1,0:T(8,128)(2,1)} fusion(bf16[128,1280]{1,0:T(8,128)(2,1)S(1)} %scatter_custom_fusion.2, f32[128,2560]{1,0:T(8,128)S(1)} %fusion.31), kind=kOutput, calls=%fused_computation.4 | convolution fusion | flops 844103680 | bytes 8192000 | tf_op jit(solution)/shard_map/dot_general | solution.py:15
  93.7 0.2 reduce-scatter.9.cloned.1.call-start
  93.9 65.4 %all-gather.3.cloned.1.call-done = bf16[2560,1280]{1,0:T(8,128)(2,1)} async-done(((bf16[640,1280]{1,0:T(8,128)(2,1)}), bf16[2560,1280]{1,0:T(8,128)(2,1)}) %all-gather.3.cloned.1.call-update) | async-done | bytes 6553616 | tf_op jit(solution)/shard_map/all_gather | solution.py:41
  159.3 5.1 %fusion.1 = bf16[128,2560]{1,0:T(8,128)(2,1)S(1)} fusion(bf16[128,1280]{1,0:T(8,128)(2,1)S(1)} %scatter_custom_fusion.2, bf16[2560,1280]{1,0:T(8,128)(2,1)} %all-gather.3.cloned.1.call-done, f32[128,2560]{1,0:T(8,128)S(1)} %fusion.31), kind=kOutput, calls=%fused_computation.7 | convolution fusion | flops 842137600 | bytes 8847360 | tf_op jit(solution)/shard_map/dot_general | solution.py:15
  164.4 4.8 %convolution_convert_fusion.1 = bf16[1280,2560]{1,0:T(8,128)(2,1)} fusion(bf16[128,2560]{1,0:T(8,128)(2,1)S(1)} %fusion.1, f32[128,1280]{1,0:T(8,128)S(1)} %get-tuple-element.32, f32[1280]{0:T(1024)S(1)} %convert_element_type.92, f32[128]{0:T(128)S(1)} %add_rsqrt_fusion, f32[128]{0:T(128)S(1)} %broadcast_multiply_fusion.3), kind=kOutput, calls=%fused_computation.5 | convolution fusion | flops 842792960 | bytes 7870464 | tf_op jit(solution)/shard_map/dot_general | solution.py:15
  169.3 0.0 reduce-scatter.15.cloned.1.call-start
  169.3 64.7 %reduce-scatter.11.cloned.1.call-done = bf16[320,1280]{1,0:T(8,128)(2,1)} async-done(((bf16[2560,1280]{1,0:T(8,128)(2,1)}), bf16[320,1280]{1,0:T(8,128)(2,1)}) %reduce-scatter.11.cloned.1.call-update) | async-done | bytes 819216 | tf_op jit(solution)/shard_map/reduce_scatter | solution.py:136
  234.0 2.2 copy.78
  236.2 0.0 reduce-scatter.13.cloned.1.call-start
  236.2 5.2 %multiply_reduce_fusion = (f32[1280]{0:T(1024)S(1)}, f32[128]{0:T(128)S(1)}, f32[128]{0:T(128)S(1)}, f32[128,1280]{1,0:T(8,128)S(1)}) fusion(f32[128,1280]{1,0:T(8,128)S(1)} %get-tuple-element.32, f32[128]{0:T(128)S(1)} %add_rsqrt_fusion, f32[128]{0:T(128)S(1)} %broadcast_multiply_fusion.3, f32[1280]{0:T(1024)S(1)} %convert_element_type.92, ...), kind=kOutput, calls=%fused_computation.26 | convolution fusion | flops 840169984 | bytes 8531968 | tf_op jit(solution)/shard_map/dot_general | solution.py:15
  241.4 0.4 add_convert_fusion
  241.8 0.2 copy.55
  242.0 64.8 %reduce-scatter.9.cloned.1.call-done = bf16[160,2560]{1,0:T(8,128)(2,1)} async-done(((bf16[1280,2560]{1,0:T(8,128)(2,1)}), bf16[160,2560]{1,0:T(8,128)(2,1)}) %reduce-scatter.9.cloned.1.call-update) | async-done | bytes 819216 | tf_op jit(solution)/shard_map/reduce_scatter | solution.py:133
  306.8 2.3 copy.76
  309.2 0.5 convolution_convert_fusion.4
  309.7 0.9 copy.62
  310.6 0.1 fusion.9
  310.7 0.4 fusion.8
  311.1 0.6 copy-done.4
  311.7 0.3 convolution_convert_fusion.2
  312.0 0.9 copy.60
  312.9 0.5 convolution_convert_fusion.5
  313.4 0.9 copy.61
  314.3 37.9 %psum.7 = f32[1280]{0:T(1024)S(1)} all-reduce(f32[1280]{0:T(1024)S(1)} %get-tuple-element.28), channel_id=1, replica_groups=mesh['seq'=8,'dp'=4] {'seq','dp'}, use_global_device_ids=true, to_apply=%region_17.18 | all-reduce | flops 1280 | bytes 10240 | tf_op jit(solution)/shard_map/psum | solution.py:149
  352.3 0.6 broadcast_multiply_fusion
  352.9 1.1 copy.79
  354.0 0.7 multiply_convert_fusion.3
  354.8 13.7 %reduce-scatter.13.cloned.1.call-done = bf16[640,160]{1,0:T(8,128)(2,1)} async-done(((bf16[2560,160]{1,0:T(8,128)(2,1)}), bf16[640,160]{1,0:T(8,128)(2,1)}) %reduce-scatter.13.cloned.1.call-update) | async-done | bytes 204816
  368.4 1.1 copy.77
  369.6 0.7 multiply_convert_fusion.4
  (59 shorter events, 0.4 us)
Async XLA Ops:
  7.2 15.0 %copy-start = (bf16[1,192,1280]{2,1,0:T(8,128)(2,1)S(1)}, bf16[1,192,1280]{2,1,0:T(8,128)(2,1)}, u32[]{:S(2)}) copy-start(bf16[1,192,1280]{2,1,0:T(8,128)(2,1)} %param.14) | copy-start | bytes 1474564
  7.2 1.5 copy-start.14
  7.2 10.8 %copy-start.16 = (s32[1,2,2]{2,1,0:T(2,128)S(1)}, s32[1,2,2]{2,1,0:T(2,128)}, u32[]{:S(2)}) copy-start(s32[1,2,2]{2,1,0:T(2,128)} %param.16) | copy-start | bytes 52
  7.2 11.0 %copy-start.8 = (bf16[1,128,1280]{2,1,0:T(8,128)(2,1)S(1)}, bf16[1,128,1280]{2,1,0:T(8,128)(2,1)}, u32[]{:S(2)}) copy-start(bf16[1,128,1280]{2,1,0:T(8,128)(2,1)} %param.10) | copy-start | bytes 983044
  7.2 77.9 %all-gather.5.cloned.1.call-start = ((), (), s32[]{:S(2)}) async-start(), calls=%async_computation.7 | async-start | bytes 8192000 | tf_op jit(solution)/shard_map/all_gather | solution.py:40
  7.9 10.5 %copy-start.9 = (bf16[1,128,1280]{2,1,0:T(8,128)(2,1)S(1)}, bf16[1,128,1280]{2,1,0:T(8,128)(2,1)}, u32[]{:S(2)}) copy-start(bf16[1,128,1280]{2,1,0:T(8,128)(2,1)} %param.11) | copy-start | bytes 983044
  8.0 10.8 %copy-start.10 = (bf16[1,128,1280]{2,1,0:T(8,128)(2,1)S(1)}, bf16[1,128,1280]{2,1,0:T(8,128)(2,1)}, u32[]{:S(2)}) copy-start(bf16[1,128,1280]{2,1,0:T(8,128)(2,1)} %param.12) | copy-start | bytes 983044
  8.0 151.3 %all-gather.3.cloned.1.call-start = ((), (), s32[]{:S(2)}) async-start(), calls=%async_computation.6 | async-start | bytes 8192000 | tf_op jit(solution)/shard_map/all_gather | solution.py:41
  11.6 12.9 %all-to-all-start = ((s32[8,1,32]{2,1,0:T(1,128)}), s32[8,1,32]{2,1,0:T(1,128)S(1)}, u32[]{:S(2)}, u32[]{:S(2)}) async-start(s32[8,1,32]{2,1,0:T(1,128)} %all_to_all.9), calls=%async_computation | async-start | bytes 8192 | tf_op jit(solution)/shard_map/all_to_all | solution.py:68
  18.5 2.0 copy-start.1
  18.7 1.8 copy-start.3
  19.0 1.5 copy-start.11
  22.2 7.7 %copy-start.6 = (bf16[16,128,80]{1,2,0:T(8,128)(2,1)}, bf16[16,128,80]{1,2,0:T(8,128)(2,1)S(1)}, u32[]{:S(2)}) copy-start(bf16[16,128,80]{1,2,0:T(8,128)(2,1)S(1)} %convolution_convert_fusion.3) | copy-start | bytes 983044
  24.5 5.4 %copy-start.17 = (u32[32]{0:T(128)S(1)}, u32[32]{0:T(128)}, u32[]{:S(2)}) copy-start(u32[32]{0:T(128)} %constant.86) | copy-start | bytes 388
  24.5 6.6 %copy-start.15 = (bf16[320]{0:T(512)(128)(2,1)S(1)}, bf16[320]{0:T(512)(128)(2,1)}, u32[]{:S(2)}) copy-start(bf16[320]{0:T(512)(128)(2,1)} %param.19) | copy-start | bytes 1924
  24.6 23.4 %all-to-all-start.1 = ((bf16[8,32,1280]{2,1,0:T(8,128)(2,1)}), bf16[8,32,1280]{2,1,0:T(8,128)(2,1)S(1)}, u32[]{:S(2)}, u32[]{:S(2)}) async-start(bf16[8,32,1280]{2,1,0:T(8,128)(2,1)} %bitcast.15), calls=%async_computation.1 | async-start | bytes 1310720 | tf_op jit(solution)/shard_map/all_to_all | solution.py:61
  29.8 12.0 %copy-start.13 = (bf16[1,128,1280]{2,1,0:T(8,128)(2,1)S(1)}, bf16[1,128,1280]{2,1,0:T(8,128)(2,1)}, u32[]{:S(2)}) copy-start(bf16[1,128,1280]{2,1,0:T(8,128)(2,1)} %param.13) | copy-start | bytes 983044
  29.8 204.2 %reduce-scatter.11.cloned.1.call-start = ((), (), s32[]{:S(2)}) async-start(), calls=%async_computation.9 | async-start | bytes 7372800 | tf_op jit(solution)/shard_map/reduce_scatter | solution.py:136
  93.7 213.1 %reduce-scatter.9.cloned.1.call-start = ((), (), s32[]{:S(2)}) async-start(), calls=%async_computation.8 | async-start | bytes 7372800 | tf_op jit(solution)/shard_map/reduce_scatter | solution.py:133
  169.3 183.6 %reduce-scatter.15.cloned.1.call-start = ((), (), s32[]{:S(2)}) async-start(), calls=%async_computation.11 | async-start | bytes 1228800
  236.2 132.2 %reduce-scatter.13.cloned.1.call-start = ((), (), s32[]{:S(2)}) async-start(), calls=%async_computation.10 | async-start | bytes 1638400
  241.8 67.3 %copy-start.5 = (bf16[128,1280]{1,0:T(8,128)(2,1)}, bf16[128,1280]{1,0:T(8,128)(2,1)S(1)}, u32[]{:S(2)}) copy-start(bf16[128,1280]{1,0:T(8,128)(2,1)S(1)} %add_convert_fusion) | copy-start | bytes 983044
  242.0 67.1 %copy-start.18 = (f32[16,128,128]{1,2,0:T(8,128)S(1)}, f32[16,128,128]{1,2,0:T(8,128)}, u32[]{:S(2)}) copy-start(f32[16,128,128]{1,2,0:T(8,128)} %get-tuple-element.36) | copy-start | bytes 3145732
  309.2 1.4 copy-start.7
  309.7 1.0 copy-start.12
  310.7 1.0 copy-start.4
  311.7 1.2 copy-start.2
Sparse Core Ops, SparseCore 0:
  9.9 75.1 all-gather.4
  86.9 72.3 all-gather.2
  161.6 72.2 reduce-scatter.10
  236.1 70.6 reduce-scatter.8
  309.6 26.1 reduce-scatter.14
  338.6 29.8 reduce-scatter.12
where the time goes:
time: 378 us; the launch traced here: 377 us
  waiting for transfers between devices  250 us (66%)
  blocking collectives  48.1 us (13%)
  matrix products  28.6 us (8%)
  local copies, waits for them, and re-layouts  19.2 us (5%)
  between operations  15.2 us (4%)
  starting transfers between devices  12 us (3%)
  other arithmetic  4.42 us (1%)
    all_gather x1, waiting for transfers between devices, per_device(): lax.all_gather(w_down, 'dp', axis=0, tiled=True)  65.4 us
    reduce_scatter x1, waiting for transfers between devices, per_device(): lax.psum_scatter(up_term.astype(jnp.bfloat16), 'seq', scatter_dimension=0...  64.8 us
    reduce_scatter x1, waiting for transfers between devices, per_device(): lax.psum_scatter(down_term.astype(jnp.bfloat16), 'seq', scatter_dimension...  64.7 us
    psum x1, blocking collectives, per_device(): gain_total = lax.psum(gain_term, ('seq', 'dp'))  37.9 us
    all_gather x1, waiting for transfers between devices, per_device(): lax.all_gather(w_up, 'dp', axis=0, tiled=True)  35.4 us
    dot_general x4, matrix products, contract(): lax.dot_general(left, right, (((left_dim,), (right_dim,)), ((), ())), pre...  19.7 us
    unnamed x8, waiting for transfers between devices  15.1 us
    unnamed x51, local copies, waits for them, and re-layouts  11.7 us
  transfers between devices with their start and end apart: 8, of which 6 were waited for; matrix products, arithmetic and copies ran while one was open for 13% of the time, Pallas kernels for 0%

commit v1 on v0

v1 whole, which is shorter than its diff:
```python
import math

import jax
import jax.numpy as jnp
from jax import lax
from jax.sharding import PartitionSpec as P

HEADS = 16
HDIM = 80
BLK = 64
PIECE = 16
CORES = 2


def contract(left, right, left_dim, right_dim):
    return lax.dot_general(
        left, right, (((left_dim,), (right_dim,)), ((), ())), preferred_element_type=jnp.float32
    )


def pick(blocks, index):
    return lax.dynamic_index_in_dim(blocks, index, 0, keepdims=False)


def swap_dp(block, count, step):
    return lax.ppermute(block, "dp", [(i, i ^ step) for i in range(count)])


def swap_seq(block, count, step):
    return lax.ppermute(block, "seq", [(i, i ^ step) for i in range(count)])


def gather_up(w_up, n_dp, n_seq, dp, core):
    rows, ff = w_up.shape
    cols, half = ff // n_dp, rows // CORES
    own = lax.dynamic_slice(w_up, (0, dp * cols), (rows, cols))
    got = []
    for k in range(1, n_dp):
        piece = lax.dynamic_slice(w_up, (core * half, (dp ^ k) * cols), (half, cols))
        got.append(swap_dp(piece, n_dp, k))
    mine = jnp.stack(got)
    mate = swap_seq(mine, n_seq, 1)
    low = jnp.where(core == 0, mine, mate)
    high = jnp.where(core == 0, mate, mine)
    pairs = jnp.concatenate([low, high], axis=1)
    full = jnp.concatenate([own[None], pairs], axis=0)
    order = dp ^ jnp.arange(n_dp)
    return full[order].reshape(n_dp * rows, cols)


def gather_gain(norm_gain, n_dp, dp):
    parts = jnp.stack(
        [norm_gain] + [swap_dp(norm_gain, n_dp, k) for k in range(1, n_dp)]
    )
    return parts[dp ^ jnp.arange(n_dp)].reshape(-1)


def owner_rows(llm_rows, slot_ids, n_seq, tokens):
    length, feat = llm_rows.shape
    per_owner = tokens // PIECE
    capacity = 1 + (per_owner + n_seq - 2) // n_seq
    first = slot_ids.reshape(length // PIECE, PIECE)[:, 0]
    tile = jnp.where(first >= 0, first // PIECE, n_seq * per_owner)
    owner = tile // per_owner
    place = tile % per_owner
    onehot = (owner[:, None] == jnp.arange(n_seq)[None, :]).astype(jnp.int32)
    rank = jnp.sum((jnp.cumsum(onehot, axis=0) - 1) * onehot, axis=1)
    target = jnp.where(first >= 0, owner * capacity + rank, -1)
    row_in = jnp.arange(length) % PIECE
    target_row = jnp.repeat(target * PIECE, PIECE) + row_in
    place_row = jnp.repeat(place * PIECE, PIECE) + row_in
    slots = n_seq * capacity * PIECE
    select = (target_row[None, :] == jnp.arange(slots)[:, None]).astype(jnp.bfloat16)
    tag = jnp.where(jnp.arange(128)[None, :] == 0, jnp.repeat(place + 1, PIECE)[:, None], 0)
    wide = jnp.concatenate([llm_rows, tag.astype(jnp.bfloat16)], axis=1)
    send = contract(select, wide, 1, 0).astype(jnp.bfloat16)
    got = lax.all_to_all(
        send.reshape(n_seq, capacity * PIECE, feat + 128),
        "seq",
        split_axis=0,
        concat_axis=0,
        tiled=True,
    ).reshape(slots, feat + 128)
    tile_got = got[:, feat : feat + 1].astype(jnp.int32) - 1
    row_got = tile_got * PIECE + (jnp.arange(slots) % PIECE)[:, None]
    place_got = jnp.where(tile_got >= 0, row_got, -1)
    landing = (place_got == jnp.arange(tokens)[None, :]).astype(jnp.bfloat16)
    return contract(landing, got[:, :feat], 0, 0).astype(jnp.bfloat16)


def gather_tokens(block, n_dp):
    return jnp.concatenate([block] + [swap_dp(block, n_dp, k) for k in range(1, n_dp)], axis=0)


def scatter_up(term, n_seq, seq):
    n_z, core, z = n_seq // CORES, seq % CORES, seq // CORES
    rows, cols = term.shape
    pieces = term.reshape(n_z, CORES, rows // n_seq, cols)
    keep = lax.dynamic_index_in_dim(pieces, core, 1, keepdims=False)
    give = lax.dynamic_index_in_dim(pieces, 1 - core, 1, keepdims=False)
    both = (
        keep.astype(jnp.float32) + swap_seq(give.astype(jnp.bfloat16), n_seq, 1).astype(jnp.float32)
    ).astype(jnp.bfloat16)
    total = pick(both, z).astype(jnp.float32)
    for k in reversed(range(1, n_z)):
        total = total + swap_seq(pick(both, z ^ k), n_seq, CORES * k).astype(jnp.float32)
    return total


def scatter_down(term, n_seq, n_dp, seq, dp):
    n_z, core, z = n_seq // CORES, seq % CORES, seq // CORES
    rows, cols = term.shape
    n_h, width = n_seq // n_dp, cols // n_dp
    if n_h != CORES:
        return scatter_down_direct(term, n_seq, n_dp, seq)
    half = rows // CORES
    keep = lax.dynamic_slice(term, (core * half, 0), (half, cols))
    give = lax.dynamic_slice(term, ((1 - core) * half, 0), (half, cols))
    both = (
        keep.astype(jnp.float32) + swap_seq(give.astype(jnp.bfloat16), n_seq, 1).astype(jnp.float32)
    ).astype(jnp.bfloat16)
    pieces = both.reshape(half, n_dp, width).transpose(1, 0, 2)
    planes = jnp.stack(
        [pick(pieces, dp)] + [swap_dp(pick(pieces, dp ^ k), n_dp, k) for k in range(1, n_dp)]
    )
    total = pick(planes, dp ^ z).astype(jnp.float32)
    for k in reversed(range(1, n_z)):
        total = total + swap_seq(pick(planes, dp ^ z ^ k), n_seq, CORES * k).astype(jnp.float32)
    return total


def scatter_down_direct(term, n_seq, n_dp, seq):
    n_z, core, z = n_seq // CORES, seq % CORES, seq // CORES
    rows, cols = term.shape
    n_h, n_e = n_seq // n_dp, n_dp // CORES
    half = cols // CORES
    keep = lax.dynamic_slice(term, (0, core * half), (rows, half))
    give = lax.dynamic_slice(term, (0, (1 - core) * half), (rows, half))
    both = keep + swap_seq(give.astype(jnp.bfloat16), n_seq, 1).astype(jnp.float32)
    pieces = (
        both.reshape(n_h, rows // n_h, n_e, half // n_e)
        .transpose(0, 2, 1, 3)
        .reshape(n_z, rows // n_h, half // n_e)
        .astype(jnp.bfloat16)
    )
    total = 0.0
    for j in range(n_z):
        pairs = []
        for a in range(n_z):
            m = (a + j) % n_z
            for c in range(CORES):
                for d in range(n_dp):
                    source = (a * CORES + c) * n_dp + d
                    goal = (d * n_h + m // n_e) * n_dp + c * n_e + m % n_e
                    pairs.append((source, goal))
        block = lax.ppermute(pick(pieces, (z + j) % n_z), ("seq", "dp"), pairs)
        total = total + block.astype(jnp.float32)
    return total


def sum_all(term, n_seq, n_dp):
    total = term + swap_seq(term, n_seq, 1)
    term = total
    for k in range(1, n_seq // CORES):
        total = total + swap_seq(term, n_seq, CORES * k)
    term = total
    for k in range(1, n_dp):
        total = total + swap_dp(term, n_dp, k)
    return total


def per_device(
    queries,
    key_rows,
    value_rows,
    resid_in,
    llm_grad,
    vision_slot,
    window_mask,
    w_up,
    w_down,
    norm_gain,
):
    n_seq = lax.axis_size("seq")
    n_dp = lax.axis_size("dp")
    seq = lax.axis_index("seq")
    dp = lax.axis_index("dp")
    core = seq % CORES
    query = queries[0]
    key_block = key_rows[0]
    value_block = value_rows[0]
    tokens, feat_dim = query.shape
    att_scale = 1.0 / math.sqrt(HDIM)

    grad_rows = owner_rows(llm_grad[0], vision_slot[0], n_seq, tokens)
    gain_full = gather_gain(norm_gain, n_dp, dp)
    up_cols = gather_up(w_up, n_dp, n_seq, dp, core)

    allowed = jnp.repeat(jnp.repeat(window_mask[0] > 0, BLK, axis=0), BLK, axis=1)
    q_heads = query.reshape(tokens, HEADS, HDIM)
    k_heads = key_block.reshape(tokens, HEADS, HDIM)
    v_heads = value_block.reshape(tokens, HEADS, HDIM)
    scores = (
        jnp.einsum("qhd,khd->hqk", q_heads, k_heads, preferred_element_type=jnp.float32) * att_scale
    )
    masked = jnp.where(allowed[None], scores, -jnp.inf)
    highest = jnp.max(masked, axis=2, keepdims=True)
    exp_terms = jnp.where(allowed[None], jnp.exp(masked - highest), 0.0)
    attn_probs = exp_terms / jnp.sum(exp_terms, axis=2, keepdims=True)
    probs_low = attn_probs.astype(jnp.bfloat16)
    attn_heads = jnp.einsum(
        "hqk,khd->qhd", probs_low, v_heads, preferred_element_type=jnp.float32
    ).astype(jnp.bfloat16)
    attn_out = attn_heads.reshape(tokens, feat_dim)
    hidden = resid_in[0].astype(jnp.float32) + attn_out.astype(jnp.float32)
    center = jnp.mean(hidden, axis=1, keepdims=True)
    variance = jnp.mean(jnp.square(hidden - center), axis=1, keepdims=True)
    inverse = lax.rsqrt(variance + 1e-06)
    normal_unit = (hidden - center) * inverse
    gain_wide = gain_full.astype(jnp.float32)
    normed = (normal_unit * gain_wide).astype(jnp.bfloat16)

    normed_all = gather_tokens(normed, n_dp)
    rows_all = gather_tokens(grad_rows, n_dp)
    pre_act = contract(normed_all, up_cols, 1, 0)
    sig_gate = jax.nn.sigmoid(1.702 * pre_act)
    act_low = (pre_act * sig_gate).astype(jnp.bfloat16)
    d_act = contract(rows_all, w_down, 1, 1)
    d_pre = (d_act * (sig_gate + 1.702 * pre_act * sig_gate * (1.0 - sig_gate))).astype(
        jnp.bfloat16
    )
    d_part = contract(d_pre, up_cols, 1, 1)
    d_normed = d_part[:tokens]
    for k in range(1, n_dp):
        block = d_part[k * tokens : (k + 1) * tokens].astype(jnp.bfloat16)
        d_normed = d_normed + swap_dp(block, n_dp, k).astype(jnp.float32)

    up_term = contract(normed_all, d_pre, 0, 0)
    down_term = contract(act_low, rows_all, 0, 0)
    up_panel = scatter_up(up_term, n_seq, seq)
    down_panel = scatter_down(down_term, n_seq, n_dp, seq, dp)

    gain_term = jnp.sum(d_normed * normal_unit, axis=0)
    d_unit = d_normed * gain_wide
    d_hidden = inverse * (
        d_unit
        - jnp.mean(d_unit, axis=1, keepdims=True)
        - normal_unit * jnp.mean(d_unit * normal_unit, axis=1, keepdims=True)
    )
    grad_resid = (grad_rows.astype(jnp.float32) + d_hidden).astype(jnp.bfloat16)
    grad_heads = grad_resid.reshape(tokens, HEADS, HDIM)
    grad_value = jnp.einsum(
        "hqk,qhd->khd", probs_low, grad_heads, preferred_element_type=jnp.float32
    ).astype(jnp.bfloat16)
    d_probs = jnp.einsum("qhd,khd->hqk", grad_heads, v_heads, preferred_element_type=jnp.float32)
    delta = jnp.einsum("qhd,qhd->hq", grad_heads, attn_heads, preferred_element_type=jnp.float32)
    d_scores = (attn_probs * (d_probs - delta[:, :, None]) * att_scale).astype(jnp.bfloat16)
    grad_query = jnp.einsum(
        "hqk,khd->qhd", d_scores, k_heads, preferred_element_type=jnp.float32
    ).astype(jnp.bfloat16)
    grad_key = jnp.einsum(
        "hqk,qhd->khd", d_scores, q_heads, preferred_element_type=jnp.float32
    ).astype(jnp.bfloat16)
    factor = 1.0 / math.sqrt(n_dp * n_seq * tokens)
    gain_total = sum_all(gain_term, n_seq, n_dp)
    return (
        grad_query.reshape(1, tokens, feat_dim),
        grad_key.reshape(1, tokens, feat_dim),
        grad_value.reshape(1, tokens, feat_dim),
        grad_resid[None],
        (up_panel * factor).astype(jnp.bfloat16),
        (down_panel * factor).astype(jnp.bfloat16),
        gain_total * factor,
    )


def solution(mesh):
    in_specs = (
        P("dp", "seq", None),
        P("dp", "seq", None),
        P("dp", "seq", None),
        P("dp", "seq", None),
        P("dp", "seq", None),
        P("dp", "seq"),
        P("dp", "seq", None),
        P("dp", None),
        P("dp", None),
        P("dp"),
    )
    out_specs = (
        P("dp", "seq", None),
        P("dp", "seq", None),
        P("dp", "seq", None),
        P("dp", "seq", None),
        P("seq", "dp"),
        P("seq", "dp"),
        P(),
    )
    return jax.shard_map(
        per_device, mesh=mesh, in_specs=in_specs, out_specs=out_specs, check_vma=False
    )
```

time: 378 us -> 164 us (0.43)
  waiting for transfers between devices: 250 us -> 52.7 us
  blocking collectives: 48.1 us -> 0 us
  starting transfers between devices: 12 us -> 51.9 us
  between operations: 15.2 us -> 1.22 us
  other arithmetic: 4.42 us -> 15.8 us
  matrix products: 28.6 us -> 18.2 us
  local copies, waits for them, and re-layouts: 19.2 us -> 23.1 us
    reduce_scatter x2 -> x0, waiting for transfers between devices: 129 us -> none  [the longest x1 64.8 us: per_device(): lax.psum_scatter(up_term.astype(jnp.bfloat16), 'seq', scatter_dimension=0...]
    all_gather x2 -> x0, waiting for transfers between devices: 101 us -> none  [the longest x1 65.4 us: per_device(): lax.all_gather(w_down, 'dp', axis=0, tiled=True)]
    ppermute x0 -> x34, waiting for transfers between devices: none -> 52.7 us  [the longest x21 30.7 us: swap_dp(): return lax.ppermute(block, 'dp', [(i, i ^ step) for i in range(count)])]
    ppermute x0 -> x34, starting transfers between devices: none -> 47 us  [the longest x21 26.3 us: swap_dp(): return lax.ppermute(block, 'dp', [(i, i ^ step) for i in range(count)])]
    psum x1 -> x0, blocking collectives: 37.9 us -> none  [per_device(): gain_total = lax.psum(gain_term, ('seq', 'dp'))]
    unnamed x8 -> x0, waiting for transfers between devices: 15.1 us -> none
    unnamed x1 -> x0, blocking collectives: 10.1 us -> none
    dot_general x4 -> x7, matrix products: 19.7 us -> 11.9 us  [contract(): lax.dot_general(left, right, (((left_dim,), (right_dim,)), ((), ())), pre...]
  transfers between devices with their start and end apart: 8 -> 35, of which waited for: 6 -> 15; matrix products, arithmetic and copies ran while one was open for 13% -> 31% of each run, Pallas kernels for 0% -> 0%
where the time goes in v1:
time: 164 us; the launch traced here: 163 us
  waiting for transfers between devices  52.7 us (32%)
  starting transfers between devices  51.9 us (32%)
  local copies, waits for them, and re-layouts  23.1 us (14%)
  matrix products  18.2 us (11%)
  other arithmetic  15.8 us (10%)
    ppermute x21, waiting for transfers between devices, swap_dp(): return lax.ppermute(block, 'dp', [(i, i ^ step) for i in range(count)])  30.7 us
    ppermute x21, starting transfers between devices, swap_dp(): return lax.ppermute(block, 'dp', [(i, i ^ step) for i in range(count)])  26.3 us
    ppermute x13, waiting for transfers between devices, swap_seq(): return lax.ppermute(block, 'seq', [(i, i ^ step) for i in range(count)])  22 us
    ppermute x13, starting transfers between devices, swap_seq(): return lax.ppermute(block, 'seq', [(i, i ^ step) for i in range(count)])  20.8 us
    dot_general x7, matrix products, contract(): lax.dot_general(left, right, (((left_dim,), (right_dim,)), ((), ())), pre...  11.9 us
    unnamed x48, local copies, waits for them, and re-layouts  8.7 us
    all_to_all x1, starting transfers between devices, owner_rows(): lax.all_to_all(send.reshape(n_seq, capacity * PIECE, feat + 128), 'seq',...  4.88 us
    gather x1, local copies, waits for them, and re-layouts, gather_up(): return full[order].reshape(n_dp * rows, cols)  3.33 us
  transfers between devices with their start and end apart: 35, of which 15 were waited for; matrix products, arithmetic and copies ran while one was open for 31% of the time, Pallas kernels for 0%

profile of v1, /device:TPU:0, one launch (start us, length us, event | category | flops | bytes accessed | tf_op | source)
XLA Modules:
  0.0 162.9 jit_solution(7763571247577819946)
XLA Ops:
  0.6 3.0 %collective-permute-start.3 = (bf16[320]{0:T(512)(128)(2,1)}, bf16[320]{0:T(512)(128)(2,1)S(1)}, u32[]{:S(2)}, u32[]{:S(2)}) collective-permute-start(bf16[320]{0:T(512)(128)(2,1)} %param.19), channel_id=1, source_target_pairs={{0,1},{1,0},{2,3},{3,2},{4,5},{5,4},{6,7},{7,6},{8,9},{9,8},{10,11... | collective-permute-start | bytes 1928 | tf_op jit(solution)/shard_map/ppermute | solution.py:26
  3.7 1.5 collective-permute-start.5
  5.1 2.0 %fusion.61 = (bf16[160,640]{1,0:T(8,128)(2,1)}, bf16[160,640]{1,0:T(8,128)(2,1)}, bf16[160,640]{1,0:T(8,128)(2,1)}) fusion(bf16[320,2560]{1,0:T(8,128)(2,1)} %param.17, s32[]{:T(128)S(6)} %select_n.193, s32[]{:T(128)S(6)} %select_n.194, s32[]{:T(128)S(6)} %select_n.196, s32[]{:T(128)S(6)} %select_n.195), kind=kLoop, calls=%fused_computation.152 | loop fusion | bytes 1228816 | tf_op jit(solution)/shard_map/dynamic_slice | solution.py:39
  7.1 1.5 collective-permute-start.9
  8.6 2.0 %collective-permute-start.10 = (bf16[160,640]{1,0:T(8,128)(2,1)}, bf16[160,640]{1,0:T(8,128)(2,1)}, u32[]{:S(2)}, u32[]{:S(2)}) collective-permute-start(bf16[160,640]{1,0:T(8,128)(2,1)} %get-tuple-element.45), channel_id=1, source_target_pairs={{0,2},{1,3},{2,0},{3,1},{4,6},{5,7},{6,4},{7,5},{8,10},{9,11},{10,... | collective-permute-start | bytes 614408 | tf_op jit(solution)/shard_map/ppermute | solution.py:26
  11.1 1.3 reduce.7
  13.3 2.3 %convolution_convert_fusion = bf16[256,1408]{1,0:T(8,128)(2,1)} fusion(bf16[192,128]{1,0:T(8,128)(2,1)S(1)} %select_convert_fusion, bf16[192,1280]{1,0:T(8,128)(2,1)} %bitcast.146, s32[192]{0:T(256)S(1)} %fusion.42), kind=kOutput, calls=%fused_computation.3 | convolution fusion | flops 139902976 | bytes 1262336 | tf_op jit(solution)/shard_map/dot_general | solution.py:16
  15.6 4.9 %all-to-all-start = ((bf16[8,32,1408]{2,1,0:T(8,128)(2,1)}), bf16[8,32,1408]{2,1,0:T(8,128)(2,1)S(1)}, u32[]{:S(2)}, u32[]{:S(2)}) async-start(bf16[8,32,1408]{2,1,0:T(8,128)(2,1)} %bitcast.134), calls=%async_computation | async-start | bytes 1441792 | tf_op jit(solution)/shard_map/all_to_all | solution.py:77
  21.3 2.0 %copy.82 = bf16[1,128,1280]{1,2,0:T(8,128)(2,1)} copy(bf16[1,128,1280]{2,1,0:T(8,128)(2,1)} %param.12) | data formatting | bytes 655360 | tf_op args[2]
  23.3 1.0 dynamic-slice_bitcast_fusion
  24.3 1.5 fusion.63
  25.8 1.7 %convolution_convert_fusion.3 = bf16[16,128,80]{1,2,0:T(8,128)(2,1)S(1)} fusion(bf16[128,16,80]{0,2,1:T(8,128)(2,1)} %bitcast.135, f32[16,128,128]{1,2,0:T(8,128)} %get-tuple-element.62, f32[16,128]{1,0:T(8,128)S(1)} %get-tuple-element.61), kind=kOutput, calls=%fused_computation.27 | convolution fusion | flops 42631168 | bytes 1712128 | tf_op jit(solution)/shard_map/hqk,khd->qhd/dot_general | solution.py:211
  28.3 1.1 copy.84
  29.4 1.3 fusion.60
  31.5 2.1 %pad_maximum_fusion.3 = bf16[3,160,640]{2,1,0:T(8,128)(2,1)} fusion(bf16[1,160,640]{2,1,0:T(8,128)(2,1)} %bitcast.19, bf16[1,160,640]{2,1,0:T(8,128)(2,1)} %bitcast.18, bf16[1,160,640]{2,1,0:T(8,128)(2,1)} %bitcast.17), kind=kLoop, calls=%fused_computation.48 | loop fusion | flops 614400 | bytes 1228800 | tf_op jit(solution)/shard_map/stack | solution.py:41
  35.3 0.9 multiply_convert_fusion.2
  36.1 1.8 %collective-permute-start.8 = (bf16[128,1280]{1,0:T(8,128)(2,1)}, bf16[128,1280]{1,0:T(8,128)(2,1)}, u32[]{:S(2)}, u32[]{:S(2)}) collective-permute-start(bf16[128,1280]{1,0:T(8,128)(2,1)} %multiply_convert_fusion.2), channel_id=1, source_target_pairs={{0,3},{1,2},{2,1},{3,0},{4,7},{5,6},{6,5},{7,4},{8,11},{9,10},{10,... | collective-permute-start | bytes 983048 | tf_op jit(solution)/shard_map/ppermute | solution.py:26
  38.0 1.1 collective-permute-start.7
  39.6 1.4 broadcast_select_fusion.1
  41.1 1.4 maximum_maximum_fusion
  42.4 3.3 %gather_fusion.1 = bf16[4,320,640]{2,1,0:T(8,128)(2,1)} fusion(bf16[4,320,640]{2,1,0:T(8,128)(2,1)} %maximum_maximum_fusion, s32[1024]{0:T(1024)S(1)} %pad_clamp_fusion), kind=kCustom, calls=%fused_computation.1 | custom fusion | bytes 3276816 | tf_op jit(solution)/shard_map/gather | solution.py:48
  46.3 1.9 %collective-permute-start.2 = (bf16[128,1280]{1,0:T(8,128)(2,1)S(1)}, bf16[128,1280]{1,0:T(8,128)(2,1)S(1)}, u32[]{:S(2)}, u32[]{:S(2)}) collective-permute-start(bf16[128,1280]{1,0:T(8,128)(2,1)S(1)} %convolution_convert_fusion.1), channel_id=1, source_target_pairs={{0,3},{1,2},{2,1},{3,0},{4,7},{5,6},{6,5},{7,4},{8,11},{9,10},{10,... | collective-permute-start | bytes 983048 | tf_op jit(solution)/shard_map/ppermute | solution.py:26
  48.2 1.1 collective-permute-start.1
  49.8 5.3 %collective-permute-done.7 = bf16[128,1280]{1,0:T(8,128)(2,1)} collective-permute-done((bf16[128,1280]{1,0:T(8,128)(2,1)}, bf16[128,1280]{1,0:T(8,128)(2,1)}, u32[]{:S(2)}, u32[]{:S(2)}) %collective-permute-start.7) | collective-permute-done | bytes 327712 | tf_op jit(solution)/shard_map/ppermute | solution.py:26
  55.1 3.0 %fusion.31 = f32[512,640]{1,0:T(8,128)S(1)} fusion(bf16[1280,640]{1,0:T(8,128)(2,1)} %bitcast.117, bf16[128,1280]{1,0:T(8,128)(2,1)} %collective-permute-done.8, bf16[128,1280]{1,0:T(8,128)(2,1)} %collective-permute-done.7, bf16[128,1280]{1,0:T(8,128)(2,1)} %collective-permute-done.6, bf16[128,1280]{1,0:T(8,128)(2,1)} %multiply_convert_fusion.2), kind=kOutput, calls=%fused_computation.78 | convolution fusion | flops 844103680 | bytes 4259840 | tf_op jit(solution)/shard_map/dot_general | solution.py:16
  58.1 3.9 %collective-permute-done.2 = bf16[128,1280]{1,0:T(8,128)(2,1)S(1)} collective-permute-done((bf16[128,1280]{1,0:T(8,128)(2,1)S(1)}, bf16[128,1280]{1,0:T(8,128)(2,1)S(1)}, u32[]{:S(2)}, u32[]{:S(2)}) %collective-permute-start.2) | collective-permute-done | bytes 327712 | tf_op jit(solution)/shard_map/ppermute | solution.py:26
  62.0 5.6 %collective-permute-done.1 = bf16[128,1280]{1,0:T(8,128)(2,1)S(1)} collective-permute-done((bf16[128,1280]{1,0:T(8,128)(2,1)S(1)}, bf16[128,1280]{1,0:T(8,128)(2,1)S(1)}, u32[]{:S(2)}, u32[]{:S(2)}) %collective-permute-start.1) | collective-permute-done | bytes 327712 | tf_op jit(solution)/shard_map/ppermute | solution.py:26
  67.8 1.1 fusion.11
  68.9 1.7 %copy-done.4 = f32[640,1280]{1,0:T(8,128)} copy-done((f32[640,1280]{1,0:T(8,128)}, f32[640,1280]{1,0:T(8,128)S(1)}, u32[]{:S(2)}) %copy-start.4) | copy-done | bytes 3276824
  70.5 1.0 dynamic-slice_convert_fusion
  71.6 1.4 fusion.8
  73.0 1.2 fusion.64
  74.3 1.6 collective-permute-start.13
  75.9 1.3 collective-permute-start.15
  77.9 2.5 %fusion.30 = f32[1280,640]{1,0:T(8,128)S(1)} fusion(bf16[512,640]{1,0:T(8,128)(2,1)S(1)} %fusion.8, bf16[128,1280]{1,0:T(8,128)(2,1)} %collective-permute-done.8, bf16[128,1280]{1,0:T(8,128)(2,1)} %collective-permute-done.7, bf16[128,1280]{1,0:T(8,128)(2,1)} %collective-permute-done.6, bf16[128,1280]{1,0:T(8,128)(2,1)} %multiply_convert_fusion.2), kind=kOutput, calls=%fused_computation.77 | convolution fusion | flops 844103680 | bytes 5242880 | tf_op jit(solution)/shard_map/dot_general | solution.py:16
  80.4 1.1 fusion.10
  81.5 3.4 %collective-permute-done.13 = bf16[128,1280]{1,0:T(8,128)(2,1)S(1)} collective-permute-done((bf16[128,1280]{1,0:T(8,128)(2,1)S(1)}, bf16[128,1280]{1,0:T(8,128)(2,1)S(1)}, u32[]{:S(2)}, u32[]{:S(2)}) %collective-permute-start.13) | collective-permute-done | bytes 327712 | tf_op jit(solution)/shard_map/ppermute | solution.py:26
  84.9 7.5 %collective-permute-done.15 = bf16[128,1280]{1,0:T(8,128)(2,1)S(1)} collective-permute-done((bf16[128,1280]{1,0:T(8,128)(2,1)S(1)}, bf16[128,1280]{1,0:T(8,128)(2,1)S(1)}, u32[]{:S(2)}, u32[]{:S(2)}) %collective-permute-start.15) | collective-permute-done | bytes 327712 | tf_op jit(solution)/shard_map/ppermute | solution.py:26
  92.4 1.4 collective-permute-done.14
  95.3 1.7 %fusion.9 = bf16[16,128,128]{1,2,0:T(8,128)(2,1)S(1)} fusion(bf16[128,16,80]{0,2,1:T(8,128)(2,1)S(1)} %bitcast.130, bf16[128,16,80]{0,2,1:T(8,128)(2,1)S(1)} %bitcast.136, f32[16,128]{1,0:T(8,128)S(1)} %fusion.15, f32[16,128,128]{1,2,0:T(8,128)} %get-tuple-element.62, f32[16,128]{1,0:T(8,128)S(1)} %get-tuple-element.61), kind=kOutput, calls=%fused_computation.25 | convolution fusion | flops 43253760 | bytes 2244608 | tf_op jit(solution)/shard_map/qhd,khd->hqk/dot_general | solution.py:255
  97.5 3.9 %collective-permute-start.30 = (f32[1280]{0:T(1024)S(1)}, f32[1280]{0:T(1024)S(1)}, u32[]{:S(2)}, u32[]{:S(2)}) collective-permute-start(f32[1280]{0:T(1024)S(1)} %add.262), channel_id=1, source_target_pairs={{0,24},{4,28},{8,16},{12,20},{16,8},{20,12},{24,0},{28,4},{1,25},{... | collective-permute-start | bytes 15368 | tf_op jit(solution)/shard_map/ppermute | solution.py:30
  103.1 2.9 %collective-permute-done.29 = f32[1280]{0:T(1024)S(1)} collective-permute-done((f32[1280]{0:T(1024)S(1)}, f32[1280]{0:T(1024)S(1)}, u32[]{:S(2)}, u32[]{:S(2)}) %collective-permute-start.29) | collective-permute-done | bytes 5152 | tf_op jit(solution)/shard_map/ppermute | solution.py:30
  106.0 1.6 %collective-permute-start.33 = (f32[1280]{0:T(1024)S(1)}, f32[1280]{0:T(1024)S(1)}, u32[]{:S(2)}, u32[]{:S(2)}) collective-permute-start(f32[1280]{0:T(1024)S(1)} %add_add_fusion), channel_id=1, source_target_pairs={{0,3},{1,2},{2,1},{3,0},{4,7},{5,6},{6,5},{7,4},{8,11},{9,10},{10,... | collective-permute-start | bytes 15368 | tf_op jit(solution)/shard_map/ppermute | solution.py:26
  108.3 1.3 collective-permute-start.31
  110.1 0.9 copy.97
  111.0 0.9 copy.95
  111.9 0.9 copy.96
  113.4 1.8 %add_convert_fusion = bf16[320,1280]{1,0:T(8,128)(2,1)S(1)} fusion(bf16[320,1280]{1,0:T(8,128)(2,1)} %collective-permute-done.20, f32[640,1280]{1,0:T(8,128)} %copy-done.4, s32[]{:T(128)S(6)} %select_n.206), kind=kLoop, calls=%fused_computation.9 | loop fusion | flops 1228800 | bytes 3276804 | tf_op jit(solution)/shard_map/convert_element_type | solution.py:121
  115.2 1.1 reshape.166
  116.3 2.0 %constant_dynamic-slice_fusion.3 = (bf16[320,1,320]{2,1,0:T(2,128)(2,1)S(1)}, bf16[320,1,320]{2,1,0:T(2,128)(2,1)S(1)}, bf16[320,1,320]{2,1,0:T(2,128)(2,1)S(1)}, bf16[320,1,320]{2,1,0:T(2,128)(2,1)S(1)}) fusion(bf16[320,4,320]{2,1,0:T(4,128)(2,1)S(1)} %reshape.166, s32[]{:T(128)S(6)} %select_n.208, s32[]{:T(128)S(6)} %select_n.210, s32[]{:T(128)S(6)} %select_n.209, ...), kind=kLoop, calls=%fused_computation.101 | loop fusion | bytes 1638416 | tf_op jit(solution)/shard_map/dynamic-slice
  118.5 1.6 %collective-permute-start.23 = (bf16[320,320]{1,0:T(8,128)(2,1)S(1)}, bf16[320,320]{1,0:T(8,128)(2,1)S(1)}, u32[]{:S(2)}, u32[]{:S(2)}) collective-permute-start(bf16[320,320]{1,0:T(8,128)(2,1)S(1)} %bitcast.143), channel_id=1, source_target_pairs={{0,3},{1,2},{2,1},{3,0},{4,7},{5,6},{6,5},{7,4},{8,11},{9,10},{10,... | collective-permute-start | bytes 614408 | tf_op jit(solution)/shard_map/ppermute | solution.py:26
  120.7 1.4 collective-permute-start.22
  122.0 1.4 fusion.1
  123.5 1.5 collective-permute-start.17
  125.0 1.1 collective-permute-start.19
  126.1 2.1 %collective-permute-done.23 = bf16[320,320]{1,0:T(8,128)(2,1)S(1)} collective-permute-done((bf16[320,320]{1,0:T(8,128)(2,1)S(1)}, bf16[320,320]{1,0:T(8,128)(2,1)S(1)}, u32[]{:S(2)}, u32[]{:S(2)}) %collective-permute-start.23) | collective-permute-done | bytes 204832 | tf_op jit(solution)/shard_map/ppermute | solution.py:26
  128.2 1.7 %collective-permute-start.18 = (bf16[160,640]{1,0:T(8,128)(2,1)S(1)}, bf16[160,640]{1,0:T(8,128)(2,1)S(1)}, u32[]{:S(2)}, u32[]{:S(2)}) collective-permute-start(bf16[160,640]{1,0:T(8,128)(2,1)S(1)} %get-tuple-element.60), channel_id=1, source_target_pairs={{0,16},{4,20},{8,24},{12,28},{16,0},{20,4},{24,8},{28,12},{1,17},{... | collective-permute-start | bytes 614408 | tf_op jit(solution)/shard_map/ppermute | solution.py:30
  129.9 0.8 collective-permute-done.22
  131.1 1.8 %collective-permute-start.24 = (bf16[320,320]{1,0:T(8,128)(2,1)S(1)}, bf16[320,320]{1,0:T(8,128)(2,1)S(1)}, u32[]{:S(2)}, u32[]{:S(2)}) collective-permute-start(bf16[320,320]{1,0:T(8,128)(2,1)S(1)} %get-tuple-element.51), channel_id=1, source_target_pairs={{0,24},{4,28},{8,16},{12,20},{16,8},{20,12},{24,0},{28,4},{1,25},{... | collective-permute-start | bytes 614408 | tf_op jit(solution)/shard_map/ppermute | solution.py:30
  133.5 9.3 %collective-permute-start.25 = (bf16[320,320]{1,0:T(8,128)(2,1)S(1)}, bf16[320,320]{1,0:T(8,128)(2,1)S(1)}, u32[]{:S(2)}, u32[]{:S(2)}) collective-permute-start(bf16[320,320]{1,0:T(8,128)(2,1)S(1)} %get-tuple-element.53), channel_id=1, source_target_pairs={{0,16},{4,20},{8,24},{12,28},{16,0},{20,4},{24,8},{28,12},{1,17},{... | collective-permute-start | bytes 614408 | tf_op jit(solution)/shard_map/ppermute | solution.py:30
  142.8 8.1 %collective-permute-done.18 = bf16[160,640]{1,0:T(8,128)(2,1)S(1)} collective-permute-done((bf16[160,640]{1,0:T(8,128)(2,1)S(1)}, bf16[160,640]{1,0:T(8,128)(2,1)S(1)}, u32[]{:S(2)}, u32[]{:S(2)}) %collective-permute-start.18) | collective-permute-done | bytes 204832 | tf_op jit(solution)/shard_map/ppermute | solution.py:30
  151.0 0.8 fusion.29
  151.8 10.3 %collective-permute-done.25 = bf16[320,320]{1,0:T(8,128)(2,1)S(1)} collective-permute-done((bf16[320,320]{1,0:T(8,128)(2,1)S(1)}, bf16[320,320]{1,0:T(8,128)(2,1)S(1)}, u32[]{:S(2)}, u32[]{:S(2)}) %collective-permute-start.25) | collective-permute-done | bytes 204832 | tf_op jit(solution)/shard_map/ppermute | solution.py:30
  162.1 0.8 fusion.24
  (130 shorter events, 14.9 us)
Async XLA Ops:
  0.6 71.0 %copy-start = (bf16[640,1280]{1,0:T(8,128)(2,1)S(1)}, bf16[640,1280]{1,0:T(8,128)(2,1)}, u32[]{:S(2)}) copy-start(bf16[640,1280]{1,0:T(8,128)(2,1)} %param.18) | copy-start | bytes 4915204
  0.6 33.3 %collective-permute-start.3 = (bf16[320]{0:T(512)(128)(2,1)}, bf16[320]{0:T(512)(128)(2,1)S(1)}, u32[]{:S(2)}, u32[]{:S(2)}) collective-permute-start(bf16[320]{0:T(512)(128)(2,1)} %param.19), channel_id=1, source_target_pairs={{0,1},{1,0},{2,3},{3,2},{4,5},{5,4},{6,7},{7,6},{8,9},{9,8},{10,11... | collective-permute-start | bytes 1928 | tf_op jit(solution)/shard_map/ppermute | solution.py:26
  3.7 30.3 %collective-permute-start.5 = (bf16[320]{0:T(512)(128)(2,1)}, bf16[320]{0:T(512)(128)(2,1)S(1)}, u32[]{:S(2)}, u32[]{:S(2)}) collective-permute-start(bf16[320]{0:T(512)(128)(2,1)} %param.19), channel_id=1, source_target_pairs={{0,3},{1,2},{2,1},{3,0},{4,7},{5,6},{6,5},{7,4},{8,11},{9,10},{10,... | collective-permute-start | bytes 1928 | tf_op jit(solution)/shard_map/ppermute | solution.py:26
  7.1 13.4 %copy-start.16 = (s32[1,2,2]{2,1,0:T(2,128)S(1)}, s32[1,2,2]{2,1,0:T(2,128)}, u32[]{:S(2)}) copy-start(s32[1,2,2]{2,1,0:T(2,128)} %param.16) | copy-start | bytes 52
  7.1 13.7 %copy-start.12 = (bf16[1,128,1280]{2,1,0:T(8,128)(2,1)S(1)}, bf16[1,128,1280]{2,1,0:T(8,128)(2,1)}, u32[]{:S(2)}) copy-start(bf16[1,128,1280]{2,1,0:T(8,128)(2,1)} %param.10) | copy-start | bytes 983044
  7.1 23.8 %collective-permute-start.9 = (bf16[160,640]{1,0:T(8,128)(2,1)}, bf16[160,640]{1,0:T(8,128)(2,1)}, u32[]{:S(2)}, u32[]{:S(2)}) collective-permute-start(bf16[160,640]{1,0:T(8,128)(2,1)} %get-tuple-element.43), channel_id=1, source_target_pairs={{0,1},{1,0},{2,3},{3,2},{4,5},{5,4},{6,7},{7,6},{8,9},{9,8},{10,11... | collective-permute-start | bytes 614408 | tf_op jit(solution)/shard_map/ppermute | solution.py:26
  8.6 22.9 %collective-permute-start.11 = (bf16[160,640]{1,0:T(8,128)(2,1)}, bf16[160,640]{1,0:T(8,128)(2,1)}, u32[]{:S(2)}, u32[]{:S(2)}) collective-permute-start(bf16[160,640]{1,0:T(8,128)(2,1)} %get-tuple-element.44), channel_id=1, source_target_pairs={{0,3},{1,2},{2,1},{3,0},{4,7},{5,6},{6,5},{7,4},{8,11},{9,10},{10,... | collective-permute-start | bytes 614408 | tf_op jit(solution)/shard_map/ppermute | solution.py:26
  8.6 22.9 %collective-permute-start.10 = (bf16[160,640]{1,0:T(8,128)(2,1)}, bf16[160,640]{1,0:T(8,128)(2,1)}, u32[]{:S(2)}, u32[]{:S(2)}) collective-permute-start(bf16[160,640]{1,0:T(8,128)(2,1)} %get-tuple-element.45), channel_id=1, source_target_pairs={{0,2},{1,3},{2,0},{3,1},{4,6},{5,7},{6,4},{7,5},{8,10},{9,11},{10,... | collective-permute-start | bytes 614408 | tf_op jit(solution)/shard_map/ppermute | solution.py:26
  13.3 7.7 %copy-start.13 = (bf16[1,128,1280]{2,1,0:T(8,128)(2,1)S(1)}, bf16[1,128,1280]{2,1,0:T(8,128)(2,1)}, u32[]{:S(2)}) copy-start(bf16[1,128,1280]{2,1,0:T(8,128)(2,1)} %param.11) | copy-start | bytes 983044
  15.6 30.1 %all-to-all-start = ((bf16[8,32,1408]{2,1,0:T(8,128)(2,1)}), bf16[8,32,1408]{2,1,0:T(8,128)(2,1)S(1)}, u32[]{:S(2)}, u32[]{:S(2)}) async-start(bf16[8,32,1408]{2,1,0:T(8,128)(2,1)} %bitcast.134), calls=%async_computation | async-start | bytes 1441792 | tf_op jit(solution)/shard_map/all_to_all | solution.py:77
  21.0 4.8 %copy-start.7 = (bf16[1,128,1280]{1,2,0:T(8,128)(2,1)}, bf16[1,128,1280]{1,2,0:T(8,128)(2,1)S(1)}, u32[]{:S(2)}) copy-start(bf16[1,128,1280]{1,2,0:T(8,128)(2,1)S(1)} %copy.79) | copy-start | bytes 983044
  21.3 4.6 %copy-start.5 = (bf16[1,128,1280]{1,2,0:T(8,128)(2,1)}, bf16[1,128,1280]{1,2,0:T(8,128)(2,1)S(1)}, u32[]{:S(2)}) copy-start(bf16[1,128,1280]{1,2,0:T(8,128)(2,1)S(1)} %copy.80) | copy-start | bytes 983044
  27.5 0.7 copy-start.10
  28.3 2.7 %copy-start.15 = (bf16[320]{0:T(512)(128)(2,1)S(1)}, bf16[320]{0:T(512)(128)(2,1)}, u32[]{:S(2)}) copy-start(bf16[320]{0:T(512)(128)(2,1)} %param.19) | copy-start | bytes 1924
  31.0 3.6 %collective-permute-start.4 = (bf16[320]{0:T(512)(128)(2,1)S(1)}, bf16[320]{0:T(512)(128)(2,1)S(1)}, u32[]{:S(2)}, u32[]{:S(2)}) collective-permute-start(bf16[320]{0:T(512)(128)(2,1)S(1)} %copy-done.15), channel_id=1, source_target_pairs={{0,2},{1,3},{2,0},{3,1},{4,6},{5,7},{6,4},{7,5},{8,10},{9,11},{10,... | collective-permute-start | bytes 1928 | tf_op jit(solution)/shard_map/ppermute | solution.py:26
  33.6 6.0 %collective-permute-start.12 = (bf16[3,160,640]{2,1,0:T(8,128)(2,1)}, bf16[3,160,640]{2,1,0:T(8,128)(2,1)}, u32[]{:S(2)}, u32[]{:S(2)}) collective-permute-start(bf16[3,160,640]{2,1,0:T(8,128)(2,1)} %pad_maximum_fusion.3), channel_id=1, source_target_pairs={{0,4},{4,0},{8,12},{12,8},{16,20},{20,16},{24,28},{28,24},{1,5},{5... | collective-permute-start | bytes 1843208 | tf_op jit(solution)/shard_map/ppermute | solution.py:30
  36.1 13.2 %collective-permute-start.8 = (bf16[128,1280]{1,0:T(8,128)(2,1)}, bf16[128,1280]{1,0:T(8,128)(2,1)}, u32[]{:S(2)}, u32[]{:S(2)}) collective-permute-start(bf16[128,1280]{1,0:T(8,128)(2,1)} %multiply_convert_fusion.2), channel_id=1, source_target_pairs={{0,3},{1,2},{2,1},{3,0},{4,7},{5,6},{6,5},{7,4},{8,11},{9,10},{10,... | collective-permute-start | bytes 983048 | tf_op jit(solution)/shard_map/ppermute | solution.py:26
  38.0 17.1 %collective-permute-start.7 = (bf16[128,1280]{1,0:T(8,128)(2,1)}, bf16[128,1280]{1,0:T(8,128)(2,1)}, u32[]{:S(2)}, u32[]{:S(2)}) collective-permute-start(bf16[128,1280]{1,0:T(8,128)(2,1)} %multiply_convert_fusion.2), channel_id=1, source_target_pairs={{0,2},{1,3},{2,0},{3,1},{4,6},{5,7},{6,4},{7,5},{8,10},{9,11},{10,... | collective-permute-start | bytes 983048 | tf_op jit(solution)/shard_map/ppermute | solution.py:26
  39.1 16.0 %collective-permute-start.6 = (bf16[128,1280]{1,0:T(8,128)(2,1)}, bf16[128,1280]{1,0:T(8,128)(2,1)}, u32[]{:S(2)}, u32[]{:S(2)}) collective-permute-start(bf16[128,1280]{1,0:T(8,128)(2,1)} %multiply_convert_fusion.2), channel_id=1, source_target_pairs={{0,1},{1,0},{2,3},{3,2},{4,5},{5,4},{6,7},{7,6},{8,9},{9,8},{10,11... | collective-permute-start | bytes 983048 | tf_op jit(solution)/shard_map/ppermute | solution.py:26
  46.3 15.7 %collective-permute-start.2 = (bf16[128,1280]{1,0:T(8,128)(2,1)S(1)}, bf16[128,1280]{1,0:T(8,128)(2,1)S(1)}, u32[]{:S(2)}, u32[]{:S(2)}) collective-permute-start(bf16[128,1280]{1,0:T(8,128)(2,1)S(1)} %convolution_convert_fusion.1), channel_id=1, source_target_pairs={{0,3},{1,2},{2,1},{3,0},{4,7},{5,6},{6,5},{7,4},{8,11},{9,10},{10,... | collective-permute-start | bytes 983048 | tf_op jit(solution)/shard_map/ppermute | solution.py:26
  48.2 19.4 %collective-permute-start.1 = (bf16[128,1280]{1,0:T(8,128)(2,1)S(1)}, bf16[128,1280]{1,0:T(8,128)(2,1)S(1)}, u32[]{:S(2)}, u32[]{:S(2)}) collective-permute-start(bf16[128,1280]{1,0:T(8,128)(2,1)S(1)} %convolution_convert_fusion.1), channel_id=1, source_target_pairs={{0,2},{1,3},{2,0},{3,1},{4,6},{5,7},{6,4},{7,5},{8,10},{9,11},{10,... | collective-permute-start | bytes 983048 | tf_op jit(solution)/shard_map/ppermute | solution.py:26
  49.3 18.4 %collective-permute-start = (bf16[128,1280]{1,0:T(8,128)(2,1)S(1)}, bf16[128,1280]{1,0:T(8,128)(2,1)S(1)}, u32[]{:S(2)}, u32[]{:S(2)}) collective-permute-start(bf16[128,1280]{1,0:T(8,128)(2,1)S(1)} %convolution_convert_fusion.1), channel_id=1, source_target_pairs={{0,1},{1,0},{2,3},{3,2},{4,5},{5,4},{6,7},{7,6},{8,9},{9,8},{10,11... | collective-permute-start | bytes 983048 | tf_op jit(solution)/shard_map/ppermute | solution.py:26
  68.9 1.7 %copy-start.4 = (f32[640,1280]{1,0:T(8,128)}, f32[640,1280]{1,0:T(8,128)S(1)}, u32[]{:S(2)}) copy-start(f32[640,1280]{1,0:T(8,128)S(1)} %fusion.11) | copy-start | bytes 9830404
  71.6 1.4 copy-start.1
  71.6 41.8 %collective-permute-start.20 = (bf16[320,1280]{1,0:T(8,128)(2,1)}, bf16[320,1280]{1,0:T(8,128)(2,1)}, u32[]{:S(2)}, u32[]{:S(2)}) collective-permute-start(bf16[320,1280]{1,0:T(8,128)(2,1)} %dynamic-slice_convert_fusion), channel_id=1, source_target_pairs={{0,4},{4,0},{8,12},{12,8},{16,20},{20,16},{24,28},{28,24},{1,5},{5... | collective-permute-start | bytes 2457608 | tf_op jit(solution)/shard_map/ppermute | solution.py:30
  74.3 10.6 %collective-permute-start.13 = (bf16[128,1280]{1,0:T(8,128)(2,1)S(1)}, bf16[128,1280]{1,0:T(8,128)(2,1)S(1)}, u32[]{:S(2)}, u32[]{:S(2)}) collective-permute-start(bf16[128,1280]{1,0:T(8,128)(2,1)S(1)} %get-tuple-element.46), channel_id=1, source_target_pairs={{0,1},{1,0},{2,3},{3,2},{4,5},{5,4},{6,7},{7,6},{8,9},{9,8},{10,11... | collective-permute-start | bytes 983048 | tf_op jit(solution)/shard_map/ppermute | solution.py:26
  75.9 16.5 %collective-permute-start.15 = (bf16[128,1280]{1,0:T(8,128)(2,1)S(1)}, bf16[128,1280]{1,0:T(8,128)(2,1)S(1)}, u32[]{:S(2)}, u32[]{:S(2)}) collective-permute-start(bf16[128,1280]{1,0:T(8,128)(2,1)S(1)} %get-tuple-element.47), channel_id=1, source_target_pairs={{0,3},{1,2},{2,1},{3,0},{4,7},{5,6},{6,5},{7,4},{8,11},{9,10},{10,... | collective-permute-start | bytes 983048 | tf_op jit(solution)/shard_map/ppermute | solution.py:26
  77.2 16.5 %collective-permute-start.14 = (bf16[128,1280]{1,0:T(8,128)(2,1)S(1)}, bf16[128,1280]{1,0:T(8,128)(2,1)S(1)}, u32[]{:S(2)}, u32[]{:S(2)}) collective-permute-start(bf16[128,1280]{1,0:T(8,128)(2,1)S(1)} %get-tuple-element.48), channel_id=1, source_target_pairs={{0,2},{1,3},{2,0},{3,1},{4,6},{5,7},{6,4},{7,5},{8,10},{9,11},{10,... | collective-permute-start | bytes 983048 | tf_op jit(solution)/shard_map/ppermute | solution.py:26
  80.4 13.8 %copy-start.2 = (f32[1280,640]{1,0:T(8,128)}, f32[1280,640]{1,0:T(8,128)S(1)}, u32[]{:S(2)}) copy-start(f32[1280,640]{1,0:T(8,128)S(1)} %fusion.30) | copy-start | bytes 9830404
  81.5 40.6 %collective-permute-start.16 = (bf16[4,160,640]{2,1,0:T(8,128)(2,1)}, bf16[4,160,640]{2,1,0:T(8,128)(2,1)}, u32[]{:S(2)}, u32[]{:S(2)}) collective-permute-start(bf16[4,160,640]{2,1,0:T(8,128)(2,1)} %fusion.10), channel_id=1, source_target_pairs={{0,4},{4,0},{8,12},{12,8},{16,20},{20,16},{24,28},{28,24},{1,5},{5... | collective-permute-start | bytes 2457608 | tf_op jit(solution)/shard_map/ppermute | solution.py:30
  94.2 1.0 copy-start.11
  94.2 3.3 %collective-permute-start.27 = (f32[1280]{0:T(1024)S(1)}, f32[1280]{0:T(1024)S(1)}, u32[]{:S(2)}, u32[]{:S(2)}) collective-permute-start(f32[1280]{0:T(1024)S(1)} %get-tuple-element.35), channel_id=1, source_target_pairs={{0,4},{4,0},{8,12},{12,8},{16,20},{20,16},{24,28},{28,24},{1,5},{5... | collective-permute-start | bytes 15368 | tf_op jit(solution)/shard_map/ppermute | solution.py:30
  94.3 1.0 copy-start.14
  94.6 2.3 %copy-start.9 = (bf16[128,1280]{1,0:T(8,128)(2,1)}, bf16[128,1280]{1,0:T(8,128)(2,1)S(1)}, u32[]{:S(2)}) copy-start(bf16[128,1280]{1,0:T(8,128)(2,1)S(1)} %add_convert_fusion.1) | copy-start | bytes 983044
  95.3 1.7 %copy-start.17 = (f32[16,128,128]{1,2,0:T(8,128)S(1)}, f32[16,128,128]{1,2,0:T(8,128)}, u32[]{:S(2)}) copy-start(f32[16,128,128]{1,2,0:T(8,128)} %get-tuple-element.62) | copy-start | bytes 3145732
  97.0 5.1 %copy-start.8 = (bf16[1,128,1280]{1,2,0:T(8,128)(2,1)S(1)}, bf16[1,128,1280]{1,2,0:T(8,128)(2,1)}, u32[]{:S(2)}) copy-start(bf16[1,128,1280]{1,2,0:T(8,128)(2,1)} %copy-done.7) | copy-start | bytes 983044
  97.0 12.5 %copy-start.6 = (bf16[1,128,1280]{1,2,0:T(8,128)(2,1)S(1)}, bf16[1,128,1280]{1,2,0:T(8,128)(2,1)}, u32[]{:S(2)}) copy-start(bf16[1,128,1280]{1,2,0:T(8,128)(2,1)} %copy-done.5) | copy-start | bytes 983044
  97.5 5.5 %collective-permute-start.30 = (f32[1280]{0:T(1024)S(1)}, f32[1280]{0:T(1024)S(1)}, u32[]{:S(2)}, u32[]{:S(2)}) collective-permute-start(f32[1280]{0:T(1024)S(1)} %add.262), channel_id=1, source_target_pairs={{0,24},{4,28},{8,16},{12,20},{16,8},{20,12},{24,0},{28,4},{1,25},{... | collective-permute-start | bytes 15368 | tf_op jit(solution)/shard_map/ppermute | solution.py:30
  101.4 4.5 %collective-permute-start.29 = (f32[1280]{0:T(1024)S(1)}, f32[1280]{0:T(1024)S(1)}, u32[]{:S(2)}, u32[]{:S(2)}) collective-permute-start(f32[1280]{0:T(1024)S(1)} %add.262), channel_id=1, source_target_pairs={{0,16},{4,20},{8,24},{12,28},{16,0},{20,4},{24,8},{28,12},{1,17},{... | collective-permute-start | bytes 15368 | tf_op jit(solution)/shard_map/ppermute | solution.py:30
  101.4 4.5 %collective-permute-start.28 = (f32[1280]{0:T(1024)S(1)}, f32[1280]{0:T(1024)S(1)}, u32[]{:S(2)}, u32[]{:S(2)}) collective-permute-start(f32[1280]{0:T(1024)S(1)} %add.262), channel_id=1, source_target_pairs={{0,8},{4,12},{8,0},{12,4},{16,24},{20,28},{24,16},{28,20},{1,9},{5... | collective-permute-start | bytes 15368 | tf_op jit(solution)/shard_map/ppermute | solution.py:30
  106.0 6.8 %collective-permute-start.33 = (f32[1280]{0:T(1024)S(1)}, f32[1280]{0:T(1024)S(1)}, u32[]{:S(2)}, u32[]{:S(2)}) collective-permute-start(f32[1280]{0:T(1024)S(1)} %add_add_fusion), channel_id=1, source_target_pairs={{0,3},{1,2},{2,1},{3,0},{4,7},{5,6},{6,5},{7,4},{8,11},{9,10},{10,... | collective-permute-start | bytes 15368 | tf_op jit(solution)/shard_map/ppermute | solution.py:26
  107.6 5.1 %collective-permute-start.32 = (f32[1280]{0:T(1024)S(1)}, f32[1280]{0:T(1024)S(1)}, u32[]{:S(2)}, u32[]{:S(2)}) collective-permute-start(f32[1280]{0:T(1024)S(1)} %add_add_fusion), channel_id=1, source_target_pairs={{0,2},{1,3},{2,0},{3,1},{4,6},{5,7},{6,4},{7,5},{8,10},{9,11},{10,... | collective-permute-start | bytes 15368 | tf_op jit(solution)/shard_map/ppermute | solution.py:26
  108.3 4.5 %collective-permute-start.31 = (f32[1280]{0:T(1024)S(1)}, f32[1280]{0:T(1024)S(1)}, u32[]{:S(2)}, u32[]{:S(2)}) collective-permute-start(f32[1280]{0:T(1024)S(1)} %add_add_fusion), channel_id=1, source_target_pairs={{0,1},{1,0},{2,3},{3,2},{4,5},{5,4},{6,7},{7,6},{8,9},{9,8},{10,11... | collective-permute-start | bytes 15368 | tf_op jit(solution)/shard_map/ppermute | solution.py:26
  116.3 5.7 %copy-start.3 = (f32[1280,640]{1,0:T(8,128)S(1)}, f32[1280,640]{1,0:T(8,128)}, u32[]{:S(2)}) copy-start(f32[1280,640]{1,0:T(8,128)} %copy-done.2) | copy-start | bytes 9830404
  118.5 9.7 %collective-permute-start.23 = (bf16[320,320]{1,0:T(8,128)(2,1)S(1)}, bf16[320,320]{1,0:T(8,128)(2,1)S(1)}, u32[]{:S(2)}, u32[]{:S(2)}) collective-permute-start(bf16[320,320]{1,0:T(8,128)(2,1)S(1)} %bitcast.143), channel_id=1, source_target_pairs={{0,3},{1,2},{2,1},{3,0},{4,7},{5,6},{6,5},{7,4},{8,11},{9,10},{10,... | collective-permute-start | bytes 614408 | tf_op jit(solution)/shard_map/ppermute | solution.py:26
  120.1 9.8 %collective-permute-start.21 = (bf16[320,320]{1,0:T(8,128)(2,1)S(1)}, bf16[320,320]{1,0:T(8,128)(2,1)S(1)}, u32[]{:S(2)}, u32[]{:S(2)}) collective-permute-start(bf16[320,320]{1,0:T(8,128)(2,1)S(1)} %bitcast.140), channel_id=1, source_target_pairs={{0,1},{1,0},{2,3},{3,2},{4,5},{5,4},{6,7},{7,6},{8,9},{9,8},{10,11... | collective-permute-start | bytes 614408 | tf_op jit(solution)/shard_map/ppermute | solution.py:26
  120.7 10.1 %collective-permute-start.22 = (bf16[320,320]{1,0:T(8,128)(2,1)S(1)}, bf16[320,320]{1,0:T(8,128)(2,1)S(1)}, u32[]{:S(2)}, u32[]{:S(2)}) collective-permute-start(bf16[320,320]{1,0:T(8,128)(2,1)S(1)} %bitcast.138), channel_id=1, source_target_pairs={{0,2},{1,3},{2,0},{3,1},{4,6},{5,7},{6,4},{7,5},{8,10},{9,11},{10,... | collective-permute-start | bytes 614408 | tf_op jit(solution)/shard_map/ppermute | solution.py:26
  123.5 10.0 %collective-permute-start.17 = (bf16[160,640]{1,0:T(8,128)(2,1)S(1)}, bf16[160,640]{1,0:T(8,128)(2,1)S(1)}, u32[]{:S(2)}, u32[]{:S(2)}) collective-permute-start(bf16[160,640]{1,0:T(8,128)(2,1)S(1)} %get-tuple-element.58), channel_id=1, source_target_pairs={{0,24},{4,28},{8,16},{12,20},{16,8},{20,12},{24,0},{28,4},{1,25},{... | collective-permute-start | bytes 614408 | tf_op jit(solution)/shard_map/ppermute | solution.py:30
  125.0 17.8 %collective-permute-start.19 = (bf16[160,640]{1,0:T(8,128)(2,1)S(1)}, bf16[160,640]{1,0:T(8,128)(2,1)S(1)}, u32[]{:S(2)}, u32[]{:S(2)}) collective-permute-start(bf16[160,640]{1,0:T(8,128)(2,1)S(1)} %get-tuple-element.59), channel_id=1, source_target_pairs={{0,8},{4,12},{8,0},{12,4},{16,24},{20,28},{24,16},{28,20},{1,9},{5... | collective-permute-start | bytes 614408 | tf_op jit(solution)/shard_map/ppermute | solution.py:30
  128.2 22.8 %collective-permute-start.18 = (bf16[160,640]{1,0:T(8,128)(2,1)S(1)}, bf16[160,640]{1,0:T(8,128)(2,1)S(1)}, u32[]{:S(2)}, u32[]{:S(2)}) collective-permute-start(bf16[160,640]{1,0:T(8,128)(2,1)S(1)} %get-tuple-element.60), channel_id=1, source_target_pairs={{0,16},{4,20},{8,24},{12,28},{16,0},{20,4},{24,8},{28,12},{1,17},{... | collective-permute-start | bytes 614408 | tf_op jit(solution)/shard_map/ppermute | solution.py:30
  131.1 20.7 %collective-permute-start.24 = (bf16[320,320]{1,0:T(8,128)(2,1)S(1)}, bf16[320,320]{1,0:T(8,128)(2,1)S(1)}, u32[]{:S(2)}, u32[]{:S(2)}) collective-permute-start(bf16[320,320]{1,0:T(8,128)(2,1)S(1)} %get-tuple-element.51), channel_id=1, source_target_pairs={{0,24},{4,28},{8,16},{12,20},{16,8},{20,12},{24,0},{28,4},{1,25},{... | collective-permute-start | bytes 614408 | tf_op jit(solution)/shard_map/ppermute | solution.py:30
  132.8 18.9 %collective-permute-start.26 = (bf16[320,320]{1,0:T(8,128)(2,1)S(1)}, bf16[320,320]{1,0:T(8,128)(2,1)S(1)}, u32[]{:S(2)}, u32[]{:S(2)}) collective-permute-start(bf16[320,320]{1,0:T(8,128)(2,1)S(1)} %get-tuple-element.52), channel_id=1, source_target_pairs={{0,8},{4,12},{8,0},{12,4},{16,24},{20,28},{24,16},{28,20},{1,9},{5... | collective-permute-start | bytes 614408 | tf_op jit(solution)/shard_map/ppermute | solution.py:30
  133.5 28.6 %collective-permute-start.25 = (bf16[320,320]{1,0:T(8,128)(2,1)S(1)}, bf16[320,320]{1,0:T(8,128)(2,1)S(1)}, u32[]{:S(2)}, u32[]{:S(2)}) collective-permute-start(bf16[320,320]{1,0:T(8,128)(2,1)S(1)} %get-tuple-element.53), channel_id=1, source_target_pairs={{0,16},{4,20},{8,24},{12,28},{16,0},{20,4},{24,8},{28,12},{1,17},{... | collective-permute-start | bytes 614408 | tf_op jit(solution)/shard_map/ppermute | solution.py:30

commit v2 on v1

--- a/solution.py
+++ b/solution.py
@@ -3,6 +3,8 @@
 import jax
 import jax.numpy as jnp
 from jax import lax
+from jax.experimental import pallas as pl
+from jax.experimental.pallas import tpu as pltpu
 from jax.sharding import PartitionSpec as P
 
 HEADS = 16
@@ -10,6 +12,19 @@
 BLK = 64
 PIECE = 16
 CORES = 2
+LANES = 128
+VMEM_BYTES = 48 * 1024 * 1024
+
+
+def vmem_call(body, out_shape, in_spaces, flops):
+    return pl.pallas_call(
+        body,
+        out_shape=out_shape,
+        in_specs=[pl.BlockSpec(memory_space=space) for space in in_spaces],
+        out_specs=jax.tree.map(lambda _: pl.BlockSpec(memory_space=pltpu.VMEM), out_shape),
+        compiler_params=pltpu.CompilerParams(vmem_limit_bytes=VMEM_BYTES),
+        cost_estimate=pl.CostEstimate(flops=flops, bytes_accessed=4 << 20, transcendentals=0),
+    )
 
 
 def contract(left, right, left_dim, right_dim):
@@ -55,37 +70,193 @@
     return parts[dp ^ jnp.arange(n_dp)].reshape(-1)
 
 
+def send_kernel(n_seq, capacity, per_owner, slot_ref, rows_ref, out_ref):
+    length, feat = rows_ref.shape
+    out_ref[...] = jnp.zeros(out_ref.shape, jnp.bfloat16)
+    row = lax.broadcasted_iota(jnp.int32, (PIECE, LANES), 0)
+    firsts = [slot_ref[0, t * PIECE] for t in range(length // PIECE)]
+    owners = [jnp.where(f >= 0, f // (per_owner * PIECE), n_seq) for f in firsts]
+    for t, first in enumerate(firsts):
+        rank = jnp.int32(0)
+        for earlier in range(t):
+            rank = rank + jnp.where(owners[earlier] == owners[t], 1, 0)
+
+        @pl.when(first >= 0)
+        def _(t=t, first=first, rank=rank):
+            place = pl.ds(pl.multiple_of(rank * PIECE, PIECE), PIECE)
+            out_ref[owners[t], place, :feat] = rows_ref[t * PIECE : (t + 1) * PIECE, :]
+            landing = first % (per_owner * PIECE) + row + 1
+            out_ref[owners[t], place, feat:] = landing.astype(jnp.float32).astype(jnp.bfloat16)
+
+
+def land_kernel(got_ref, out_ref):
+    tokens, feat = out_ref.shape
+    slots = got_ref.shape[0]
+    marks = got_ref[:, feat:].astype(jnp.float32)
+    goal = lax.broadcasted_iota(jnp.int32, (slots, LANES), 1) + 1
+    rows = got_ref[:, :feat]
+    for part in range(tokens // LANES):
+        select = (marks == (goal + part * LANES).astype(jnp.float32)).astype(jnp.bfloat16)
+        out_ref[part * LANES : (part + 1) * LANES, :] = contract(select, rows, 0, 0).astype(
+            jnp.bfloat16
+        )
+
+
 def owner_rows(llm_rows, slot_ids, n_seq, tokens):
     length, feat = llm_rows.shape
     per_owner = tokens // PIECE
     capacity = 1 + (per_owner + n_seq - 2) // n_seq
-    first = slot_ids.reshape(length // PIECE, PIECE)[:, 0]
-    tile = jnp.where(first >= 0, first // PIECE, n_seq * per_owner)
-    owner = tile // per_owner
-    place = tile % per_owner
-    onehot = (owner[:, None] == jnp.arange(n_seq)[None, :]).astype(jnp.int32)
-    rank = jnp.sum((jnp.cumsum(onehot, axis=0) - 1) * onehot, axis=1)
-    target = jnp.where(first >= 0, owner * capacity + rank, -1)
-    row_in = jnp.arange(length) % PIECE
-    target_row = jnp.repeat(target * PIECE, PIECE) + row_in
-    place_row = jnp.repeat(place * PIECE, PIECE) + row_in
-    slots = n_seq * capacity * PIECE
-    select = (target_row[None, :] == jnp.arange(slots)[:, None]).astype(jnp.bfloat16)
-    tag = jnp.where(jnp.arange(128)[None, :] == 0, jnp.repeat(place + 1, PIECE)[:, None], 0)
-    wide = jnp.concatenate([llm_rows, tag.astype(jnp.bfloat16)], axis=1)
-    send = contract(select, wide, 1, 0).astype(jnp.bfloat16)
-    got = lax.all_to_all(
-        send.reshape(n_seq, capacity * PIECE, feat + 128),
-        "seq",
-        split_axis=0,
-        concat_axis=0,
-        tiled=True,
-    ).reshape(slots, feat + 128)
-    tile_got = got[:, feat : feat + 1].astype(jnp.int32) - 1
-    row_got = tile_got * PIECE + (jnp.arange(slots) % PIECE)[:, None]
-    place_got = jnp.where(tile_got >= 0, row_got, -1)
-    landing = (place_got == jnp.arange(tokens)[None, :]).astype(jnp.bfloat16)
-    return contract(landing, got[:, :feat], 0, 0).astype(jnp.bfloat16)
+    rows = capacity * PIECE
+    send = vmem_call(
+        lambda *refs: send_kernel(n_seq, capacity, per_owner, *refs),
+        jax.ShapeDtypeStruct((n_seq, rows, feat + LANES), jnp.bfloat16),
+        [pltpu.SMEM, pltpu.VMEM],
+        1 << 20,
+    )(slot_ids, llm_rows)
+    got = lax.all_to_all(send, "seq", split_axis=0, concat_axis=0, tiled=True)
+    landed = vmem_call(
+        land_kernel,
+        jax.ShapeDtypeStruct((tokens, feat), jnp.bfloat16),
+        [pltpu.VMEM],
+        1 << 26,
+    )(got.reshape(n_seq * rows, feat + LANES))
+    return send, landed
+
+
+def head_lanes(head, rows, width, start):
+    lane = lax.broadcasted_iota(jnp.int32, (rows, width), 1) + start
+    return (lane >= head * HDIM) & (lane < (head + 1) * HDIM)
+
+
+def span_of(head):
+    start = head * HDIM // LANES * LANES
+    stop = -(-(head + 1) * HDIM // LANES) * LANES
+    return start, stop
+
+
+def masked_head(ref, head):
+    start, stop = span_of(head)
+    block = ref[:, start:stop]
+    return jnp.where(head_lanes(head, block.shape[0], stop - start, start), block, 0).astype(
+        block.dtype
+    )
+
+
+def add_span(total, head, part):
+    start, stop = span_of(head)
+    for at in range(start, stop, LANES):
+        piece = part[:, at - start : at - start + LANES]
+        total[at] = total[at] + piece if at in total else piece
+
+
+def forward_kernel(
+    mask_ref, q_ref, k_ref, v_ref, resid_ref, probs_ref, out_ref, unit_ref, inverse_ref
+):
+    tokens, feat = q_ref.shape
+    scale = 1.0 / math.sqrt(HDIM)
+    row = lax.broadcasted_iota(jnp.int32, (tokens, tokens), 0) // BLK
+    col = lax.broadcasted_iota(jnp.int32, (tokens, tokens), 1) // BLK
+    allowed = row == col
+    for i in range(tokens // BLK):
+        for j in range(tokens // BLK):
+            if i != j:
+                allowed = allowed | ((row == i) & (col == j) & (mask_ref[i, j] > 0))
+    total = {}
+    for head in range(HEADS):
+        start, stop = span_of(head)
+        scores = contract(q_ref[:, start:stop], masked_head(k_ref, head), 1, 1) * scale
+        scores = jnp.where(allowed, scores, -jnp.inf)
+        exp_terms = jnp.exp(scores - jnp.max(scores, axis=1, keepdims=True))
+        probs = exp_terms / jnp.sum(exp_terms, axis=1, keepdims=True)
+        probs_ref[head] = probs
+        add_span(total, head, contract(probs.astype(jnp.bfloat16), masked_head(v_ref, head), 1, 0))
+    for at, value in total.items():
+        out_ref[:, at : at + LANES] = value.astype(jnp.bfloat16)
+    hidden = resid_ref[...].astype(jnp.float32) + out_ref[...].astype(jnp.float32)
+    center = jnp.mean(hidden, axis=1, keepdims=True)
+    hidden = hidden - center
+    variance = jnp.mean(jnp.square(hidden), axis=1, keepdims=True)
+    inverse = lax.rsqrt(variance + 1e-06)
+    unit_ref[...] = hidden * inverse
+    inverse_ref[...] = jnp.broadcast_to(inverse, inverse_ref.shape)
+
+
+def forward(mask, query, key_block, value_block, resid):
+    tokens, feat = query.shape
+    return vmem_call(
+        forward_kernel,
+        (
+            jax.ShapeDtypeStruct((HEADS, tokens, tokens), jnp.float32),
+            jax.ShapeDtypeStruct((tokens, feat), jnp.bfloat16),
+            jax.ShapeDtypeStruct((tokens, feat), jnp.float32),
+            jax.ShapeDtypeStruct((tokens, LANES), jnp.float32),
+        ),
+        [pltpu.SMEM] + [pltpu.VMEM] * 4,
+        1 << 31,
+    )(mask, query, key_block, value_block, resid)
+
+
+def backward_kernel(
+    own_ref,
+    got_ref,
+    rows_ref,
+    unit_ref,
+    inverse_ref,
+    gain_ref,
+    probs_ref,
+    out_ref,
+    q_ref,
+    k_ref,
+    v_ref,
+    gq_ref,
+    gk_ref,
+    gv_ref,
+    gr_ref,
+    gain_term_ref,
+):
+    tokens, feat = q_ref.shape
+    scale = 1.0 / math.sqrt(HDIM)
+    d_normed = own_ref[...]
+    for part in range(got_ref.shape[0]):
+        d_normed = d_normed + got_ref[part].astype(jnp.float32)
+    unit = unit_ref[...]
+    gain_term_ref[...] = jnp.sum(d_normed * unit, axis=0, keepdims=True)
+    d_unit = d_normed * gain_ref[...].astype(jnp.float32)
+    d_hidden = inverse_ref[:, :1] * (
+        d_unit
+        - jnp.mean(d_unit, axis=1, keepdims=True)
+        - unit * jnp.mean(d_unit * unit, axis=1, keepdims=True)
+    )
+    gr_ref[...] = (rows_ref[...].astype(jnp.float32) + d_hidden).astype(jnp.bfloat16)
+    totals = ({}, {}, {})
+    for head in range(HEADS):
+        start, stop = span_of(head)
+        probs = probs_ref[head]
+        grad = masked_head(gr_ref, head)
+        add_span(totals[0], head, contract(probs.astype(jnp.bfloat16), grad, 0, 0))
+        d_probs = contract(grad, v_ref[:, start:stop], 1, 1)
+        delta = jnp.sum(
+            grad.astype(jnp.float32) * out_ref[:, start:stop].astype(jnp.float32),
+            axis=1,
+            keepdims=True,
+        )
+        d_scores = (probs * (d_probs - delta) * scale).astype(jnp.bfloat16)
+        add_span(totals[1], head, contract(d_scores, masked_head(k_ref, head), 1, 0))
+        add_span(totals[2], head, contract(d_scores, masked_head(q_ref, head), 0, 0))
+    for ref, total in zip((gv_ref, gq_ref, gk_ref), totals):
+        for at, value in total.items():
+            ref[:, at : at + LANES] = value.astype(jnp.bfloat16)
+
+
+def backward(*operands):
+    tokens, feat = operands[0].shape
+    return vmem_call(
+        backward_kernel,
+        tuple(jax.ShapeDtypeStruct((tokens, feat), jnp.bfloat16) for _ in range(4))
+        + (jax.ShapeDtypeStruct((1, feat), jnp.float32),),
+        [pltpu.VMEM] * 11,
+        1 << 32,
+    )(*operands)
 
 
 def gather_tokens(block, n_dp):
@@ -186,39 +357,17 @@
     seq = lax.axis_index("seq")
     dp = lax.axis_index("dp")
     core = seq % CORES
-    query = queries[0]
-    key_block = key_rows[0]
-    value_block = value_rows[0]
-    tokens, feat_dim = query.shape
-    att_scale = 1.0 / math.sqrt(HDIM)
-
-    grad_rows = owner_rows(llm_grad[0], vision_slot[0], n_seq, tokens)
+    tokens, feat_dim = queries.shape[1:]
+
+    send, grad_rows = owner_rows(llm_grad[0], vision_slot, n_seq, tokens)
+    w_up, norm_gain, send = lax.optimization_barrier((w_up, norm_gain, send))
     gain_full = gather_gain(norm_gain, n_dp, dp)
     up_cols = gather_up(w_up, n_dp, n_seq, dp, core)
 
-    allowed = jnp.repeat(jnp.repeat(window_mask[0] > 0, BLK, axis=0), BLK, axis=1)
-    q_heads = query.reshape(tokens, HEADS, HDIM)
-    k_heads = key_block.reshape(tokens, HEADS, HDIM)
-    v_heads = value_block.reshape(tokens, HEADS, HDIM)
-    scores = (
-        jnp.einsum("qhd,khd->hqk", q_heads, k_heads, preferred_element_type=jnp.float32) * att_scale
-    )
-    masked = jnp.where(allowed[None], scores, -jnp.inf)
-    highest = jnp.max(masked, axis=2, keepdims=True)
-    exp_terms = jnp.where(allowed[None], jnp.exp(masked - highest), 0.0)
-    attn_probs = exp_terms / jnp.sum(exp_terms, axis=2, keepdims=True)
-    probs_low = attn_probs.astype(jnp.bfloat16)
-    attn_heads = jnp.einsum(
-        "hqk,khd->qhd", probs_low, v_heads, preferred_element_type=jnp.float32
-    ).astype(jnp.bfloat16)
-    attn_out = attn_heads.reshape(tokens, feat_dim)
-    hidden = resid_in[0].astype(jnp.float32) + attn_out.astype(jnp.float32)
-    center = jnp.mean(hidden, axis=1, keepdims=True)
-    variance = jnp.mean(jnp.square(hidden - center), axis=1, keepdims=True)
-    inverse = lax.rsqrt(variance + 1e-06)
-    normal_unit = (hidden - center) * inverse
-    gain_wide = gain_full.astype(jnp.float32)
-    normed = (normal_unit * gain_wide).astype(jnp.bfloat16)
+    attn_probs, attn_out, normal_unit, inverse = forward(
+        window_mask[0], queries[0], key_rows[0], value_rows[0], resid_in[0]
+    )
+    normed = (normal_unit * gain_full.astype(jnp.float32)).astype(jnp.bfloat16)
 
     normed_all = gather_tokens(normed, n_dp)
     rows_all = gather_tokens(grad_rows, n_dp)
@@ -230,43 +379,37 @@
         jnp.bfloat16
     )
     d_part = contract(d_pre, up_cols, 1, 1)
-    d_normed = d_part[:tokens]
-    for k in range(1, n_dp):
-        block = d_part[k * tokens : (k + 1) * tokens].astype(jnp.bfloat16)
-        d_normed = d_normed + swap_dp(block, n_dp, k).astype(jnp.float32)
+    d_got = jnp.stack(
+        [
+            swap_dp(d_part[k * tokens : (k + 1) * tokens].astype(jnp.bfloat16), n_dp, k)
+            for k in range(1, n_dp)
+        ]
+    )
 
     up_term = contract(normed_all, d_pre, 0, 0)
     down_term = contract(act_low, rows_all, 0, 0)
     up_panel = scatter_up(up_term, n_seq, seq)
     down_panel = scatter_down(down_term, n_seq, n_dp, seq, dp)
 
-    gain_term = jnp.sum(d_normed * normal_unit, axis=0)
-    d_unit = d_normed * gain_wide
-    d_hidden = inverse * (
-        d_unit
-        - jnp.mean(d_unit, axis=1, keepdims=True)
-        - normal_unit * jnp.mean(d_unit * normal_unit, axis=1, keepdims=True)
-    )
-    grad_resid = (grad_rows.astype(jnp.float32) + d_hidden).astype(jnp.bfloat16)
-    grad_heads = grad_resid.reshape(tokens, HEADS, HDIM)
-    grad_value = jnp.einsum(
-        "hqk,qhd->khd", probs_low, grad_heads, preferred_element_type=jnp.float32
-    ).astype(jnp.bfloat16)
-    d_probs = jnp.einsum("qhd,khd->hqk", grad_heads, v_heads, preferred_element_type=jnp.float32)
-    delta = jnp.einsum("qhd,qhd->hq", grad_heads, attn_heads, preferred_element_type=jnp.float32)
-    d_scores = (attn_probs * (d_probs - delta[:, :, None]) * att_scale).astype(jnp.bfloat16)
-    grad_query = jnp.einsum(
-        "hqk,khd->qhd", d_scores, k_heads, preferred_element_type=jnp.float32
-    ).astype(jnp.bfloat16)
-    grad_key = jnp.einsum(
-        "hqk,qhd->khd", d_scores, q_heads, preferred_element_type=jnp.float32
-    ).astype(jnp.bfloat16)
+    grad_query, grad_key, grad_value, grad_resid, gain_term = backward(
+        d_part[:tokens],
+        d_got,
+        grad_rows,
+        normal_unit,
+        inverse,
+        gain_full[None],
+        attn_probs,
+        attn_out,
+        queries[0],
+        key_rows[0],
+        value_rows[0],
+    )
     factor = 1.0 / math.sqrt(n_dp * n_seq * tokens)
-    gain_total = sum_all(gain_term, n_seq, n_dp)
+    gain_total = sum_all(gain_term[0], n_seq, n_dp)
     return (
-        grad_query.reshape(1, tokens, feat_dim),
-        grad_key.reshape(1, tokens, feat_dim),
-        grad_value.reshape(1, tokens, feat_dim),
+        grad_query[None],
+        grad_key[None],
+        grad_value[None],
         grad_resid[None],
         (up_panel * factor).astype(jnp.bfloat16),
         (down_panel * factor).astype(jnp.bfloat16),

time: 164 us -> 161 us (0.982)
  Pallas kernels: 0 us -> 10.5 us
  matrix products: 18.2 us -> 11 us
  other arithmetic: 15.8 us -> 9.97 us
    pallas_call x0 -> x4, Pallas kernels: none -> 10.5 us  [the longest x1 4.71 us: backward(): vmem_call(backward_kernel, tuple((jax.ShapeDtypeStruct((tokens, feat), jn...]
    dot_general x5 -> x0, matrix products: 4.82 us -> none  [the longest x1 1.7 us: per_device(): jnp.einsum('qhd,khd->hqk', grad_heads, v_heads, preferred_element_type=jn...]
    ppermute x13, waiting for transfers between devices: 22 us -> 19.2 us  [swap_seq(): return lax.ppermute(block, 'seq', [(i, i ^ step) for i in range(count)])]
    ppermute x21, waiting for transfers between devices: 30.7 us -> 33.2 us  [swap_dp(): return lax.ppermute(block, 'dp', [(i, i ^ step) for i in range(count)])]
    unnamed x48 -> x50, local copies, waits for them, and re-layouts: 8.7 us -> 6.63 us
    reduce_sum x4 -> x0, other arithmetic: 1.97 us -> none  [the longest x1 1.32 us: per_device(): center = jnp.mean(hidden, axis=1, keepdims=True)]
    dot_general x7 -> x5, matrix products: 11.9 us -> 11 us  [contract(): lax.dot_general(left, right, (((left_dim,), (right_dim,)), ((), ())), pre...]
  transfers between devices with their start and end apart: 35 -> 35, of which waited for: 15 -> 16; matrix products, arithmetic and copies ran while one was open for 31% -> 20% of each run, Pallas kernels for 0% -> 3%
where the time goes in v2:
time: 161 us; the launch traced here: 160 us
  starting transfers between devices  53.3 us (33%)
  waiting for transfers between devices  52.4 us (33%)
  local copies, waits for them, and re-layouts  22 us (14%)
  matrix products  11 us (7%)
  Pallas kernels  10.5 us (7%)
  other arithmetic  9.97 us (6%)
    ppermute x21, waiting for transfers between devices, swap_dp(): return lax.ppermute(block, 'dp', [(i, i ^ step) for i in range(count)])  33.2 us
    ppermute x21, starting transfers between devices, swap_dp(): return lax.ppermute(block, 'dp', [(i, i ^ step) for i in range(count)])  24.8 us
    ppermute x13, starting transfers between devices, swap_seq(): return lax.ppermute(block, 'seq', [(i, i ^ step) for i in range(count)])  22 us
    ppermute x13, waiting for transfers between devices, swap_seq(): return lax.ppermute(block, 'seq', [(i, i ^ step) for i in range(count)])  19.2 us
    dot_general x5, matrix products, contract(): lax.dot_general(left, right, (((left_dim,), (right_dim,)), ((), ())), pre...  11 us
    unnamed x50, local copies, waits for them, and re-layouts  6.63 us
    all_to_all x1, starting transfers between devices, owner_rows(): got = lax.all_to_all(send, 'seq', split_axis=0, concat_axis=0, tiled=True)  6.46 us
    pallas_call x1, Pallas kernels, backward(): vmem_call(backward_kernel, tuple((jax.ShapeDtypeStruct((tokens, feat), jn...  4.71 us
  transfers between devices with their start and end apart: 35, of which 16 were waited for; matrix products, arithmetic and copies ran while one was open for 20% of the time, Pallas kernels for 3%

profile of v2, /device:TPU:0, one launch (start us, length us, event | category | flops | bytes accessed | tf_op | source)
XLA Modules:
  0.0 160.4 jit_solution(8144142694620415240)
XLA Ops:
  0.7 1.1 copy-done.1
  1.8 0.7 copy-done.2
  2.5 1.7 %shard_map.153 = bf16[8,32,1408]{2,1,0:T(8,128)(2,1)} custom-call(s32[1,192]{1,0:T(1,128)S(1)} %copy-done.2, bf16[192,1280]{1,0:T(8,128)(2,1)S(1)} %bitcast.72), custom_call_target="tpu_custom_call" | custom-call | flops 1048576 | bytes 4194304 | tf_op jit(solution)/shard_map/pallas_call | solution.py:110
  4.2 6.5 %all-to-all-start = ((bf16[8,32,1408]{2,1,0:T(8,128)(2,1)}), bf16[8,32,1408]{2,1,0:T(8,128)(2,1)S(1)}, u32[]{:S(2)}, u32[]{:S(2)}) async-start(bf16[8,32,1408]{2,1,0:T(8,128)(2,1)} %shard_map.153), calls=%async_computation | async-start | bytes 1441792 | tf_op jit(solution)/shard_map/all_to_all | solution.py:116
  10.6 2.5 %collective-permute-start.5 = (bf16[320]{0:T(512)(128)(2,1)S(1)}, bf16[320]{0:T(512)(128)(2,1)S(1)}, u32[]{:S(2)}, u32[]{:S(2)}) collective-permute-start(bf16[320]{0:T(512)(128)(2,1)S(1)} %copy-done.22), channel_id=1, source_target_pairs={{0,3},{1,2},{2,1},{3,0},{4,7},{5,6},{6,5},{7,4},{8,11},{9,10},{10,... | collective-permute-start | bytes 1928 | tf_op jit(solution)/shard_map/ppermute | solution.py:41
  13.7 2.0 %fusion.23 = (bf16[160,640]{1,0:T(8,128)(2,1)}, bf16[160,640]{1,0:T(8,128)(2,1)}, bf16[160,640]{1,0:T(8,128)(2,1)}) fusion(bf16[320,2560]{1,0:T(8,128)(2,1)} %param.17, s32[]{:T(128)S(6)} %select_n.111, s32[]{:T(128)S(6)} %select_n.112, s32[]{:T(128)S(6)} %select_n.114, s32[]{:T(128)S(6)} %select_n.113), kind=kLoop, calls=%fused_computation.63 | loop fusion | bytes 1228816 | tf_op jit(solution)/shard_map/dynamic_slice | solution.py:54
  16.2 2.4 %collective-permute-start.11 = (bf16[160,640]{1,0:T(8,128)(2,1)}, bf16[160,640]{1,0:T(8,128)(2,1)}, u32[]{:S(2)}, u32[]{:S(2)}) collective-permute-start(bf16[160,640]{1,0:T(8,128)(2,1)} %get-tuple-element.30), channel_id=1, source_target_pairs={{0,3},{1,2},{2,1},{3,0},{4,7},{5,6},{6,5},{7,4},{8,11},{9,10},{10,... | collective-permute-start | bytes 614408 | tf_op jit(solution)/shard_map/ppermute | solution.py:41
  19.1 1.8 %dynamic-slice_bitcast_fusion = bf16[1,320,640]{2,1,0:T(8,128)(2,1)} fusion(bf16[320,2560]{1,0:T(8,128)(2,1)} %param.17, s32[]{:T(128)S(6)} %select_n.108), kind=kLoop, calls=%fused_computation.34 | loop fusion | bytes 819204 | tf_op jit(solution)/shard_map/broadcast_in_dim | solution.py:61
  20.9 1.0 copy-done.4
  21.9 1.0 copy-done.6
  22.9 1.0 copy-done.8
  23.8 3.8 %shard_map.155 = (f32[16,128,128]{2,1,0:T(8,128)S(1)}, bf16[128,1280]{1,0:T(8,128)(2,1)S(1)}, f32[128,1280]{1,0:T(8,128)S(1)}, f32[128,128]{1,0:T(8,128)S(1)}) custom-call(s32[2,2]{1,0:T(2,128)S(1)} %bitcast.80, bf16[128,1280]{1,0:T(8,128)(2,1)S(1)} %bitcast.74, bf16[128,1280]{1,0:T(8,128)(2,1)S(1)} %bitcast.76, bf16[128,1280]{1,0:T(8,128)(2,1)S(1)} %bitcast.78, ...), custom_call_target="tpu_custom_call" | custom-call | flops 2147483648 | bytes 4194304 | tf_op jit(solution)/shard_map/pallas_call | solution.py:186
  27.7 1.0 copy-done.11
  28.6 0.7 copy-done.13
  29.9 2.0 %pad_maximum_fusion.4 = bf16[3,160,640]{2,1,0:T(8,128)(2,1)} fusion(bf16[1,160,640]{2,1,0:T(8,128)(2,1)} %bitcast.11, bf16[1,160,640]{2,1,0:T(8,128)(2,1)} %bitcast.10, bf16[1,160,640]{2,1,0:T(8,128)(2,1)} %bitcast.9), kind=kLoop, calls=%fused_computation.21 | loop fusion | flops 614400 | bytes 1228800 | tf_op jit(solution)/shard_map/stack | solution.py:56
  32.2 0.7 collective-permute-done.3
  32.9 0.6 gather_fusion
  33.7 1.8 %collective-permute-start.8 = (bf16[128,1280]{1,0:T(8,128)(2,1)S(1)}, bf16[128,1280]{1,0:T(8,128)(2,1)}, u32[]{:S(2)}, u32[]{:S(2)}) collective-permute-start(bf16[128,1280]{1,0:T(8,128)(2,1)S(1)} %multiply_convert_fusion.2), channel_id=1, source_target_pairs={{0,3},{1,2},{2,1},{3,0},{4,7},{5,6},{6,5},{7,4},{8,11},{9,10},{10,... | collective-permute-start | bytes 983048 | tf_op jit(solution)/shard_map/ppermute | solution.py:41
  36.0 1.3 collective-permute-start.6
  37.3 1.4 broadcast_select_fusion.1
  38.7 1.3 maximum_maximum_fusion
  40.1 3.4 %gather_fusion.1 = bf16[4,320,640]{2,1,0:T(8,128)(2,1)} fusion(bf16[4,320,640]{2,1,0:T(8,128)(2,1)} %maximum_maximum_fusion, s32[1024]{0:T(1024)S(1)} %pad_clamp_fusion), kind=kCustom, calls=%fused_computation.1 | custom fusion | bytes 3276816 | tf_op jit(solution)/shard_map/gather | solution.py:63
  43.7 1.8 %collective-permute-start.2 = (bf16[128,1280]{1,0:T(8,128)(2,1)S(1)}, bf16[128,1280]{1,0:T(8,128)(2,1)S(1)}, u32[]{:S(2)}, u32[]{:S(2)}) collective-permute-start(bf16[128,1280]{1,0:T(8,128)(2,1)S(1)} %shard_map.154.rows_ref), channel_id=1, source_target_pairs={{0,3},{1,2},{2,1},{3,0},{4,7},{5,6},{6,5},{7,4},{8,11},{9,10},{10,... | collective-permute-start | bytes 983048 | tf_op jit(solution)/shard_map/ppermute | solution.py:41
  46.0 1.3 collective-permute-start
  47.3 5.2 %collective-permute-done.7 = bf16[128,1280]{1,0:T(8,128)(2,1)} collective-permute-done((bf16[128,1280]{1,0:T(8,128)(2,1)S(1)}, bf16[128,1280]{1,0:T(8,128)(2,1)}, u32[]{:S(2)}, u32[]{:S(2)}) %collective-permute-start.7) | collective-permute-done | bytes 327712 | tf_op jit(solution)/shard_map/ppermute | solution.py:41
  52.5 2.9 %fusion.15 = f32[512,640]{1,0:T(8,128)S(1)} fusion(bf16[1280,640]{1,0:T(8,128)(2,1)} %bitcast.81, bf16[128,1280]{1,0:T(8,128)(2,1)} %collective-permute-done.8, bf16[128,1280]{1,0:T(8,128)(2,1)} %collective-permute-done.7, bf16[128,1280]{1,0:T(8,128)(2,1)} %collective-permute-done.6, bf16[128,1280]{1,0:T(8,128)(2,1)S(1)} %multiply_convert_fusion.2), kind=kOutput, calls=%fused_computation.43 | convolution fusion | flops 844103680 | bytes 4259840 | tf_op jit(solution)/shard_map/dot_general | solution.py:31
  55.5 3.9 %collective-permute-done.2 = bf16[128,1280]{1,0:T(8,128)(2,1)S(1)} collective-permute-done((bf16[128,1280]{1,0:T(8,128)(2,1)S(1)}, bf16[128,1280]{1,0:T(8,128)(2,1)S(1)}, u32[]{:S(2)}, u32[]{:S(2)}) %collective-permute-start.2) | collective-permute-done | bytes 327712 | tf_op jit(solution)/shard_map/ppermute | solution.py:41
  59.4 5.6 %collective-permute-done.1 = bf16[128,1280]{1,0:T(8,128)(2,1)S(1)} collective-permute-done((bf16[128,1280]{1,0:T(8,128)(2,1)S(1)}, bf16[128,1280]{1,0:T(8,128)(2,1)S(1)}, u32[]{:S(2)}, u32[]{:S(2)}) %collective-permute-start.1) | collective-permute-done | bytes 327712 | tf_op jit(solution)/shard_map/ppermute | solution.py:41
  65.2 1.3 fusion.1
  66.6 1.2 fusion.25
  67.9 1.6 collective-permute-start.13
  69.5 1.3 collective-permute-start.15
  70.8 0.7 collective-permute-start.14
  71.5 2.8 %fusion.3 = f32[640,1280]{1,0:T(8,128)} fusion(f32[512,640]{1,0:T(8,128)S(1)} %fusion.15, bf16[128,1280]{1,0:T(8,128)(2,1)S(1)} %collective-permute-done.2, bf16[128,1280]{1,0:T(8,128)(2,1)S(1)} %collective-permute-done.1, bf16[128,1280]{1,0:T(8,128)(2,1)S(1)} %collective-permute-done, bf16[128,1280]{1,0:T(8,128)(2,1)S(1)} %shard_map.154.rows_ref), kind=kOutput, calls=%fused_computation.17 | convolution fusion | flops 846069760 | bytes 5898240 | tf_op jit(solution)/shard_map/dot_general | solution.py:31
  74.3 4.3 %collective-permute-done.13 = bf16[128,1280]{1,0:T(8,128)(2,1)S(1)} collective-permute-done((bf16[128,1280]{1,0:T(8,128)(2,1)S(1)}, bf16[128,1280]{1,0:T(8,128)(2,1)S(1)}, u32[]{:S(2)}, u32[]{:S(2)}) %collective-permute-start.13) | collective-permute-done | bytes 327712 | tf_op jit(solution)/shard_map/ppermute | solution.py:41
  78.5 7.0 %collective-permute-done.15 = bf16[128,1280]{1,0:T(8,128)(2,1)S(1)} collective-permute-done((bf16[128,1280]{1,0:T(8,128)(2,1)S(1)}, bf16[128,1280]{1,0:T(8,128)(2,1)S(1)}, u32[]{:S(2)}, u32[]{:S(2)}) %collective-permute-start.15) | collective-permute-done | bytes 327712 | tf_op jit(solution)/shard_map/ppermute | solution.py:41
  85.5 1.4 collective-permute-done.14
  87.0 4.7 %shard_map.156 = (bf16[128,1280]{1,0:T(8,128)(2,1)}, bf16[128,1280]{1,0:T(8,128)(2,1)}, bf16[128,1280]{1,0:T(8,128)(2,1)}, bf16[128,1280]{1,0:T(8,128)(2,1)}, f32[1,1280]{1,0:T(1,128)S(1)}) custom-call(f32[128,1280]{1,0:T(8,128)S(1)} %slice.23.own_ref, bf16[3,128,1280]{2,1,0:T(8,128)(2,1)S(1)} %pad_maximum_fusion.2.got_ref, ...), custom_call_target="tpu_custom_call" | custom-call | flops 4294967296 | bytes 4194304 | tf_op jit(solution)/shard_map/pallas_call | solution.py:253
  91.9 1.6 dynamic-slice_convert_fusion
  94.0 3.8 %collective-permute-start.30 = (f32[1280]{0:T(1024)S(1)}, f32[1280]{0:T(1024)S(1)}, u32[]{:S(2)}, u32[]{:S(2)}) collective-permute-start(f32[1280]{0:T(1024)S(1)} %add.171), channel_id=1, source_target_pairs={{0,24},{4,28},{8,16},{12,20},{16,8},{20,12},{24,0},{28,4},{1,25},{... | collective-permute-start | bytes 15368 | tf_op jit(solution)/shard_map/ppermute | solution.py:45
  97.7 0.6 collective-permute-start.28
  98.3 2.7 %fusion.14 = f32[1280,640]{1,0:T(8,128)S(1)} fusion(bf16[512,640]{1,0:T(8,128)(2,1)S(1)} %copy-done.21, bf16[128,1280]{1,0:T(8,128)(2,1)} %collective-permute-done.8, bf16[128,1280]{1,0:T(8,128)(2,1)} %collective-permute-done.7, bf16[128,1280]{1,0:T(8,128)(2,1)} %collective-permute-done.6, bf16[128,1280]{1,0:T(8,128)(2,1)S(1)} %multiply_convert_fusion.2), kind=kOutput, calls=%fused_computation.42 | convolution fusion | flops 844103680 | bytes 5242880 | tf_op jit(solution)/shard_map/dot_general | solution.py:31
  101.1 1.2 collective-permute-done.29
  102.3 1.5 collective-permute-start.33
  104.2 1.7 %collective-permute-start.31 = (f32[1280]{0:T(1024)S(1)}, f32[1280]{0:T(1024)S(1)}, u32[]{:S(2)}, u32[]{:S(2)}) collective-permute-start(f32[1280]{0:T(1024)S(1)} %add_add_fusion), channel_id=1, source_target_pairs={{0,1},{1,0},{2,3},{3,2},{4,5},{5,4},{6,7},{7,6},{8,9},{9,8},{10,11... | collective-permute-start | bytes 15368 | tf_op jit(solution)/shard_map/ppermute | solution.py:41
  105.8 1.0 fusion.2
  107.8 0.6 add_multiply_fusion
  108.4 1.1 add_convert_fusion
  109.5 2.5 %reshape.68 = bf16[320,4,320]{2,1,0:T(4,128)(2,1)S(1)} reshape(bf16[320,1280]{1,0:T(8,128)(2,1)} %add_convert_fusion) | data formatting | bytes 1638400 | tf_op jit(solution)/shard_map/reshape | solution.py:293
  112.1 2.0 %constant_dynamic-slice_fusion.3 = (bf16[320,1,320]{2,1,0:T(2,128)(2,1)S(1)}, bf16[320,1,320]{2,1,0:T(2,128)(2,1)S(1)}, bf16[320,1,320]{2,1,0:T(2,128)(2,1)S(1)}, bf16[320,1,320]{2,1,0:T(2,128)(2,1)S(1)}) fusion(bf16[320,4,320]{2,1,0:T(4,128)(2,1)S(1)} %reshape.68, s32[]{:T(128)S(6)} %select_n.126, s32[]{:T(128)S(6)} %select_n.128, s32[]{:T(128)S(6)} %select_n.127, ...), kind=kLoop, calls=%fused_computation.52 | loop fusion | bytes 1638416 | tf_op jit(solution)/shard_map/dynamic-slice
  114.2 1.7 %collective-permute-start.23 = (bf16[320,320]{1,0:T(8,128)(2,1)S(1)}, bf16[320,320]{1,0:T(8,128)(2,1)S(1)}, u32[]{:S(2)}, u32[]{:S(2)}) collective-permute-start(bf16[320,320]{1,0:T(8,128)(2,1)S(1)} %bitcast.94), channel_id=1, source_target_pairs={{0,3},{1,2},{2,1},{3,0},{4,7},{5,6},{6,5},{7,4},{8,11},{9,10},{10,... | collective-permute-start | bytes 614408 | tf_op jit(solution)/shard_map/ppermute | solution.py:41
  115.9 1.5 collective-permute-start.21
  117.8 1.4 fusion
  119.3 2.7 %collective-permute-start.17 = (bf16[160,640]{1,0:T(8,128)(2,1)S(1)}, bf16[160,640]{1,0:T(8,128)(2,1)S(1)}, u32[]{:S(2)}, u32[]{:S(2)}) collective-permute-start(bf16[160,640]{1,0:T(8,128)(2,1)S(1)} %get-tuple-element.44), channel_id=1, source_target_pairs={{0,24},{4,28},{8,16},{12,20},{16,8},{20,12},{24,0},{28,4},{1,25},{... | collective-permute-start | bytes 614408 | tf_op jit(solution)/shard_map/ppermute | solution.py:45
  122.0 2.1 %collective-permute-done.23 = bf16[320,320]{1,0:T(8,128)(2,1)S(1)} collective-permute-done((bf16[320,320]{1,0:T(8,128)(2,1)S(1)}, bf16[320,320]{1,0:T(8,128)(2,1)S(1)}, u32[]{:S(2)}, u32[]{:S(2)}) %collective-permute-start.23) | collective-permute-done | bytes 204832 | tf_op jit(solution)/shard_map/ppermute | solution.py:41
  124.1 2.0 %collective-permute-start.18 = (bf16[160,640]{1,0:T(8,128)(2,1)S(1)}, bf16[160,640]{1,0:T(8,128)(2,1)S(1)}, u32[]{:S(2)}, u32[]{:S(2)}) collective-permute-start(bf16[160,640]{1,0:T(8,128)(2,1)S(1)} %get-tuple-element.46), channel_id=1, source_target_pairs={{0,16},{4,20},{8,24},{12,28},{16,0},{20,4},{24,8},{28,12},{1,17},{... | collective-permute-start | bytes 614408 | tf_op jit(solution)/shard_map/ppermute | solution.py:45
  126.1 0.9 collective-permute-done.21
  126.9 1.0 collective-permute-done.22
  128.2 2.7 %collective-permute-start.24 = (bf16[320,320]{1,0:T(8,128)(2,1)S(1)}, bf16[320,320]{1,0:T(8,128)(2,1)S(1)}, u32[]{:S(2)}, u32[]{:S(2)}) collective-permute-start(bf16[320,320]{1,0:T(8,128)(2,1)S(1)} %get-tuple-element.37), channel_id=1, source_target_pairs={{0,24},{4,28},{8,16},{12,20},{16,8},{20,12},{24,0},{28,4},{1,25},{... | collective-permute-start | bytes 614408 | tf_op jit(solution)/shard_map/ppermute | solution.py:45
  130.9 9.7 %collective-permute-start.25 = (bf16[320,320]{1,0:T(8,128)(2,1)S(1)}, bf16[320,320]{1,0:T(8,128)(2,1)S(1)}, u32[]{:S(2)}, u32[]{:S(2)}) collective-permute-start(bf16[320,320]{1,0:T(8,128)(2,1)S(1)} %get-tuple-element.39), channel_id=1, source_target_pairs={{0,16},{4,20},{8,24},{12,28},{16,0},{20,4},{24,8},{28,12},{1,17},{... | collective-permute-start | bytes 614408 | tf_op jit(solution)/shard_map/ppermute | solution.py:45
  140.7 6.3 %collective-permute-done.18 = bf16[160,640]{1,0:T(8,128)(2,1)S(1)} collective-permute-done((bf16[160,640]{1,0:T(8,128)(2,1)S(1)}, bf16[160,640]{1,0:T(8,128)(2,1)S(1)}, u32[]{:S(2)}, u32[]{:S(2)}) %collective-permute-start.18) | collective-permute-done | bytes 204832 | tf_op jit(solution)/shard_map/ppermute | solution.py:45
  147.0 0.8 fusion.13
  147.8 11.7 %collective-permute-done.25 = bf16[320,320]{1,0:T(8,128)(2,1)S(1)} collective-permute-done((bf16[320,320]{1,0:T(8,128)(2,1)S(1)}, bf16[320,320]{1,0:T(8,128)(2,1)S(1)}, u32[]{:S(2)}, u32[]{:S(2)}) %collective-permute-start.25) | collective-permute-done | bytes 204832 | tf_op jit(solution)/shard_map/ppermute | solution.py:45
  159.5 0.8 fusion.9
  (100 shorter events, 7.0 us)
Async XLA Ops:
  0.6 64.6 %copy-start = (bf16[640,1280]{1,0:T(8,128)(2,1)S(1)}, bf16[640,1280]{1,0:T(8,128)(2,1)}, u32[]{:S(2)}) copy-start(bf16[640,1280]{1,0:T(8,128)(2,1)} %param.18) | copy-start | bytes 4915204
  0.6 10.0 %copy-start.22 = (bf16[320]{0:T(512)(128)(2,1)S(1)}, bf16[320]{0:T(512)(128)(2,1)}, u32[]{:S(2)}) copy-start(bf16[320]{0:T(512)(128)(2,1)} %param.19) | copy-start | bytes 1924
  0.7 1.2 copy-start.1
  1.8 0.7 copy-start.2
  4.2 16.7 %copy-start.3 = (bf16[1,128,1280]{2,1,0:T(8,128)(2,1)S(1)}, bf16[1,128,1280]{2,1,0:T(8,128)(2,1)}, u32[]{:S(2)}) copy-start(bf16[1,128,1280]{2,1,0:T(8,128)(2,1)} %param.13) | copy-start | bytes 983044
  4.2 16.7 %copy-start.10 = (s32[1,2,2]{2,1,0:T(2,128)S(1)}, s32[1,2,2]{2,1,0:T(2,128)}, u32[]{:S(2)}) copy-start(s32[1,2,2]{2,1,0:T(2,128)} %param.16) | copy-start | bytes 52
  4.2 39.3 %all-to-all-start = ((bf16[8,32,1408]{2,1,0:T(8,128)(2,1)}), bf16[8,32,1408]{2,1,0:T(8,128)(2,1)S(1)}, u32[]{:S(2)}, u32[]{:S(2)}) async-start(bf16[8,32,1408]{2,1,0:T(8,128)(2,1)} %shard_map.153), calls=%async_computation | async-start | bytes 1441792 | tf_op jit(solution)/shard_map/all_to_all | solution.py:116
  10.6 21.5 %collective-permute-start.5 = (bf16[320]{0:T(512)(128)(2,1)S(1)}, bf16[320]{0:T(512)(128)(2,1)S(1)}, u32[]{:S(2)}, u32[]{:S(2)}) collective-permute-start(bf16[320]{0:T(512)(128)(2,1)S(1)} %copy-done.22), channel_id=1, source_target_pairs={{0,3},{1,2},{2,1},{3,0},{4,7},{5,6},{6,5},{7,4},{8,11},{9,10},{10,... | collective-permute-start | bytes 1928 | tf_op jit(solution)/shard_map/ppermute | solution.py:41
  13.2 19.0 %collective-permute-start.4 = (bf16[320]{0:T(512)(128)(2,1)S(1)}, bf16[320]{0:T(512)(128)(2,1)S(1)}, u32[]{:S(2)}, u32[]{:S(2)}) collective-permute-start(bf16[320]{0:T(512)(128)(2,1)S(1)} %copy-done.22), channel_id=1, source_target_pairs={{0,2},{1,3},{2,0},{3,1},{4,6},{5,7},{6,4},{7,5},{8,10},{9,11},{10,... | collective-permute-start | bytes 1928 | tf_op jit(solution)/shard_map/ppermute | solution.py:41
  15.6 13.7 %collective-permute-start.9 = (bf16[160,640]{1,0:T(8,128)(2,1)}, bf16[160,640]{1,0:T(8,128)(2,1)}, u32[]{:S(2)}, u32[]{:S(2)}) collective-permute-start(bf16[160,640]{1,0:T(8,128)(2,1)} %get-tuple-element.29), channel_id=1, source_target_pairs={{0,1},{1,0},{2,3},{3,2},{4,5},{5,4},{6,7},{7,6},{8,9},{9,8},{10,11... | collective-permute-start | bytes 614408 | tf_op jit(solution)/shard_map/ppermute | solution.py:41
  16.2 13.7 %collective-permute-start.11 = (bf16[160,640]{1,0:T(8,128)(2,1)}, bf16[160,640]{1,0:T(8,128)(2,1)}, u32[]{:S(2)}, u32[]{:S(2)}) collective-permute-start(bf16[160,640]{1,0:T(8,128)(2,1)} %get-tuple-element.30), channel_id=1, source_target_pairs={{0,3},{1,2},{2,1},{3,0},{4,7},{5,6},{6,5},{7,4},{8,11},{9,10},{10,... | collective-permute-start | bytes 614408 | tf_op jit(solution)/shard_map/ppermute | solution.py:41
  18.6 11.3 %collective-permute-start.10 = (bf16[160,640]{1,0:T(8,128)(2,1)}, bf16[160,640]{1,0:T(8,128)(2,1)}, u32[]{:S(2)}, u32[]{:S(2)}) collective-permute-start(bf16[160,640]{1,0:T(8,128)(2,1)} %get-tuple-element.31), channel_id=1, source_target_pairs={{0,2},{1,3},{2,0},{3,1},{4,6},{5,7},{6,4},{7,5},{8,10},{9,11},{10,... | collective-permute-start | bytes 614408 | tf_op jit(solution)/shard_map/ppermute | solution.py:41
  20.9 1.0 copy-start.4
  21.9 1.0 copy-start.6
  22.9 1.0 copy-start.8
  27.6 1.0 copy-start.11
  28.6 0.7 copy-start.13
  29.3 3.6 %collective-permute-start.3 = (bf16[320]{0:T(512)(128)(2,1)S(1)}, bf16[320]{0:T(512)(128)(2,1)S(1)}, u32[]{:S(2)}, u32[]{:S(2)}) collective-permute-start(bf16[320]{0:T(512)(128)(2,1)S(1)} %copy-done.22), channel_id=1, source_target_pairs={{0,1},{1,0},{2,3},{3,2},{4,5},{5,4},{6,7},{7,6},{8,9},{9,8},{10,11... | collective-permute-start | bytes 1928 | tf_op jit(solution)/shard_map/ppermute | solution.py:41
  31.9 5.4 %collective-permute-start.12 = (bf16[3,160,640]{2,1,0:T(8,128)(2,1)}, bf16[3,160,640]{2,1,0:T(8,128)(2,1)}, u32[]{:S(2)}, u32[]{:S(2)}) collective-permute-start(bf16[3,160,640]{2,1,0:T(8,128)(2,1)} %pad_maximum_fusion.4), channel_id=1, source_target_pairs={{0,4},{4,0},{8,12},{12,8},{16,20},{20,16},{24,28},{28,24},{1,5},{5... | collective-permute-start | bytes 1843208 | tf_op jit(solution)/shard_map/ppermute | solution.py:45
  33.7 5.1 %copy-start.19 = (bf16[1,320,640]{2,1,0:T(8,128)(2,1)S(1)}, bf16[1,320,640]{2,1,0:T(8,128)(2,1)}, u32[]{:S(2)}) copy-start(bf16[1,320,640]{2,1,0:T(8,128)(2,1)} %dynamic-slice_bitcast_fusion) | copy-start | bytes 1228804
  33.7 12.3 %collective-permute-start.8 = (bf16[128,1280]{1,0:T(8,128)(2,1)S(1)}, bf16[128,1280]{1,0:T(8,128)(2,1)}, u32[]{:S(2)}, u32[]{:S(2)}) collective-permute-start(bf16[128,1280]{1,0:T(8,128)(2,1)S(1)} %multiply_convert_fusion.2), channel_id=1, source_target_pairs={{0,3},{1,2},{2,1},{3,0},{4,7},{5,6},{6,5},{7,4},{8,11},{9,10},{10,... | collective-permute-start | bytes 983048 | tf_op jit(solution)/shard_map/ppermute | solution.py:41
  35.5 17.0 %collective-permute-start.7 = (bf16[128,1280]{1,0:T(8,128)(2,1)S(1)}, bf16[128,1280]{1,0:T(8,128)(2,1)}, u32[]{:S(2)}, u32[]{:S(2)}) collective-permute-start(bf16[128,1280]{1,0:T(8,128)(2,1)S(1)} %multiply_convert_fusion.2), channel_id=1, source_target_pairs={{0,2},{1,3},{2,0},{3,1},{4,6},{5,7},{6,4},{7,5},{8,10},{9,11},{10,... | collective-permute-start | bytes 983048 | tf_op jit(solution)/shard_map/ppermute | solution.py:41
  36.0 16.5 %collective-permute-start.6 = (bf16[128,1280]{1,0:T(8,128)(2,1)S(1)}, bf16[128,1280]{1,0:T(8,128)(2,1)}, u32[]{:S(2)}, u32[]{:S(2)}) collective-permute-start(bf16[128,1280]{1,0:T(8,128)(2,1)S(1)} %multiply_convert_fusion.2), channel_id=1, source_target_pairs={{0,1},{1,0},{2,3},{3,2},{4,5},{5,4},{6,7},{7,6},{8,9},{9,8},{10,11... | collective-permute-start | bytes 983048 | tf_op jit(solution)/shard_map/ppermute | solution.py:41
  43.7 15.7 %collective-permute-start.2 = (bf16[128,1280]{1,0:T(8,128)(2,1)S(1)}, bf16[128,1280]{1,0:T(8,128)(2,1)S(1)}, u32[]{:S(2)}, u32[]{:S(2)}) collective-permute-start(bf16[128,1280]{1,0:T(8,128)(2,1)S(1)} %shard_map.154.rows_ref), channel_id=1, source_target_pairs={{0,3},{1,2},{2,1},{3,0},{4,7},{5,6},{6,5},{7,4},{8,11},{9,10},{10,... | collective-permute-start | bytes 983048 | tf_op jit(solution)/shard_map/ppermute | solution.py:41
  45.5 19.5 %collective-permute-start.1 = (bf16[128,1280]{1,0:T(8,128)(2,1)S(1)}, bf16[128,1280]{1,0:T(8,128)(2,1)S(1)}, u32[]{:S(2)}, u32[]{:S(2)}) collective-permute-start(bf16[128,1280]{1,0:T(8,128)(2,1)S(1)} %shard_map.154.rows_ref), channel_id=1, source_target_pairs={{0,2},{1,3},{2,0},{3,1},{4,6},{5,7},{6,4},{7,5},{8,10},{9,11},{10,... | collective-permute-start | bytes 983048 | tf_op jit(solution)/shard_map/ppermute | solution.py:41
  46.0 19.2 %collective-permute-start = (bf16[128,1280]{1,0:T(8,128)(2,1)S(1)}, bf16[128,1280]{1,0:T(8,128)(2,1)S(1)}, u32[]{:S(2)}, u32[]{:S(2)}) collective-permute-start(bf16[128,1280]{1,0:T(8,128)(2,1)S(1)} %shard_map.154.rows_ref), channel_id=1, source_target_pairs={{0,1},{1,0},{2,3},{3,2},{4,5},{5,4},{6,7},{7,6},{8,9},{9,8},{10,11... | collective-permute-start | bytes 983048 | tf_op jit(solution)/shard_map/ppermute | solution.py:41
  55.5 11.1 %copy-start.15 = (bf16[4,320,640]{2,1,0:T(8,128)(2,1)S(1)}, bf16[4,320,640]{2,1,0:T(8,128)(2,1)}, u32[]{:S(2)}) copy-start(bf16[4,320,640]{2,1,0:T(8,128)(2,1)} %gather_fusion.1) | copy-start | bytes 4915204
  66.6 1.2 copy-start.20
  67.9 10.7 %collective-permute-start.13 = (bf16[128,1280]{1,0:T(8,128)(2,1)S(1)}, bf16[128,1280]{1,0:T(8,128)(2,1)S(1)}, u32[]{:S(2)}, u32[]{:S(2)}) collective-permute-start(bf16[128,1280]{1,0:T(8,128)(2,1)S(1)} %get-tuple-element.32), channel_id=1, source_target_pairs={{0,1},{1,0},{2,3},{3,2},{4,5},{5,4},{6,7},{7,6},{8,9},{9,8},{10,11... | collective-permute-start | bytes 983048 | tf_op jit(solution)/shard_map/ppermute | solution.py:41
  69.5 16.1 %collective-permute-start.15 = (bf16[128,1280]{1,0:T(8,128)(2,1)S(1)}, bf16[128,1280]{1,0:T(8,128)(2,1)S(1)}, u32[]{:S(2)}, u32[]{:S(2)}) collective-permute-start(bf16[128,1280]{1,0:T(8,128)(2,1)S(1)} %get-tuple-element.33), channel_id=1, source_target_pairs={{0,3},{1,2},{2,1},{3,0},{4,7},{5,6},{6,5},{7,4},{8,11},{9,10},{10,... | collective-permute-start | bytes 983048 | tf_op jit(solution)/shard_map/ppermute | solution.py:41
  70.8 16.1 %collective-permute-start.14 = (bf16[128,1280]{1,0:T(8,128)(2,1)S(1)}, bf16[128,1280]{1,0:T(8,128)(2,1)S(1)}, u32[]{:S(2)}, u32[]{:S(2)}) collective-permute-start(bf16[128,1280]{1,0:T(8,128)(2,1)S(1)} %get-tuple-element.34), channel_id=1, source_target_pairs={{0,2},{1,3},{2,0},{3,1},{4,6},{5,7},{6,4},{7,5},{8,10},{9,11},{10,... | collective-permute-start | bytes 983048 | tf_op jit(solution)/shard_map/ppermute | solution.py:41
  71.5 15.5 %copy-start.12 = (f32[16,128,128]{2,1,0:T(8,128)S(1)}, f32[16,128,128]{2,1,0:T(8,128)}, u32[]{:S(2)}) copy-start(f32[16,128,128]{2,1,0:T(8,128)} %copy-done.11) | copy-start | bytes 3145732
  74.3 12.8 %copy-start.5 = (bf16[1,128,1280]{2,1,0:T(8,128)(2,1)S(1)}, bf16[1,128,1280]{2,1,0:T(8,128)(2,1)}, u32[]{:S(2)}) copy-start(bf16[1,128,1280]{2,1,0:T(8,128)(2,1)} %param.10) | copy-start | bytes 983044
  74.3 12.8 %copy-start.7 = (bf16[1,128,1280]{2,1,0:T(8,128)(2,1)S(1)}, bf16[1,128,1280]{2,1,0:T(8,128)(2,1)}, u32[]{:S(2)}) copy-start(bf16[1,128,1280]{2,1,0:T(8,128)(2,1)} %param.11) | copy-start | bytes 983044
  74.3 12.8 %copy-start.9 = (bf16[1,128,1280]{2,1,0:T(8,128)(2,1)S(1)}, bf16[1,128,1280]{2,1,0:T(8,128)(2,1)}, u32[]{:S(2)}) copy-start(bf16[1,128,1280]{2,1,0:T(8,128)(2,1)} %param.12) | copy-start | bytes 983044
  74.3 12.8 %copy-start.14 = (bf16[128,1280]{1,0:T(8,128)(2,1)S(1)}, bf16[128,1280]{1,0:T(8,128)(2,1)}, u32[]{:S(2)}) copy-start(bf16[128,1280]{1,0:T(8,128)(2,1)} %copy-done.13) | copy-start | bytes 983044
  91.8 6.6 %copy-start.21 = (bf16[512,640]{1,0:T(8,128)(2,1)S(1)}, bf16[512,640]{1,0:T(8,128)(2,1)}, u32[]{:S(2)}) copy-start(bf16[512,640]{1,0:T(8,128)(2,1)} %copy-done.20) | copy-start | bytes 1966084
  91.8 2.2 %collective-permute-start.27 = (f32[1280]{0:T(1024)S(1)}, f32[1280]{0:T(1024)S(1)}, u32[]{:S(2)}, u32[]{:S(2)}) collective-permute-start(f32[1280]{0:T(1024)S(1)} %reduce), channel_id=1, source_target_pairs={{0,4},{4,0},{8,12},{12,8},{16,20},{20,16},{24,28},{28,24},{1,5},{5... | collective-permute-start | bytes 15368 | tf_op jit(solution)/shard_map/ppermute | solution.py:45
  93.4 15.0 %collective-permute-start.20 = (bf16[320,1280]{1,0:T(8,128)(2,1)S(1)}, bf16[320,1280]{1,0:T(8,128)(2,1)S(1)}, u32[]{:S(2)}, u32[]{:S(2)}) collective-permute-start(bf16[320,1280]{1,0:T(8,128)(2,1)S(1)} %dynamic-slice_convert_fusion), channel_id=1, source_target_pairs={{0,4},{4,0},{8,12},{12,8},{16,20},{20,16},{24,28},{28,24},{1,5},{5... | collective-permute-start | bytes 2457608 | tf_op jit(solution)/shard_map/ppermute | solution.py:45
  94.0 7.1 %collective-permute-start.30 = (f32[1280]{0:T(1024)S(1)}, f32[1280]{0:T(1024)S(1)}, u32[]{:S(2)}, u32[]{:S(2)}) collective-permute-start(f32[1280]{0:T(1024)S(1)} %add.171), channel_id=1, source_target_pairs={{0,24},{4,28},{8,16},{12,20},{16,8},{20,12},{24,0},{28,4},{1,25},{... | collective-permute-start | bytes 15368 | tf_op jit(solution)/shard_map/ppermute | solution.py:45
  97.7 4.5 %collective-permute-start.29 = (f32[1280]{0:T(1024)S(1)}, f32[1280]{0:T(1024)S(1)}, u32[]{:S(2)}, u32[]{:S(2)}) collective-permute-start(f32[1280]{0:T(1024)S(1)} %add.171), channel_id=1, source_target_pairs={{0,16},{4,20},{8,24},{12,28},{16,0},{20,4},{24,8},{28,12},{1,17},{... | collective-permute-start | bytes 15368 | tf_op jit(solution)/shard_map/ppermute | solution.py:45
  97.7 4.5 %collective-permute-start.28 = (f32[1280]{0:T(1024)S(1)}, f32[1280]{0:T(1024)S(1)}, u32[]{:S(2)}, u32[]{:S(2)}) collective-permute-start(f32[1280]{0:T(1024)S(1)} %add.171), channel_id=1, source_target_pairs={{0,8},{4,12},{8,0},{12,4},{16,24},{20,28},{24,16},{28,20},{1,9},{5... | collective-permute-start | bytes 15368 | tf_op jit(solution)/shard_map/ppermute | solution.py:45
  98.3 10.1 %copy-start.16 = (f32[640,1280]{1,0:T(8,128)S(1)}, f32[640,1280]{1,0:T(8,128)}, u32[]{:S(2)}) copy-start(f32[640,1280]{1,0:T(8,128)} %fusion.3) | copy-start | bytes 9830404
  101.1 7.3 %copy-start.17 = (f32[1280,640]{1,0:T(8,128)}, f32[1280,640]{1,0:T(8,128)S(1)}, u32[]{:S(2)}) copy-start(f32[1280,640]{1,0:T(8,128)S(1)} %fusion.14) | copy-start | bytes 9830404
  102.3 4.6 %collective-permute-start.33 = (f32[1280]{0:T(1024)S(1)}, f32[1280]{0:T(1024)S(1)}, u32[]{:S(2)}, u32[]{:S(2)}) collective-permute-start(f32[1280]{0:T(1024)S(1)} %add_add_fusion), channel_id=1, source_target_pairs={{0,3},{1,2},{2,1},{3,0},{4,7},{5,6},{6,5},{7,4},{8,11},{9,10},{10,... | collective-permute-start | bytes 15368 | tf_op jit(solution)/shard_map/ppermute | solution.py:41
  103.8 3.7 %collective-permute-start.32 = (f32[1280]{0:T(1024)S(1)}, f32[1280]{0:T(1024)S(1)}, u32[]{:S(2)}, u32[]{:S(2)}) collective-permute-start(f32[1280]{0:T(1024)S(1)} %add_add_fusion), channel_id=1, source_target_pairs={{0,2},{1,3},{2,0},{3,1},{4,6},{5,7},{6,4},{7,5},{8,10},{9,11},{10,... | collective-permute-start | bytes 15368 | tf_op jit(solution)/shard_map/ppermute | solution.py:41
  104.2 3.7 %collective-permute-start.31 = (f32[1280]{0:T(1024)S(1)}, f32[1280]{0:T(1024)S(1)}, u32[]{:S(2)}, u32[]{:S(2)}) collective-permute-start(f32[1280]{0:T(1024)S(1)} %add_add_fusion), channel_id=1, source_target_pairs={{0,1},{1,0},{2,3},{3,2},{4,5},{5,4},{6,7},{7,6},{8,9},{9,8},{10,11... | collective-permute-start | bytes 15368 | tf_op jit(solution)/shard_map/ppermute | solution.py:41
  106.9 10.9 %collective-permute-start.16 = (bf16[4,160,640]{2,1,0:T(8,128)(2,1)}, bf16[4,160,640]{2,1,0:T(8,128)(2,1)}, u32[]{:S(2)}, u32[]{:S(2)}) collective-permute-start(bf16[4,160,640]{2,1,0:T(8,128)(2,1)} %fusion.2), channel_id=1, source_target_pairs={{0,4},{4,0},{8,12},{12,8},{16,20},{20,16},{24,28},{28,24},{1,5},{5... | collective-permute-start | bytes 2457608 | tf_op jit(solution)/shard_map/ppermute | solution.py:45
  112.1 5.7 %copy-start.18 = (f32[1280,640]{1,0:T(8,128)S(1)}, f32[1280,640]{1,0:T(8,128)}, u32[]{:S(2)}) copy-start(f32[1280,640]{1,0:T(8,128)} %copy-done.17) | copy-start | bytes 9830404
  114.2 9.9 %collective-permute-start.23 = (bf16[320,320]{1,0:T(8,128)(2,1)S(1)}, bf16[320,320]{1,0:T(8,128)(2,1)S(1)}, u32[]{:S(2)}, u32[]{:S(2)}) collective-permute-start(bf16[320,320]{1,0:T(8,128)(2,1)S(1)} %bitcast.94), channel_id=1, source_target_pairs={{0,3},{1,2},{2,1},{3,0},{4,7},{5,6},{6,5},{7,4},{8,11},{9,10},{10,... | collective-permute-start | bytes 614408 | tf_op jit(solution)/shard_map/ppermute | solution.py:41
  115.9 11.0 %collective-permute-start.21 = (bf16[320,320]{1,0:T(8,128)(2,1)S(1)}, bf16[320,320]{1,0:T(8,128)(2,1)S(1)}, u32[]{:S(2)}, u32[]{:S(2)}) collective-permute-start(bf16[320,320]{1,0:T(8,128)(2,1)S(1)} %bitcast.91), channel_id=1, source_target_pairs={{0,1},{1,0},{2,3},{3,2},{4,5},{5,4},{6,7},{7,6},{8,9},{9,8},{10,11... | collective-permute-start | bytes 614408 | tf_op jit(solution)/shard_map/ppermute | solution.py:41
  117.4 10.5 %collective-permute-start.22 = (bf16[320,320]{1,0:T(8,128)(2,1)S(1)}, bf16[320,320]{1,0:T(8,128)(2,1)S(1)}, u32[]{:S(2)}, u32[]{:S(2)}) collective-permute-start(bf16[320,320]{1,0:T(8,128)(2,1)S(1)} %bitcast.89), channel_id=1, source_target_pairs={{0,2},{1,3},{2,0},{3,1},{4,6},{5,7},{6,4},{7,5},{8,10},{9,11},{10,... | collective-permute-start | bytes 614408 | tf_op jit(solution)/shard_map/ppermute | solution.py:41
  119.3 11.6 %collective-permute-start.17 = (bf16[160,640]{1,0:T(8,128)(2,1)S(1)}, bf16[160,640]{1,0:T(8,128)(2,1)S(1)}, u32[]{:S(2)}, u32[]{:S(2)}) collective-permute-start(bf16[160,640]{1,0:T(8,128)(2,1)S(1)} %get-tuple-element.44), channel_id=1, source_target_pairs={{0,24},{4,28},{8,16},{12,20},{16,8},{20,12},{24,0},{28,4},{1,25},{... | collective-permute-start | bytes 614408 | tf_op jit(solution)/shard_map/ppermute | solution.py:45
  122.0 18.7 %collective-permute-start.19 = (bf16[160,640]{1,0:T(8,128)(2,1)S(1)}, bf16[160,640]{1,0:T(8,128)(2,1)S(1)}, u32[]{:S(2)}, u32[]{:S(2)}) collective-permute-start(bf16[160,640]{1,0:T(8,128)(2,1)S(1)} %get-tuple-element.45), channel_id=1, source_target_pairs={{0,8},{4,12},{8,0},{12,4},{16,24},{20,28},{24,16},{28,20},{1,9},{5... | collective-permute-start | bytes 614408 | tf_op jit(solution)/shard_map/ppermute | solution.py:45
  124.1 22.8 %collective-permute-start.18 = (bf16[160,640]{1,0:T(8,128)(2,1)S(1)}, bf16[160,640]{1,0:T(8,128)(2,1)S(1)}, u32[]{:S(2)}, u32[]{:S(2)}) collective-permute-start(bf16[160,640]{1,0:T(8,128)(2,1)S(1)} %get-tuple-element.46), channel_id=1, source_target_pairs={{0,16},{4,20},{8,24},{12,28},{16,0},{20,4},{24,8},{28,12},{1,17},{... | collective-permute-start | bytes 614408 | tf_op jit(solution)/shard_map/ppermute | solution.py:45
  128.2 19.5 %collective-permute-start.24 = (bf16[320,320]{1,0:T(8,128)(2,1)S(1)}, bf16[320,320]{1,0:T(8,128)(2,1)S(1)}, u32[]{:S(2)}, u32[]{:S(2)}) collective-permute-start(bf16[320,320]{1,0:T(8,128)(2,1)S(1)} %get-tuple-element.37), channel_id=1, source_target_pairs={{0,24},{4,28},{8,16},{12,20},{16,8},{20,12},{24,0},{28,4},{1,25},{... | collective-permute-start | bytes 614408 | tf_op jit(solution)/shard_map/ppermute | solution.py:45
  130.9 16.8 %collective-permute-start.26 = (bf16[320,320]{1,0:T(8,128)(2,1)S(1)}, bf16[320,320]{1,0:T(8,128)(2,1)S(1)}, u32[]{:S(2)}, u32[]{:S(2)}) collective-permute-start(bf16[320,320]{1,0:T(8,128)(2,1)S(1)} %get-tuple-element.38), channel_id=1, source_target_pairs={{0,8},{4,12},{8,0},{12,4},{16,24},{20,28},{24,16},{28,20},{1,9},{5... | collective-permute-start | bytes 614408 | tf_op jit(solution)/shard_map/ppermute | solution.py:45
  130.9 28.6 %collective-permute-start.25 = (bf16[320,320]{1,0:T(8,128)(2,1)S(1)}, bf16[320,320]{1,0:T(8,128)(2,1)S(1)}, u32[]{:S(2)}, u32[]{:S(2)}) collective-permute-start(bf16[320,320]{1,0:T(8,128)(2,1)S(1)} %get-tuple-element.39), channel_id=1, source_target_pairs={{0,16},{4,20},{8,24},{12,28},{16,0},{20,4},{24,8},{28,12},{1,17},{... | collective-permute-start | bytes 614408 | tf_op jit(solution)/shard_map/ppermute | solution.py:45

commit v3 on v2

--- a/solution.py
+++ b/solution.py
@@ -13,7 +13,7 @@
 PIECE = 16
 CORES = 2
 LANES = 128
-VMEM_BYTES = 48 * 1024 * 1024
+VMEM_BYTES = 32 * 1024 * 1024
 
 
 def vmem_call(body, out_shape, in_spaces, flops):
@@ -45,7 +45,7 @@
     return lax.ppermute(block, "seq", [(i, i ^ step) for i in range(count)])
 
 
-def gather_up(w_up, n_dp, n_seq, dp, core):
+def fetch_up(w_up, n_dp, n_seq, dp, core):
     rows, ff = w_up.shape
     cols, half = ff // n_dp, rows // CORES
     own = lax.dynamic_slice(w_up, (0, dp * cols), (rows, cols))
@@ -54,13 +54,15 @@
         piece = lax.dynamic_slice(w_up, (core * half, (dp ^ k) * cols), (half, cols))
         got.append(swap_dp(piece, n_dp, k))
     mine = jnp.stack(got)
-    mate = swap_seq(mine, n_seq, 1)
+    return own, mine, swap_seq(mine, n_seq, 1)
+
+
+def join_up(own, mine, mate, n_dp, dp, core):
     low = jnp.where(core == 0, mine, mate)
     high = jnp.where(core == 0, mate, mine)
     pairs = jnp.concatenate([low, high], axis=1)
     full = jnp.concatenate([own[None], pairs], axis=0)
-    order = dp ^ jnp.arange(n_dp)
-    return full[order].reshape(n_dp * rows, cols)
+    return full[dp ^ jnp.arange(n_dp)].reshape(-1, own.shape[1])
 
 
 def gather_gain(norm_gain, n_dp, dp):
@@ -212,7 +214,6 @@
     gk_ref,
     gv_ref,
     gr_ref,
-    gain_term_ref,
 ):
     tokens, feat = q_ref.shape
     scale = 1.0 / math.sqrt(HDIM)
@@ -220,7 +221,6 @@
     for part in range(got_ref.shape[0]):
         d_normed = d_normed + got_ref[part].astype(jnp.float32)
     unit = unit_ref[...]
-    gain_term_ref[...] = jnp.sum(d_normed * unit, axis=0, keepdims=True)
     d_unit = d_normed * gain_ref[...].astype(jnp.float32)
     d_hidden = inverse_ref[:, :1] * (
         d_unit
@@ -252,8 +252,7 @@
     tokens, feat = operands[0].shape
     return vmem_call(
         backward_kernel,
-        tuple(jax.ShapeDtypeStruct((tokens, feat), jnp.bfloat16) for _ in range(4))
-        + (jax.ShapeDtypeStruct((1, feat), jnp.float32),),
+        tuple(jax.ShapeDtypeStruct((tokens, feat), jnp.bfloat16) for _ in range(4)),
         [pltpu.VMEM] * 11,
         1 << 32,
     )(*operands)
@@ -278,29 +277,7 @@
     return total
 
 
-def scatter_down(term, n_seq, n_dp, seq, dp):
-    n_z, core, z = n_seq // CORES, seq % CORES, seq // CORES
-    rows, cols = term.shape
-    n_h, width = n_seq // n_dp, cols // n_dp
-    if n_h != CORES:
-        return scatter_down_direct(term, n_seq, n_dp, seq)
-    half = rows // CORES
-    keep = lax.dynamic_slice(term, (core * half, 0), (half, cols))
-    give = lax.dynamic_slice(term, ((1 - core) * half, 0), (half, cols))
-    both = (
-        keep.astype(jnp.float32) + swap_seq(give.astype(jnp.bfloat16), n_seq, 1).astype(jnp.float32)
-    ).astype(jnp.bfloat16)
-    pieces = both.reshape(half, n_dp, width).transpose(1, 0, 2)
-    planes = jnp.stack(
-        [pick(pieces, dp)] + [swap_dp(pick(pieces, dp ^ k), n_dp, k) for k in range(1, n_dp)]
-    )
-    total = pick(planes, dp ^ z).astype(jnp.float32)
-    for k in reversed(range(1, n_z)):
-        total = total + swap_seq(pick(planes, dp ^ z ^ k), n_seq, CORES * k).astype(jnp.float32)
-    return total
-
-
-def scatter_down_direct(term, n_seq, n_dp, seq):
+def scatter_down(term, n_seq, n_dp, seq):
     n_z, core, z = n_seq // CORES, seq % CORES, seq // CORES
     rows, cols = term.shape
     n_h, n_e = n_seq // n_dp, n_dp // CORES
@@ -338,6 +315,174 @@
     for k in range(1, n_dp):
         total = total + swap_dp(term, n_dp, k)
     return total
+
+
+def assemble_kernel(place_ref, own_ref, mine_ref, mate_ref, normed_ref, up_ref, act_ref, slope_ref):
+    rows = own_ref.shape[0]
+    half = rows // CORES
+    dp, core = place_ref[0], place_ref[1]
+    up_ref[pl.ds(pl.multiple_of(dp * rows, PIECE), rows), :] = own_ref[...]
+    for k in range(mine_ref.shape[0]):
+        base = (dp ^ (k + 1)) * rows
+        for ref, which in ((mine_ref, core), (mate_ref, 1 - core)):
+            up_ref[pl.ds(pl.multiple_of(base + which * half, PIECE), half), :] = ref[k]
+    pre_act = contract(normed_ref[...], up_ref[...], 1, 0)
+    sig_gate = jax.nn.sigmoid(1.702 * pre_act)
+    act_ref[...] = (pre_act * sig_gate).astype(jnp.bfloat16)
+    slope_ref[...] = sig_gate + 1.702 * pre_act * sig_gate * (1.0 - sig_gate)
+
+
+def assemble(place, own, mine, mate, normed_all):
+    tokens, feat = normed_all.shape
+    cols = own.shape[1]
+    return vmem_call(
+        assemble_kernel,
+        (
+            jax.ShapeDtypeStruct((feat, cols), jnp.bfloat16),
+            jax.ShapeDtypeStruct((tokens, cols), jnp.bfloat16),
+            jax.ShapeDtypeStruct((tokens, cols), jnp.float32),
+        ),
+        [pltpu.SMEM] + [pltpu.VMEM] * 4,
+        2 * tokens * feat * cols,
+    )(place, own, mine, mate, normed_all)
+
+
+def store_by_core(core, value, which, keep_ref, give_ref, index):
+    @pl.when(core == which)
+    def _():
+        keep_ref[index] = value
+
+    @pl.when(core != which)
+    def _():
+        give_ref[index] = value
+
+
+def down_kernel(place_ref, act_ref, rows_ref, keep_ref, give_ref):
+    n_dp, half, width = keep_ref.shape
+    term = contract(act_ref[...], rows_ref[...], 0, 0).astype(jnp.bfloat16)
+    for which in range(CORES):
+        for d in range(n_dp):
+            piece = term[which * half : (which + 1) * half, d * width : (d + 1) * width]
+            store_by_core(place_ref[1], piece, which, keep_ref, give_ref, d)
+
+
+def down_pieces(place, act_low, rows_all, n_dp):
+    tokens, feat = rows_all.shape
+    cols = act_low.shape[1]
+    piece = jax.ShapeDtypeStruct((n_dp, cols // CORES, feat // n_dp), jnp.bfloat16)
+    return vmem_call(
+        down_kernel, (piece, piece), [pltpu.SMEM] + [pltpu.VMEM] * 2, 2 * tokens * feat * cols
+    )(place, act_low, rows_all)
+
+
+def hidden_kernel(
+    rows_ref, down_ref, slope_ref, up_ref, normed_ref, gain_ref, pre_ref, own_ref, *rest
+):
+    tokens = own_ref.shape[0]
+    d_act = contract(rows_ref[...], down_ref[...], 1, 1)
+    d_pre = (d_act * slope_ref[...]).astype(jnp.bfloat16)
+    pre_ref[...] = d_pre
+    part = contract(d_pre, up_ref[...], 1, 1)
+    own_ref[...] = part[:tokens]
+    for k, ref in enumerate(rest[:-1]):
+        ref[...] = part[(k + 1) * tokens : (k + 2) * tokens].astype(jnp.bfloat16)
+    term = jnp.sum(part * normed_ref[...].astype(jnp.float32), axis=0, keepdims=True)
+    rest[-1][...] = term / gain_ref[...].astype(jnp.float32)
+
+
+def hidden_grads(rows_all, w_down, slope, up_cols, normed_all, gain, tokens):
+    total, feat = rows_all.shape
+    cols = slope.shape[1]
+    return vmem_call(
+        hidden_kernel,
+        (
+            jax.ShapeDtypeStruct((total, cols), jnp.bfloat16),
+            jax.ShapeDtypeStruct((tokens, feat), jnp.float32),
+        )
+        + tuple(
+            jax.ShapeDtypeStruct((tokens, feat), jnp.bfloat16) for _ in range(total // tokens - 1)
+        )
+        + (jax.ShapeDtypeStruct((1, feat), jnp.float32),),
+        [pltpu.VMEM] * 6,
+        4 * total * feat * cols,
+    )(rows_all, w_down, slope, up_cols, normed_all, gain)
+
+
+def up_kernel(place_ref, normed_ref, pre_ref, keep_ref, give_ref):
+    n_z, rows, cols = keep_ref.shape
+    term = contract(normed_ref[...], pre_ref[...], 0, 0).astype(jnp.bfloat16)
+    for z in range(n_z):
+        for which in range(CORES):
+            start = (z * CORES + which) * rows
+            piece = term[start : start + rows]
+            store_by_core(place_ref[1], piece, which, keep_ref, give_ref, z)
+
+
+def up_pieces(place, normed_all, d_pre, n_z):
+    tokens, feat = normed_all.shape
+    cols = d_pre.shape[1]
+    piece = jax.ShapeDtypeStruct((n_z, feat // n_z // CORES, cols), jnp.bfloat16)
+    return vmem_call(
+        up_kernel, (piece, piece), [pltpu.SMEM] + [pltpu.VMEM] * 2, 2 * tokens * feat * cols
+    )(place, normed_all, d_pre)
+
+
+def wide_sum(*terms):
+    return sum(term.astype(jnp.float32) for term in terms)
+
+
+def as_rows(vector, width):
+    high = lax.reduce_precision(vector, 8, 7)
+    low = vector - high
+    rows = jnp.concatenate([high.reshape(-1, width), low.reshape(-1, width)], axis=0)
+    return jnp.pad(rows.astype(jnp.bfloat16), ((0, PIECE - rows.shape[0]), (0, 0)))
+
+
+def from_rows(rows, length):
+    count = length // rows.shape[1]
+    return wide_sum(rows[:count], rows[count : 2 * count]).reshape(length)
+
+
+def weight_sums(up_both, down_both, gain_part, n_seq, n_dp, seq, dp):
+    n_z, z = n_seq // CORES, seq // CORES
+    up_keep, up_give = up_both
+    down_keep, down_give = down_both
+    feat = gain_part.shape[0]
+    flat = up_give.reshape(-1, up_give.shape[2])
+    sent = jnp.concatenate([flat, as_rows(gain_part, flat.shape[1])], axis=0)
+    down_mate = swap_seq(down_give, n_seq, 1)
+    up_got = swap_seq(sent, n_seq, 1)
+    up_mate = up_got[: flat.shape[0]].reshape(up_give.shape)
+    gain_part = gain_part + from_rows(up_got[flat.shape[0] :], feat)
+
+    half, width = down_keep.shape[1:]
+    gain_rows = as_rows(gain_part, width)
+
+    def down_piece(index):
+        piece = wide_sum(pick(down_keep, index), pick(down_mate, index)).astype(jnp.bfloat16)
+        return jnp.concatenate([piece, gain_rows], axis=0)
+
+    planes = jnp.stack(
+        [down_piece(dp)] + [swap_dp(down_piece(dp ^ k), n_dp, k) for k in range(1, n_dp)]
+    )
+    gain_part = sum(from_rows(planes[k, half:], feat) for k in range(n_dp))
+    gain_rows = as_rows(gain_part, width)
+
+    def up_piece(index):
+        return wide_sum(pick(up_keep, index), pick(up_mate, index))
+
+    up_total = up_piece(z)
+    for k in reversed(range(1, n_z)):
+        block = swap_seq(up_piece(z ^ k).astype(jnp.bfloat16), n_seq, CORES * k)
+        up_total = up_total + block.astype(jnp.float32)
+
+    down_total = pick(planes, dp ^ z)[:half].astype(jnp.float32)
+    for k in reversed(range(1, n_z)):
+        piece = jnp.concatenate([pick(planes, dp ^ z ^ k)[:half], gain_rows], axis=0)
+        block = swap_seq(piece, n_seq, CORES * k)
+        down_total = down_total + block[:half].astype(jnp.float32)
+        gain_part = gain_part + from_rows(block[half:], feat)
+    return up_total, down_total, gain_part
 
 
 def per_device(
@@ -362,7 +507,7 @@
     send, grad_rows = owner_rows(llm_grad[0], vision_slot, n_seq, tokens)
     w_up, norm_gain, send = lax.optimization_barrier((w_up, norm_gain, send))
     gain_full = gather_gain(norm_gain, n_dp, dp)
-    up_cols = gather_up(w_up, n_dp, n_seq, dp, core)
+    own, mine, mate = fetch_up(w_up, n_dp, n_seq, dp, core)
 
     attn_probs, attn_out, normal_unit, inverse = forward(
         window_mask[0], queries[0], key_rows[0], value_rows[0], resid_in[0]
@@ -371,29 +516,41 @@
 
     normed_all = gather_tokens(normed, n_dp)
     rows_all = gather_tokens(grad_rows, n_dp)
-    pre_act = contract(normed_all, up_cols, 1, 0)
-    sig_gate = jax.nn.sigmoid(1.702 * pre_act)
-    act_low = (pre_act * sig_gate).astype(jnp.bfloat16)
-    d_act = contract(rows_all, w_down, 1, 1)
-    d_pre = (d_act * (sig_gate + 1.702 * pre_act * sig_gate * (1.0 - sig_gate))).astype(
-        jnp.bfloat16
-    )
-    d_part = contract(d_pre, up_cols, 1, 1)
-    d_got = jnp.stack(
-        [
+    if n_seq == CORES * n_dp:
+        place = jnp.stack([dp, core]).astype(jnp.int32)
+        up_cols, act_low, slope = assemble(place, own, mine, mate, normed_all)
+        down_both = down_pieces(place, act_low, rows_all, n_dp)
+        d_pre, d_own, *d_parts, gain_part = hidden_grads(
+            rows_all, w_down, slope, up_cols, normed_all, gain_full[None], tokens
+        )
+        d_got = [swap_dp(part, n_dp, k + 1) for k, part in enumerate(d_parts)]
+        up_both = up_pieces(place, normed_all, d_pre, n_seq // CORES)
+        up_panel, down_panel, gain_total = weight_sums(
+            up_both, down_both, gain_part[0], n_seq, n_dp, seq, dp
+        )
+    else:
+        up_cols = join_up(own, mine, mate, n_dp, dp, core)
+        pre_act = contract(normed_all, up_cols, 1, 0)
+        sig_gate = jax.nn.sigmoid(1.702 * pre_act)
+        act_low = (pre_act * sig_gate).astype(jnp.bfloat16)
+        d_act = contract(rows_all, w_down, 1, 1)
+        d_pre = (d_act * (sig_gate + 1.702 * pre_act * sig_gate * (1.0 - sig_gate))).astype(
+            jnp.bfloat16
+        )
+        d_part = contract(d_pre, up_cols, 1, 1)
+        d_own = d_part[:tokens]
+        d_got = [
             swap_dp(d_part[k * tokens : (k + 1) * tokens].astype(jnp.bfloat16), n_dp, k)
             for k in range(1, n_dp)
         ]
-    )
-
-    up_term = contract(normed_all, d_pre, 0, 0)
-    down_term = contract(act_low, rows_all, 0, 0)
-    up_panel = scatter_up(up_term, n_seq, seq)
-    down_panel = scatter_down(down_term, n_seq, n_dp, seq, dp)
-
-    grad_query, grad_key, grad_value, grad_resid, gain_term = backward(
-        d_part[:tokens],
-        d_got,
+        up_panel = scatter_up(contract(normed_all, d_pre, 0, 0), n_seq, seq)
+        down_panel = scatter_down(contract(act_low, rows_all, 0, 0), n_seq, n_dp, seq)
+        gain_part = jnp.sum(d_part * normed_all.astype(jnp.float32), axis=0)
+        gain_total = sum_all(gain_part / gain_full.astype(jnp.float32), n_seq, n_dp)
+
+    grad_query, grad_key, grad_value, grad_resid = backward(
+        d_own,
+        jnp.stack(d_got),
         grad_rows,
         normal_unit,
         inverse,
@@ -405,7 +562,6 @@
         value_rows[0],
     )
     factor = 1.0 / math.sqrt(n_dp * n_seq * tokens)
-    gain_total = sum_all(gain_term[0], n_seq, n_dp)
     return (
         grad_query[None],
         grad_key[None],

time: 161 us -> 161 us (level); the launches traced: 160 us -> 158 us
  waiting for transfers between devices: 52.4 us -> 67.7 us
  starting transfers between devices: 53.3 us -> 38.8 us
  Pallas kernels: 10.5 us -> 21.6 us
  matrix products: 11 us -> 0 us
  local copies, waits for them, and re-layouts: 22 us -> 15.8 us
  other arithmetic: 9.97 us -> 13.1 us
    pallas_call x0 -> x4, Pallas kernels: none -> 11.2 us  [the longest x1 3.51 us: down_pieces(): vmem_call(down_kernel, (piece, piece), [pltpu.SMEM] + [pltpu.VMEM] * 2, 2...]
    dot_general x5 -> x0, matrix products: 11 us -> none  [contract(): lax.dot_general(left, right, (((left_dim,), (right_dim,)), ((), ())), pre...]
    ppermute x13 -> x9, starting transfers between devices: 22 us -> 11.1 us  [swap_seq(): return lax.ppermute(block, 'seq', [(i, i ^ step) for i in range(count)])]
    ppermute x13 -> x9, waiting for transfers between devices: 19.2 us -> 28.9 us  [swap_seq(): return lax.ppermute(block, 'seq', [(i, i ^ step) for i in range(count)])]
    ppermute x21 -> x18, waiting for transfers between devices: 33.2 us -> 38.8 us  [swap_dp(): return lax.ppermute(block, 'dp', [(i, i ^ step) for i in range(count)])]
    ppermute x21 -> x18, starting transfers between devices: 24.8 us -> 21.3 us  [swap_dp(): return lax.ppermute(block, 'dp', [(i, i ^ step) for i in range(count)])]
    unnamed x50 -> x56, local copies, waits for them, and re-layouts: 6.63 us -> 10.2 us
    gather x1 -> x0, local copies, waits for them, and re-layouts: 3.38 us -> none  [gather_up(): return full[order].reshape(n_dp * rows, cols)]
  transfers between devices with their start and end apart: 35 -> 28, of which waited for: 16 -> 12; matrix products, arithmetic and copies ran while one was open for 20% -> 9% of each run, Pallas kernels for 3% -> 7%
where the time goes in v3:
time: 161 us; the launch traced here: 158 us
  waiting for transfers between devices  67.7 us (42%)
  starting transfers between devices  38.8 us (24%)
  Pallas kernels  21.6 us (13%)
  local copies, waits for them, and re-layouts  15.8 us (10%)
  other arithmetic  13.1 us (8%)
    ppermute x18, waiting for transfers between devices, swap_dp(): return lax.ppermute(block, 'dp', [(i, i ^ step) for i in range(count)])  38.8 us
    ppermute x9, waiting for transfers between devices, swap_seq(): return lax.ppermute(block, 'seq', [(i, i ^ step) for i in range(count)])  28.9 us
    ppermute x18, starting transfers between devices, swap_dp(): return lax.ppermute(block, 'dp', [(i, i ^ step) for i in range(count)])  21.3 us
    ppermute x9, starting transfers between devices, swap_seq(): return lax.ppermute(block, 'seq', [(i, i ^ step) for i in range(count)])  11.1 us
    unnamed x56, local copies, waits for them, and re-layouts  10.2 us
    all_to_all x1, starting transfers between devices, owner_rows(): got = lax.all_to_all(send, 'seq', split_axis=0, concat_axis=0, tiled=True)  6.47 us
    pallas_call x1, Pallas kernels, backward(): vmem_call(backward_kernel, tuple((jax.ShapeDtypeStruct((tokens, feat), jn...  4.64 us
    pallas_call x1, Pallas kernels, forward(): vmem_call(forward_kernel, (jax.ShapeDtypeStruct((HEADS, tokens, tokens),...  3.81 us
  transfers between devices with their start and end apart: 28, of which 12 were waited for; matrix products, arithmetic and copies ran while one was open for 9% of the time, Pallas kernels for 7%

profile of v3, /device:TPU:0, one launch (start us, length us, event | category | flops | bytes accessed | tf_op | source)
XLA Modules:
  0.0 158.0 jit_solution(15833650099988503701)
XLA Ops:
  0.7 1.0 copy-done.5
  1.7 0.7 copy-done.6
  2.4 1.7 %shard_map.153 = bf16[8,32,1408]{2,1,0:T(8,128)(2,1)} custom-call(s32[1,192]{1,0:T(1,128)S(1)} %copy-done.6, bf16[192,1280]{1,0:T(8,128)(2,1)S(1)} %bitcast.68), custom_call_target="tpu_custom_call" | custom-call | flops 1048576 | bytes 4194304 | tf_op jit(solution)/shard_map/pallas_call | solution.py:112
  4.1 6.5 %all-to-all-start = ((bf16[8,32,1408]{2,1,0:T(8,128)(2,1)}), bf16[8,32,1408]{2,1,0:T(8,128)(2,1)S(1)}, u32[]{:S(2)}, u32[]{:S(2)}) async-start(bf16[8,32,1408]{2,1,0:T(8,128)(2,1)} %shard_map.153), calls=%async_computation | async-start | bytes 1441792 | tf_op jit(solution)/shard_map/all_to_all | solution.py:118
  10.5 2.5 %collective-permute-start.9 = (bf16[320]{0:T(512)(128)(2,1)S(1)}, bf16[320]{0:T(512)(128)(2,1)S(1)}, u32[]{:S(2)}, u32[]{:S(2)}) collective-permute-start(bf16[320]{0:T(512)(128)(2,1)S(1)} %copy-done.27), channel_id=1, source_target_pairs={{0,3},{1,2},{2,1},{3,0},{4,7},{5,6},{6,5},{7,4},{8,11},{9,10},{10,... | collective-permute-start | bytes 1928 | tf_op jit(solution)/shard_map/ppermute | solution.py:41
  14.1 1.9 %fusion.29 = (bf16[160,640]{1,0:T(8,128)(2,1)S(1)}, bf16[160,640]{1,0:T(8,128)(2,1)}, bf16[160,640]{1,0:T(8,128)(2,1)}) fusion(bf16[320,2560]{1,0:T(8,128)(2,1)} %param.17, s32[]{:T(128)S(6)} %select_n.87, s32[]{:T(128)S(6)} %select_n.88, s32[]{:T(128)S(6)} %select_n.90, s32[]{:T(128)S(6)} %select_n.89), kind=kLoop, calls=%fused_computation.76 | loop fusion | bytes 1228816 | tf_op jit(solution)/shard_map/dynamic_slice | solution.py:54
  16.0 2.4 %collective-permute-start.5 = (bf16[160,640]{1,0:T(8,128)(2,1)}, bf16[160,640]{1,0:T(8,128)(2,1)}, u32[]{:S(2)}, u32[]{:S(2)}) collective-permute-start(bf16[160,640]{1,0:T(8,128)(2,1)} %get-tuple-element.63), channel_id=1, source_target_pairs={{0,3},{1,2},{2,1},{3,0},{4,7},{5,6},{6,5},{7,4},{8,11},{9,10},{10,... | collective-permute-start | bytes 614408 | tf_op jit(solution)/shard_map/ppermute | solution.py:41
  19.0 3.8 %shard_map.155 = (f32[16,128,128]{2,1,0:T(8,128)S(1)}, bf16[128,1280]{1,0:T(8,128)(2,1)S(1)}, f32[128,1280]{1,0:T(8,128)S(1)}, f32[128,128]{1,0:T(8,128)S(1)}) custom-call(s32[2,2]{1,0:T(2,128)S(1)} %bitcast.76, bf16[128,1280]{1,0:T(8,128)(2,1)S(1)} %bitcast.70, bf16[128,1280]{1,0:T(8,128)(2,1)S(1)} %bitcast.72, bf16[128,1280]{1,0:T(8,128)(2,1)S(1)} %bitcast.74, ...), custom_call_target="tpu_custom_call" | custom-call | flops 2147483648 | bytes 4194304 | tf_op jit(solution)/shard_map/pallas_call | solution.py:188
  22.8 1.0 copy-done.22
  23.9 0.6 collective-permute-start.3
  24.5 0.6 gather_fusion
  25.2 3.0 %collective-permute-done.4 = bf16[160,640]{1,0:T(8,128)(2,1)} collective-permute-done((bf16[160,640]{1,0:T(8,128)(2,1)}, bf16[160,640]{1,0:T(8,128)(2,1)}, u32[]{:S(2)}, u32[]{:S(2)}) %collective-permute-start.4) | collective-permute-done | bytes 204832 | tf_op jit(solution)/shard_map/ppermute | solution.py:41
  28.2 1.7 %collective-permute-done.3 = bf16[160,640]{1,0:T(8,128)(2,1)S(1)} collective-permute-done((bf16[160,640]{1,0:T(8,128)(2,1)S(1)}, bf16[160,640]{1,0:T(8,128)(2,1)S(1)}, u32[]{:S(2)}, u32[]{:S(2)}) %collective-permute-start.3) | collective-permute-done | bytes 204832 | tf_op jit(solution)/shard_map/ppermute | solution.py:41
  29.9 1.1 pad_maximum_fusion.5.mine_ref
  31.1 0.8 multiply_convert_fusion
  31.9 1.5 collective-permute-start.12
  33.9 1.5 collective-permute-start.10
  35.5 1.0 constant_dynamic-slice_fusion.own_ref
  36.9 1.6 collective-permute-start.2
  38.5 5.2 %collective-permute-done.12 = bf16[128,1280]{1,0:T(8,128)(2,1)} collective-permute-done((bf16[128,1280]{1,0:T(8,128)(2,1)}, bf16[128,1280]{1,0:T(8,128)(2,1)}, u32[]{:S(2)}, u32[]{:S(2)}) %collective-permute-start.12) | collective-permute-done | bytes 327712 | tf_op jit(solution)/shard_map/ppermute | solution.py:41
  43.7 1.5 collective-permute-start.1
  45.2 5.5 %collective-permute-done.11 = bf16[128,1280]{1,0:T(8,128)(2,1)} collective-permute-done((bf16[128,1280]{1,0:T(8,128)(2,1)}, bf16[128,1280]{1,0:T(8,128)(2,1)}, u32[]{:S(2)}, u32[]{:S(2)}) %collective-permute-start.11) | collective-permute-done | bytes 327712 | tf_op jit(solution)/shard_map/ppermute | solution.py:41
  50.7 0.5 collective-permute-start
  51.3 1.4 pad_maximum_fusion.1.normed_ref
  52.6 2.6 %shard_map.156 = (bf16[1280,640]{1,0:T(8,128)(2,1)S(1)}, bf16[512,640]{1,0:T(8,128)(2,1)S(1)}, f32[512,640]{1,0:T(8,128)S(1)}) custom-call(s32[2]{0:T(128)S(1)} %pad_add_fusion.place_ref, bf16[320,640]{1,0:T(8,128)(2,1)S(1)} %constant_dynamic-slice_fusion.own_ref, bf16[3,160,640]{2,1,0:T(8,128)(2,1)S(1)} %pad_maximum_fusion.5.mine_ref, ...), custom_call_target="tpu_custom_call" | custom-call | flops 838860800 | bytes 4194304 | tf_op jit(solution)/shard_map/pallas_call | solution.py:338
  55.2 2.4 %collective-permute-done.2 = bf16[128,1280]{1,0:T(8,128)(2,1)S(1)} collective-permute-done((bf16[128,1280]{1,0:T(8,128)(2,1)S(1)}, bf16[128,1280]{1,0:T(8,128)(2,1)S(1)}, u32[]{:S(2)}, u32[]{:S(2)}) %collective-permute-start.2) | collective-permute-done | bytes 327712 | tf_op jit(solution)/shard_map/ppermute | solution.py:41
  57.6 6.5 %collective-permute-done.1 = bf16[128,1280]{1,0:T(8,128)(2,1)S(1)} collective-permute-done((bf16[128,1280]{1,0:T(8,128)(2,1)S(1)}, bf16[128,1280]{1,0:T(8,128)(2,1)S(1)}, u32[]{:S(2)}, u32[]{:S(2)}) %collective-permute-start.1) | collective-permute-done | bytes 327712 | tf_op jit(solution)/shard_map/ppermute | solution.py:41
  64.4 3.2 %shard_map.157 = (bf16[512,640]{1,0:T(8,128)(2,1)S(1)}, f32[128,1280]{1,0:T(8,128)S(1)}, bf16[128,1280]{1,0:T(8,128)(2,1)S(1)}, bf16[128,1280]{1,0:T(8,128)(2,1)...) custom-call(bf16[512,1280]{1,0:T(8,128)(2,1)S(1)} %pad_maximum_fusion.rows_ref, bf16[640,1280]{1,0:T(8,128)(2,1)S(1)} %copy-done, ...), custom_call_target="tpu_custom_call" | custom-call | flops 1677721600 | bytes 4194304 | tf_op jit(solution)/shard_map/pallas_call | solution.py:396
  67.6 0.8 copy-done.7
  68.4 0.8 copy-done.9
  69.3 0.7 copy-done.17
  70.0 1.1 copy-done.10
  71.1 2.0 %shard_map.159 = (bf16[4,160,640]{2,1,0:T(8,128)(2,1)S(1)}, bf16[4,160,640]{2,1,0:T(8,128)(2,1)S(1)}) custom-call(s32[2]{0:T(128)S(1)} %pad_add_fusion.place_ref, bf16[512,1280]{1,0:T(8,128)(2,1)S(1)} %pad_maximum_fusion.1.normed_ref, bf16[512,640]{1,0:T(8,128)(2,1)S(1)} %copy-done.10), custom_call_target="tpu_custom_call" | custom-call | flops 838860800 | bytes 4194304 | tf_op jit(solution)/shard_map/pallas_call | solution.py:425
  73.1 0.9 copy-done.1
  74.0 3.5 %shard_map.160 = (bf16[4,320,320]{2,1,0:T(8,128)(2,1)S(1)}, bf16[4,320,320]{2,1,0:T(8,128)(2,1)}) custom-call(s32[2]{0:T(128)S(1)} %pad_add_fusion.place_ref, bf16[512,640]{1,0:T(8,128)(2,1)S(1)} %copy-done.21, bf16[512,1280]{1,0:T(8,128)(2,1)S(1)} %pad_maximum_fusion.rows_ref), custom_call_target="tpu_custom_call" | custom-call | flops 838860800 | bytes 4194304 | tf_op jit(solution)/shard_map/pallas_call | solution.py:373
  77.6 1.0 pad_maximum_fusion.4
  79.1 1.3 collective-permute-start.15
  80.4 0.6 collective-permute-start.14
  81.1 1.5 collective-permute-start.13
  82.7 8.2 %collective-permute-done.15 = bf16[128,1280]{1,0:T(8,128)(2,1)S(1)} collective-permute-done((bf16[128,1280]{1,0:T(8,128)(2,1)}, bf16[128,1280]{1,0:T(8,128)(2,1)S(1)}, u32[]{:S(2)}, u32[]{:S(2)}) %collective-permute-start.15) | collective-permute-done | bytes 327712 | tf_op jit(solution)/shard_map/ppermute | solution.py:41
  90.8 6.0 %collective-permute-done.14 = bf16[128,1280]{1,0:T(8,128)(2,1)S(1)} collective-permute-done((bf16[128,1280]{1,0:T(8,128)(2,1)}, bf16[128,1280]{1,0:T(8,128)(2,1)S(1)}, u32[]{:S(2)}, u32[]{:S(2)}) %collective-permute-start.14) | collective-permute-done | bytes 327712 | tf_op jit(solution)/shard_map/ppermute | solution.py:41
  96.8 0.7 copy-done.26
  97.6 1.1 pad_maximum_fusion.3.got_ref
  98.7 2.4 %fusion.9 = (bf16[320,320]{1,0:T(8,128)(2,1)}, bf16[320,320]{1,0:T(8,128)(2,1)}, bf16[320,320]{1,0:T(8,128)(2,1)}, bf16[320,320]{1,0:T(8,128)(2,1)}) fusion(bf16[4,320,320]{2,1,0:T(8,128)(2,1)} %collective-permute-done.20, s32[]{:T(128)S(6)} %select_n.97, bf16[4,320,320]{2,1,0:T(8,128)(2,1)S(1)} %get-tuple-element.51, s32[]{:T(128)S(6)} %select_n.100, ...), kind=kLoop, calls=%fused_computation.33 | loop fusion | flops 1638400 | bytes 2457616 | tf_op jit(solution)/shard_map/convert_element_type | solution.py:462
  101.1 0.8 convert_add_fusion.4
  102.1 1.5 fusion.8
  103.5 1.5 collective-permute-start.23
  105.0 0.6 collective-permute-start.22
  105.6 1.5 collective-permute-start.21
  107.1 1.2 copy-done.23
  108.3 1.0 copy-done.25
  109.3 4.6 %shard_map.158 = (bf16[128,1280]{1,0:T(8,128)(2,1)}, bf16[128,1280]{1,0:T(8,128)(2,1)}, bf16[128,1280]{1,0:T(8,128)(2,1)}, bf16[128,1280]{1,0:T(8,128)(2,1)}) custom-call(f32[128,1280]{1,0:T(8,128)S(1)} %copy-done.8, bf16[3,128,1280]{2,1,0:T(8,128)(2,1)S(1)} %pad_maximum_fusion.3.got_ref, bf16[128,1280]{1,0:T(8,128)(2,1)S(1)} %shard_map.154.rows_ref, ...), custom_call_target="tpu_custom_call" | custom-call | flops 4294967296 | bytes 4194304 | tf_op jit(solution)/shard_map/pallas_call | solution.py:253
  113.9 1.3 slice.143
  115.5 1.8 %collective-permute-start.19 = (bf16[160,640]{1,0:T(8,128)(2,1)S(1)}, bf16[160,640]{1,0:T(8,128)(2,1)S(1)}, u32[]{:S(2)}, u32[]{:S(2)}) collective-permute-start(bf16[160,640]{1,0:T(8,128)(2,1)S(1)} %get-tuple-element.60), channel_id=1, source_target_pairs={{0,8},{4,12},{8,0},{12,4},{16,24},{20,28},{24,16},{28,20},{1,9},{5... | collective-permute-start | bytes 614408 | tf_op jit(solution)/shard_map/ppermute | solution.py:45
  117.2 2.4 %collective-permute-start.18 = (bf16[160,640]{1,0:T(8,128)(2,1)S(1)}, bf16[160,640]{1,0:T(8,128)(2,1)S(1)}, u32[]{:S(2)}, u32[]{:S(2)}) collective-permute-start(bf16[160,640]{1,0:T(8,128)(2,1)S(1)} %get-tuple-element.61), channel_id=1, source_target_pairs={{0,16},{4,20},{8,24},{12,28},{16,0},{20,4},{24,8},{28,12},{1,17},{... | collective-permute-start | bytes 614408 | tf_op jit(solution)/shard_map/ppermute | solution.py:45
  120.4 0.9 collective-permute-start.26
  121.3 5.9 %collective-permute-done.19 = bf16[160,640]{1,0:T(8,128)(2,1)S(1)} collective-permute-done((bf16[160,640]{1,0:T(8,128)(2,1)S(1)}, bf16[160,640]{1,0:T(8,128)(2,1)S(1)}, u32[]{:S(2)}, u32[]{:S(2)}) %collective-permute-start.19) | collective-permute-done | bytes 204832 | tf_op jit(solution)/shard_map/ppermute | solution.py:45
  127.2 7.7 %collective-permute-done.18 = bf16[160,640]{1,0:T(8,128)(2,1)S(1)} collective-permute-done((bf16[160,640]{1,0:T(8,128)(2,1)S(1)}, bf16[160,640]{1,0:T(8,128)(2,1)S(1)}, u32[]{:S(2)}, u32[]{:S(2)}) %collective-permute-start.18) | collective-permute-done | bytes 204832 | tf_op jit(solution)/shard_map/ppermute | solution.py:45
  134.9 0.8 fusion.7
  135.8 3.8 %collective-permute-start.25 = (bf16[336,320]{1,0:T(8,128)(2,1)S(1)}, bf16[336,320]{1,0:T(8,128)(2,1)S(1)}, u32[]{:S(2)}, u32[]{:S(2)}) collective-permute-start(bf16[336,320]{1,0:T(8,128)(2,1)S(1)} %get-tuple-element.69), channel_id=1, source_target_pairs={{0,16},{4,20},{8,24},{12,28},{16,0},{20,4},{24,8},{28,12},{1,17},{... | collective-permute-start | bytes 645128 | tf_op jit(solution)/shard_map/ppermute | solution.py:45
  139.6 1.5 collective-permute-start.24
  141.1 15.2 %collective-permute-done.25 = bf16[336,320]{1,0:T(8,128)(2,1)S(1)} collective-permute-done((bf16[336,320]{1,0:T(8,128)(2,1)S(1)}, bf16[336,320]{1,0:T(8,128)(2,1)S(1)}, u32[]{:S(2)}, u32[]{:S(2)}) %collective-permute-start.25) | collective-permute-done | bytes 215072 | tf_op jit(solution)/shard_map/ppermute | solution.py:45
  156.6 0.6 add_multiply_fusion
  157.2 0.8 fusion.3
  (104 shorter events, 5.2 us)
Async XLA Ops:
  0.6 9.9 %copy-start.27 = (bf16[320]{0:T(512)(128)(2,1)S(1)}, bf16[320]{0:T(512)(128)(2,1)}, u32[]{:S(2)}) copy-start(bf16[320]{0:T(512)(128)(2,1)} %param.19) | copy-start | bytes 1924
  0.6 1.0 copy-start.5
  1.7 0.7 copy-start.6
  4.0 14.9 %copy-start.11 = (bf16[1,128,1280]{2,1,0:T(8,128)(2,1)S(1)}, bf16[1,128,1280]{2,1,0:T(8,128)(2,1)}, u32[]{:S(2)}) copy-start(bf16[1,128,1280]{2,1,0:T(8,128)(2,1)} %param.13) | copy-start | bytes 983044
  4.0 14.9 %copy-start.12 = (bf16[1,128,1280]{2,1,0:T(8,128)(2,1)S(1)}, bf16[1,128,1280]{2,1,0:T(8,128)(2,1)}, u32[]{:S(2)}) copy-start(bf16[1,128,1280]{2,1,0:T(8,128)(2,1)} %param.10) | copy-start | bytes 983044
  4.0 14.9 %copy-start.13 = (bf16[1,128,1280]{2,1,0:T(8,128)(2,1)S(1)}, bf16[1,128,1280]{2,1,0:T(8,128)(2,1)}, u32[]{:S(2)}) copy-start(bf16[1,128,1280]{2,1,0:T(8,128)(2,1)} %param.11) | copy-start | bytes 983044
  4.0 14.9 %copy-start.15 = (bf16[1,128,1280]{2,1,0:T(8,128)(2,1)S(1)}, bf16[1,128,1280]{2,1,0:T(8,128)(2,1)}, u32[]{:S(2)}) copy-start(bf16[1,128,1280]{2,1,0:T(8,128)(2,1)} %param.12) | copy-start | bytes 983044
  4.0 14.9 %copy-start.19 = (s32[1,2,2]{2,1,0:T(2,128)S(1)}, s32[1,2,2]{2,1,0:T(2,128)}, u32[]{:S(2)}) copy-start(s32[1,2,2]{2,1,0:T(2,128)} %param.16) | copy-start | bytes 52
  4.1 32.5 %all-to-all-start = ((bf16[8,32,1408]{2,1,0:T(8,128)(2,1)}), bf16[8,32,1408]{2,1,0:T(8,128)(2,1)S(1)}, u32[]{:S(2)}, u32[]{:S(2)}) async-start(bf16[8,32,1408]{2,1,0:T(8,128)(2,1)} %shard_map.153), calls=%async_computation | async-start | bytes 1441792 | tf_op jit(solution)/shard_map/all_to_all | solution.py:118
  10.5 13.3 %collective-permute-start.9 = (bf16[320]{0:T(512)(128)(2,1)S(1)}, bf16[320]{0:T(512)(128)(2,1)S(1)}, u32[]{:S(2)}, u32[]{:S(2)}) collective-permute-start(bf16[320]{0:T(512)(128)(2,1)S(1)} %copy-done.27), channel_id=1, source_target_pairs={{0,3},{1,2},{2,1},{3,0},{4,7},{5,6},{6,5},{7,4},{8,11},{9,10},{10,... | collective-permute-start | bytes 1928 | tf_op jit(solution)/shard_map/ppermute | solution.py:41
  13.0 11.4 %collective-permute-start.8 = (bf16[320]{0:T(512)(128)(2,1)S(1)}, bf16[320]{0:T(512)(128)(2,1)S(1)}, u32[]{:S(2)}, u32[]{:S(2)}) collective-permute-start(bf16[320]{0:T(512)(128)(2,1)S(1)} %copy-done.27), channel_id=1, source_target_pairs={{0,2},{1,3},{2,0},{3,1},{4,6},{5,7},{6,4},{7,5},{8,10},{9,11},{10,... | collective-permute-start | bytes 1928 | tf_op jit(solution)/shard_map/ppermute | solution.py:41
  13.6 10.9 %collective-permute-start.7 = (bf16[320]{0:T(512)(128)(2,1)S(1)}, bf16[320]{0:T(512)(128)(2,1)S(1)}, u32[]{:S(2)}, u32[]{:S(2)}) collective-permute-start(bf16[320]{0:T(512)(128)(2,1)S(1)} %copy-done.27), channel_id=1, source_target_pairs={{0,1},{1,0},{2,3},{3,2},{4,5},{5,4},{6,7},{7,6},{8,9},{9,8},{10,11... | collective-permute-start | bytes 1928 | tf_op jit(solution)/shard_map/ppermute | solution.py:41
  16.0 9.2 %collective-permute-start.5 = (bf16[160,640]{1,0:T(8,128)(2,1)}, bf16[160,640]{1,0:T(8,128)(2,1)}, u32[]{:S(2)}, u32[]{:S(2)}) collective-permute-start(bf16[160,640]{1,0:T(8,128)(2,1)} %get-tuple-element.63), channel_id=1, source_target_pairs={{0,3},{1,2},{2,1},{3,0},{4,7},{5,6},{6,5},{7,4},{8,11},{9,10},{10,... | collective-permute-start | bytes 614408 | tf_op jit(solution)/shard_map/ppermute | solution.py:41
  18.5 9.7 %collective-permute-start.4 = (bf16[160,640]{1,0:T(8,128)(2,1)}, bf16[160,640]{1,0:T(8,128)(2,1)}, u32[]{:S(2)}, u32[]{:S(2)}) collective-permute-start(bf16[160,640]{1,0:T(8,128)(2,1)} %get-tuple-element.64), channel_id=1, source_target_pairs={{0,2},{1,3},{2,0},{3,1},{4,6},{5,7},{6,4},{7,5},{8,10},{9,11},{10,... | collective-permute-start | bytes 614408 | tf_op jit(solution)/shard_map/ppermute | solution.py:41
  22.8 1.0 copy-start.22
  23.8 11.6 %copy-start.24 = (bf16[128,1280]{1,0:T(8,128)(2,1)}, bf16[128,1280]{1,0:T(8,128)(2,1)S(1)}, u32[]{:S(2)}) copy-start(bf16[128,1280]{1,0:T(8,128)(2,1)S(1)} %get-tuple-element.41.out_ref) | copy-start | bytes 983044
  23.8 13.1 %copy-start.3 = (f32[128,1280]{1,0:T(8,128)}, f32[128,1280]{1,0:T(8,128)S(1)}, u32[]{:S(2)}) copy-start(f32[128,1280]{1,0:T(8,128)S(1)} %get-tuple-element.31.unit_ref) | copy-start | bytes 1966084
  23.9 6.1 %collective-permute-start.3 = (bf16[160,640]{1,0:T(8,128)(2,1)S(1)}, bf16[160,640]{1,0:T(8,128)(2,1)S(1)}, u32[]{:S(2)}, u32[]{:S(2)}) collective-permute-start(bf16[160,640]{1,0:T(8,128)(2,1)S(1)} %get-tuple-element.62), channel_id=1, source_target_pairs={{0,1},{1,0},{2,3},{3,2},{4,5},{5,4},{6,7},{7,6},{8,9},{9,8},{10,11... | collective-permute-start | bytes 614408 | tf_op jit(solution)/shard_map/ppermute | solution.py:41
  31.1 21.6 %collective-permute-start.6 = (bf16[3,160,640]{2,1,0:T(8,128)(2,1)S(1)}, bf16[3,160,640]{2,1,0:T(8,128)(2,1)}, u32[]{:S(2)}, u32[]{:S(2)}) collective-permute-start(bf16[3,160,640]{2,1,0:T(8,128)(2,1)S(1)} %pad_maximum_fusion.5.mine_ref), channel_id=1, source_target_pairs={{0,4},{4,0},{8,12},{12,8},{16,20},{20,16},{24,28},{28,24},{1,5},{5... | collective-permute-start | bytes 1843208 | tf_op jit(solution)/shard_map/ppermute | solution.py:45
  31.9 11.8 %collective-permute-start.12 = (bf16[128,1280]{1,0:T(8,128)(2,1)}, bf16[128,1280]{1,0:T(8,128)(2,1)}, u32[]{:S(2)}, u32[]{:S(2)}) collective-permute-start(bf16[128,1280]{1,0:T(8,128)(2,1)} %multiply_convert_fusion), channel_id=1, source_target_pairs={{0,3},{1,2},{2,1},{3,0},{4,7},{5,6},{6,5},{7,4},{8,11},{9,10},{10,... | collective-permute-start | bytes 983048 | tf_op jit(solution)/shard_map/ppermute | solution.py:41
  33.4 17.3 %collective-permute-start.11 = (bf16[128,1280]{1,0:T(8,128)(2,1)}, bf16[128,1280]{1,0:T(8,128)(2,1)}, u32[]{:S(2)}, u32[]{:S(2)}) collective-permute-start(bf16[128,1280]{1,0:T(8,128)(2,1)} %multiply_convert_fusion), channel_id=1, source_target_pairs={{0,2},{1,3},{2,0},{3,1},{4,6},{5,7},{6,4},{7,5},{8,10},{9,11},{10,... | collective-permute-start | bytes 983048 | tf_op jit(solution)/shard_map/ppermute | solution.py:41
  33.9 17.4 %collective-permute-start.10 = (bf16[128,1280]{1,0:T(8,128)(2,1)}, bf16[128,1280]{1,0:T(8,128)(2,1)}, u32[]{:S(2)}, u32[]{:S(2)}) collective-permute-start(bf16[128,1280]{1,0:T(8,128)(2,1)} %multiply_convert_fusion), channel_id=1, source_target_pairs={{0,1},{1,0},{2,3},{3,2},{4,5},{5,4},{6,7},{7,6},{8,9},{9,8},{10,11... | collective-permute-start | bytes 983048 | tf_op jit(solution)/shard_map/ppermute | solution.py:41
  36.9 20.8 %collective-permute-start.2 = (bf16[128,1280]{1,0:T(8,128)(2,1)S(1)}, bf16[128,1280]{1,0:T(8,128)(2,1)S(1)}, u32[]{:S(2)}, u32[]{:S(2)}) collective-permute-start(bf16[128,1280]{1,0:T(8,128)(2,1)S(1)} %shard_map.154.rows_ref), channel_id=1, source_target_pairs={{0,3},{1,2},{2,1},{3,0},{4,7},{5,6},{6,5},{7,4},{8,11},{9,10},{10,... | collective-permute-start | bytes 983048 | tf_op jit(solution)/shard_map/ppermute | solution.py:41
  43.7 20.5 %collective-permute-start.1 = (bf16[128,1280]{1,0:T(8,128)(2,1)S(1)}, bf16[128,1280]{1,0:T(8,128)(2,1)S(1)}, u32[]{:S(2)}, u32[]{:S(2)}) collective-permute-start(bf16[128,1280]{1,0:T(8,128)(2,1)S(1)} %shard_map.154.rows_ref), channel_id=1, source_target_pairs={{0,2},{1,3},{2,0},{3,1},{4,6},{5,7},{6,4},{7,5},{8,10},{9,11},{10,... | collective-permute-start | bytes 983048 | tf_op jit(solution)/shard_map/ppermute | solution.py:41
  50.7 13.6 %collective-permute-start = (bf16[128,1280]{1,0:T(8,128)(2,1)S(1)}, bf16[128,1280]{1,0:T(8,128)(2,1)S(1)}, u32[]{:S(2)}, u32[]{:S(2)}) collective-permute-start(bf16[128,1280]{1,0:T(8,128)(2,1)S(1)} %shard_map.154.rows_ref), channel_id=1, source_target_pairs={{0,1},{1,0},{2,3},{3,2},{4,5},{5,4},{6,7},{7,6},{8,9},{9,8},{10,11... | collective-permute-start | bytes 983048 | tf_op jit(solution)/shard_map/ppermute | solution.py:41
  55.2 12.4 %copy-start.20 = (bf16[512,640]{1,0:T(8,128)(2,1)}, bf16[512,640]{1,0:T(8,128)(2,1)S(1)}, u32[]{:S(2)}) copy-start(bf16[512,640]{1,0:T(8,128)(2,1)S(1)} %get-tuple-element.50.act_ref) | copy-start | bytes 1966084
  55.2 9.2 %copy-start = (bf16[640,1280]{1,0:T(8,128)(2,1)S(1)}, bf16[640,1280]{1,0:T(8,128)(2,1)}, u32[]{:S(2)}) copy-start(bf16[640,1280]{1,0:T(8,128)(2,1)} %down_ref.1) | copy-start | bytes 4915204
  67.6 0.8 copy-start.7
  68.4 0.8 copy-start.9
  69.3 0.7 copy-start.17
  70.0 1.1 copy-start.10
  71.1 2.9 %copy-start.21 = (bf16[512,640]{1,0:T(8,128)(2,1)S(1)}, bf16[512,640]{1,0:T(8,128)(2,1)}, u32[]{:S(2)}) copy-start(bf16[512,640]{1,0:T(8,128)(2,1)} %copy-done.20) | copy-start | bytes 1966084
  73.1 0.9 copy-start.1
  74.0 7.0 %copy-start.18 = (bf16[128,1280]{1,0:T(8,128)(2,1)S(1)}, bf16[128,1280]{1,0:T(8,128)(2,1)}, u32[]{:S(2)}) copy-start(bf16[128,1280]{1,0:T(8,128)(2,1)} %copy-done.17) | copy-start | bytes 983044
  77.6 21.1 %collective-permute-start.20 = (bf16[4,320,320]{2,1,0:T(8,128)(2,1)}, bf16[4,320,320]{2,1,0:T(8,128)(2,1)}, u32[]{:S(2)}, u32[]{:S(2)}) collective-permute-start(bf16[4,320,320]{2,1,0:T(8,128)(2,1)} %get-tuple-element.52), channel_id=1, source_target_pairs={{0,4},{4,0},{8,12},{12,8},{16,20},{20,16},{24,28},{28,24},{1,5},{5... | collective-permute-start | bytes 2457608 | tf_op jit(solution)/shard_map/ppermute | solution.py:45
  78.6 22.5 %collective-permute-start.16 = (bf16[656,640]{1,0:T(8,128)(2,1)}, bf16[656,640]{1,0:T(8,128)(2,1)}, u32[]{:S(2)}, u32[]{:S(2)}) collective-permute-start(bf16[656,640]{1,0:T(8,128)(2,1)} %pad_maximum_fusion.4), channel_id=1, source_target_pairs={{0,4},{4,0},{8,12},{12,8},{16,20},{20,16},{24,28},{28,24},{1,5},{5... | collective-permute-start | bytes 2519048 | tf_op jit(solution)/shard_map/ppermute | solution.py:45
  79.1 11.7 %collective-permute-start.15 = (bf16[128,1280]{1,0:T(8,128)(2,1)}, bf16[128,1280]{1,0:T(8,128)(2,1)S(1)}, u32[]{:S(2)}, u32[]{:S(2)}) collective-permute-start(bf16[128,1280]{1,0:T(8,128)(2,1)} %get-tuple-element.38), channel_id=1, source_target_pairs={{0,3},{1,2},{2,1},{3,0},{4,7},{5,6},{6,5},{7,4},{8,11},{9,10},{10,... | collective-permute-start | bytes 983048 | tf_op jit(solution)/shard_map/ppermute | solution.py:41
  80.4 16.4 %collective-permute-start.14 = (bf16[128,1280]{1,0:T(8,128)(2,1)}, bf16[128,1280]{1,0:T(8,128)(2,1)S(1)}, u32[]{:S(2)}, u32[]{:S(2)}) collective-permute-start(bf16[128,1280]{1,0:T(8,128)(2,1)} %get-tuple-element.37), channel_id=1, source_target_pairs={{0,2},{1,3},{2,0},{3,1},{4,6},{5,7},{6,4},{7,5},{8,10},{9,11},{10,... | collective-permute-start | bytes 983048 | tf_op jit(solution)/shard_map/ppermute | solution.py:41
  81.1 15.8 %collective-permute-start.13 = (bf16[128,1280]{1,0:T(8,128)(2,1)S(1)}, bf16[128,1280]{1,0:T(8,128)(2,1)S(1)}, u32[]{:S(2)}, u32[]{:S(2)}) collective-permute-start(bf16[128,1280]{1,0:T(8,128)(2,1)S(1)} %copy-done.18), channel_id=1, source_target_pairs={{0,1},{1,0},{2,3},{3,2},{4,5},{5,4},{6,7},{7,6},{8,9},{9,8},{10,11... | collective-permute-start | bytes 983048 | tf_op jit(solution)/shard_map/ppermute | solution.py:41
  96.8 0.7 copy-start.26
  101.1 6.0 %copy-start.4 = (f32[128,1280]{1,0:T(8,128)S(1)}, f32[128,1280]{1,0:T(8,128)}, u32[]{:S(2)}) copy-start(f32[128,1280]{1,0:T(8,128)} %copy-done.3) | copy-start | bytes 1966084
  101.1 6.0 %copy-start.8 = (f32[128,1280]{1,0:T(8,128)S(1)}, f32[128,1280]{1,0:T(8,128)}, u32[]{:S(2)}) copy-start(f32[128,1280]{1,0:T(8,128)} %copy-done.7) | copy-start | bytes 1966084
  101.1 6.0 %copy-start.14 = (bf16[1,128,1280]{2,1,0:T(8,128)(2,1)S(1)}, bf16[1,128,1280]{2,1,0:T(8,128)(2,1)}, u32[]{:S(2)}) copy-start(bf16[1,128,1280]{2,1,0:T(8,128)(2,1)} %param.11) | copy-start | bytes 983044
  102.0 5.1 %copy-start.16 = (bf16[1,128,1280]{2,1,0:T(8,128)(2,1)S(1)}, bf16[1,128,1280]{2,1,0:T(8,128)(2,1)}, u32[]{:S(2)}) copy-start(bf16[1,128,1280]{2,1,0:T(8,128)(2,1)} %param.12) | copy-start | bytes 983044
  103.5 16.1 %collective-permute-start.23 = (bf16[336,320]{1,0:T(8,128)(2,1)S(1)}, bf16[336,320]{1,0:T(8,128)(2,1)S(1)}, u32[]{:S(2)}, u32[]{:S(2)}) collective-permute-start(bf16[336,320]{1,0:T(8,128)(2,1)S(1)} %get-tuple-element.74), channel_id=1, source_target_pairs={{0,3},{1,2},{2,1},{3,0},{4,7},{5,6},{6,5},{7,4},{8,11},{9,10},{10,... | collective-permute-start | bytes 645128 | tf_op jit(solution)/shard_map/ppermute | solution.py:41
  105.0 15.0 %collective-permute-start.22 = (bf16[336,320]{1,0:T(8,128)(2,1)S(1)}, bf16[336,320]{1,0:T(8,128)(2,1)S(1)}, u32[]{:S(2)}, u32[]{:S(2)}) collective-permute-start(bf16[336,320]{1,0:T(8,128)(2,1)S(1)} %get-tuple-element.73), channel_id=1, source_target_pairs={{0,2},{1,3},{2,0},{3,1},{4,6},{5,7},{6,4},{7,5},{8,10},{9,11},{10,... | collective-permute-start | bytes 645128 | tf_op jit(solution)/shard_map/ppermute | solution.py:41
  105.6 14.4 %collective-permute-start.21 = (bf16[336,320]{1,0:T(8,128)(2,1)S(1)}, bf16[336,320]{1,0:T(8,128)(2,1)S(1)}, u32[]{:S(2)}, u32[]{:S(2)}) collective-permute-start(bf16[336,320]{1,0:T(8,128)(2,1)S(1)} %get-tuple-element.72), channel_id=1, source_target_pairs={{0,1},{1,0},{2,3},{3,2},{4,5},{5,4},{6,7},{7,6},{8,9},{9,8},{10,11... | collective-permute-start | bytes 645128 | tf_op jit(solution)/shard_map/ppermute | solution.py:41
  107.1 1.2 copy-start.23
  108.3 1.0 copy-start.25
  113.9 1.4 copy-start.2
  115.5 11.7 %collective-permute-start.19 = (bf16[160,640]{1,0:T(8,128)(2,1)S(1)}, bf16[160,640]{1,0:T(8,128)(2,1)S(1)}, u32[]{:S(2)}, u32[]{:S(2)}) collective-permute-start(bf16[160,640]{1,0:T(8,128)(2,1)S(1)} %get-tuple-element.60), channel_id=1, source_target_pairs={{0,8},{4,12},{8,0},{12,4},{16,24},{20,28},{24,16},{28,20},{1,9},{5... | collective-permute-start | bytes 614408 | tf_op jit(solution)/shard_map/ppermute | solution.py:45
  117.2 17.7 %collective-permute-start.18 = (bf16[160,640]{1,0:T(8,128)(2,1)S(1)}, bf16[160,640]{1,0:T(8,128)(2,1)S(1)}, u32[]{:S(2)}, u32[]{:S(2)}) collective-permute-start(bf16[160,640]{1,0:T(8,128)(2,1)S(1)} %get-tuple-element.61), channel_id=1, source_target_pairs={{0,16},{4,20},{8,24},{12,28},{16,0},{20,4},{24,8},{28,12},{1,17},{... | collective-permute-start | bytes 614408 | tf_op jit(solution)/shard_map/ppermute | solution.py:45
  119.6 15.3 %collective-permute-start.17 = (bf16[160,640]{1,0:T(8,128)(2,1)S(1)}, bf16[160,640]{1,0:T(8,128)(2,1)S(1)}, u32[]{:S(2)}, u32[]{:S(2)}) collective-permute-start(bf16[160,640]{1,0:T(8,128)(2,1)S(1)} %get-tuple-element.59), channel_id=1, source_target_pairs={{0,24},{4,28},{8,16},{12,20},{16,8},{20,12},{24,0},{28,4},{1,25},{... | collective-permute-start | bytes 614408 | tf_op jit(solution)/shard_map/ppermute | solution.py:45
  120.4 20.6 %collective-permute-start.26 = (bf16[336,320]{1,0:T(8,128)(2,1)S(1)}, bf16[336,320]{1,0:T(8,128)(2,1)S(1)}, u32[]{:S(2)}, u32[]{:S(2)}) collective-permute-start(bf16[336,320]{1,0:T(8,128)(2,1)S(1)} %get-tuple-element.70), channel_id=1, source_target_pairs={{0,8},{4,12},{8,0},{12,4},{16,24},{20,28},{24,16},{28,20},{1,9},{5... | collective-permute-start | bytes 645128 | tf_op jit(solution)/shard_map/ppermute | solution.py:45
  135.8 20.6 %collective-permute-start.25 = (bf16[336,320]{1,0:T(8,128)(2,1)S(1)}, bf16[336,320]{1,0:T(8,128)(2,1)S(1)}, u32[]{:S(2)}, u32[]{:S(2)}) collective-permute-start(bf16[336,320]{1,0:T(8,128)(2,1)S(1)} %get-tuple-element.69), channel_id=1, source_target_pairs={{0,16},{4,20},{8,24},{12,28},{16,0},{20,4},{24,8},{28,12},{1,17},{... | collective-permute-start | bytes 645128 | tf_op jit(solution)/shard_map/ppermute | solution.py:45
  139.6 16.9 %collective-permute-start.24 = (bf16[336,320]{1,0:T(8,128)(2,1)S(1)}, bf16[336,320]{1,0:T(8,128)(2,1)S(1)}, u32[]{:S(2)}, u32[]{:S(2)}) collective-permute-start(bf16[336,320]{1,0:T(8,128)(2,1)S(1)} %get-tuple-element.68), channel_id=1, source_target_pairs={{0,24},{4,28},{8,16},{12,20},{16,8},{20,12},{24,0},{28,4},{1,25},{... | collective-permute-start | bytes 645128 | tf_op jit(solution)/shard_map/ppermute | solution.py:45

commit v4 on v2

--- a/solution.py
+++ b/solution.py
@@ -13,7 +13,7 @@
 PIECE = 16
 CORES = 2
 LANES = 128
-VMEM_BYTES = 48 * 1024 * 1024
+VMEM_BYTES = 32 * 1024 * 1024
 
 
 def vmem_call(body, out_shape, in_spaces, flops):
@@ -45,7 +45,7 @@
     return lax.ppermute(block, "seq", [(i, i ^ step) for i in range(count)])
 
 
-def gather_up(w_up, n_dp, n_seq, dp, core):
+def fetch_pieces(w_up, n_dp, n_seq, dp, core):
     rows, ff = w_up.shape
     cols, half = ff // n_dp, rows // CORES
     own = lax.dynamic_slice(w_up, (0, dp * cols), (rows, cols))
@@ -54,13 +54,15 @@
         piece = lax.dynamic_slice(w_up, (core * half, (dp ^ k) * cols), (half, cols))
         got.append(swap_dp(piece, n_dp, k))
     mine = jnp.stack(got)
-    mate = swap_seq(mine, n_seq, 1)
+    return own, mine, swap_seq(mine, n_seq, 1)
+
+
+def join_up(own, mine, mate, n_dp, dp, core):
     low = jnp.where(core == 0, mine, mate)
     high = jnp.where(core == 0, mate, mine)
     pairs = jnp.concatenate([low, high], axis=1)
     full = jnp.concatenate([own[None], pairs], axis=0)
-    order = dp ^ jnp.arange(n_dp)
-    return full[order].reshape(n_dp * rows, cols)
+    return full[dp ^ jnp.arange(n_dp)].reshape(-1, own.shape[1])
 
 
 def gather_gain(norm_gain, n_dp, dp):
@@ -120,7 +122,7 @@
         [pltpu.VMEM],
         1 << 26,
     )(got.reshape(n_seq * rows, feat + LANES))
-    return send, landed
+    return landed
 
 
 def head_lanes(head, rows, width, start):
@@ -197,7 +199,6 @@
 
 
 def backward_kernel(
-    own_ref,
     got_ref,
     rows_ref,
     unit_ref,
@@ -212,15 +213,11 @@
     gk_ref,
     gv_ref,
     gr_ref,
-    gain_term_ref,
 ):
     tokens, feat = q_ref.shape
     scale = 1.0 / math.sqrt(HDIM)
-    d_normed = own_ref[...]
-    for part in range(got_ref.shape[0]):
-        d_normed = d_normed + got_ref[part].astype(jnp.float32)
+    d_normed = sum(got_ref[part].astype(jnp.float32) for part in range(got_ref.shape[0]))
     unit = unit_ref[...]
-    gain_term_ref[...] = jnp.sum(d_normed * unit, axis=0, keepdims=True)
     d_unit = d_normed * gain_ref[...].astype(jnp.float32)
     d_hidden = inverse_ref[:, :1] * (
         d_unit
@@ -249,12 +246,11 @@
 
 
 def backward(*operands):
-    tokens, feat = operands[0].shape
+    tokens, feat = operands[1].shape
     return vmem_call(
         backward_kernel,
-        tuple(jax.ShapeDtypeStruct((tokens, feat), jnp.bfloat16) for _ in range(4))
-        + (jax.ShapeDtypeStruct((1, feat), jnp.float32),),
-        [pltpu.VMEM] * 11,
+        tuple(jax.ShapeDtypeStruct((tokens, feat), jnp.bfloat16) for _ in range(4)),
+        [pltpu.VMEM] * 10,
         1 << 32,
     )(*operands)
 
@@ -278,29 +274,7 @@
     return total
 
 
-def scatter_down(term, n_seq, n_dp, seq, dp):
-    n_z, core, z = n_seq // CORES, seq % CORES, seq // CORES
-    rows, cols = term.shape
-    n_h, width = n_seq // n_dp, cols // n_dp
-    if n_h != CORES:
-        return scatter_down_direct(term, n_seq, n_dp, seq)
-    half = rows // CORES
-    keep = lax.dynamic_slice(term, (core * half, 0), (half, cols))
-    give = lax.dynamic_slice(term, ((1 - core) * half, 0), (half, cols))
-    both = (
-        keep.astype(jnp.float32) + swap_seq(give.astype(jnp.bfloat16), n_seq, 1).astype(jnp.float32)
-    ).astype(jnp.bfloat16)
-    pieces = both.reshape(half, n_dp, width).transpose(1, 0, 2)
-    planes = jnp.stack(
-        [pick(pieces, dp)] + [swap_dp(pick(pieces, dp ^ k), n_dp, k) for k in range(1, n_dp)]
-    )
-    total = pick(planes, dp ^ z).astype(jnp.float32)
-    for k in reversed(range(1, n_z)):
-        total = total + swap_seq(pick(planes, dp ^ z ^ k), n_seq, CORES * k).astype(jnp.float32)
-    return total
-
-
-def scatter_down_direct(term, n_seq, n_dp, seq):
+def scatter_down(term, n_seq, n_dp, seq):
     n_z, core, z = n_seq // CORES, seq % CORES, seq // CORES
     rows, cols = term.shape
     n_h, n_e = n_seq // n_dp, n_dp // CORES
@@ -338,6 +312,232 @@
     for k in range(1, n_dp):
         total = total + swap_dp(term, n_dp, k)
     return total
+
+
+def fetch_kernel(place_ref, up_ref, gain_ref, out_ref):
+    n_dp, _, cols = out_ref.shape
+    half = up_ref.shape[0] // CORES
+    rows = pl.ds(pl.multiple_of(place_ref[1] * half, PIECE), half)
+    gain = gain_ref[...].astype(jnp.float32)
+    gain = jnp.concatenate([gain, jnp.zeros((1, cols - gain.shape[1]), jnp.float32)], axis=1)
+    gain = jnp.broadcast_to(gain, (PIECE, cols)).astype(jnp.bfloat16)
+    for d in range(n_dp):
+        out_ref[d, :half, :] = up_ref[rows, d * cols : (d + 1) * cols]
+        out_ref[d, half:, :] = gain
+
+
+def fetch_up(place, w_up, norm_gain, n_dp):
+    rows, ff = w_up.shape
+    shape = (n_dp, rows // CORES + PIECE, ff // n_dp)
+    sent = vmem_call(
+        fetch_kernel,
+        jax.ShapeDtypeStruct(shape, jnp.bfloat16),
+        [pltpu.SMEM, pltpu.VMEM, pltpu.VMEM],
+        1 << 20,
+    )(place, w_up, norm_gain[None])
+    return lax.all_to_all(sent, "dp", split_axis=0, concat_axis=0, tiled=True)
+
+
+def assemble_kernel(place_ref, mine_ref, mate_ref, *refs):
+    *normed_refs, up_ref, act_ref, slope_ref, flip_ref, all_ref = refs
+    n_dp, half, cols = mine_ref.shape
+    half = half - PIECE
+    core = place_ref[1]
+    for d in range(n_dp):
+        for ref, which in ((mine_ref, core), (mate_ref, 1 - core)):
+            base = (d * CORES + which) * half
+            up_ref[pl.ds(pl.multiple_of(base, PIECE), half), :] = ref[d, :half, :]
+    tokens = normed_refs[0].shape[0]
+    for k, ref in enumerate(normed_refs):
+        all_ref[k * tokens : (k + 1) * tokens, :] = ref[...]
+        flip_ref[:, k * tokens : (k + 1) * tokens] = ref[...].T
+    pre_act = contract(all_ref[...], up_ref[...], 1, 0)
+    sig_gate = jax.nn.sigmoid(1.702 * pre_act)
+    act_ref[...] = (pre_act * sig_gate).astype(jnp.bfloat16).T
+    slope_ref[...] = sig_gate + 1.702 * pre_act * sig_gate * (1.0 - sig_gate)
+
+
+def assemble(place, mine, mate, normed_blocks):
+    tokens, feat = normed_blocks[0].shape
+    total = tokens * len(normed_blocks)
+    cols = mine.shape[2]
+    return vmem_call(
+        assemble_kernel,
+        (
+            jax.ShapeDtypeStruct((feat, cols), jnp.bfloat16),
+            jax.ShapeDtypeStruct((cols, total), jnp.bfloat16),
+            jax.ShapeDtypeStruct((total, cols), jnp.float32),
+            jax.ShapeDtypeStruct((feat, total), jnp.bfloat16),
+            jax.ShapeDtypeStruct((total, feat), jnp.bfloat16),
+        ),
+        [pltpu.SMEM] + [pltpu.VMEM] * (2 + len(normed_blocks)),
+        2 * total * feat * cols,
+    )(place, mine, mate, *normed_blocks)
+
+
+def store_by_core(core, value, which, keep_ref, give_ref, index):
+    @pl.when(core == which)
+    def _():
+        keep_ref[index] = value
+
+    @pl.when(core != which)
+    def _():
+        give_ref[index] = value
+
+
+def up_kernel(
+    place_ref, rows_ref, down_ref, slope_ref, flip_ref, pre_ref, keep_ref, give_ref
+):
+    n_z, rows, cols = keep_ref.shape
+    d_act = contract(rows_ref[...], down_ref[...], 1, 1)
+    d_pre = (d_act * slope_ref[...]).astype(jnp.bfloat16)
+    pre_ref[...] = d_pre
+    term = contract(flip_ref[...], d_pre, 1, 0).astype(jnp.bfloat16)
+    for z in range(n_z):
+        for which in range(CORES):
+            start = (z * CORES + which) * rows
+            piece = term[start : start + rows]
+            store_by_core(place_ref[1], piece, which, keep_ref, give_ref, z)
+
+
+def up_pieces(place, rows_all, w_down, slope, normed_flip, n_z):
+    total, feat = rows_all.shape
+    cols = slope.shape[1]
+    piece = jax.ShapeDtypeStruct((n_z, feat // n_z // CORES, cols), jnp.bfloat16)
+    return vmem_call(
+        up_kernel,
+        (jax.ShapeDtypeStruct((total, cols), jnp.bfloat16), piece, piece),
+        [pltpu.SMEM] + [pltpu.VMEM] * 4,
+        4 * total * feat * cols,
+    )(place, rows_all, w_down, slope, normed_flip)
+
+
+def down_kernel(place_ref, act_ref, rows_ref, keep_ref, give_ref):
+    n_dp, half, width = keep_ref.shape
+    term = contract(act_ref[...], rows_ref[...], 1, 0).astype(jnp.bfloat16)
+    for which in range(CORES):
+        for d in range(n_dp):
+            piece = term[which * half : (which + 1) * half, d * width : (d + 1) * width]
+            store_by_core(place_ref[1], piece, which, keep_ref, give_ref, d)
+
+
+def down_pieces(place, act_flip, rows_all, n_dp):
+    tokens, feat = rows_all.shape
+    cols = act_flip.shape[0]
+    piece = jax.ShapeDtypeStruct((n_dp, cols // CORES, feat // n_dp), jnp.bfloat16)
+    return vmem_call(
+        down_kernel, (piece, piece), [pltpu.SMEM] + [pltpu.VMEM] * 2, 2 * tokens * feat * cols
+    )(place, act_flip, rows_all)
+
+
+def part_kernel(place_ref, pre_ref, up_ref, normed_ref, gain_ref, parts_ref, term_ref):
+    n_dp, tokens, _ = parts_ref.shape
+    part = contract(pre_ref[...], up_ref[...], 1, 1)
+    for k in range(n_dp):
+        rows = part[k * tokens : (k + 1) * tokens]
+        parts_ref[place_ref[0] ^ k] = rows.astype(jnp.bfloat16)
+    term = jnp.sum(part * normed_ref[...].astype(jnp.float32), axis=0, keepdims=True)
+    term_ref[...] = term / gain_ref[...].astype(jnp.float32)
+
+
+def normed_parts(place, d_pre, up_cols, normed_all, gain, n_dp):
+    total, feat = normed_all.shape
+    return vmem_call(
+        part_kernel,
+        (
+            jax.ShapeDtypeStruct((n_dp, total // n_dp, feat), jnp.bfloat16),
+            jax.ShapeDtypeStruct((1, feat), jnp.float32),
+        ),
+        [pltpu.SMEM] + [pltpu.VMEM] * 4,
+        2 * total * feat * d_pre.shape[1],
+    )(place, d_pre, up_cols, normed_all, gain)
+
+
+def wide_sum(*terms):
+    return sum(term.astype(jnp.float32) for term in terms)
+
+
+def to_rows(vector, width):
+    high = vector.astype(jnp.bfloat16).astype(jnp.float32)
+    rows = [
+        part[:, at : at + width]
+        for part in (high, vector - high)
+        for at in range(0, vector.shape[1], width)
+    ]
+    rows.append(jnp.zeros((PIECE - len(rows), width), jnp.float32))
+    return jnp.concatenate(rows, axis=0).astype(jnp.bfloat16)
+
+
+def plane_kernel(keep_ref, mate_ref, term_ref, other_ref, out_ref):
+    n_dp, half, width = keep_ref.shape
+    rows = to_rows(term_ref[...] + other_ref[...], width)
+    for d in range(n_dp):
+        out_ref[d, :half, :] = wide_sum(keep_ref[d], mate_ref[d]).astype(jnp.bfloat16)
+        out_ref[d, half:, :] = rows
+
+
+def rise_kernel(place_ref, got_ref, own_ref, *send_refs):
+    half = got_ref.shape[1] - PIECE
+    z = place_ref[2]
+    rows = wide_sum(*(got_ref[d, half:, :] for d in range(got_ref.shape[0])))
+    count = got_ref.shape[0]
+    total = rows[:count] + rows[count : 2 * count]
+    high = total.astype(jnp.bfloat16).astype(jnp.float32)
+    pad = jnp.zeros((PIECE - 2 * count, rows.shape[1]), jnp.float32)
+    rows = jnp.concatenate([high, total - high, pad], axis=0).astype(jnp.bfloat16)
+    for k, ref in enumerate((own_ref,) + send_refs):
+        ref[:half, :] = got_ref[z ^ k, :half, :]
+        ref[half:, :] = rows
+
+
+def last_kernel(factor, *refs):
+    *in_refs, down_ref, gain_ref = refs
+    half = down_ref.shape[0]
+    count = gain_ref.shape[0]
+    down_ref[...] = (wide_sum(*(ref[:half, :] for ref in in_refs)) * factor).astype(jnp.bfloat16)
+    rows = wide_sum(*(ref[half:, :] for ref in in_refs))
+    gain_ref[...] = (rows[:count] + rows[count : 2 * count]) * factor
+
+
+def weight_sums(place, up_both, down_both, term, factor, n_seq, n_dp, seq):
+    n_z, z = n_seq // CORES, seq // CORES
+    up_keep, up_give = up_both
+    down_keep, down_give = down_both
+    up_mate = swap_seq(up_give, n_seq, 1)
+    down_mate = swap_seq(down_give, n_seq, 1)
+    other = swap_seq(term, n_seq, 1)
+
+    def up_piece(index):
+        return wide_sum(pick(up_keep, index), pick(up_mate, index))
+
+    up_total = up_piece(z)
+    for k in reversed(range(1, n_z)):
+        block = swap_seq(up_piece(z ^ k).astype(jnp.bfloat16), n_seq, CORES * k)
+        up_total = up_total + block.astype(jnp.float32)
+
+    half, width = down_keep.shape[1:]
+    planes = vmem_call(
+        plane_kernel,
+        jax.ShapeDtypeStruct((n_dp, half + PIECE, width), jnp.bfloat16),
+        [pltpu.VMEM] * 4,
+        1 << 20,
+    )(down_keep, down_mate, term, other)
+    planes = lax.all_to_all(planes, "dp", split_axis=0, concat_axis=0, tiled=True)
+    piece = jax.ShapeDtypeStruct((half + PIECE, width), jnp.bfloat16)
+    own, *sends = vmem_call(
+        rise_kernel, (piece,) * n_z, [pltpu.SMEM, pltpu.VMEM], 1 << 20
+    )(place, planes)
+    got = [swap_seq(block, n_seq, CORES * (k + 1)) for k, block in enumerate(sends)]
+    down_total, gain_total = vmem_call(
+        lambda *refs: last_kernel(factor, *refs),
+        (
+            jax.ShapeDtypeStruct((half, width), jnp.bfloat16),
+            jax.ShapeDtypeStruct((n_dp, width), jnp.float32),
+        ),
+        [pltpu.VMEM] * n_z,
+        1 << 20,
+    )(own, *got)
+    return (up_total * factor).astype(jnp.bfloat16), down_total, gain_total.reshape(-1)
 
 
 def per_device(
@@ -359,40 +559,57 @@
     core = seq % CORES
     tokens, feat_dim = queries.shape[1:]
 
-    send, grad_rows = owner_rows(llm_grad[0], vision_slot, n_seq, tokens)
-    w_up, norm_gain, send = lax.optimization_barrier((w_up, norm_gain, send))
-    gain_full = gather_gain(norm_gain, n_dp, dp)
-    up_cols = gather_up(w_up, n_dp, n_seq, dp, core)
+    factor = 1.0 / math.sqrt(n_dp * n_seq * tokens)
+    place = jnp.stack([dp, core, seq // CORES]).astype(jnp.int32)
+    quick = n_seq == CORES * n_dp
+
+    if quick:
+        mine = fetch_up(place, w_up, norm_gain, n_dp)
+        mate = swap_seq(mine, n_seq, 1)
+        gain_full = mine[:, -1, : norm_gain.shape[0]].reshape(-1)
+    else:
+        gain_full = gather_gain(norm_gain, n_dp, dp)
+        own, mine, mate = fetch_pieces(w_up, n_dp, n_seq, dp, core)
+    grad_rows = owner_rows(llm_grad[0], vision_slot, n_seq, tokens)
 
     attn_probs, attn_out, normal_unit, inverse = forward(
         window_mask[0], queries[0], key_rows[0], value_rows[0], resid_in[0]
     )
     normed = (normal_unit * gain_full.astype(jnp.float32)).astype(jnp.bfloat16)
-
-    normed_all = gather_tokens(normed, n_dp)
+    normed_blocks = [normed] + [swap_dp(normed, n_dp, k) for k in range(1, n_dp)]
     rows_all = gather_tokens(grad_rows, n_dp)
-    pre_act = contract(normed_all, up_cols, 1, 0)
-    sig_gate = jax.nn.sigmoid(1.702 * pre_act)
-    act_low = (pre_act * sig_gate).astype(jnp.bfloat16)
-    d_act = contract(rows_all, w_down, 1, 1)
-    d_pre = (d_act * (sig_gate + 1.702 * pre_act * sig_gate * (1.0 - sig_gate))).astype(
-        jnp.bfloat16
-    )
-    d_part = contract(d_pre, up_cols, 1, 1)
-    d_got = jnp.stack(
-        [
-            swap_dp(d_part[k * tokens : (k + 1) * tokens].astype(jnp.bfloat16), n_dp, k)
-            for k in range(1, n_dp)
-        ]
-    )
-
-    up_term = contract(normed_all, d_pre, 0, 0)
-    down_term = contract(act_low, rows_all, 0, 0)
-    up_panel = scatter_up(up_term, n_seq, seq)
-    down_panel = scatter_down(down_term, n_seq, n_dp, seq, dp)
-
-    grad_query, grad_key, grad_value, grad_resid, gain_term = backward(
-        d_part[:tokens],
+    if quick:
+        up_cols, act_flip, slope, normed_flip, normed_all = assemble(
+            place, mine, mate, normed_blocks
+        )
+        d_pre, *up_both = up_pieces(place, rows_all, w_down, slope, normed_flip, n_seq // CORES)
+        down_both = down_pieces(place, act_flip, rows_all, n_dp)
+        parts, term = normed_parts(place, d_pre, up_cols, normed_all, gain_full[None], n_dp)
+        d_got = lax.all_to_all(parts, "dp", split_axis=0, concat_axis=0, tiled=True)
+        grad_up, grad_down, grad_gain = weight_sums(
+            place, up_both, down_both, term, factor, n_seq, n_dp, seq
+        )
+    else:
+        normed_all = jnp.concatenate(normed_blocks, axis=0)
+        up_cols = join_up(own, mine, mate, n_dp, dp, core)
+        pre_act = contract(normed_all, up_cols, 1, 0)
+        sig_gate = jax.nn.sigmoid(1.702 * pre_act)
+        act_low = (pre_act * sig_gate).astype(jnp.bfloat16)
+        d_act = contract(rows_all, w_down, 1, 1)
+        d_pre = (d_act * (sig_gate + 1.702 * pre_act * sig_gate * (1.0 - sig_gate))).astype(
+            jnp.bfloat16
+        )
+        d_part = contract(d_pre, up_cols, 1, 1)
+        blocks = d_part.astype(jnp.bfloat16).reshape(n_dp, tokens, feat_dim)
+        d_got = jnp.stack([blocks[0]] + [swap_dp(blocks[k], n_dp, k) for k in range(1, n_dp)])
+        up_sum = scatter_up(contract(normed_all, d_pre, 0, 0), n_seq, seq)
+        down_sum = scatter_down(contract(act_low, rows_all, 0, 0), n_seq, n_dp, seq)
+        gain_part = jnp.sum(d_part * normed_all.astype(jnp.float32), axis=0)
+        grad_gain = factor * sum_all(gain_part / gain_full.astype(jnp.float32), n_seq, n_dp)
+        grad_up = (up_sum * factor).astype(jnp.bfloat16)
+        grad_down = (down_sum * factor).astype(jnp.bfloat16)
+
+    grad_query, grad_key, grad_value, grad_resid = backward(
         d_got,
         grad_rows,
         normal_unit,
@@ -404,16 +621,14 @@
         key_rows[0],
         value_rows[0],
     )
-    factor = 1.0 / math.sqrt(n_dp * n_seq * tokens)
-    gain_total = sum_all(gain_term[0], n_seq, n_dp)
     return (
         grad_query[None],
         grad_key[None],
         grad_value[None],
         grad_resid[None],
-        (up_panel * factor).astype(jnp.bfloat16),
-        (down_panel * factor).astype(jnp.bfloat16),
-        gain_total * factor,
+        grad_up,
+        grad_down,
+        grad_gain,
     )
 
 

time: 161 us -> 146 us (0.907)
  the two profiles are of different devices: /device:TPU:0 before, /device:TPU:8 now
where the time goes in v4:
time: 146 us
  waiting for transfers between devices  64.8 us (44%)
  starting transfers between devices  33.2 us (23%)
  Pallas kernels  25.7 us (18%)
  local copies, waits for them, and re-layouts  14.4 us (10%)
  other arithmetic  6.53 us (4%)
    ppermute x10, waiting for transfers between devices, swap_seq(): return lax.ppermute(block, 'seq', [(i, i ^ step) for i in range(count)])  25.8 us
    ppermute x6, waiting for transfers between devices, swap_dp(): return lax.ppermute(block, 'dp', [(i, i ^ step) for i in range(count)])  17.2 us
    all_to_all x1, waiting for transfers between devices, fetch_up(): return lax.all_to_all(sent, 'dp', split_axis=0, concat_axis=0, tiled=True)  10.4 us
    unnamed x48, local copies, waits for them, and re-layouts  9.8 us
    all_to_all x1, waiting for transfers between devices, per_device(): d_got = lax.all_to_all(parts, 'dp', split_axis=0, concat_axis=0, tiled=True)  8.32 us
    ppermute x10, starting transfers between devices, swap_seq(): return lax.ppermute(block, 'seq', [(i, i ^ step) for i in range(count)])  8.18 us
    ppermute x6, starting transfers between devices, swap_dp(): return lax.ppermute(block, 'dp', [(i, i ^ step) for i in range(count)])  7.94 us
    all_to_all x1, starting transfers between devices, owner_rows(): got = lax.all_to_all(send, 'seq', split_axis=0, concat_axis=0, tiled=True)  5.32 us
  transfers between devices with their start and end apart: 20, of which 13 were waited for; matrix products, arithmetic and copies ran while one was open for 6% of the time, Pallas kernels for 11%

profile of v4, /device:TPU:8, one launch (start us, length us, event | category | flops | bytes accessed | tf_op | source)
XLA Modules:
  0.0 145.6 jit_solution(6814330090125641096)
XLA Ops:
  0.6 0.7 broadcast_in_dim.16.gain_ref
  1.3 0.1 pad_add_fusion.place_ref
  1.4 1.4 copy-done
  2.8 1.6 %shard_map.155 = bf16[4,176,640]{2,1,0:T(8,128)(2,1)} custom-call(s32[3]{0:T(128)S(1)} %pad_add_fusion.place_ref, bf16[320,2560]{1,0:T(8,128)(2,1)S(1)} %copy-done, bf16[1,320]{1,0:T(2,128)(2,1)S(1)} %broadcast_in_dim.16.gain_ref), custom_call_target="tpu_custom_call" | custom-call | flops 1048576 | bytes 4194304 | tf_op jit(solution)/shard_map/pallas_call | solution.py:332
  4.4 3.8 %all-to-all-start.1 = ((bf16[4,176,640]{2,1,0:T(8,128)(2,1)}), bf16[4,176,640]{2,1,0:T(8,128)(2,1)S(1)}, u32[]{:S(2)}, u32[]{:S(2)}) async-start(bf16[4,176,640]{2,1,0:T(8,128)(2,1)} %shard_map.155), calls=%async_computation.1 | async-start | bytes 1802240 | tf_op jit(solution)/shard_map/all_to_all | solution.py:338
  8.3 1.6 %shard_map.153 = bf16[8,32,1408]{2,1,0:T(8,128)(2,1)} custom-call(s32[1,192]{1,0:T(1,128)S(1)} %copy-done.6, bf16[192,1280]{1,0:T(8,128)(2,1)S(1)} %bitcast.31), custom_call_target="tpu_custom_call" | custom-call | flops 1048576 | bytes 4194304 | tf_op jit(solution)/shard_map/pallas_call | solution.py:112
  9.9 10.4 %all-to-all-done.1.mine_ref = bf16[4,176,640]{2,1,0:T(8,128)(2,1)S(1)} async-done(((bf16[4,176,640]{2,1,0:T(8,128)(2,1)}), bf16[4,176,640]{2,1,0:T(8,128)(2,1)S(1)}, u32[]{:S(2)}, u32[]{:S(2)}) %all-to-all-start.1) | async-done | bytes 901152 | tf_op jit(solution)/shard_map/all_to_all | solution.py:338
  20.4 5.3 %all-to-all-start = ((bf16[8,32,1408]{2,1,0:T(8,128)(2,1)}), bf16[8,32,1408]{2,1,0:T(8,128)(2,1)S(1)}, u32[]{:S(2)}, u32[]{:S(2)}) async-start(bf16[8,32,1408]{2,1,0:T(8,128)(2,1)} %shard_map.153), calls=%async_computation | async-start | bytes 1441792 | tf_op jit(solution)/shard_map/all_to_all | solution.py:118
  25.7 1.0 copy-done.15
  26.7 3.8 %shard_map.156 = (f32[16,128,128]{2,1,0:T(8,128)S(1)}, bf16[128,1280]{1,0:T(8,128)(2,1)S(1)}, f32[128,1280]{1,0:T(8,128)S(1)}, f32[128,128]{1,0:T(8,128)S(1)}) custom-call(s32[2,2]{1,0:T(2,128)S(1)} %bitcast.39, bf16[128,1280]{1,0:T(8,128)(2,1)S(1)} %bitcast.33, bf16[128,1280]{1,0:T(8,128)(2,1)S(1)} %bitcast.35, bf16[128,1280]{1,0:T(8,128)(2,1)S(1)} %bitcast.37, ...), custom_call_target="tpu_custom_call" | custom-call | flops 2147483648 | bytes 4194304 | tf_op jit(solution)/shard_map/pallas_call | solution.py:188
  30.5 0.8 copy-done.3
  31.4 1.0 copy-done.18
  32.3 0.7 copy-done.20
  33.1 0.6 copy-done.22
  33.7 0.1 reshape.44
  33.8 0.1 collective-permute-start.3
  34.0 1.1 multiply_convert_fusion.refs_0_
  35.1 1.5 %collective-permute-start.6 = (bf16[128,1280]{1,0:T(8,128)(2,1)S(1)}, bf16[128,1280]{1,0:T(8,128)(2,1)S(1)}, u32[]{:S(2)}, u32[]{:S(2)}) collective-permute-start(bf16[128,1280]{1,0:T(8,128)(2,1)S(1)} %multiply_convert_fusion.refs_0_), channel_id=1, source_target_pairs={{0,3},{1,2},{2,1},{3,0},{4,7},{5,6},{6,5},{7,4},{8,11},{9,10},{10,... | collective-permute-start | bytes 983048 | tf_op jit(solution)/shard_map/ppermute | solution.py:41
  36.6 1.5 %collective-permute-start.5 = (bf16[128,1280]{1,0:T(8,128)(2,1)S(1)}, bf16[128,1280]{1,0:T(8,128)(2,1)}, u32[]{:S(2)}, u32[]{:S(2)}) collective-permute-start(bf16[128,1280]{1,0:T(8,128)(2,1)S(1)} %multiply_convert_fusion.refs_0_), channel_id=1, source_target_pairs={{0,2},{1,3},{2,0},{3,1},{4,6},{5,7},{6,4},{7,5},{8,10},{9,11},{10,... | collective-permute-start | bytes 983048 | tf_op jit(solution)/shard_map/ppermute | solution.py:41
  38.1 0.6 collective-permute-start.4
  38.7 3.1 %all-to-all-done = bf16[8,32,1408]{2,1,0:T(8,128)(2,1)S(1)} async-done(((bf16[8,32,1408]{2,1,0:T(8,128)(2,1)}), bf16[8,32,1408]{2,1,0:T(8,128)(2,1)S(1)}, u32[]{:S(2)}, u32[]{:S(2)}) %all-to-all-start) | async-done | bytes 720928 | tf_op jit(solution)/shard_map/all_to_all | solution.py:118
  41.8 0.3 shard_map.154.rows_ref
  42.1 1.5 %collective-permute-start.2 = (bf16[128,1280]{1,0:T(8,128)(2,1)S(1)}, bf16[128,1280]{1,0:T(8,128)(2,1)}, u32[]{:S(2)}, u32[]{:S(2)}) collective-permute-start(bf16[128,1280]{1,0:T(8,128)(2,1)S(1)} %shard_map.154.rows_ref), channel_id=1, source_target_pairs={{0,3},{1,2},{2,1},{3,0},{4,7},{5,6},{6,5},{7,4},{8,11},{9,10},{10,... | collective-permute-start | bytes 983048 | tf_op jit(solution)/shard_map/ppermute | solution.py:41
  43.5 3.1 %collective-permute-done.6.refs_3_ = bf16[128,1280]{1,0:T(8,128)(2,1)S(1)} collective-permute-done((bf16[128,1280]{1,0:T(8,128)(2,1)S(1)}, bf16[128,1280]{1,0:T(8,128)(2,1)S(1)}, u32[]{:S(2)}, u32[]{:S(2)}) %collective-permute-start.6) | collective-permute-done | bytes 327712 | tf_op jit(solution)/shard_map/ppermute | solution.py:41
  46.6 1.5 %collective-permute-start.1 = (bf16[128,1280]{1,0:T(8,128)(2,1)S(1)}, bf16[128,1280]{1,0:T(8,128)(2,1)}, u32[]{:S(2)}, u32[]{:S(2)}) collective-permute-start(bf16[128,1280]{1,0:T(8,128)(2,1)S(1)} %shard_map.154.rows_ref), channel_id=1, source_target_pairs={{0,2},{1,3},{2,0},{3,1},{4,6},{5,7},{6,4},{7,5},{8,10},{9,11},{10,... | collective-permute-start | bytes 983048 | tf_op jit(solution)/shard_map/ppermute | solution.py:41
  48.1 5.7 %collective-permute-done.5.refs_2_ = bf16[128,1280]{1,0:T(8,128)(2,1)} collective-permute-done((bf16[128,1280]{1,0:T(8,128)(2,1)S(1)}, bf16[128,1280]{1,0:T(8,128)(2,1)}, u32[]{:S(2)}, u32[]{:S(2)}) %collective-permute-start.5) | collective-permute-done | bytes 327712 | tf_op jit(solution)/shard_map/ppermute | solution.py:41
  53.8 1.4 collective-permute-start
  55.3 0.1 reshape_squeeze.3.gain_ref
  55.4 2.7 %shard_map.157 = (bf16[1280,640]{1,0:T(8,128)(2,1)S(1)}, bf16[640,512]{1,0:T(8,128)(2,1)S(1)}, f32[512,640]{1,0:T(8,128)S(1)}, bf16[1280,512]{1,0:T(8,128)(2,1)S(1)}, bf16[512,1280]{1,0:T(8,128)(2,1)S(1)}) custom-call(s32[3]{0:T(128)S(1)} %pad_add_fusion.place_ref, bf16[4,176,640]{2,1,0:T(8,128)(2,1)S(1)} %all-to-all-done.1.mine_ref, ...), custom_call_target="tpu_custom_call" | custom-call | flops 838860800 | bytes 4194304 | tf_op jit(solution)/shard_map/pallas_call | solution.py:364
  58.1 0.9 copy-done.8
  58.9 1.9 %collective-permute-done.2 = bf16[128,1280]{1,0:T(8,128)(2,1)} collective-permute-done((bf16[128,1280]{1,0:T(8,128)(2,1)S(1)}, bf16[128,1280]{1,0:T(8,128)(2,1)}, u32[]{:S(2)}, u32[]{:S(2)}) %collective-permute-start.2) | collective-permute-done | bytes 327712 | tf_op jit(solution)/shard_map/ppermute | solution.py:41
  60.8 6.4 %collective-permute-done.1 = bf16[128,1280]{1,0:T(8,128)(2,1)} collective-permute-done((bf16[128,1280]{1,0:T(8,128)(2,1)S(1)}, bf16[128,1280]{1,0:T(8,128)(2,1)}, u32[]{:S(2)}, u32[]{:S(2)}) %collective-permute-start.1) | collective-permute-done | bytes 327712 | tf_op jit(solution)/shard_map/ppermute | solution.py:41
  67.2 0.1 collective-permute-done
  67.3 1.3 pad_maximum_fusion.rows_ref
  68.6 4.0 %shard_map.158 = (bf16[512,640]{1,0:T(8,128)(2,1)S(1)}, bf16[4,160,640]{2,1,0:T(8,128)(2,1)S(1)}, bf16[4,160,640]{2,1,0:T(8,128)(2,1)}) custom-call(s32[3]{0:T(128)S(1)} %pad_add_fusion.place_ref, bf16[512,1280]{1,0:T(8,128)(2,1)S(1)} %pad_maximum_fusion.rows_ref, bf16[640,1280]{1,0:T(8,128)(2,1)S(1)} %copy-done.7, ...), custom_call_target="tpu_custom_call" | custom-call | flops 1677721600 | bytes 4194304 | tf_op jit(solution)/shard_map/pallas_call | solution.py:407
  72.5 2.9 %shard_map.159 = (bf16[4,128,1280]{2,1,0:T(8,128)(2,1)}, f32[1,1280]{1,0:T(1,128)S(1)}) custom-call(s32[3]{0:T(128)S(1)} %pad_add_fusion.place_ref, bf16[512,640]{1,0:T(8,128)(2,1)S(1)} %get-tuple-element.36.pre_ref, bf16[1280,640]{1,0:T(8,128)(2,1)S(1)} %get-tuple-element.37.up_ref, bf16[512,1280]{1,0:T(8,128)(2,1)S(1)} %get-tuple-element.38.normed_ref, ...), custom_call_target="tpu_custom_call" | custom-call | flops 838860800 | bytes 4194304 | tf_op jit(solution)/shard_map/pallas_call | solution.py:445
  75.4 3.5 %all-to-all-start.2 = ((bf16[4,128,1280]{2,1,0:T(8,128)(2,1)}), bf16[4,128,1280]{2,1,0:T(8,128)(2,1)S(1)}, u32[]{:S(2)}, u32[]{:S(2)}) async-start(bf16[4,128,1280]{2,1,0:T(8,128)(2,1)} %get-tuple-element.39), calls=%async_computation.2 | async-start | bytes 2621440 | tf_op jit(solution)/shard_map/all_to_all | solution.py:588
  79.0 1.1 copy-done.9
  80.1 2.3 %shard_map.161 = (bf16[4,320,320]{2,1,0:T(8,128)(2,1)S(1)}, bf16[4,320,320]{2,1,0:T(8,128)(2,1)S(1)}) custom-call(s32[3]{0:T(128)S(1)} %pad_add_fusion.place_ref, bf16[640,512]{1,0:T(8,128)(2,1)S(1)} %copy-done.9, bf16[512,1280]{1,0:T(8,128)(2,1)S(1)} %pad_maximum_fusion.rows_ref), custom_call_target="tpu_custom_call" | custom-call | flops 838860800 | bytes 4194304 | tf_op jit(solution)/shard_map/pallas_call | solution.py:428
  82.5 0.5 collective-permute-start.7
  83.0 0.1 collective-permute-start.12
  83.0 2.6 %collective-permute-done.12.other_ref = f32[1,1280]{1,0:T(1,128)S(1)} collective-permute-done((f32[1,1280]{1,0:T(1,128)S(1)}, f32[1,1280]{1,0:T(1,128)S(1)}, u32[]{:S(2)}, u32[]{:S(2)}) %collective-permute-start.12) | collective-permute-done | bytes 5152 | tf_op jit(solution)/shard_map/ppermute | solution.py:45
  85.7 0.4 shard_map.162
  86.1 1.4 copy.17
  87.4 8.3 %all-to-all-done.2.got_ref = bf16[4,128,1280]{2,1,0:T(8,128)(2,1)S(1)} async-done(((bf16[4,128,1280]{2,1,0:T(8,128)(2,1)}), bf16[4,128,1280]{2,1,0:T(8,128)(2,1)S(1)}, u32[]{:S(2)}, u32[]{:S(2)}) %all-to-all-start.2) | async-done | bytes 1310752 | tf_op jit(solution)/shard_map/all_to_all | solution.py:588
  95.8 4.4 %all-to-all-start.3 = ((bf16[4,336,320]{1,2,0:T(8,128)(2,1)}), bf16[4,336,320]{1,2,0:T(8,128)(2,1)}, u32[]{:S(2)}, u32[]{:S(2)}) async-start(bf16[4,336,320]{1,2,0:T(8,128)(2,1)} %copy.17), calls=%async_computation.3 | async-start | bytes 1966080 | tf_op jit(solution)/shard_map/all_to_all | solution.py:525
  100.3 2.2 %fusion.4 = (bf16[160,640]{1,0:T(8,128)(2,1)}, bf16[160,640]{1,0:T(8,128)(2,1)}, bf16[160,640]{1,0:T(8,128)(2,1)}) fusion(bf16[4,160,640]{2,1,0:T(8,128)(2,1)} %collective-permute-done.7, s32[]{:T(128)S(6)} %select_n.32, bf16[4,160,640]{2,1,0:T(8,128)(2,1)S(1)} %copy-done.2, s32[]{:T(128)S(6)} %select_n.34, s32[]{:T(128)S(6)} %select_n.33), kind=kLoop, calls=%fused_computation.10 | loop fusion | flops 1228800 | bytes 1843212 | tf_op jit(solution)/shard_map/convert_element_type | solution.py:515
  102.5 1.5 collective-permute-start.8
  103.9 2.4 %collective-permute-start.10 = (bf16[160,640]{1,0:T(8,128)(2,1)}, bf16[160,640]{1,0:T(8,128)(2,1)S(1)}, u32[]{:S(2)}, u32[]{:S(2)}) collective-permute-start(bf16[160,640]{1,0:T(8,128)(2,1)} %get-tuple-element.60), channel_id=1, source_target_pairs={{0,8},{4,12},{8,0},{12,4},{16,24},{20,28},{24,16},{28,20},{1,9},{5... | collective-permute-start | bytes 614408 | tf_op jit(solution)/shard_map/ppermute | solution.py:45
  106.3 1.2 copy-done.19
  107.6 1.0 copy-done.21
  108.5 4.7 %shard_map.160 = (bf16[128,1280]{1,0:T(8,128)(2,1)}, bf16[128,1280]{1,0:T(8,128)(2,1)}, bf16[128,1280]{1,0:T(8,128)(2,1)}, bf16[128,1280]{1,0:T(8,128)(2,1)}) custom-call(bf16[4,128,1280]{2,1,0:T(8,128)(2,1)S(1)} %all-to-all-done.2.got_ref, bf16[128,1280]{1,0:T(8,128)(2,1)S(1)} %shard_map.154.rows_ref, f32[128,1280]{1,0:T(8,128)S(1)} %copy-done.4, ...), custom_call_target="tpu_custom_call" | custom-call | flops 4294967296 | bytes 4194304 | tf_op jit(solution)/shard_map/pallas_call | solution.py:250
  113.2 1.6 %copy.18.got_ref = bf16[4,336,320]{2,1,0:T(8,128)(2,1)S(1)} copy(bf16[4,336,320]{1,2,0:T(8,128)(2,1)} %all-to-all-done.3) | data formatting | bytes 1720320 | tf_op jit(solution)/shard_map/all_to_all | solution.py:525
  114.9 0.6 shard_map.163
  115.5 0.6 collective-permute-start.13
  116.1 2.4 %collective-permute-start.14 = (bf16[336,320]{1,0:T(8,128)(2,1)S(1)}, bf16[336,320]{1,0:T(8,128)(2,1)S(1)}, u32[]{:S(2)}, u32[]{:S(2)}) collective-permute-start(bf16[336,320]{1,0:T(8,128)(2,1)S(1)} %get-tuple-element.55), channel_id=1, source_target_pairs={{0,16},{4,20},{8,24},{12,28},{16,0},{20,4},{24,8},{28,12},{1,17},{... | collective-permute-start | bytes 645128 | tf_op jit(solution)/shard_map/ppermute | solution.py:45
  118.6 0.5 collective-permute-start.15
  119.1 4.2 %collective-permute-done.9 = bf16[160,640]{1,0:T(8,128)(2,1)S(1)} collective-permute-done((bf16[160,640]{1,0:T(8,128)(2,1)}, bf16[160,640]{1,0:T(8,128)(2,1)S(1)}, u32[]{:S(2)}, u32[]{:S(2)}) %collective-permute-start.9) | collective-permute-done | bytes 204832 | tf_op jit(solution)/shard_map/ppermute | solution.py:45
  123.3 1.9 %fusion.3 = bf16[160,640]{1,0:T(8,128)(2,1)} fusion(bf16[160,640]{1,0:T(8,128)(2,1)S(1)} %collective-permute-done.10, bf16[160,640]{1,0:T(8,128)(2,1)S(1)} %collective-permute-done.9, bf16[160,640]{1,0:T(8,128)(2,1)S(1)} %collective-permute-done.8, bf16[4,160,640]{2,1,0:T(8,128)(2,1)} %collective-permute-done.7, s32[]{:T(128)S(6)} %select_n.31, ...), kind=kLoop, calls=%fused_computation.6 | loop fusion | flops 1126400 | bytes 1228804 | tf_op jit(solution)/shard_map/convert_element_type | solution.py:540
  125.2 1.6 %collective-permute-done.13.refs_1_ = bf16[336,320]{1,0:T(8,128)(2,1)S(1)} collective-permute-done((bf16[336,320]{1,0:T(8,128)(2,1)S(1)}, bf16[336,320]{1,0:T(8,128)(2,1)S(1)}, u32[]{:S(2)}, u32[]{:S(2)}) %collective-permute-start.13) | collective-permute-done | bytes 215072 | tf_op jit(solution)/shard_map/ppermute | solution.py:45
  126.8 12.7 %collective-permute-done.14.refs_2_ = bf16[336,320]{1,0:T(8,128)(2,1)S(1)} collective-permute-done((bf16[336,320]{1,0:T(8,128)(2,1)S(1)}, bf16[336,320]{1,0:T(8,128)(2,1)S(1)}, u32[]{:S(2)}, u32[]{:S(2)}) %collective-permute-start.14) | collective-permute-done | bytes 215072 | tf_op jit(solution)/shard_map/ppermute | solution.py:45
  139.4 4.6 %collective-permute-done.15.refs_3_ = bf16[336,320]{1,0:T(8,128)(2,1)S(1)} collective-permute-done((bf16[336,320]{1,0:T(8,128)(2,1)S(1)}, bf16[336,320]{1,0:T(8,128)(2,1)S(1)}, u32[]{:S(2)}, u32[]{:S(2)}) %collective-permute-start.15) | collective-permute-done | bytes 215072 | tf_op jit(solution)/shard_map/ppermute | solution.py:45
  144.1 0.8 shard_map.164
  144.9 0.7 reshape.43
  (49 shorter events, 0.2 us)
Async XLA Ops:
  1.4 1.4 copy-start
  4.4 3.9 %copy-start.5 = (bf16[1,192,1280]{2,1,0:T(8,128)(2,1)S(1)}, bf16[1,192,1280]{2,1,0:T(8,128)(2,1)}, u32[]{:S(2)}) copy-start(bf16[1,192,1280]{2,1,0:T(8,128)(2,1)} %param.14) | copy-start | bytes 1474564
  4.4 3.9 %copy-start.6 = (s32[1,192]{1,0:T(1,128)S(1)}, s32[1,192]{1,0:T(1,128)}, u32[]{:S(2)}) copy-start(s32[1,192]{1,0:T(1,128)} %refs_0_.1) | copy-start | bytes 2308
  4.4 15.9 %all-to-all-start.1 = ((bf16[4,176,640]{2,1,0:T(8,128)(2,1)}), bf16[4,176,640]{2,1,0:T(8,128)(2,1)S(1)}, u32[]{:S(2)}, u32[]{:S(2)}) async-start(bf16[4,176,640]{2,1,0:T(8,128)(2,1)} %shard_map.155), calls=%async_computation.1 | async-start | bytes 1802240 | tf_op jit(solution)/shard_map/all_to_all | solution.py:338
  8.3 17.4 %copy-start.10 = (bf16[1,128,1280]{2,1,0:T(8,128)(2,1)S(1)}, bf16[1,128,1280]{2,1,0:T(8,128)(2,1)}, u32[]{:S(2)}) copy-start(bf16[1,128,1280]{2,1,0:T(8,128)(2,1)} %param.13) | copy-start | bytes 983044
  8.3 17.4 %copy-start.11 = (bf16[1,128,1280]{2,1,0:T(8,128)(2,1)S(1)}, bf16[1,128,1280]{2,1,0:T(8,128)(2,1)}, u32[]{:S(2)}) copy-start(bf16[1,128,1280]{2,1,0:T(8,128)(2,1)} %param.10) | copy-start | bytes 983044
  8.3 17.4 %copy-start.17 = (s32[1,2,2]{2,1,0:T(2,128)S(1)}, s32[1,2,2]{2,1,0:T(2,128)}, u32[]{:S(2)}) copy-start(s32[1,2,2]{2,1,0:T(2,128)} %param.16) | copy-start | bytes 52
  9.9 15.8 %copy-start.13 = (bf16[1,128,1280]{2,1,0:T(8,128)(2,1)S(1)}, bf16[1,128,1280]{2,1,0:T(8,128)(2,1)}, u32[]{:S(2)}) copy-start(bf16[1,128,1280]{2,1,0:T(8,128)(2,1)} %param.11) | copy-start | bytes 983044
  20.4 21.4 %all-to-all-start = ((bf16[8,32,1408]{2,1,0:T(8,128)(2,1)}), bf16[8,32,1408]{2,1,0:T(8,128)(2,1)S(1)}, u32[]{:S(2)}, u32[]{:S(2)}) async-start(bf16[8,32,1408]{2,1,0:T(8,128)(2,1)} %shard_map.153), calls=%async_computation | async-start | bytes 1441792 | tf_op jit(solution)/shard_map/all_to_all | solution.py:118
  25.7 1.0 copy-start.15
  30.5 0.9 copy-start.3
  31.4 1.0 copy-start.18
  32.3 0.7 copy-start.20
  33.1 0.6 copy-start.22
  33.8 21.6 %collective-permute-start.3 = (bf16[4,176,640]{2,1,0:T(8,128)(2,1)S(1)}, bf16[4,176,640]{2,1,0:T(8,128)(2,1)S(1)}, u32[]{:S(2)}, u32[]{:S(2)}) collective-permute-start(bf16[4,176,640]{2,1,0:T(8,128)(2,1)S(1)} %all-to-all-done.1.mine_ref), channel_id=1, source_target_pairs={{0,4},{4,0},{8,12},{12,8},{16,20},{20,16},{24,28},{28,24},{1,5},{5... | collective-permute-start | bytes 2703368 | tf_op jit(solution)/shard_map/ppermute | solution.py:45
  35.1 11.6 %collective-permute-start.6 = (bf16[128,1280]{1,0:T(8,128)(2,1)S(1)}, bf16[128,1280]{1,0:T(8,128)(2,1)S(1)}, u32[]{:S(2)}, u32[]{:S(2)}) collective-permute-start(bf16[128,1280]{1,0:T(8,128)(2,1)S(1)} %multiply_convert_fusion.refs_0_), channel_id=1, source_target_pairs={{0,3},{1,2},{2,1},{3,0},{4,7},{5,6},{6,5},{7,4},{8,11},{9,10},{10,... | collective-permute-start | bytes 983048 | tf_op jit(solution)/shard_map/ppermute | solution.py:41
  36.6 17.2 %collective-permute-start.5 = (bf16[128,1280]{1,0:T(8,128)(2,1)S(1)}, bf16[128,1280]{1,0:T(8,128)(2,1)}, u32[]{:S(2)}, u32[]{:S(2)}) collective-permute-start(bf16[128,1280]{1,0:T(8,128)(2,1)S(1)} %multiply_convert_fusion.refs_0_), channel_id=1, source_target_pairs={{0,2},{1,3},{2,0},{3,1},{4,6},{5,7},{6,4},{7,5},{8,10},{9,11},{10,... | collective-permute-start | bytes 983048 | tf_op jit(solution)/shard_map/ppermute | solution.py:41
  38.1 17.3 %collective-permute-start.4 = (bf16[128,1280]{1,0:T(8,128)(2,1)S(1)}, bf16[128,1280]{1,0:T(8,128)(2,1)}, u32[]{:S(2)}, u32[]{:S(2)}) collective-permute-start(bf16[128,1280]{1,0:T(8,128)(2,1)S(1)} %multiply_convert_fusion.refs_0_), channel_id=1, source_target_pairs={{0,1},{1,0},{2,3},{3,2},{4,5},{5,4},{6,7},{7,6},{8,9},{9,8},{10,11... | collective-permute-start | bytes 983048 | tf_op jit(solution)/shard_map/ppermute | solution.py:41
  42.1 18.8 %collective-permute-start.2 = (bf16[128,1280]{1,0:T(8,128)(2,1)S(1)}, bf16[128,1280]{1,0:T(8,128)(2,1)}, u32[]{:S(2)}, u32[]{:S(2)}) collective-permute-start(bf16[128,1280]{1,0:T(8,128)(2,1)S(1)} %shard_map.154.rows_ref), channel_id=1, source_target_pairs={{0,3},{1,2},{2,1},{3,0},{4,7},{5,6},{6,5},{7,4},{8,11},{9,10},{10,... | collective-permute-start | bytes 983048 | tf_op jit(solution)/shard_map/ppermute | solution.py:41
  46.6 20.6 %collective-permute-start.1 = (bf16[128,1280]{1,0:T(8,128)(2,1)S(1)}, bf16[128,1280]{1,0:T(8,128)(2,1)}, u32[]{:S(2)}, u32[]{:S(2)}) collective-permute-start(bf16[128,1280]{1,0:T(8,128)(2,1)S(1)} %shard_map.154.rows_ref), channel_id=1, source_target_pairs={{0,2},{1,3},{2,0},{3,1},{4,6},{5,7},{6,4},{7,5},{8,10},{9,11},{10,... | collective-permute-start | bytes 983048 | tf_op jit(solution)/shard_map/ppermute | solution.py:41
  53.8 13.5 %collective-permute-start = (bf16[128,1280]{1,0:T(8,128)(2,1)S(1)}, bf16[128,1280]{1,0:T(8,128)(2,1)}, u32[]{:S(2)}, u32[]{:S(2)}) collective-permute-start(bf16[128,1280]{1,0:T(8,128)(2,1)S(1)} %shard_map.154.rows_ref), channel_id=1, source_target_pairs={{0,1},{1,0},{2,3},{3,2},{4,5},{5,4},{6,7},{7,6},{8,9},{9,8},{10,11... | collective-permute-start | bytes 983048 | tf_op jit(solution)/shard_map/ppermute | solution.py:41
  58.1 0.9 copy-start.8
  58.9 9.6 %copy-start.7 = (bf16[640,1280]{1,0:T(8,128)(2,1)S(1)}, bf16[640,1280]{1,0:T(8,128)(2,1)}, u32[]{:S(2)}) copy-start(bf16[640,1280]{1,0:T(8,128)(2,1)} %down_ref.1) | copy-start | bytes 4915204
  72.5 2.9 %copy-start.1 = (bf16[4,160,640]{2,1,0:T(8,128)(2,1)}, bf16[4,160,640]{2,1,0:T(8,128)(2,1)S(1)}, u32[]{:S(2)}) copy-start(bf16[4,160,640]{2,1,0:T(8,128)(2,1)S(1)} %get-tuple-element.47) | copy-start | bytes 2457604
  75.4 20.3 %all-to-all-start.2 = ((bf16[4,128,1280]{2,1,0:T(8,128)(2,1)}), bf16[4,128,1280]{2,1,0:T(8,128)(2,1)S(1)}, u32[]{:S(2)}, u32[]{:S(2)}) async-start(bf16[4,128,1280]{2,1,0:T(8,128)(2,1)} %get-tuple-element.39), calls=%async_computation.2 | async-start | bytes 2621440 | tf_op jit(solution)/shard_map/all_to_all | solution.py:588
  79.0 1.1 copy-start.9
  82.4 3.3 %collective-permute-start.11 = (bf16[4,320,320]{2,1,0:T(8,128)(2,1)S(1)}, bf16[4,320,320]{2,1,0:T(8,128)(2,1)S(1)}, u32[]{:S(2)}, u32[]{:S(2)}) collective-permute-start(bf16[4,320,320]{2,1,0:T(8,128)(2,1)S(1)} %get-tuple-element.51), channel_id=1, source_target_pairs={{0,4},{4,0},{8,12},{12,8},{16,20},{20,16},{24,28},{28,24},{1,5},{5... | collective-permute-start | bytes 2457608 | tf_op jit(solution)/shard_map/ppermute | solution.py:45
  82.5 17.8 %collective-permute-start.7 = (bf16[4,160,640]{2,1,0:T(8,128)(2,1)}, bf16[4,160,640]{2,1,0:T(8,128)(2,1)}, u32[]{:S(2)}, u32[]{:S(2)}) collective-permute-start(bf16[4,160,640]{2,1,0:T(8,128)(2,1)} %get-tuple-element.48), channel_id=1, source_target_pairs={{0,4},{4,0},{8,12},{12,8},{16,20},{20,16},{24,28},{28,24},{1,5},{5... | collective-permute-start | bytes 2457608 | tf_op jit(solution)/shard_map/ppermute | solution.py:45
  83.0 2.7 %collective-permute-start.12 = (f32[1,1280]{1,0:T(1,128)S(1)}, f32[1,1280]{1,0:T(1,128)S(1)}, u32[]{:S(2)}, u32[]{:S(2)}) collective-permute-start(f32[1,1280]{1,0:T(1,128)S(1)} %get-tuple-element.52.term_ref), channel_id=1, source_target_pairs={{0,4},{4,0},{8,12},{12,8},{16,20},{20,16},{24,28},{28,24},{1,5},{5... | collective-permute-start | bytes 15368 | tf_op jit(solution)/shard_map/ppermute | solution.py:45
  87.4 12.8 %copy-start.2 = (bf16[4,160,640]{2,1,0:T(8,128)(2,1)S(1)}, bf16[4,160,640]{2,1,0:T(8,128)(2,1)}, u32[]{:S(2)}) copy-start(bf16[4,160,640]{2,1,0:T(8,128)(2,1)} %copy-done.1) | copy-start | bytes 2457604
  95.8 17.5 %all-to-all-start.3 = ((bf16[4,336,320]{1,2,0:T(8,128)(2,1)}), bf16[4,336,320]{1,2,0:T(8,128)(2,1)}, u32[]{:S(2)}, u32[]{:S(2)}) async-start(bf16[4,336,320]{1,2,0:T(8,128)(2,1)} %copy.17), calls=%async_computation.3 | async-start | bytes 1966080 | tf_op jit(solution)/shard_map/all_to_all | solution.py:525
  100.2 6.1 %copy-start.4 = (f32[128,1280]{1,0:T(8,128)S(1)}, f32[128,1280]{1,0:T(8,128)}, u32[]{:S(2)}) copy-start(f32[128,1280]{1,0:T(8,128)} %copy-done.3) | copy-start | bytes 1966084
  100.2 6.1 %copy-start.12 = (bf16[1,128,1280]{2,1,0:T(8,128)(2,1)S(1)}, bf16[1,128,1280]{2,1,0:T(8,128)(2,1)}, u32[]{:S(2)}) copy-start(bf16[1,128,1280]{2,1,0:T(8,128)(2,1)} %param.10) | copy-start | bytes 983044
  100.2 6.1 %copy-start.23 = (f32[128,128]{1,0:T(8,128)S(1)}, f32[128,128]{1,0:T(8,128)}, u32[]{:S(2)}) copy-start(f32[128,128]{1,0:T(8,128)} %copy-done.22) | copy-start | bytes 196612
  100.2 6.1 %copy-start.14 = (bf16[1,128,1280]{2,1,0:T(8,128)(2,1)S(1)}, bf16[1,128,1280]{2,1,0:T(8,128)(2,1)}, u32[]{:S(2)}) copy-start(bf16[1,128,1280]{2,1,0:T(8,128)(2,1)} %param.11) | copy-start | bytes 983044
  100.2 6.1 %copy-start.16 = (bf16[1,128,1280]{2,1,0:T(8,128)(2,1)S(1)}, bf16[1,128,1280]{2,1,0:T(8,128)(2,1)}, u32[]{:S(2)}) copy-start(bf16[1,128,1280]{2,1,0:T(8,128)(2,1)} %param.12) | copy-start | bytes 983044
  102.5 16.1 %collective-permute-start.8 = (bf16[160,640]{1,0:T(8,128)(2,1)}, bf16[160,640]{1,0:T(8,128)(2,1)S(1)}, u32[]{:S(2)}, u32[]{:S(2)}) collective-permute-start(bf16[160,640]{1,0:T(8,128)(2,1)} %get-tuple-element.59), channel_id=1, source_target_pairs={{0,24},{4,28},{8,16},{12,20},{16,8},{20,12},{24,0},{28,4},{1,25},{... | collective-permute-start | bytes 614408 | tf_op jit(solution)/shard_map/ppermute | solution.py:45
  103.9 15.2 %collective-permute-start.10 = (bf16[160,640]{1,0:T(8,128)(2,1)}, bf16[160,640]{1,0:T(8,128)(2,1)S(1)}, u32[]{:S(2)}, u32[]{:S(2)}) collective-permute-start(bf16[160,640]{1,0:T(8,128)(2,1)} %get-tuple-element.60), channel_id=1, source_target_pairs={{0,8},{4,12},{8,0},{12,4},{16,24},{20,28},{24,16},{28,20},{1,9},{5... | collective-permute-start | bytes 614408 | tf_op jit(solution)/shard_map/ppermute | solution.py:45
  106.3 17.0 %collective-permute-start.9 = (bf16[160,640]{1,0:T(8,128)(2,1)}, bf16[160,640]{1,0:T(8,128)(2,1)S(1)}, u32[]{:S(2)}, u32[]{:S(2)}) collective-permute-start(bf16[160,640]{1,0:T(8,128)(2,1)} %get-tuple-element.61), channel_id=1, source_target_pairs={{0,16},{4,20},{8,24},{12,28},{16,0},{20,4},{24,8},{28,12},{1,17},{... | collective-permute-start | bytes 614408 | tf_op jit(solution)/shard_map/ppermute | solution.py:45
  106.3 1.2 copy-start.19
  107.5 1.0 copy-start.21
  115.5 11.3 %collective-permute-start.13 = (bf16[336,320]{1,0:T(8,128)(2,1)S(1)}, bf16[336,320]{1,0:T(8,128)(2,1)S(1)}, u32[]{:S(2)}, u32[]{:S(2)}) collective-permute-start(bf16[336,320]{1,0:T(8,128)(2,1)S(1)} %get-tuple-element.54), channel_id=1, source_target_pairs={{0,8},{4,12},{8,0},{12,4},{16,24},{20,28},{24,16},{28,20},{1,9},{5... | collective-permute-start | bytes 645128 | tf_op jit(solution)/shard_map/ppermute | solution.py:45
  116.1 23.3 %collective-permute-start.14 = (bf16[336,320]{1,0:T(8,128)(2,1)S(1)}, bf16[336,320]{1,0:T(8,128)(2,1)S(1)}, u32[]{:S(2)}, u32[]{:S(2)}) collective-permute-start(bf16[336,320]{1,0:T(8,128)(2,1)S(1)} %get-tuple-element.55), channel_id=1, source_target_pairs={{0,16},{4,20},{8,24},{12,28},{16,0},{20,4},{24,8},{28,12},{1,17},{... | collective-permute-start | bytes 645128 | tf_op jit(solution)/shard_map/ppermute | solution.py:45
  118.6 25.5 %collective-permute-start.15 = (bf16[336,320]{1,0:T(8,128)(2,1)S(1)}, bf16[336,320]{1,0:T(8,128)(2,1)S(1)}, u32[]{:S(2)}, u32[]{:S(2)}) collective-permute-start(bf16[336,320]{1,0:T(8,128)(2,1)S(1)} %get-tuple-element.56), channel_id=1, source_target_pairs={{0,24},{4,28},{8,16},{12,20},{16,8},{20,12},{24,0},{28,4},{1,25},{... | collective-permute-start | bytes 645128 | tf_op jit(solution)/shard_map/ppermute | solution.py:45

commit v5 on v4

--- a/solution.py
+++ b/solution.py
@@ -13,18 +13,43 @@
 PIECE = 16
 CORES = 2
 LANES = 128
-VMEM_BYTES = 32 * 1024 * 1024
+VMEM_BYTES = 16 * 1024 * 1024
 
 
 def vmem_call(body, out_shape, in_spaces, flops):
-    return pl.pallas_call(
-        body,
-        out_shape=out_shape,
-        in_specs=[pl.BlockSpec(memory_space=space) for space in in_spaces],
-        out_specs=jax.tree.map(lambda _: pl.BlockSpec(memory_space=pltpu.VMEM), out_shape),
-        compiler_params=pltpu.CompilerParams(vmem_limit_bytes=VMEM_BYTES),
-        cost_estimate=pl.CostEstimate(flops=flops, bytes_accessed=4 << 20, transcendentals=0),
-    )
+    def run(*operands):
+        places = [i for i, space in enumerate(in_spaces) if space == pl.ANY]
+        outs = len(jax.tree.leaves(out_shape))
+
+        def kernel(*refs):
+            refs = list(refs)
+            ins, rest = refs[: len(in_spaces)], refs[len(in_spaces) :]
+            held, sems = rest[outs : outs + len(places)], rest[outs + len(places) :]
+            copies = [
+                pltpu.make_async_copy(ins[i], held[n], sems[n]) for n, i in enumerate(places)
+            ]
+            for copy in copies:
+                copy.start()
+            for copy in copies:
+                copy.wait()
+            for n, i in enumerate(places):
+                ins[i] = held[n]
+            body(*ins, *rest[:outs])
+
+        return pl.pallas_call(
+            kernel if places else body,
+            out_shape=out_shape,
+            in_specs=[pl.BlockSpec(memory_space=space) for space in in_spaces],
+            out_specs=jax.tree.map(lambda _: pl.BlockSpec(memory_space=pltpu.VMEM), out_shape),
+            scratch_shapes=[pltpu.VMEM(operands[i].shape, operands[i].dtype) for i in places]
+            + [pltpu.SemaphoreType.DMA for _ in places],
+            compiler_params=pltpu.CompilerParams(vmem_limit_bytes=VMEM_BYTES),
+            cost_estimate=pl.CostEstimate(
+                flops=flops, bytes_accessed=4 << 20, transcendentals=0
+            ),
+        )(*operands)
+
+    return run
 
 
 def contract(left, right, left_dim, right_dim):
@@ -104,25 +129,26 @@
         )
 
 
-def owner_rows(llm_rows, slot_ids, n_seq, tokens):
-    length, feat = llm_rows.shape
+def send_tiles(llm_rows, slot_ids, n_seq, tokens):
     per_owner = tokens // PIECE
     capacity = 1 + (per_owner + n_seq - 2) // n_seq
-    rows = capacity * PIECE
-    send = vmem_call(
+    return vmem_call(
         lambda *refs: send_kernel(n_seq, capacity, per_owner, *refs),
-        jax.ShapeDtypeStruct((n_seq, rows, feat + LANES), jnp.bfloat16),
+        jax.ShapeDtypeStruct(
+            (n_seq, capacity * PIECE, llm_rows.shape[1] + LANES), jnp.bfloat16
+        ),
         [pltpu.SMEM, pltpu.VMEM],
         1 << 20,
     )(slot_ids, llm_rows)
-    got = lax.all_to_all(send, "seq", split_axis=0, concat_axis=0, tiled=True)
-    landed = vmem_call(
+
+
+def land_tiles(got, tokens):
+    return vmem_call(
         land_kernel,
-        jax.ShapeDtypeStruct((tokens, feat), jnp.bfloat16),
+        jax.ShapeDtypeStruct((tokens, got.shape[2] - LANES), jnp.bfloat16),
         [pltpu.VMEM],
         1 << 26,
-    )(got.reshape(n_seq * rows, feat + LANES))
-    return landed
+    )(got.reshape(-1, got.shape[2]))
 
 
 def head_lanes(head, rows, width, start):
@@ -151,9 +177,7 @@
         total[at] = total[at] + piece if at in total else piece
 
 
-def forward_kernel(
-    mask_ref, q_ref, k_ref, v_ref, resid_ref, probs_ref, out_ref, unit_ref, inverse_ref
-):
+def forward_kernel(mask_ref, q_ref, k_ref, v_ref, resid_ref, out_ref, unit_ref, *saved_refs):
     tokens, feat = q_ref.shape
     scale = 1.0 / math.sqrt(HDIM)
     row = lax.broadcasted_iota(jnp.int32, (tokens, tokens), 0) // BLK
@@ -170,7 +194,8 @@
         scores = jnp.where(allowed, scores, -jnp.inf)
         exp_terms = jnp.exp(scores - jnp.max(scores, axis=1, keepdims=True))
         probs = exp_terms / jnp.sum(exp_terms, axis=1, keepdims=True)
-        probs_ref[head] = probs
+        if saved_refs:
+            saved_refs[0][head] = probs
         add_span(total, head, contract(probs.astype(jnp.bfloat16), masked_head(v_ref, head), 1, 0))
     for at, value in total.items():
         out_ref[:, at : at + LANES] = value.astype(jnp.bfloat16)
@@ -179,22 +204,26 @@
     hidden = hidden - center
     variance = jnp.mean(jnp.square(hidden), axis=1, keepdims=True)
     inverse = lax.rsqrt(variance + 1e-06)
-    unit_ref[...] = hidden * inverse
-    inverse_ref[...] = jnp.broadcast_to(inverse, inverse_ref.shape)
-
-
-def forward(mask, query, key_block, value_block, resid):
+    unit_ref[...] = (hidden * inverse).astype(unit_ref.dtype)
+    if saved_refs:
+        saved_refs[1][...] = jnp.broadcast_to(inverse, saved_refs[1].shape)
+
+
+def forward(mask, query, key_block, value_block, resid, flops, saved):
     tokens, feat = query.shape
+    rest = (
+        jax.ShapeDtypeStruct((HEADS, tokens, tokens), jnp.float32),
+        jax.ShapeDtypeStruct((tokens, LANES), jnp.float32),
+    )
     return vmem_call(
         forward_kernel,
         (
-            jax.ShapeDtypeStruct((HEADS, tokens, tokens), jnp.float32),
             jax.ShapeDtypeStruct((tokens, feat), jnp.bfloat16),
-            jax.ShapeDtypeStruct((tokens, feat), jnp.float32),
-            jax.ShapeDtypeStruct((tokens, LANES), jnp.float32),
-        ),
+            jax.ShapeDtypeStruct((tokens, feat), jnp.float32 if saved else jnp.bfloat16),
+        )
+        + (rest if saved else ()),
         [pltpu.SMEM] + [pltpu.VMEM] * 4,
-        1 << 31,
+        flops,
     )(mask, query, key_block, value_block, resid)
 
 
@@ -255,10 +284,6 @@
     )(*operands)
 
 
-def gather_tokens(block, n_dp):
-    return jnp.concatenate([block] + [swap_dp(block, n_dp, k) for k in range(1, n_dp)], axis=0)
-
-
 def scatter_up(term, n_seq, seq):
     n_z, core, z = n_seq // CORES, seq % CORES, seq // CORES
     rows, cols = term.shape
@@ -314,65 +339,89 @@
     return total
 
 
-def fetch_kernel(place_ref, up_ref, gain_ref, out_ref):
-    n_dp, _, cols = out_ref.shape
-    half = up_ref.shape[0] // CORES
-    rows = pl.ds(pl.multiple_of(place_ref[1] * half, PIECE), half)
+def fetch_kernel(place_ref, up_ref, gain_ref, *out_refs):
+    rows, cols = out_refs[0].shape
+    half = rows - PIECE
+    own = pl.ds(pl.multiple_of(place_ref[1] * half, PIECE), half)
     gain = gain_ref[...].astype(jnp.float32)
     gain = jnp.concatenate([gain, jnp.zeros((1, cols - gain.shape[1]), jnp.float32)], axis=1)
     gain = jnp.broadcast_to(gain, (PIECE, cols)).astype(jnp.bfloat16)
-    for d in range(n_dp):
-        out_ref[d, :half, :] = up_ref[rows, d * cols : (d + 1) * cols]
-        out_ref[d, half:, :] = gain
+    for k, ref in enumerate(out_refs):
+        at = pl.multiple_of((place_ref[0] ^ k) * cols, LANES)
+        ref[:half, :] = up_ref[own, pl.ds(at, cols)]
+        ref[half:, :] = gain
 
 
 def fetch_up(place, w_up, norm_gain, n_dp):
     rows, ff = w_up.shape
-    shape = (n_dp, rows // CORES + PIECE, ff // n_dp)
-    sent = vmem_call(
-        fetch_kernel,
-        jax.ShapeDtypeStruct(shape, jnp.bfloat16),
-        [pltpu.SMEM, pltpu.VMEM, pltpu.VMEM],
-        1 << 20,
+    piece = jax.ShapeDtypeStruct((rows // CORES + PIECE, ff // n_dp), jnp.bfloat16)
+    return vmem_call(
+        fetch_kernel, (piece,) * n_dp, [pltpu.SMEM, pltpu.VMEM, pltpu.VMEM], 1 << 20
     )(place, w_up, norm_gain[None])
-    return lax.all_to_all(sent, "dp", split_axis=0, concat_axis=0, tiled=True)
-
-
-def assemble_kernel(place_ref, mine_ref, mate_ref, *refs):
-    *normed_refs, up_ref, act_ref, slope_ref, flip_ref, all_ref = refs
+
+
+def join_kernel(place_ref, mine_ref, mate_ref, up_ref, gain_ref):
     n_dp, half, cols = mine_ref.shape
     half = half - PIECE
     core = place_ref[1]
     for d in range(n_dp):
         for ref, which in ((mine_ref, core), (mate_ref, 1 - core)):
-            base = (d * CORES + which) * half
+            base = ((place_ref[0] ^ d) * CORES + which) * half
             up_ref[pl.ds(pl.multiple_of(base, PIECE), half), :] = ref[d, :half, :]
-    tokens = normed_refs[0].shape[0]
-    for k, ref in enumerate(normed_refs):
-        all_ref[k * tokens : (k + 1) * tokens, :] = ref[...]
-        flip_ref[:, k * tokens : (k + 1) * tokens] = ref[...].T
+    size = gain_ref.shape[1] // n_dp
+    parts = [mine_ref[k, half:, :].astype(jnp.float32)[:1, :size] for k in range(n_dp)]
+    row = []
+    for d in range(n_dp):
+        total = jnp.zeros((1, size), jnp.float32)
+        for k, part in enumerate(parts):
+            total = jnp.where((place_ref[0] ^ k) == d, part, total)
+        row.append(total)
+    gain_ref[...] = jnp.concatenate(row, axis=1)
+
+
+def join_columns(place, mine, mate):
+    n_dp, half, cols = mine.shape
+    feat = n_dp * CORES * (half - PIECE)
+    return vmem_call(
+        join_kernel,
+        (
+            jax.ShapeDtypeStruct((feat, cols), jnp.bfloat16),
+            jax.ShapeDtypeStruct((1, feat), jnp.float32),
+        ),
+        [pltpu.SMEM, pl.ANY, pl.ANY],
+        1 << 20,
+    )(place, mine, mate)
+
+
+def mlp_kernel(up_ref, gain_ref, *refs):
+    *unit_refs, act_ref, slope_ref, flip_ref, all_ref = refs
+    tokens = unit_refs[0].shape[0]
+    gain = gain_ref[...]
+    for k, ref in enumerate(unit_refs):
+        normed = (ref[...].astype(jnp.float32) * gain).astype(jnp.bfloat16)
+        all_ref[k * tokens : (k + 1) * tokens, :] = normed
+        flip_ref[:, k * tokens : (k + 1) * tokens] = normed.T
     pre_act = contract(all_ref[...], up_ref[...], 1, 0)
     sig_gate = jax.nn.sigmoid(1.702 * pre_act)
     act_ref[...] = (pre_act * sig_gate).astype(jnp.bfloat16).T
     slope_ref[...] = sig_gate + 1.702 * pre_act * sig_gate * (1.0 - sig_gate)
 
 
-def assemble(place, mine, mate, normed_blocks):
-    tokens, feat = normed_blocks[0].shape
-    total = tokens * len(normed_blocks)
-    cols = mine.shape[2]
-    return vmem_call(
-        assemble_kernel,
+def mlp(up_cols, gain, unit_blocks):
+    tokens, feat = unit_blocks[0].shape
+    total = tokens * len(unit_blocks)
+    cols = up_cols.shape[1]
+    return vmem_call(
+        mlp_kernel,
         (
-            jax.ShapeDtypeStruct((feat, cols), jnp.bfloat16),
             jax.ShapeDtypeStruct((cols, total), jnp.bfloat16),
             jax.ShapeDtypeStruct((total, cols), jnp.float32),
             jax.ShapeDtypeStruct((feat, total), jnp.bfloat16),
             jax.ShapeDtypeStruct((total, feat), jnp.bfloat16),
         ),
-        [pltpu.SMEM] + [pltpu.VMEM] * (2 + len(normed_blocks)),
+        [pltpu.VMEM] * (2 + len(unit_blocks)),
         2 * total * feat * cols,
-    )(place, mine, mate, *normed_blocks)
+    )(up_cols, gain, *unit_blocks)
 
 
 def store_by_core(core, value, which, keep_ref, give_ref, index):
@@ -385,9 +434,33 @@
         give_ref[index] = value
 
 
-def up_kernel(
-    place_ref, rows_ref, down_ref, slope_ref, flip_ref, pre_ref, keep_ref, give_ref
-):
+def down_kernel(place_ref, act_ref, *refs):
+    *rows_refs, all_ref, keep_ref, give_ref = refs
+    n_dp, half, width = keep_ref.shape
+    tokens = rows_refs[0].shape[0]
+    for k, ref in enumerate(rows_refs):
+        all_ref[k * tokens : (k + 1) * tokens, :] = ref[...]
+    term = contract(act_ref[...], all_ref[...], 1, 0).astype(jnp.bfloat16)
+    for which in range(CORES):
+        for d in range(n_dp):
+            piece = term[which * half : (which + 1) * half, d * width : (d + 1) * width]
+            store_by_core(place_ref[1], piece, which, keep_ref, give_ref, d)
+
+
+def down_pieces(place, act_flip, rows_blocks):
+    n_dp = len(rows_blocks)
+    tokens, feat = rows_blocks[0].shape
+    cols = act_flip.shape[0]
+    piece = jax.ShapeDtypeStruct((n_dp, cols // CORES, feat // n_dp), jnp.bfloat16)
+    return vmem_call(
+        down_kernel,
+        (jax.ShapeDtypeStruct((n_dp * tokens, feat), jnp.bfloat16), piece, piece),
+        [pltpu.SMEM] + [pltpu.VMEM] * (1 + n_dp),
+        2 * n_dp * tokens * feat * cols,
+    )(place, act_flip, *rows_blocks)
+
+
+def up_kernel(place_ref, rows_ref, down_ref, slope_ref, flip_ref, pre_ref, keep_ref, give_ref):
     n_z, rows, cols = keep_ref.shape
     d_act = contract(rows_ref[...], down_ref[...], 1, 1)
     d_pre = (d_act * slope_ref[...]).astype(jnp.bfloat16)
@@ -401,56 +474,40 @@
 
 
 def up_pieces(place, rows_all, w_down, slope, normed_flip, n_z):
-    total, feat = rows_all.shape
-    cols = slope.shape[1]
+    total, cols = slope.shape
+    feat = w_down.shape[1]
     piece = jax.ShapeDtypeStruct((n_z, feat // n_z // CORES, cols), jnp.bfloat16)
     return vmem_call(
         up_kernel,
         (jax.ShapeDtypeStruct((total, cols), jnp.bfloat16), piece, piece),
-        [pltpu.SMEM] + [pltpu.VMEM] * 4,
+        [pltpu.SMEM] + [pl.ANY] * 4,
         4 * total * feat * cols,
     )(place, rows_all, w_down, slope, normed_flip)
 
 
-def down_kernel(place_ref, act_ref, rows_ref, keep_ref, give_ref):
-    n_dp, half, width = keep_ref.shape
-    term = contract(act_ref[...], rows_ref[...], 1, 0).astype(jnp.bfloat16)
-    for which in range(CORES):
-        for d in range(n_dp):
-            piece = term[which * half : (which + 1) * half, d * width : (d + 1) * width]
-            store_by_core(place_ref[1], piece, which, keep_ref, give_ref, d)
-
-
-def down_pieces(place, act_flip, rows_all, n_dp):
-    tokens, feat = rows_all.shape
-    cols = act_flip.shape[0]
-    piece = jax.ShapeDtypeStruct((n_dp, cols // CORES, feat // n_dp), jnp.bfloat16)
-    return vmem_call(
-        down_kernel, (piece, piece), [pltpu.SMEM] + [pltpu.VMEM] * 2, 2 * tokens * feat * cols
-    )(place, act_flip, rows_all)
-
-
-def part_kernel(place_ref, pre_ref, up_ref, normed_ref, gain_ref, parts_ref, term_ref):
+def part_kernel(place_ref, pre_ref, up_ref, *refs):
+    *unit_refs, parts_ref, term_ref = refs
     n_dp, tokens, _ = parts_ref.shape
     part = contract(pre_ref[...], up_ref[...], 1, 1)
     for k in range(n_dp):
         rows = part[k * tokens : (k + 1) * tokens]
         parts_ref[place_ref[0] ^ k] = rows.astype(jnp.bfloat16)
-    term = jnp.sum(part * normed_ref[...].astype(jnp.float32), axis=0, keepdims=True)
-    term_ref[...] = term / gain_ref[...].astype(jnp.float32)
-
-
-def normed_parts(place, d_pre, up_cols, normed_all, gain, n_dp):
-    total, feat = normed_all.shape
+        term = jnp.sum(rows * unit_refs[k][...].astype(jnp.float32), axis=0, keepdims=True)
+        term_ref[...] = term if k == 0 else term_ref[...] + term
+
+
+def normed_parts(place, d_pre, up_cols, unit_blocks):
+    tokens, feat = unit_blocks[0].shape
+    n_dp = len(unit_blocks)
     return vmem_call(
         part_kernel,
         (
-            jax.ShapeDtypeStruct((n_dp, total // n_dp, feat), jnp.bfloat16),
+            jax.ShapeDtypeStruct((n_dp, tokens, feat), jnp.bfloat16),
             jax.ShapeDtypeStruct((1, feat), jnp.float32),
         ),
-        [pltpu.SMEM] + [pltpu.VMEM] * 4,
-        2 * total * feat * d_pre.shape[1],
-    )(place, d_pre, up_cols, normed_all, gain)
+        [pltpu.SMEM] + [pl.ANY] * (2 + n_dp),
+        2 * n_dp * tokens * feat * d_pre.shape[1],
+    )(place, d_pre, up_cols, *unit_blocks)
 
 
 def wide_sum(*terms):
@@ -468,76 +525,107 @@
     return jnp.concatenate(rows, axis=0).astype(jnp.bfloat16)
 
 
-def plane_kernel(keep_ref, mate_ref, term_ref, other_ref, out_ref):
-    n_dp, half, width = keep_ref.shape
+def side_kernel(place_ref, keep_ref, mate_ref, keep_out, give_out):
+    z = place_ref[2]
+    count = keep_out.shape[0]
+    for i in range(count):
+        for ref, at in ((keep_out, z ^ (2 * i)), (give_out, z ^ (2 * i + 1))):
+            ref[i] = wide_sum(keep_ref[at], mate_ref[at]).astype(jnp.bfloat16)
+
+
+def middle_kernel(keep_ref, got_ref, keep_out, give_out):
+    keep_out[...] = wide_sum(keep_ref[0], got_ref[0]).astype(jnp.bfloat16)
+    give_out[...] = wide_sum(keep_ref[1], got_ref[1]).astype(jnp.bfloat16)
+
+
+def plane_kernel(place_ref, keep_ref, mate_ref, *out_refs):
+    for k, ref in enumerate(out_refs):
+        at = place_ref[0] ^ k
+        ref[...] = wide_sum(keep_ref[at], mate_ref[at]).astype(jnp.bfloat16)
+
+
+def rise_kernel(place_ref, term_ref, other_ref, *refs):
+    count = len(refs) // 2
+    got_refs, out_refs = refs[:count], refs[count:]
+    half, width = got_refs[0].shape
     rows = to_rows(term_ref[...] + other_ref[...], width)
-    for d in range(n_dp):
-        out_ref[d, :half, :] = wide_sum(keep_ref[d], mate_ref[d]).astype(jnp.bfloat16)
-        out_ref[d, half:, :] = rows
-
-
-def rise_kernel(place_ref, got_ref, own_ref, *send_refs):
-    half = got_ref.shape[1] - PIECE
-    z = place_ref[2]
-    rows = wide_sum(*(got_ref[d, half:, :] for d in range(got_ref.shape[0])))
-    count = got_ref.shape[0]
-    total = rows[:count] + rows[count : 2 * count]
-    high = total.astype(jnp.bfloat16).astype(jnp.float32)
-    pad = jnp.zeros((PIECE - 2 * count, rows.shape[1]), jnp.float32)
-    rows = jnp.concatenate([high, total - high, pad], axis=0).astype(jnp.bfloat16)
-    for k, ref in enumerate((own_ref,) + send_refs):
-        ref[:half, :] = got_ref[z ^ k, :half, :]
+    for k, ref in enumerate(out_refs):
+        for step, got_ref in enumerate(got_refs):
+
+            @pl.when((place_ref[2] ^ k) == (place_ref[0] ^ step))
+            def _(ref=ref, got_ref=got_ref):
+                ref[:half, :] = got_ref[...]
+
         ref[half:, :] = rows
+
+
+def total_kernel(factor, *refs):
+    *in_refs, out_ref = refs
+    out_ref[...] = (wide_sum(*(ref[...] for ref in in_refs)) * factor).astype(jnp.bfloat16)
 
 
 def last_kernel(factor, *refs):
     *in_refs, down_ref, gain_ref = refs
     half = down_ref.shape[0]
-    count = gain_ref.shape[0]
+    count = len(in_refs)
     down_ref[...] = (wide_sum(*(ref[:half, :] for ref in in_refs)) * factor).astype(jnp.bfloat16)
     rows = wide_sum(*(ref[half:, :] for ref in in_refs))
-    gain_ref[...] = (rows[:count] + rows[count : 2 * count]) * factor
-
-
-def weight_sums(place, up_both, down_both, term, factor, n_seq, n_dp, seq):
-    n_z, z = n_seq // CORES, seq // CORES
-    up_keep, up_give = up_both
-    down_keep, down_give = down_both
-    up_mate = swap_seq(up_give, n_seq, 1)
-    down_mate = swap_seq(down_give, n_seq, 1)
-    other = swap_seq(term, n_seq, 1)
-
-    def up_piece(index):
-        return wide_sum(pick(up_keep, index), pick(up_mate, index))
-
-    up_total = up_piece(z)
-    for k in reversed(range(1, n_z)):
-        block = swap_seq(up_piece(z ^ k).astype(jnp.bfloat16), n_seq, CORES * k)
-        up_total = up_total + block.astype(jnp.float32)
-
-    half, width = down_keep.shape[1:]
-    planes = vmem_call(
-        plane_kernel,
-        jax.ShapeDtypeStruct((n_dp, half + PIECE, width), jnp.bfloat16),
-        [pltpu.VMEM] * 4,
-        1 << 20,
-    )(down_keep, down_mate, term, other)
-    planes = lax.all_to_all(planes, "dp", split_axis=0, concat_axis=0, tiled=True)
+    rows = (rows[:count] + rows[count : 2 * count]) * factor
+    gain_ref[...] = jnp.concatenate([rows[i : i + 1] for i in range(count)], axis=1)
+
+
+def up_sides(place, keep, mate):
+    pair = jax.ShapeDtypeStruct((keep.shape[0] // 2,) + keep.shape[1:], jnp.bfloat16)
+    return vmem_call(side_kernel, (pair, pair), [pltpu.SMEM, pltpu.VMEM, pltpu.VMEM], 1 << 20)(
+        place, keep, mate
+    )
+
+
+def up_middle(keep, got):
+    piece = jax.ShapeDtypeStruct(keep.shape[1:], jnp.bfloat16)
+    return vmem_call(middle_kernel, (piece, piece), [pltpu.VMEM] * 2, 1 << 20)(keep, got)
+
+
+def up_total(keep, got, factor):
+    piece = jax.ShapeDtypeStruct(keep.shape, jnp.bfloat16)
+    return vmem_call(
+        lambda *refs: total_kernel(factor, *refs), piece, [pltpu.VMEM] * 2, 1 << 20
+    )(keep, got)
+
+
+def down_planes(place, keep, mate):
+    n_dp, half, width = keep.shape
+    piece = jax.ShapeDtypeStruct((half, width), jnp.bfloat16)
+    return vmem_call(
+        plane_kernel, (piece,) * n_dp, [pltpu.SMEM] + [pltpu.VMEM] * 2, 1 << 20
+    )(place, keep, mate)
+
+
+def down_rise(place, term, other, planes):
+    count = len(planes)
+    half, width = planes[0].shape
     piece = jax.ShapeDtypeStruct((half + PIECE, width), jnp.bfloat16)
-    own, *sends = vmem_call(
-        rise_kernel, (piece,) * n_z, [pltpu.SMEM, pltpu.VMEM], 1 << 20
-    )(place, planes)
-    got = [swap_seq(block, n_seq, CORES * (k + 1)) for k, block in enumerate(sends)]
-    down_total, gain_total = vmem_call(
+    return vmem_call(
+        rise_kernel, (piece,) * count, [pltpu.SMEM] + [pltpu.VMEM] * (2 + count), 1 << 20
+    )(place, term, other, *planes)
+
+
+def down_total(pieces, factor):
+    rows, width = pieces[0].shape
+    down, gain = vmem_call(
         lambda *refs: last_kernel(factor, *refs),
         (
-            jax.ShapeDtypeStruct((half, width), jnp.bfloat16),
-            jax.ShapeDtypeStruct((n_dp, width), jnp.float32),
+            jax.ShapeDtypeStruct((rows - PIECE, width), jnp.bfloat16),
+            jax.ShapeDtypeStruct((1, width * len(pieces)), jnp.float32),
         ),
-        [pltpu.VMEM] * n_z,
+        [pltpu.VMEM] * len(pieces),
         1 << 20,
-    )(own, *got)
-    return (up_total * factor).astype(jnp.bfloat16), down_total, gain_total.reshape(-1)
+    )(*pieces)
+    return down, gain[0]
+
+
+def after(value, *others):
+    return lax.optimization_barrier((value,) + others)[0]
 
 
 def per_device(
@@ -561,36 +649,75 @@
 
     factor = 1.0 / math.sqrt(n_dp * n_seq * tokens)
     place = jnp.stack([dp, core, seq // CORES]).astype(jnp.int32)
-    quick = n_seq == CORES * n_dp
-
+    quick = n_seq == CORES * n_dp == 8
+
+    def backward_pass(d_got, saved):
+        attn_out, normal_unit, attn_probs, inverse = saved
+        return backward(
+            d_got,
+            grad_rows,
+            normal_unit,
+            inverse,
+            gain_row,
+            attn_probs,
+            attn_out,
+            queries[0],
+            key_rows[0],
+            value_rows[0],
+        )
+
+    def all_dp(block):
+        return [block] + [swap_dp(block, n_dp, k) for k in range(1, n_dp)]
+
+    sent = send_tiles(llm_grad[0], vision_slot, n_seq, tokens)
+    landing = lax.all_to_all(sent, "seq", split_axis=0, concat_axis=0, tiled=True)
+    attention = (queries[0], key_rows[0], value_rows[0], resid_in[0])
     if quick:
-        mine = fetch_up(place, w_up, norm_gain, n_dp)
-        mate = swap_seq(mine, n_seq, 1)
-        gain_full = mine[:, -1, : norm_gain.shape[0]].reshape(-1)
+        _, unit_low = forward(window_mask[0], *attention, 1 << 31, False)
+        unit_blocks = all_dp(unit_low)
+        own, *others = fetch_up(place, after(w_up, sent), norm_gain, n_dp)
+        mine = jnp.stack([own] + [swap_dp(block, n_dp, k + 1) for k, block in enumerate(others)])
+        up_cols, gain_row = join_columns(place, mine, swap_seq(mine, n_seq, 1))
+        landing = after(landing, up_cols)
     else:
-        gain_full = gather_gain(norm_gain, n_dp, dp)
+        gain_row = gather_gain(norm_gain, n_dp, dp).astype(jnp.float32)[None]
         own, mine, mate = fetch_pieces(w_up, n_dp, n_seq, dp, core)
-    grad_rows = owner_rows(llm_grad[0], vision_slot, n_seq, tokens)
-
-    attn_probs, attn_out, normal_unit, inverse = forward(
-        window_mask[0], queries[0], key_rows[0], value_rows[0], resid_in[0]
-    )
-    normed = (normal_unit * gain_full.astype(jnp.float32)).astype(jnp.bfloat16)
-    normed_blocks = [normed] + [swap_dp(normed, n_dp, k) for k in range(1, n_dp)]
-    rows_all = gather_tokens(grad_rows, n_dp)
+        saved = forward(window_mask[0], *attention, 1 << 31, True)
+        normed_blocks = all_dp((saved[1] * gain_row).astype(jnp.bfloat16))
+    grad_rows = land_tiles(landing, tokens)
+    rows_blocks = all_dp(grad_rows)
     if quick:
-        up_cols, act_flip, slope, normed_flip, normed_all = assemble(
-            place, mine, mate, normed_blocks
+        act_flip, slope, normed_flip, normed_all = mlp(up_cols, gain_row, unit_blocks)
+        rows_all, down_keep, down_give = down_pieces(place, act_flip, rows_blocks)
+        down_mate = swap_seq(down_give, n_seq, 1)
+        d_pre, up_keep, up_give = up_pieces(
+            place, rows_all, w_down, slope, normed_flip, n_seq // CORES
         )
-        d_pre, *up_both = up_pieces(place, rows_all, w_down, slope, normed_flip, n_seq // CORES)
-        down_both = down_pieces(place, act_flip, rows_all, n_dp)
-        parts, term = normed_parts(place, d_pre, up_cols, normed_all, gain_full[None], n_dp)
-        d_got = lax.all_to_all(parts, "dp", split_axis=0, concat_axis=0, tiled=True)
-        grad_up, grad_down, grad_gain = weight_sums(
-            place, up_both, down_both, term, factor, n_seq, n_dp, seq
+        up_mate = swap_seq(up_give, n_seq, 1)
+        own, *sends = down_planes(place, after(down_keep, d_pre), down_mate)
+        planes = [own] + [swap_dp(block, n_dp, k + 1) for k, block in enumerate(sends)]
+        parts, term = normed_parts(place, after(d_pre, own), up_cols, unit_blocks)
+        term = term + swap_seq(term, n_seq, 1)
+        up_keep, up_give = up_sides(place, after(up_keep, own), up_mate)
+        up_got = swap_seq(up_give, n_seq, CORES)
+        term = term + swap_dp(term, n_dp, 1)
+        own, *sends = down_rise(place, term, swap_dp(term, n_dp, 2), planes)
+        pieces = [own] + [
+            swap_seq(block, n_seq, CORES * (k + 1)) for k, block in enumerate(sends)
+        ]
+        up_keep, up_give = up_middle(up_keep, up_got)
+        up_got = swap_seq(up_give, n_seq, 2 * CORES)
+        d_got = lax.all_to_all(
+            after(parts, own, up_give), "dp", split_axis=0, concat_axis=0, tiled=True
         )
+        saved = forward(after(window_mask[0], own), *attention, 1 << 31, True)
+        grads = backward_pass(after(d_got, up_got), saved)
+        pieces[0] = after(pieces[0], grads[3])
+        grad_up = up_total(up_keep, up_got, factor)
+        grad_down, grad_gain = down_total(pieces, factor)
     else:
         normed_all = jnp.concatenate(normed_blocks, axis=0)
+        rows_all = jnp.concatenate(rows_blocks, axis=0)
         up_cols = join_up(own, mine, mate, n_dp, dp, core)
         pre_act = contract(normed_all, up_cols, 1, 0)
         sig_gate = jax.nn.sigmoid(1.702 * pre_act)
@@ -605,22 +732,12 @@
         up_sum = scatter_up(contract(normed_all, d_pre, 0, 0), n_seq, seq)
         down_sum = scatter_down(contract(act_low, rows_all, 0, 0), n_seq, n_dp, seq)
         gain_part = jnp.sum(d_part * normed_all.astype(jnp.float32), axis=0)
-        grad_gain = factor * sum_all(gain_part / gain_full.astype(jnp.float32), n_seq, n_dp)
+        grad_gain = factor * sum_all(gain_part / gain_row[0], n_seq, n_dp)
         grad_up = (up_sum * factor).astype(jnp.bfloat16)
         grad_down = (down_sum * factor).astype(jnp.bfloat16)
-
-    grad_query, grad_key, grad_value, grad_resid = backward(
-        d_got,
-        grad_rows,
-        normal_unit,
-        inverse,
-        gain_full[None],
-        attn_probs,
-        attn_out,
-        queries[0],
-        key_rows[0],
-        value_rows[0],
-    )
+        grads = backward_pass(d_got, saved)
+    grad_query, grad_key, grad_value, grad_resid = grads
+
     return (
         grad_query[None],
         grad_key[None],

time: 146 us -> 127 us (0.87)
  the two profiles are of different devices: /device:TPU:8 before, /device:TPU:18 now
where the time goes in v5:
time: 127 us; the launch traced here: 126 us
  waiting for transfers between devices  41.5 us (33%)
  Pallas kernels  35.2 us (28%)
  starting transfers between devices  31.4 us (25%)
  local copies, waits for them, and re-layouts  15 us (12%)
  other arithmetic  1.89 us (1%)
    pallas_call x17, Pallas kernels, run(): pl.pallas_call(kernel if places else body, out_shape=out_shape, in_specs=...  35.2 us
    ppermute x14, waiting for transfers between devices, swap_dp(): return lax.ppermute(block, 'dp', [(i, i ^ step) for i in range(count)])  30.2 us
    ppermute x14, starting transfers between devices, swap_dp(): return lax.ppermute(block, 'dp', [(i, i ^ step) for i in range(count)])  15.3 us
    unnamed x48, local copies, waits for them, and re-layouts  14.3 us
    ppermute x9, waiting for transfers between devices, swap_seq(): return lax.ppermute(block, 'seq', [(i, i ^ step) for i in range(count)])  8.64 us
    ppermute x9, starting transfers between devices, swap_seq(): return lax.ppermute(block, 'seq', [(i, i ^ step) for i in range(count)])  6.25 us
    all_to_all x1, starting transfers between devices, per_device(): lax.all_to_all(sent, 'seq', split_axis=0, concat_axis=0, tiled=True)  5.21 us
    all_to_all x1, starting transfers between devices, per_device(): lax.all_to_all(after(parts, own, up_give), 'dp', split_axis=0, concat_axi...  4.57 us
  transfers between devices with their start and end apart: 25, of which 13 were waited for; matrix products, arithmetic and copies ran while one was open for 1% of the time, Pallas kernels for 22%

profile of v5, /device:TPU:18, one launch (start us, length us, event | category | flops | bytes accessed | tf_op | source)
XLA Modules:
  0.0 125.8 jit_solution(9984281294796074290)
XLA Ops:
  0.6 0.7 broadcast_in_dim.15.gain_ref
  1.3 1.0 copy-done.1
  2.4 0.7 copy-done.2
  3.0 1.7 %shard_map.153 = bf16[8,32,1408]{2,1,0:T(8,128)(2,1)} custom-call(s32[1,192]{1,0:T(1,128)S(1)} %copy-done.2, bf16[192,1280]{1,0:T(8,128)(2,1)S(1)} %bitcast.19), custom_call_target="tpu_custom_call" | custom-call | flops 1048576 | bytes 4194304 | tf_op jit(solution)/shard_map/pallas_call | solution.py:39
  4.8 1.4 %copy-done = bf16[320,2560]{1,0:T(8,128)(2,1)S(1)} copy-done((bf16[320,2560]{1,0:T(8,128)(2,1)S(1)}, bf16[320,2560]{1,0:T(8,128)(2,1)}, u32[]{:S(2)}) %copy-start) | copy-done | bytes 1638424
  6.2 0.6 shard_map.154
  6.9 0.6 collective-permute-start
  7.5 1.5 %collective-permute-start.1 = (bf16[176,640]{1,0:T(8,128)(2,1)S(1)}, bf16[176,640]{1,0:T(8,128)(2,1)}, u32[]{:S(2)}, u32[]{:S(2)}) collective-permute-start(bf16[176,640]{1,0:T(8,128)(2,1)S(1)} %get-tuple-element.59), channel_id=1, source_target_pairs={{0,2},{1,3},{2,0},{3,1},{4,6},{5,7},{6,4},{7,5},{8,10},{9,11},{10,... | collective-permute-start | bytes 675848 | tf_op jit(solution)/shard_map/ppermute | solution.py:66
  9.0 1.5 %collective-permute-start.2 = (bf16[176,640]{1,0:T(8,128)(2,1)S(1)}, bf16[176,640]{1,0:T(8,128)(2,1)}, u32[]{:S(2)}, u32[]{:S(2)}) collective-permute-start(bf16[176,640]{1,0:T(8,128)(2,1)S(1)} %get-tuple-element.60), channel_id=1, source_target_pairs={{0,3},{1,2},{2,1},{3,0},{4,7},{5,6},{6,5},{7,4},{8,11},{9,10},{10,... | collective-permute-start | bytes 675848 | tf_op jit(solution)/shard_map/ppermute | solution.py:66
  10.5 5.2 %all-to-all-start = ((bf16[8,32,1408]{2,1,0:T(8,128)(2,1)}), bf16[8,32,1408]{2,1,0:T(8,128)(2,1)S(1)}, u32[]{:S(2)}, u32[]{:S(2)}) async-start(bf16[8,32,1408]{2,1,0:T(8,128)(2,1)} %shard_map.153), calls=%async_computation | async-start | bytes 1441792 | tf_op jit(solution)/shard_map/all_to_all | solution.py:673
  15.7 2.6 %collective-permute-done.1 = bf16[176,640]{1,0:T(8,128)(2,1)} collective-permute-done((bf16[176,640]{1,0:T(8,128)(2,1)S(1)}, bf16[176,640]{1,0:T(8,128)(2,1)}, u32[]{:S(2)}, u32[]{:S(2)}) %collective-permute-start.1) | collective-permute-done | bytes 225312 | tf_op jit(solution)/shard_map/ppermute | solution.py:66
  18.3 1.7 %collective-permute-done.2 = bf16[176,640]{1,0:T(8,128)(2,1)} collective-permute-done((bf16[176,640]{1,0:T(8,128)(2,1)S(1)}, bf16[176,640]{1,0:T(8,128)(2,1)}, u32[]{:S(2)}, u32[]{:S(2)}) %collective-permute-start.2) | collective-permute-done | bytes 225312 | tf_op jit(solution)/shard_map/ppermute | solution.py:66
  20.1 1.2 pad_maximum_fusion.refs_1_
  21.4 4.3 %shard_map.156 = (bf16[128,1280]{1,0:T(8,128)(2,1)}, bf16[128,1280]{1,0:T(8,128)(2,1)S(1)}) custom-call(s32[2,2]{1,0:T(2,128)S(1)} %bitcast.32, bf16[128,1280]{1,0:T(8,128)(2,1)S(1)} %bitcast.23, bf16[128,1280]{1,0:T(8,128)(2,1)S(1)} %bitcast.26, bf16[128,1280]{1,0:T(8,128)(2,1)S(1)} %bitcast.29, bf16[128,1280]{1,0:T(8,128)(2,1)S(1)} %bitcast.21), custom_call_target="tpu_custom_call" | custom-call | flops 2147483648 | bytes 4194304 | tf_op jit(solution)/shard_map/pallas_call | solution.py:39
  25.7 1.7 %collective-permute-start.6 = (bf16[128,1280]{1,0:T(8,128)(2,1)S(1)}, bf16[128,1280]{1,0:T(8,128)(2,1)S(1)}, u32[]{:S(2)}, u32[]{:S(2)}) collective-permute-start(bf16[128,1280]{1,0:T(8,128)(2,1)S(1)} %get-tuple-element.63.refs_0_.refs_3_), channel_id=1, source_target_pairs={{0,3},{1,2},{2,1},{3,0},{4,7},{5,6},{6,5},{7,4},{8,11},{9,10},{10,... | collective-permute-start | bytes 983048 | tf_op jit(solution)/shard_map/ppermute | solution.py:66
  27.9 1.2 collective-permute-start.4
  29.2 1.1 shard_map.155
  30.3 1.7 %all-to-all-done = bf16[8,32,1408]{2,1,0:T(8,128)(2,1)S(1)} async-done(((bf16[8,32,1408]{2,1,0:T(8,128)(2,1)}), bf16[8,32,1408]{2,1,0:T(8,128)(2,1)S(1)}, u32[]{:S(2)}, u32[]{:S(2)}) %all-to-all-start) | async-done | bytes 720928 | tf_op jit(solution)/shard_map/all_to_all | solution.py:673
  32.3 1.6 %collective-permute-start.9 = (bf16[128,1280]{1,0:T(8,128)(2,1)S(1)}, bf16[128,1280]{1,0:T(8,128)(2,1)S(1)}, u32[]{:S(2)}, u32[]{:S(2)}) collective-permute-start(bf16[128,1280]{1,0:T(8,128)(2,1)S(1)} %shard_map.158.refs_0_.rows_ref), channel_id=1, source_target_pairs={{0,3},{1,2},{2,1},{3,0},{4,7},{5,6},{6,5},{7,4},{8,11},{9,10},{10,... | collective-permute-start | bytes 983048 | tf_op jit(solution)/shard_map/ppermute | solution.py:66
  34.4 2.8 %collective-permute-done.6.refs_3_.refs_6_ = bf16[128,1280]{1,0:T(8,128)(2,1)S(1)} collective-permute-done((bf16[128,1280]{1,0:T(8,128)(2,1)S(1)}, bf16[128,1280]{1,0:T(8,128)(2,1)S(1)}, u32[]{:S(2)}, u32[]{:S(2)}) %collective-permute-start.6) | collective-permute-done | bytes 327712 | tf_op jit(solution)/shard_map/ppermute | solution.py:66
  37.1 0.8 collective-permute-start.7
  37.9 6.4 %collective-permute-done.5.refs_2_.refs_5_ = bf16[128,1280]{1,0:T(8,128)(2,1)} collective-permute-done((bf16[128,1280]{1,0:T(8,128)(2,1)S(1)}, bf16[128,1280]{1,0:T(8,128)(2,1)}, u32[]{:S(2)}, u32[]{:S(2)}) %collective-permute-start.5) | collective-permute-done | bytes 327712 | tf_op jit(solution)/shard_map/ppermute | solution.py:66
  44.3 2.6 %shard_map.157 = (bf16[640,512]{1,0:T(8,128)(2,1)S(1)}, f32[512,640]{1,0:T(8,128)S(1)}, bf16[1280,512]{1,0:T(8,128)(2,1)S(1)}, bf16[512,1280]{1,0:T(8,128)(2,1)}) custom-call(bf16[1280,640]{1,0:T(8,128)(2,1)S(1)} %get-tuple-element.61.up_ref.refs_2_, f32[1,1280]{1,0:T(1,128)S(1)} %get-tuple-element.62.gain_ref, ...), custom_call_target="tpu_custom_call" | custom-call | flops 838860800 | bytes 4194304 | tf_op jit(solution)/shard_map/pallas_call | solution.py:39
  46.9 4.3 %collective-permute-done.9.refs_3_ = bf16[128,1280]{1,0:T(8,128)(2,1)S(1)} collective-permute-done((bf16[128,1280]{1,0:T(8,128)(2,1)S(1)}, bf16[128,1280]{1,0:T(8,128)(2,1)S(1)}, u32[]{:S(2)}, u32[]{:S(2)}) %collective-permute-start.9) | collective-permute-done | bytes 327712 | tf_op jit(solution)/shard_map/ppermute | solution.py:66
  51.2 6.5 %collective-permute-done.8.refs_2_ = bf16[128,1280]{1,0:T(8,128)(2,1)S(1)} collective-permute-done((bf16[128,1280]{1,0:T(8,128)(2,1)S(1)}, bf16[128,1280]{1,0:T(8,128)(2,1)S(1)}, u32[]{:S(2)}, u32[]{:S(2)}) %collective-permute-start.8) | collective-permute-done | bytes 327712 | tf_op jit(solution)/shard_map/ppermute | solution.py:66
  57.7 2.3 %shard_map.159 = (bf16[512,1280]{1,0:T(8,128)(2,1)S(1)}, bf16[4,320,320]{2,1,0:T(8,128)(2,1)S(1)}, bf16[4,320,320]{2,1,0:T(8,128)(2,1)S(1)}) custom-call(s32[3]{0:T(128)S(1)} %pad_add_fusion.place_ref.refs_0_, bf16[640,512]{1,0:T(8,128)(2,1)S(1)} %get-tuple-element.64.act_ref, bf16[128,1280]{1,0:T(8,128)(2,1)S(1)} %shard_map.158.refs_0_.rows_ref, ...), custom_call_target="tpu_custom_call" | custom-call | flops 838860800 | bytes 4194304 | tf_op jit(solution)/shard_map/pallas_call | solution.py:39
  60.2 3.5 %shard_map.160 = (bf16[512,640]{1,0:T(8,128)(2,1)S(1)}, bf16[4,160,640]{2,1,0:T(8,128)(2,1)S(1)}, bf16[4,160,640]{2,1,0:T(8,128)(2,1)S(1)}) custom-call(s32[3]{0:T(128)S(1)} %pad_add_fusion.place_ref.refs_0_, bf16[512,1280]{1,0:T(8,128)(2,1)S(1)} %get-tuple-element.66.refs_1_, bf16[640,1280]{1,0:T(8,128)(2,1)S(1)} %copy-done.3, ...), custom_call_target="tpu_custom_call" | custom-call | flops 1677721600 | bytes 4194304 | tf_op jit(solution)/shard_map/pallas_call | solution.py:39
  63.7 0.5 collective-permute-start.17
  64.3 0.8 shard_map.161
  65.1 1.2 collective-permute-done.17.mate_ref
  66.2 0.7 shard_map.164
  67.0 1.7 %collective-permute-start.18 = (bf16[2,160,640]{2,1,0:T(8,128)(2,1)S(1)}, bf16[2,160,640]{2,1,0:T(8,128)(2,1)S(1)}, u32[]{:S(2)}, u32[]{:S(2)}) collective-permute-start(bf16[2,160,640]{2,1,0:T(8,128)(2,1)S(1)} %get-tuple-element.85), channel_id=1, source_target_pairs={{0,8},{4,12},{8,0},{12,4},{16,24},{20,28},{24,16},{28,20},{1,9},{5... | collective-permute-start | bytes 1228808 | tf_op jit(solution)/shard_map/ppermute | solution.py:70
  68.6 0.9 collective-permute-start.14
  69.6 1.4 %collective-permute-start.15 = (bf16[320,320]{1,0:T(8,128)(2,1)S(1)}, bf16[320,320]{1,0:T(8,128)(2,1)S(1)}, u32[]{:S(2)}, u32[]{:S(2)}) collective-permute-start(bf16[320,320]{1,0:T(8,128)(2,1)S(1)} %get-tuple-element.78), channel_id=1, source_target_pairs={{0,2},{1,3},{2,0},{3,1},{4,6},{5,7},{6,4},{7,5},{8,10},{9,11},{10,... | collective-permute-start | bytes 614408 | tf_op jit(solution)/shard_map/ppermute | solution.py:66
  70.9 1.2 collective-permute-start.16
  72.1 4.5 %shard_map.162 = (bf16[4,128,1280]{2,1,0:T(8,128)(2,1)}, f32[1,1280]{1,0:T(1,128)S(1)}) custom-call(s32[3]{0:T(128)S(1)} %pad_add_fusion.place_ref.refs_0_, bf16[512,640]{1,0:T(8,128)(2,1)S(1)} %get-tuple-element.74.refs_1_, bf16[1280,640]{1,0:T(8,128)(2,1)S(1)} %get-tuple-element.61.up_ref.refs_2_, bf16[128,1280]{1,0:T(8,128)(2,1)S(1)} %get-tuple-element.63.refs_0_.refs_3_, ...), custom_call_target="tpu_custom_call" | custom-call | flops 838860800 | bytes 4194304 | tf_op jit(solution)/shard_map/pallas_call | solution.py:39
  76.7 1.2 collective-permute-done.11
  77.9 1.0 collective-permute-start.12
  78.9 3.1 %collective-permute-done.12 = f32[1,1280]{1,0:T(1,128)S(1)} collective-permute-done((f32[1,1280]{1,0:T(1,128)S(1)}, f32[1,1280]{1,0:T(1,128)S(1)}, u32[]{:S(2)}, u32[]{:S(2)}) %collective-permute-start.12) | collective-permute-done | bytes 5152 | tf_op jit(solution)/shard_map/ppermute | solution.py:66
  82.0 0.9 collective-permute-start.13
  82.9 2.8 %collective-permute-done.13.other_ref = f32[1,1280]{1,0:T(1,128)S(1)} collective-permute-done((f32[1,1280]{1,0:T(1,128)S(1)}, f32[1,1280]{1,0:T(1,128)S(1)}, u32[]{:S(2)}, u32[]{:S(2)}) %collective-permute-start.13) | collective-permute-done | bytes 5152 | tf_op jit(solution)/shard_map/ppermute | solution.py:66
  85.7 1.8 %shard_map.163 = (bf16[336,320]{1,0:T(8,128)(2,1)S(1)}, bf16[336,320]{1,0:T(8,128)(2,1)}, bf16[336,320]{1,0:T(8,128)(2,1)}, bf16[336,320]{1,0:T(8,128)(2,1)S(1)}) custom-call(s32[3]{0:T(128)S(1)} %pad_add_fusion.place_ref.refs_0_, f32[1,1280]{1,0:T(1,128)S(1)} %add.13.term_ref, f32[1,1280]{1,0:T(1,128)S(1)} %collective-permute-done.13.other_ref, ...), custom_call_target="tpu_custom_call" | custom-call | flops 1048576 | bytes 4194304 | tf_op jit(solution)/shard_map/pallas_call | solution.py:39
  87.5 0.8 shard_map.165
  88.3 4.6 %all-to-all-start.1 = ((bf16[4,128,1280]{2,1,0:T(8,128)(2,1)}), bf16[4,128,1280]{2,1,0:T(8,128)(2,1)S(1)}, u32[]{:S(2)}, u32[]{:S(2)}) async-start(bf16[4,128,1280]{2,1,0:T(8,128)(2,1)} %get-tuple-element.87), calls=%async_computation.1 | async-start | bytes 2621440 | tf_op jit(solution)/shard_map/all_to_all | solution.py:710
  93.6 2.6 %collective-permute-start.21 = (bf16[336,320]{1,0:T(8,128)(2,1)}, bf16[336,320]{1,0:T(8,128)(2,1)S(1)}, u32[]{:S(2)}, u32[]{:S(2)}) collective-permute-start(bf16[336,320]{1,0:T(8,128)(2,1)} %get-tuple-element.101), channel_id=1, source_target_pairs={{0,16},{4,20},{8,24},{12,28},{16,0},{20,4},{24,8},{28,12},{1,17},{... | collective-permute-start | bytes 645128 | tf_op jit(solution)/shard_map/ppermute | solution.py:70
  96.7 1.0 copy-done.9
  97.6 1.0 copy-done.12
  98.6 3.8 %shard_map.166 = (bf16[128,1280]{1,0:T(8,128)(2,1)S(1)}, f32[128,1280]{1,0:T(8,128)S(1)}, f32[16,128,128]{2,1,0:T(8,128)S(1)}, f32[128,128]{1,0:T(8,128)S(1)}) custom-call(s32[2,2]{1,0:T(2,128)S(1)} %bitcast.33, bf16[128,1280]{1,0:T(8,128)(2,1)S(1)} %bitcast.24, bf16[128,1280]{1,0:T(8,128)(2,1)S(1)} %bitcast.27, bf16[128,1280]{1,0:T(8,128)(2,1)S(1)} %bitcast.30, ...), custom_call_target="tpu_custom_call" | custom-call | flops 2147483648 | bytes 4194304 | tf_op jit(solution)/shard_map/pallas_call | solution.py:39
  102.4 1.0 copy-done.16
  103.4 0.8 copy-done.18
  104.2 0.7 copy-done.20
  104.9 0.6 copy-done.22
  105.6 0.7 shard_map.168
  106.3 0.9 all-to-all-done.1.got_ref
  107.2 1.0 copy-done.10
  108.2 1.0 copy-done.13
  109.2 1.2 copy-done.17
  110.4 1.1 copy-done.19
  111.5 1.0 copy-done.21
  112.4 0.8 copy-done.23
  113.3 4.7 %shard_map.167 = (bf16[128,1280]{1,0:T(8,128)(2,1)}, bf16[128,1280]{1,0:T(8,128)(2,1)}, bf16[128,1280]{1,0:T(8,128)(2,1)}, bf16[128,1280]{1,0:T(8,128)(2,1)}) custom-call(bf16[4,128,1280]{2,1,0:T(8,128)(2,1)S(1)} %all-to-all-done.1.got_ref, bf16[128,1280]{1,0:T(8,128)(2,1)S(1)} %shard_map.158.refs_0_.rows_ref, f32[128,1280]{1,0:T(8,128)S(1)} %copy-done.19, ...), custom_call_target="tpu_custom_call" | custom-call | flops 4294967296 | bytes 4194304 | tf_op jit(solution)/shard_map/pallas_call | solution.py:39
  118.0 6.3 %collective-permute-done.22.refs_3_ = bf16[336,320]{1,0:T(8,128)(2,1)S(1)} collective-permute-done((bf16[336,320]{1,0:T(8,128)(2,1)}, bf16[336,320]{1,0:T(8,128)(2,1)S(1)}, u32[]{:S(2)}, u32[]{:S(2)}) %collective-permute-start.22) | collective-permute-done | bytes 215072 | tf_op jit(solution)/shard_map/ppermute | solution.py:70
  124.3 0.9 shard_map.169
  125.2 0.6 reduce
  (57 shorter events, 2.9 us)
Async XLA Ops:
  1.3 1.0 copy-start.1
  2.4 0.7 copy-start.2
  4.8 1.4 %copy-start = (bf16[320,2560]{1,0:T(8,128)(2,1)S(1)}, bf16[320,2560]{1,0:T(8,128)(2,1)}, u32[]{:S(2)}) copy-start(bf16[320,2560]{1,0:T(8,128)(2,1)} %up_ref) | copy-start | bytes 4915204
  6.9 8.9 %collective-permute-start = (bf16[176,640]{1,0:T(8,128)(2,1)S(1)}, bf16[176,640]{1,0:T(8,128)(2,1)S(1)}, u32[]{:S(2)}, u32[]{:S(2)}) collective-permute-start(bf16[176,640]{1,0:T(8,128)(2,1)S(1)} %get-tuple-element.58), channel_id=1, source_target_pairs={{0,1},{1,0},{2,3},{3,2},{4,5},{5,4},{6,7},{7,6},{8,9},{9,8},{10,11... | collective-permute-start | bytes 675848 | tf_op jit(solution)/shard_map/ppermute | solution.py:66
  7.5 10.9 %collective-permute-start.1 = (bf16[176,640]{1,0:T(8,128)(2,1)S(1)}, bf16[176,640]{1,0:T(8,128)(2,1)}, u32[]{:S(2)}, u32[]{:S(2)}) collective-permute-start(bf16[176,640]{1,0:T(8,128)(2,1)S(1)} %get-tuple-element.59), channel_id=1, source_target_pairs={{0,2},{1,3},{2,0},{3,1},{4,6},{5,7},{6,4},{7,5},{8,10},{9,11},{10,... | collective-permute-start | bytes 675848 | tf_op jit(solution)/shard_map/ppermute | solution.py:66
  9.0 12.4 %copy-start.4 = (bf16[1,128,1280]{2,1,0:T(8,128)(2,1)S(1)}, bf16[1,128,1280]{2,1,0:T(8,128)(2,1)}, u32[]{:S(2)}) copy-start(bf16[1,128,1280]{2,1,0:T(8,128)(2,1)} %param.13) | copy-start | bytes 983044
  9.0 12.4 %copy-start.6 = (bf16[1,128,1280]{2,1,0:T(8,128)(2,1)S(1)}, bf16[1,128,1280]{2,1,0:T(8,128)(2,1)}, u32[]{:S(2)}) copy-start(bf16[1,128,1280]{2,1,0:T(8,128)(2,1)} %param.10) | copy-start | bytes 983044
  9.0 12.4 %copy-start.8 = (bf16[1,128,1280]{2,1,0:T(8,128)(2,1)S(1)}, bf16[1,128,1280]{2,1,0:T(8,128)(2,1)}, u32[]{:S(2)}) copy-start(bf16[1,128,1280]{2,1,0:T(8,128)(2,1)} %param.11) | copy-start | bytes 983044
  9.0 12.4 %copy-start.11 = (bf16[1,128,1280]{2,1,0:T(8,128)(2,1)S(1)}, bf16[1,128,1280]{2,1,0:T(8,128)(2,1)}, u32[]{:S(2)}) copy-start(bf16[1,128,1280]{2,1,0:T(8,128)(2,1)} %param.12) | copy-start | bytes 983044
  9.0 12.4 %copy-start.15 = (s32[1,2,2]{2,1,0:T(2,128)S(1)}, s32[1,2,2]{2,1,0:T(2,128)}, u32[]{:S(2)}) copy-start(s32[1,2,2]{2,1,0:T(2,128)} %param.16) | copy-start | bytes 52
  9.0 11.1 %collective-permute-start.2 = (bf16[176,640]{1,0:T(8,128)(2,1)S(1)}, bf16[176,640]{1,0:T(8,128)(2,1)}, u32[]{:S(2)}, u32[]{:S(2)}) collective-permute-start(bf16[176,640]{1,0:T(8,128)(2,1)S(1)} %get-tuple-element.60), channel_id=1, source_target_pairs={{0,3},{1,2},{2,1},{3,0},{4,7},{5,6},{6,5},{7,4},{8,11},{9,10},{10,... | collective-permute-start | bytes 675848 | tf_op jit(solution)/shard_map/ppermute | solution.py:66
  10.5 21.5 %all-to-all-start = ((bf16[8,32,1408]{2,1,0:T(8,128)(2,1)}), bf16[8,32,1408]{2,1,0:T(8,128)(2,1)S(1)}, u32[]{:S(2)}, u32[]{:S(2)}) async-start(bf16[8,32,1408]{2,1,0:T(8,128)(2,1)} %shard_map.153), calls=%async_computation | async-start | bytes 1441792 | tf_op jit(solution)/shard_map/all_to_all | solution.py:673
  21.2 7.9 %collective-permute-start.3 = (bf16[4,176,640]{2,1,0:T(8,128)(2,1)S(1)}, bf16[4,176,640]{2,1,0:T(8,128)(2,1)S(1)}, u32[]{:S(2)}, u32[]{:S(2)}) collective-permute-start(bf16[4,176,640]{2,1,0:T(8,128)(2,1)S(1)} %pad_maximum_fusion.refs_1_), channel_id=1, source_target_pairs={{0,4},{4,0},{8,12},{12,8},{16,20},{20,16},{24,28},{28,24},{1,5},{5... | collective-permute-start | bytes 2703368 | tf_op jit(solution)/shard_map/ppermute | solution.py:70
  25.7 11.5 %collective-permute-start.6 = (bf16[128,1280]{1,0:T(8,128)(2,1)S(1)}, bf16[128,1280]{1,0:T(8,128)(2,1)S(1)}, u32[]{:S(2)}, u32[]{:S(2)}) collective-permute-start(bf16[128,1280]{1,0:T(8,128)(2,1)S(1)} %get-tuple-element.63.refs_0_.refs_3_), channel_id=1, source_target_pairs={{0,3},{1,2},{2,1},{3,0},{4,7},{5,6},{6,5},{7,4},{8,11},{9,10},{10,... | collective-permute-start | bytes 983048 | tf_op jit(solution)/shard_map/ppermute | solution.py:66
  27.4 16.9 %collective-permute-start.5 = (bf16[128,1280]{1,0:T(8,128)(2,1)S(1)}, bf16[128,1280]{1,0:T(8,128)(2,1)}, u32[]{:S(2)}, u32[]{:S(2)}) collective-permute-start(bf16[128,1280]{1,0:T(8,128)(2,1)S(1)} %get-tuple-element.63.refs_0_.refs_3_), channel_id=1, source_target_pairs={{0,2},{1,3},{2,0},{3,1},{4,6},{5,7},{6,4},{7,5},{8,10},{9,11},{10,... | collective-permute-start | bytes 983048 | tf_op jit(solution)/shard_map/ppermute | solution.py:66
  27.9 16.4 %collective-permute-start.4 = (bf16[128,1280]{1,0:T(8,128)(2,1)S(1)}, bf16[128,1280]{1,0:T(8,128)(2,1)}, u32[]{:S(2)}, u32[]{:S(2)}) collective-permute-start(bf16[128,1280]{1,0:T(8,128)(2,1)S(1)} %get-tuple-element.63.refs_0_.refs_3_), channel_id=1, source_target_pairs={{0,1},{1,0},{2,3},{3,2},{4,5},{5,4},{6,7},{7,6},{8,9},{9,8},{10,11... | collective-permute-start | bytes 983048 | tf_op jit(solution)/shard_map/ppermute | solution.py:66
  32.3 18.9 %collective-permute-start.9 = (bf16[128,1280]{1,0:T(8,128)(2,1)S(1)}, bf16[128,1280]{1,0:T(8,128)(2,1)S(1)}, u32[]{:S(2)}, u32[]{:S(2)}) collective-permute-start(bf16[128,1280]{1,0:T(8,128)(2,1)S(1)} %shard_map.158.refs_0_.rows_ref), channel_id=1, source_target_pairs={{0,3},{1,2},{2,1},{3,0},{4,7},{5,6},{6,5},{7,4},{8,11},{9,10},{10,... | collective-permute-start | bytes 983048 | tf_op jit(solution)/shard_map/ppermute | solution.py:66
  33.9 23.9 %collective-permute-start.8 = (bf16[128,1280]{1,0:T(8,128)(2,1)S(1)}, bf16[128,1280]{1,0:T(8,128)(2,1)S(1)}, u32[]{:S(2)}, u32[]{:S(2)}) collective-permute-start(bf16[128,1280]{1,0:T(8,128)(2,1)S(1)} %shard_map.158.refs_0_.rows_ref), channel_id=1, source_target_pairs={{0,2},{1,3},{2,0},{3,1},{4,6},{5,7},{6,4},{7,5},{8,10},{9,11},{10,... | collective-permute-start | bytes 983048 | tf_op jit(solution)/shard_map/ppermute | solution.py:66
  37.1 20.6 %collective-permute-start.7 = (bf16[128,1280]{1,0:T(8,128)(2,1)S(1)}, bf16[128,1280]{1,0:T(8,128)(2,1)S(1)}, u32[]{:S(2)}, u32[]{:S(2)}) collective-permute-start(bf16[128,1280]{1,0:T(8,128)(2,1)S(1)} %shard_map.158.refs_0_.rows_ref), channel_id=1, source_target_pairs={{0,1},{1,0},{2,3},{3,2},{4,5},{5,4},{6,7},{7,6},{8,9},{9,8},{10,11... | collective-permute-start | bytes 983048 | tf_op jit(solution)/shard_map/ppermute | solution.py:66
  57.7 2.4 %copy-start.3 = (bf16[640,1280]{1,0:T(8,128)(2,1)S(1)}, bf16[640,1280]{1,0:T(8,128)(2,1)}, u32[]{:S(2)}) copy-start(bf16[640,1280]{1,0:T(8,128)(2,1)} %refs_2_.1) | copy-start | bytes 4915204
  60.1 4.2 %collective-permute-start.10 = (bf16[4,320,320]{2,1,0:T(8,128)(2,1)S(1)}, bf16[4,320,320]{2,1,0:T(8,128)(2,1)S(1)}, u32[]{:S(2)}, u32[]{:S(2)}) collective-permute-start(bf16[4,320,320]{2,1,0:T(8,128)(2,1)S(1)} %get-tuple-element.72), channel_id=1, source_target_pairs={{0,4},{4,0},{8,12},{12,8},{16,20},{20,16},{24,28},{28,24},{1,5},{5... | collective-permute-start | bytes 2457608 | tf_op jit(solution)/shard_map/ppermute | solution.py:70
  63.7 2.5 %collective-permute-start.17 = (bf16[4,160,640]{2,1,0:T(8,128)(2,1)S(1)}, bf16[4,160,640]{2,1,0:T(8,128)(2,1)S(1)}, u32[]{:S(2)}, u32[]{:S(2)}) collective-permute-start(bf16[4,160,640]{2,1,0:T(8,128)(2,1)S(1)} %get-tuple-element.83), channel_id=1, source_target_pairs={{0,4},{4,0},{8,12},{12,8},{16,20},{20,16},{24,28},{28,24},{1,5},{5... | collective-permute-start | bytes 2457608 | tf_op jit(solution)/shard_map/ppermute | solution.py:70
  67.0 20.5 %collective-permute-start.18 = (bf16[2,160,640]{2,1,0:T(8,128)(2,1)S(1)}, bf16[2,160,640]{2,1,0:T(8,128)(2,1)S(1)}, u32[]{:S(2)}, u32[]{:S(2)}) collective-permute-start(bf16[2,160,640]{2,1,0:T(8,128)(2,1)S(1)} %get-tuple-element.85), channel_id=1, source_target_pairs={{0,8},{4,12},{8,0},{12,4},{16,24},{20,28},{24,16},{28,20},{1,9},{5... | collective-permute-start | bytes 1228808 | tf_op jit(solution)/shard_map/ppermute | solution.py:70
  68.6 17.0 %collective-permute-start.14 = (bf16[320,320]{1,0:T(8,128)(2,1)S(1)}, bf16[320,320]{1,0:T(8,128)(2,1)S(1)}, u32[]{:S(2)}, u32[]{:S(2)}) collective-permute-start(bf16[320,320]{1,0:T(8,128)(2,1)S(1)} %get-tuple-element.77), channel_id=1, source_target_pairs={{0,1},{1,0},{2,3},{3,2},{4,5},{5,4},{6,7},{7,6},{8,9},{9,8},{10,11... | collective-permute-start | bytes 614408 | tf_op jit(solution)/shard_map/ppermute | solution.py:66
  69.6 16.1 %collective-permute-start.15 = (bf16[320,320]{1,0:T(8,128)(2,1)S(1)}, bf16[320,320]{1,0:T(8,128)(2,1)S(1)}, u32[]{:S(2)}, u32[]{:S(2)}) collective-permute-start(bf16[320,320]{1,0:T(8,128)(2,1)S(1)} %get-tuple-element.78), channel_id=1, source_target_pairs={{0,2},{1,3},{2,0},{3,1},{4,6},{5,7},{6,4},{7,5},{8,10},{9,11},{10,... | collective-permute-start | bytes 614408 | tf_op jit(solution)/shard_map/ppermute | solution.py:66
  70.9 14.7 %collective-permute-start.16 = (bf16[320,320]{1,0:T(8,128)(2,1)S(1)}, bf16[320,320]{1,0:T(8,128)(2,1)S(1)}, u32[]{:S(2)}, u32[]{:S(2)}) collective-permute-start(bf16[320,320]{1,0:T(8,128)(2,1)S(1)} %get-tuple-element.79), channel_id=1, source_target_pairs={{0,3},{1,2},{2,1},{3,0},{4,7},{5,6},{6,5},{7,4},{8,11},{9,10},{10,... | collective-permute-start | bytes 614408 | tf_op jit(solution)/shard_map/ppermute | solution.py:66
  76.6 1.2 collective-permute-start.11
  77.9 4.1 %collective-permute-start.12 = (f32[1,1280]{1,0:T(1,128)S(1)}, f32[1,1280]{1,0:T(1,128)S(1)}, u32[]{:S(2)}, u32[]{:S(2)}) collective-permute-start(f32[1,1280]{1,0:T(1,128)S(1)} %add.12), channel_id=1, source_target_pairs={{0,1},{1,0},{2,3},{3,2},{4,5},{5,4},{6,7},{7,6},{8,9},{9,8},{10,11... | collective-permute-start | bytes 15368 | tf_op jit(solution)/shard_map/ppermute | solution.py:66
  82.0 3.7 %collective-permute-start.13 = (f32[1,1280]{1,0:T(1,128)S(1)}, f32[1,1280]{1,0:T(1,128)S(1)}, u32[]{:S(2)}, u32[]{:S(2)}) collective-permute-start(f32[1,1280]{1,0:T(1,128)S(1)} %add.13.term_ref), channel_id=1, source_target_pairs={{0,2},{1,3},{2,0},{3,1},{4,6},{5,7},{6,4},{7,5},{8,10},{9,11},{10,... | collective-permute-start | bytes 15368 | tf_op jit(solution)/shard_map/ppermute | solution.py:66
  87.5 0.8 copy-start.14
  88.3 8.4 %copy-start.5 = (bf16[1,128,1280]{2,1,0:T(8,128)(2,1)S(1)}, bf16[1,128,1280]{2,1,0:T(8,128)(2,1)}, u32[]{:S(2)}) copy-start(bf16[1,128,1280]{2,1,0:T(8,128)(2,1)} %param.13) | copy-start | bytes 983044
  88.3 8.4 %copy-start.7 = (bf16[1,128,1280]{2,1,0:T(8,128)(2,1)S(1)}, bf16[1,128,1280]{2,1,0:T(8,128)(2,1)}, u32[]{:S(2)}) copy-start(bf16[1,128,1280]{2,1,0:T(8,128)(2,1)} %param.10) | copy-start | bytes 983044
  88.3 18.9 %all-to-all-start.1 = ((bf16[4,128,1280]{2,1,0:T(8,128)(2,1)}), bf16[4,128,1280]{2,1,0:T(8,128)(2,1)S(1)}, u32[]{:S(2)}, u32[]{:S(2)}) async-start(bf16[4,128,1280]{2,1,0:T(8,128)(2,1)} %get-tuple-element.87), calls=%async_computation.1 | async-start | bytes 2621440 | tf_op jit(solution)/shard_map/all_to_all | solution.py:710
  92.8 12.8 %collective-permute-start.19 = (bf16[160,640]{1,0:T(8,128)(2,1)}, bf16[160,640]{1,0:T(8,128)(2,1)S(1)}, u32[]{:S(2)}, u32[]{:S(2)}) collective-permute-start(bf16[160,640]{1,0:T(8,128)(2,1)} %get-tuple-element.86), channel_id=1, source_target_pairs={{0,16},{4,20},{8,24},{12,28},{16,0},{20,4},{24,8},{28,12},{1,17},{... | collective-permute-start | bytes 614408 | tf_op jit(solution)/shard_map/ppermute | solution.py:70
  93.2 24.8 %collective-permute-start.20 = (bf16[336,320]{1,0:T(8,128)(2,1)}, bf16[336,320]{1,0:T(8,128)(2,1)S(1)}, u32[]{:S(2)}, u32[]{:S(2)}) collective-permute-start(bf16[336,320]{1,0:T(8,128)(2,1)} %get-tuple-element.100), channel_id=1, source_target_pairs={{0,8},{4,12},{8,0},{12,4},{16,24},{20,28},{24,16},{28,20},{1,9},{5... | collective-permute-start | bytes 645128 | tf_op jit(solution)/shard_map/ppermute | solution.py:70
  93.6 24.3 %collective-permute-start.21 = (bf16[336,320]{1,0:T(8,128)(2,1)}, bf16[336,320]{1,0:T(8,128)(2,1)S(1)}, u32[]{:S(2)}, u32[]{:S(2)}) collective-permute-start(bf16[336,320]{1,0:T(8,128)(2,1)} %get-tuple-element.101), channel_id=1, source_target_pairs={{0,16},{4,20},{8,24},{12,28},{16,0},{20,4},{24,8},{28,12},{1,17},{... | collective-permute-start | bytes 645128 | tf_op jit(solution)/shard_map/ppermute | solution.py:70
  96.2 28.1 %collective-permute-start.22 = (bf16[336,320]{1,0:T(8,128)(2,1)}, bf16[336,320]{1,0:T(8,128)(2,1)S(1)}, u32[]{:S(2)}, u32[]{:S(2)}) collective-permute-start(bf16[336,320]{1,0:T(8,128)(2,1)} %copy-done.14), channel_id=1, source_target_pairs={{0,24},{4,28},{8,16},{12,20},{16,8},{20,12},{24,0},{28,4},{1,25},{... | collective-permute-start | bytes 645128 | tf_op jit(solution)/shard_map/ppermute | solution.py:70
  96.7 1.0 copy-start.9
  97.6 1.0 copy-start.12
  102.4 1.0 copy-start.16
  103.4 0.8 copy-start.18
  104.2 0.7 copy-start.20
  104.9 0.6 copy-start.22
  107.2 1.0 copy-start.10
  108.2 1.0 copy-start.13
  109.2 1.2 copy-start.17
  110.4 1.1 copy-start.19
  111.5 1.0 copy-start.21
  112.4 0.8 copy-start.23

commit v6 on v5

--- a/solution.py
+++ b/solution.py
@@ -14,9 +14,10 @@
 CORES = 2
 LANES = 128
 VMEM_BYTES = 16 * 1024 * 1024
-
-
-def vmem_call(body, out_shape, in_spaces, flops):
+MOST_BYTES = 60 * 1024 * 1024
+
+
+def vmem_call(body, out_shape, in_spaces, flops, late=(), limit=VMEM_BYTES):
     def run(*operands):
         places = [i for i, space in enumerate(in_spaces) if space == pl.ANY]
         outs = len(jax.tree.leaves(out_shape))
@@ -30,11 +31,12 @@
             ]
             for copy in copies:
                 copy.start()
-            for copy in copies:
-                copy.wait()
             for n, i in enumerate(places):
                 ins[i] = held[n]
-            body(*ins, *rest[:outs])
+                if i not in late:
+                    copies[n].wait()
+            waits = [copies[places.index(i)].wait for i in late]
+            body(*waits, *ins, *rest[:outs])
 
         return pl.pallas_call(
             kernel if places else body,
@@ -43,7 +45,7 @@
             out_specs=jax.tree.map(lambda _: pl.BlockSpec(memory_space=pltpu.VMEM), out_shape),
             scratch_shapes=[pltpu.VMEM(operands[i].shape, operands[i].dtype) for i in places]
             + [pltpu.SemaphoreType.DMA for _ in places],
-            compiler_params=pltpu.CompilerParams(vmem_limit_bytes=VMEM_BYTES),
+            compiler_params=pltpu.CompilerParams(vmem_limit_bytes=limit),
             cost_estimate=pl.CostEstimate(
                 flops=flops, bytes_accessed=4 << 20, transcendentals=0
             ),
@@ -228,6 +230,11 @@
 
 
 def backward_kernel(
+    wait_probs,
+    wait_out,
+    wait_q,
+    wait_k,
+    wait_v,
     got_ref,
     rows_ref,
     unit_ref,
@@ -254,6 +261,8 @@
         - unit * jnp.mean(d_unit * unit, axis=1, keepdims=True)
     )
     gr_ref[...] = (rows_ref[...].astype(jnp.float32) + d_hidden).astype(jnp.bfloat16)
+    for wait in (wait_probs, wait_out, wait_q, wait_k, wait_v):
+        wait()
     totals = ({}, {}, {})
     for head in range(HEADS):
         start, stop = span_of(head)
@@ -279,8 +288,10 @@
     return vmem_call(
         backward_kernel,
         tuple(jax.ShapeDtypeStruct((tokens, feat), jnp.bfloat16) for _ in range(4)),
-        [pltpu.VMEM] * 10,
+        [pl.ANY] * 10,
         1 << 32,
+        late=(5, 6, 7, 8, 9),
+        limit=MOST_BYTES,
     )(*operands)
 
 
@@ -352,12 +363,28 @@
         ref[half:, :] = gain
 
 
-def fetch_up(place, w_up, norm_gain, n_dp):
+def send_first(place, slot_ids, llm_rows, w_up, norm_gain, n_seq, n_dp, tokens):
     rows, ff = w_up.shape
+    per_owner = tokens // PIECE
+    capacity = 1 + (per_owner + n_seq - 2) // n_seq
     piece = jax.ShapeDtypeStruct((rows // CORES + PIECE, ff // n_dp), jnp.bfloat16)
-    return vmem_call(
-        fetch_kernel, (piece,) * n_dp, [pltpu.SMEM, pltpu.VMEM, pltpu.VMEM], 1 << 20
-    )(place, w_up, norm_gain[None])
+    tiles = jax.ShapeDtypeStruct(
+        (n_seq, capacity * PIECE, llm_rows.shape[1] + LANES), jnp.bfloat16
+    )
+
+    def body(wait_up, place_ref, slot_ref, gain_ref, rows_ref, up_ref, tiles_ref, *piece_refs):
+        send_kernel(n_seq, capacity, per_owner, slot_ref, rows_ref, tiles_ref)
+        wait_up()
+        fetch_kernel(place_ref, up_ref, gain_ref, *piece_refs)
+
+    return vmem_call(
+        body,
+        (tiles,) + (piece,) * n_dp,
+        [pltpu.SMEM, pltpu.SMEM, pltpu.VMEM, pl.ANY, pl.ANY],
+        1 << 20,
+        late=(4,),
+        limit=MOST_BYTES,
+    )(place, slot_ids, norm_gain[None], llm_rows, w_up)
 
 
 def join_kernel(place_ref, mine_ref, mate_ref, up_ref, gain_ref):
@@ -480,7 +507,7 @@
     return vmem_call(
         up_kernel,
         (jax.ShapeDtypeStruct((total, cols), jnp.bfloat16), piece, piece),
-        [pltpu.SMEM] + [pl.ANY] * 4,
+        [pltpu.SMEM] + [pltpu.VMEM] * 4,
         4 * total * feat * cols,
     )(place, rows_all, w_down, slope, normed_flip)
 
@@ -505,9 +532,18 @@
             jax.ShapeDtypeStruct((n_dp, tokens, feat), jnp.bfloat16),
             jax.ShapeDtypeStruct((1, feat), jnp.float32),
         ),
-        [pltpu.SMEM] + [pl.ANY] * (2 + n_dp),
+        [pltpu.SMEM] + [pltpu.VMEM] * (2 + n_dp),
         2 * n_dp * tokens * feat * d_pre.shape[1],
     )(place, d_pre, up_cols, *unit_blocks)
+
+
+def copy_kernel(in_ref, out_ref):
+    out_ref[...] = in_ref[...]
+
+
+def again(value):
+    shape = jax.ShapeDtypeStruct(value.shape, value.dtype)
+    return vmem_call(copy_kernel, shape, [pltpu.VMEM], 1 << 20)(value)
 
 
 def wide_sum(*terms):
@@ -545,18 +581,36 @@
 
 
 def rise_kernel(place_ref, term_ref, other_ref, *refs):
-    count = len(refs) // 2
-    got_refs, out_refs = refs[:count], refs[count:]
+    *got_refs, keep_ref, give_ref, sum_ref = refs
     half, width = got_refs[0].shape
-    rows = to_rows(term_ref[...] + other_ref[...], width)
-    for k, ref in enumerate(out_refs):
+    for k in range(len(got_refs)):
+        ref = (keep_ref, give_ref)[k % 2]
+        at = k // 2 * half
         for step, got_ref in enumerate(got_refs):
 
             @pl.when((place_ref[2] ^ k) == (place_ref[0] ^ step))
-            def _(ref=ref, got_ref=got_ref):
-                ref[:half, :] = got_ref[...]
-
-        ref[half:, :] = rows
+            def _(ref=ref, at=at, got_ref=got_ref):
+                ref[at : at + half, :] = got_ref[...]
+
+    total = term_ref[...] + other_ref[...]
+    sum_ref[...] = total
+    give_ref[2 * half :, :] = to_rows(total, width)
+
+
+def from_rows(rows, count):
+    rows = rows.astype(jnp.float32)
+    rows = rows[:count] + rows[count : 2 * count]
+    return jnp.concatenate([rows[i : i + 1] for i in range(count)], axis=1)
+
+
+def climb_kernel(keep_ref, got_ref, term_ref, own_ref, give_ref, sum_ref):
+    half, width = own_ref.shape
+    own_ref[...] = wide_sum(keep_ref[:half, :], got_ref[:half, :]).astype(jnp.bfloat16)
+    give = wide_sum(keep_ref[half:, :], got_ref[half : 2 * half, :])
+    give_ref[:half, :] = give.astype(jnp.bfloat16)
+    total = term_ref[...] + from_rows(got_ref[2 * half :, :], term_ref.shape[1] // width)
+    sum_ref[...] = total
+    give_ref[half:, :] = to_rows(total, width)
 
 
 def total_kernel(factor, *refs):
@@ -564,14 +618,11 @@
     out_ref[...] = (wide_sum(*(ref[...] for ref in in_refs)) * factor).astype(jnp.bfloat16)
 
 
-def last_kernel(factor, *refs):
-    *in_refs, down_ref, gain_ref = refs
-    half = down_ref.shape[0]
-    count = len(in_refs)
-    down_ref[...] = (wide_sum(*(ref[:half, :] for ref in in_refs)) * factor).astype(jnp.bfloat16)
-    rows = wide_sum(*(ref[half:, :] for ref in in_refs))
-    rows = (rows[:count] + rows[count : 2 * count]) * factor
-    gain_ref[...] = jnp.concatenate([rows[i : i + 1] for i in range(count)], axis=1)
+def last_kernel(factor, own_ref, got_ref, term_ref, down_ref, gain_ref):
+    half, width = own_ref.shape
+    down_ref[...] = (wide_sum(own_ref[...], got_ref[:half, :]) * factor).astype(jnp.bfloat16)
+    rest = from_rows(got_ref[half:, :], term_ref.shape[1] // width)
+    gain_ref[...] = (term_ref[...] + rest) * factor
 
 
 def up_sides(place, keep, mate):
@@ -583,7 +634,7 @@
 
 def up_middle(keep, got):
     piece = jax.ShapeDtypeStruct(keep.shape[1:], jnp.bfloat16)
-    return vmem_call(middle_kernel, (piece, piece), [pltpu.VMEM] * 2, 1 << 20)(keep, got)
+    return vmem_call(middle_kernel, (piece, piece), [pltpu.VMEM] * 2, 1 << 37)(keep, got)
 
 
 def up_total(keep, got, factor):
@@ -602,26 +653,44 @@
 
 
 def down_rise(place, term, other, planes):
-    count = len(planes)
     half, width = planes[0].shape
-    piece = jax.ShapeDtypeStruct((half + PIECE, width), jnp.bfloat16)
-    return vmem_call(
-        rise_kernel, (piece,) * count, [pltpu.SMEM] + [pltpu.VMEM] * (2 + count), 1 << 20
+    return vmem_call(
+        rise_kernel,
+        (
+            jax.ShapeDtypeStruct((2 * half, width), jnp.bfloat16),
+            jax.ShapeDtypeStruct((2 * half + PIECE, width), jnp.bfloat16),
+            jax.ShapeDtypeStruct(term.shape, jnp.float32),
+        ),
+        [pltpu.SMEM] + [pltpu.VMEM] * (2 + len(planes)),
+        1 << 20,
     )(place, term, other, *planes)
 
 
-def down_total(pieces, factor):
-    rows, width = pieces[0].shape
+def down_climb(keep, got, term):
+    half, width = keep.shape[0] // 2, keep.shape[1]
+    return vmem_call(
+        climb_kernel,
+        (
+            jax.ShapeDtypeStruct((half, width), jnp.bfloat16),
+            jax.ShapeDtypeStruct((half + PIECE, width), jnp.bfloat16),
+            jax.ShapeDtypeStruct(term.shape, jnp.float32),
+        ),
+        [pltpu.VMEM] * 3,
+        1 << 35,
+    )(keep, got, term)
+
+
+def down_total(own, got, term, factor):
     down, gain = vmem_call(
         lambda *refs: last_kernel(factor, *refs),
         (
-            jax.ShapeDtypeStruct((rows - PIECE, width), jnp.bfloat16),
-            jax.ShapeDtypeStruct((1, width * len(pieces)), jnp.float32),
+            jax.ShapeDtypeStruct(own.shape, jnp.bfloat16),
+            jax.ShapeDtypeStruct(term.shape, jnp.float32),
         ),
-        [pltpu.VMEM] * len(pieces),
+        [pltpu.VMEM] * 3,
         1 << 20,
-    )(*pieces)
-    return down, gain[0]
+    )(own, got, term)
+    return down, gain.reshape(-1)
 
 
 def after(value, *others):
@@ -669,17 +738,20 @@
     def all_dp(block):
         return [block] + [swap_dp(block, n_dp, k) for k in range(1, n_dp)]
 
-    sent = send_tiles(llm_grad[0], vision_slot, n_seq, tokens)
-    landing = lax.all_to_all(sent, "seq", split_axis=0, concat_axis=0, tiled=True)
     attention = (queries[0], key_rows[0], value_rows[0], resid_in[0])
     if quick:
+        sent, own, *others = send_first(
+            place, vision_slot, llm_grad[0], w_up, norm_gain, n_seq, n_dp, tokens
+        )
+        landing = lax.all_to_all(sent, "seq", split_axis=0, concat_axis=0, tiled=True)
         _, unit_low = forward(window_mask[0], *attention, 1 << 31, False)
         unit_blocks = all_dp(unit_low)
-        own, *others = fetch_up(place, after(w_up, sent), norm_gain, n_dp)
         mine = jnp.stack([own] + [swap_dp(block, n_dp, k + 1) for k, block in enumerate(others)])
         up_cols, gain_row = join_columns(place, mine, swap_seq(mine, n_seq, 1))
         landing = after(landing, up_cols)
     else:
+        sent = send_tiles(llm_grad[0], vision_slot, n_seq, tokens)
+        landing = lax.all_to_all(sent, "seq", split_axis=0, concat_axis=0, tiled=True)
         gain_row = gather_gain(norm_gain, n_dp, dp).astype(jnp.float32)[None]
         own, mine, mate = fetch_pieces(w_up, n_dp, n_seq, dp, core)
         saved = forward(window_mask[0], *attention, 1 << 31, True)
@@ -701,20 +773,19 @@
         up_keep, up_give = up_sides(place, after(up_keep, own), up_mate)
         up_got = swap_seq(up_give, n_seq, CORES)
         term = term + swap_dp(term, n_dp, 1)
-        own, *sends = down_rise(place, term, swap_dp(term, n_dp, 2), planes)
-        pieces = [own] + [
-            swap_seq(block, n_seq, CORES * (k + 1)) for k, block in enumerate(sends)
-        ]
+        down_keep, down_give, term = down_rise(place, term, swap_dp(term, n_dp, 2), planes)
+        down_got = swap_seq(down_give, n_seq, CORES)
         up_keep, up_give = up_middle(up_keep, up_got)
         up_got = swap_seq(up_give, n_seq, 2 * CORES)
         d_got = lax.all_to_all(
-            after(parts, own, up_give), "dp", split_axis=0, concat_axis=0, tiled=True
+            (after(parts, *planes, up_give)), "dp", split_axis=0, concat_axis=0, tiled=True
         )
-        saved = forward(after(window_mask[0], own), *attention, 1 << 31, True)
-        grads = backward_pass(after(d_got, up_got), saved)
-        pieces[0] = after(pieces[0], grads[3])
-        grad_up = up_total(up_keep, up_got, factor)
-        grad_down, grad_gain = down_total(pieces, factor)
+        own, down_give, term = down_climb(down_keep, down_got, term)
+        down_got = swap_seq(down_give, n_seq, 2 * CORES)
+        saved = forward(after(window_mask[0], up_give), *attention, 1 << 31, True)
+        grads = backward_pass(d_got, saved)
+        grad_up = up_total(after(up_keep, own), up_got, factor)
+        grad_down, grad_gain = down_total(after(own, grads[3]), down_got, term, factor)
     else:
         normed_all = jnp.concatenate(normed_blocks, axis=0)
         rows_all = jnp.concatenate(rows_blocks, axis=0)

time: 127 us -> 117 us (0.921)
  the two profiles are of different devices: /device:TPU:18 before, /device:TPU:0 now
where the time goes in v6:
time: 117 us
  waiting for transfers between devices  44.1 us (38%)
  Pallas kernels  35.3 us (30%)
  starting transfers between devices  33.7 us (29%)
  other arithmetic  1.36 us (1%)
  local copies, waits for them, and re-layouts  1.33 us (1%)
    pallas_call x17, Pallas kernels, run(): pl.pallas_call(kernel if places else body, out_shape=out_shape, in_specs=...  35.3 us
    ppermute x14, waiting for transfers between devices, swap_dp(): return lax.ppermute(block, 'dp', [(i, i ^ step) for i in range(count)])  27.3 us
    ppermute x14, starting transfers between devices, swap_dp(): return lax.ppermute(block, 'dp', [(i, i ^ step) for i in range(count)])  17.6 us
    ppermute x8, waiting for transfers between devices, swap_seq(): return lax.ppermute(block, 'seq', [(i, i ^ step) for i in range(count)])  6.82 us
    ppermute x8, starting transfers between devices, swap_seq(): return lax.ppermute(block, 'seq', [(i, i ^ step) for i in range(count)])  6.12 us
    all_to_all x1, starting transfers between devices, per_device(): lax.all_to_all(sent, 'seq', split_axis=0, concat_axis=0, tiled=True)  5.48 us
    all_to_all x1, waiting for transfers between devices, per_device(): lax.all_to_all(sent, 'seq', split_axis=0, concat_axis=0, tiled=True)  5.39 us
    all_to_all x1, waiting for transfers between devices, per_device(): lax.all_to_all(after(parts, *planes, up_give), 'dp', split_axis=0, concat...  4.59 us
  transfers between devices with their start and end apart: 24, of which 14 were waited for; matrix products, arithmetic and copies ran while one was open for 0% of the time, Pallas kernels for 24%

profile of v6, /device:TPU:0, one launch (start us, length us, event | category | flops | bytes accessed | tf_op | source)
XLA Modules:
  0.0 116.8 jit_solution(1955015242403401583)
XLA Ops:
  0.6 1.2 %broadcast_in_dim.15.refs_2_ = bf16[1,320]{1,0:T(2,128)(2,1)} reshape(bf16[320]{0:T(512)(128)(2,1)} %param.19) | data formatting | bytes 1280 | tf_op jit(solution)/shard_map/broadcast_in_dim | solution.py:387
  1.9 0.6 pad_add_fusion.refs_0_.place_ref
  2.5 3.5 %shard_map.153 = (bf16[8,32,1408]{2,1,0:T(8,128)(2,1)}, bf16[176,640]{1,0:T(8,128)(2,1)}, bf16[176,640]{1,0:T(8,128)(2,1)}, bf16[176,640]{1,0:T(8,128)(2,1)}, bf16[176,640]{1,0:T(8,128)(2,1)}) custom-call(s32[3]{0:T(128)} %pad_add_fusion.refs_0_.place_ref, s32[1,192]{1,0:T(1,128)} %refs_1_.1, bf16[1,320]{1,0:T(2,128)(2,1)} %broadcast_in_dim.15.refs_2_, ...), custom_call_target="tpu_custom_call" | custom-call | flops 1048576 | bytes 4194304 | tf_op jit(solution)/shard_map/pallas_call | solution.py:41
  6.0 0.0 copy-start.17
  6.0 3.0 %collective-permute-start = (bf16[176,640]{1,0:T(8,128)(2,1)}, bf16[176,640]{1,0:T(8,128)(2,1)S(1)}, u32[]{:S(2)}, u32[]{:S(2)}) collective-permute-start(bf16[176,640]{1,0:T(8,128)(2,1)} %get-tuple-element.59), channel_id=1, source_target_pairs={{0,1},{1,0},{2,3},{3,2},{4,5},{5,4},{6,7},{7,6},{8,9},{9,8},{10,11... | collective-permute-start | bytes 675848 | tf_op jit(solution)/shard_map/ppermute | solution.py:68
  9.0 1.5 %collective-permute-start.1 = (bf16[176,640]{1,0:T(8,128)(2,1)}, bf16[176,640]{1,0:T(8,128)(2,1)S(1)}, u32[]{:S(2)}, u32[]{:S(2)}) collective-permute-start(bf16[176,640]{1,0:T(8,128)(2,1)} %get-tuple-element.60), channel_id=1, source_target_pairs={{0,2},{1,3},{2,0},{3,1},{4,6},{5,7},{6,4},{7,5},{8,10},{9,11},{10,... | collective-permute-start | bytes 675848 | tf_op jit(solution)/shard_map/ppermute | solution.py:68
  10.5 0.0 collective-permute-start.2
  10.6 0.0 copy-start.12
  10.6 5.5 %all-to-all-start = ((bf16[8,32,1408]{2,1,0:T(8,128)(2,1)}), bf16[8,32,1408]{2,1,0:T(8,128)(2,1)S(1)}, u32[]{:S(2)}, u32[]{:S(2)}) async-start(bf16[8,32,1408]{2,1,0:T(8,128)(2,1)} %get-tuple-element.66), calls=%async_computation | async-start | bytes 1441792 | tf_op jit(solution)/shard_map/all_to_all | solution.py:746
  16.1 0.0 collective-permute-done
  16.1 5.0 %collective-permute-done.1 = bf16[176,640]{1,0:T(8,128)(2,1)S(1)} collective-permute-done((bf16[176,640]{1,0:T(8,128)(2,1)}, bf16[176,640]{1,0:T(8,128)(2,1)S(1)}, u32[]{:S(2)}, u32[]{:S(2)}) %collective-permute-start.1) | collective-permute-done | bytes 225312 | tf_op jit(solution)/shard_map/ppermute | solution.py:68
  21.0 0.1 pad_maximum_fusion.refs_1_
  21.2 0.1 collective-permute-start.3
  21.3 0.0 copy-start.1
  21.3 4.3 %shard_map.155 = (bf16[128,1280]{1,0:T(8,128)(2,1)}, bf16[128,1280]{1,0:T(8,128)(2,1)S(1)}) custom-call(s32[2,2]{1,0:T(2,128)S(1)} %bitcast.30, bf16[128,1280]{1,0:T(8,128)(2,1)S(1)} %bitcast.22, bf16[128,1280]{1,0:T(8,128)(2,1)S(1)} %bitcast.25, bf16[128,1280]{1,0:T(8,128)(2,1)S(1)} %bitcast.28, bf16[128,1280]{1,0:T(8,128)(2,1)S(1)} %bitcast.19), custom_call_target="tpu_custom_call" | custom-call | flops 2147483648 | bytes 4194304 | tf_op jit(solution)/shard_map/pallas_call | solution.py:41
  25.6 1.5 %collective-permute-start.6 = (bf16[128,1280]{1,0:T(8,128)(2,1)S(1)}, bf16[128,1280]{1,0:T(8,128)(2,1)S(1)}, u32[]{:S(2)}, u32[]{:S(2)}) collective-permute-start(bf16[128,1280]{1,0:T(8,128)(2,1)S(1)} %get-tuple-element.64.refs_0_), channel_id=1, source_target_pairs={{0,3},{1,2},{2,1},{3,0},{4,7},{5,6},{6,5},{7,4},{8,11},{9,10},{10,... | collective-permute-start | bytes 983048 | tf_op jit(solution)/shard_map/ppermute | solution.py:68
  27.1 1.2 %collective-permute-start.5 = (bf16[128,1280]{1,0:T(8,128)(2,1)S(1)}, bf16[128,1280]{1,0:T(8,128)(2,1)S(1)}, u32[]{:S(2)}, u32[]{:S(2)}) collective-permute-start(bf16[128,1280]{1,0:T(8,128)(2,1)S(1)} %get-tuple-element.64.refs_0_), channel_id=1, source_target_pairs={{0,2},{1,3},{2,0},{3,1},{4,6},{5,7},{6,4},{7,5},{8,10},{9,11},{10,... | collective-permute-start | bytes 983048 | tf_op jit(solution)/shard_map/ppermute | solution.py:68
  28.3 0.8 collective-permute-start.4
  29.1 1.1 shard_map.154
  30.2 0.0 copy-start.11
  30.2 5.4 %all-to-all-done = bf16[8,32,1408]{2,1,0:T(8,128)(2,1)S(1)} async-done(((bf16[8,32,1408]{2,1,0:T(8,128)(2,1)}), bf16[8,32,1408]{2,1,0:T(8,128)(2,1)S(1)}, u32[]{:S(2)}, u32[]{:S(2)}) %all-to-all-start) | async-done | bytes 720928 | tf_op jit(solution)/shard_map/all_to_all | solution.py:746
  35.6 0.3 shard_map.157.refs_0_.refs_1_
  35.9 2.5 %collective-permute-start.9 = (bf16[128,1280]{1,0:T(8,128)(2,1)S(1)}, bf16[128,1280]{1,0:T(8,128)(2,1)S(1)}, u32[]{:S(2)}, u32[]{:S(2)}) collective-permute-start(bf16[128,1280]{1,0:T(8,128)(2,1)S(1)} %shard_map.157.refs_0_.refs_1_), channel_id=1, source_target_pairs={{0,3},{1,2},{2,1},{3,0},{4,7},{5,6},{6,5},{7,4},{8,11},{9,10},{10,... | collective-permute-start | bytes 983048 | tf_op jit(solution)/shard_map/ppermute | solution.py:68
  38.5 0.5 collective-permute-start.8
  39.0 0.5 collective-permute-start.7
  39.5 4.6 %collective-permute-done.5.refs_2_ = bf16[128,1280]{1,0:T(8,128)(2,1)S(1)} collective-permute-done((bf16[128,1280]{1,0:T(8,128)(2,1)S(1)}, bf16[128,1280]{1,0:T(8,128)(2,1)S(1)}, u32[]{:S(2)}, u32[]{:S(2)}) %collective-permute-start.5) | collective-permute-done | bytes 327712 | tf_op jit(solution)/shard_map/ppermute | solution.py:68
  44.1 0.1 collective-permute-done.4.refs_1_
  44.3 2.5 %shard_map.156 = (bf16[640,512]{1,0:T(8,128)(2,1)S(1)}, f32[512,640]{1,0:T(8,128)S(1)}, bf16[1280,512]{1,0:T(8,128)(2,1)S(1)}, bf16[512,1280]{1,0:T(8,128)(2,1)}) custom-call(bf16[1280,640]{1,0:T(8,128)(2,1)S(1)} %get-tuple-element.62.up_ref, f32[1,1280]{1,0:T(1,128)S(1)} %get-tuple-element.63.gain_ref.refs_4_, ...), custom_call_target="tpu_custom_call" | custom-call | flops 838860800 | bytes 4194304 | tf_op jit(solution)/shard_map/pallas_call | solution.py:41
  46.8 4.4 %collective-permute-done.9.refs_3_ = bf16[128,1280]{1,0:T(8,128)(2,1)S(1)} collective-permute-done((bf16[128,1280]{1,0:T(8,128)(2,1)S(1)}, bf16[128,1280]{1,0:T(8,128)(2,1)S(1)}, u32[]{:S(2)}, u32[]{:S(2)}) %collective-permute-start.9) | collective-permute-done | bytes 327712 | tf_op jit(solution)/shard_map/ppermute | solution.py:68
  51.2 6.5 %collective-permute-done.8.refs_2_ = bf16[128,1280]{1,0:T(8,128)(2,1)S(1)} collective-permute-done((bf16[128,1280]{1,0:T(8,128)(2,1)S(1)}, bf16[128,1280]{1,0:T(8,128)(2,1)S(1)}, u32[]{:S(2)}, u32[]{:S(2)}) %collective-permute-start.8) | collective-permute-done | bytes 327712 | tf_op jit(solution)/shard_map/ppermute | solution.py:68
  57.7 0.2 collective-permute-done.7.refs_1_
  57.8 2.3 %shard_map.158 = (bf16[512,1280]{1,0:T(8,128)(2,1)S(1)}, bf16[4,320,320]{2,1,0:T(8,128)(2,1)S(1)}, bf16[4,320,320]{2,1,0:T(8,128)(2,1)S(1)}) custom-call(s32[3]{0:T(128)S(1)} %copy-done.1, bf16[640,512]{1,0:T(8,128)(2,1)S(1)} %get-tuple-element.65.act_ref, bf16[128,1280]{1,0:T(8,128)(2,1)S(1)} %shard_map.157.refs_0_.refs_1_, ...), custom_call_target="tpu_custom_call" | custom-call | flops 838860800 | bytes 4194304 | tf_op jit(solution)/shard_map/pallas_call | solution.py:41
  60.2 0.1 collective-permute-start.10
  60.3 3.1 %shard_map.159 = (bf16[512,640]{1,0:T(8,128)(2,1)S(1)}, bf16[4,160,640]{2,1,0:T(8,128)(2,1)S(1)}, bf16[4,160,640]{2,1,0:T(8,128)(2,1)S(1)}) custom-call(s32[3]{0:T(128)S(1)} %copy-done.1, bf16[512,1280]{1,0:T(8,128)(2,1)S(1)} %get-tuple-element.68.rows_ref, bf16[640,1280]{1,0:T(8,128)(2,1)S(1)} %copy-done.2, f32[512,640]{1,0:T(8,128)S(1)} %get-tuple-element.69.slope_ref, ...), custom_call_target="tpu_custom_call" | custom-call | flops 1677721600 | bytes 4194304 | tf_op jit(solution)/shard_map/pallas_call | solution.py:41
  63.3 0.6 collective-permute-start.14
  63.9 0.8 shard_map.160
  64.7 1.2 %collective-permute-done.14.mate_ref = bf16[4,160,640]{2,1,0:T(8,128)(2,1)S(1)} collective-permute-done((bf16[4,160,640]{2,1,0:T(8,128)(2,1)S(1)}, bf16[4,160,640]{2,1,0:T(8,128)(2,1)S(1)}, u32[]{:S(2)}, u32[]{:S(2)}) %collective-permute-start.14) | collective-permute-done | bytes 819232 | tf_op jit(solution)/shard_map/ppermute | solution.py:72
  65.9 0.7 shard_map.162
  66.6 1.7 %collective-permute-start.15 = (bf16[2,160,640]{2,1,0:T(8,128)(2,1)S(1)}, bf16[2,160,640]{2,1,0:T(8,128)(2,1)S(1)}, u32[]{:S(2)}, u32[]{:S(2)}) collective-permute-start(bf16[2,160,640]{2,1,0:T(8,128)(2,1)S(1)} %get-tuple-element.85), channel_id=1, source_target_pairs={{0,8},{4,12},{8,0},{12,4},{16,24},{20,28},{24,16},{28,20},{1,9},{5... | collective-permute-start | bytes 1228808 | tf_op jit(solution)/shard_map/ppermute | solution.py:72
  68.3 1.1 collective-permute-start.11
  69.3 0.8 collective-permute-start.12
  70.2 1.6 %collective-permute-start.13 = (bf16[320,320]{1,0:T(8,128)(2,1)S(1)}, bf16[320,320]{1,0:T(8,128)(2,1)S(1)}, u32[]{:S(2)}, u32[]{:S(2)}) collective-permute-start(bf16[320,320]{1,0:T(8,128)(2,1)S(1)} %get-tuple-element.80), channel_id=1, source_target_pairs={{0,3},{1,2},{2,1},{3,0},{4,7},{5,6},{6,5},{7,4},{8,11},{9,10},{10,... | collective-permute-start | bytes 614408 | tf_op jit(solution)/shard_map/ppermute | solution.py:68
  71.7 3.3 %shard_map.161 = (bf16[4,128,1280]{2,1,0:T(8,128)(2,1)}, f32[1,1280]{1,0:T(1,128)S(1)}) custom-call(s32[3]{0:T(128)S(1)} %copy-done.1, bf16[512,640]{1,0:T(8,128)(2,1)S(1)} %get-tuple-element.76.pre_ref, bf16[1280,640]{1,0:T(8,128)(2,1)S(1)} %get-tuple-element.62.up_ref, bf16[128,1280]{1,0:T(8,128)(2,1)S(1)} %get-tuple-element.64.refs_0_, ...), custom_call_target="tpu_custom_call" | custom-call | flops 838860800 | bytes 4194304 | tf_op jit(solution)/shard_map/pallas_call | solution.py:41
  75.1 1.2 collective-permute-done.16
  76.2 1.1 collective-permute-start.17
  77.4 4.2 %collective-permute-done.17 = f32[1,1280]{1,0:T(1,128)S(1)} collective-permute-done((f32[1,1280]{1,0:T(1,128)S(1)}, f32[1,1280]{1,0:T(1,128)S(1)}, u32[]{:S(2)}, u32[]{:S(2)}) %collective-permute-start.17) | collective-permute-done | bytes 5152 | tf_op jit(solution)/shard_map/ppermute | solution.py:68
  81.6 1.4 %collective-permute-start.18 = (f32[1,1280]{1,0:T(1,128)S(1)}, f32[1,1280]{1,0:T(1,128)S(1)}, u32[]{:S(2)}, u32[]{:S(2)}) collective-permute-start(f32[1,1280]{1,0:T(1,128)S(1)} %add.13.term_ref), channel_id=1, source_target_pairs={{0,2},{1,3},{2,0},{3,1},{4,6},{5,7},{6,4},{7,5},{8,10},{9,11},{10,... | collective-permute-start | bytes 15368 | tf_op jit(solution)/shard_map/ppermute | solution.py:68
  83.0 2.3 %collective-permute-done.18.other_ref = f32[1,1280]{1,0:T(1,128)S(1)} collective-permute-done((f32[1,1280]{1,0:T(1,128)S(1)}, f32[1,1280]{1,0:T(1,128)S(1)}, u32[]{:S(2)}, u32[]{:S(2)}) %collective-permute-start.18) | collective-permute-done | bytes 5152 | tf_op jit(solution)/shard_map/ppermute | solution.py:68
  85.3 1.0 shard_map.166
  86.3 0.5 collective-permute-start.19
  86.9 0.1 shard_map.163
  87.0 2.6 %collective-permute-start.20 = (bf16[160,640]{1,0:T(8,128)(2,1)S(1)}, bf16[160,640]{1,0:T(8,128)(2,1)S(1)}, u32[]{:S(2)}, u32[]{:S(2)}) collective-permute-start(bf16[160,640]{1,0:T(8,128)(2,1)S(1)} %get-tuple-element.86), channel_id=1, source_target_pairs={{0,16},{4,20},{8,24},{12,28},{16,0},{20,4},{24,8},{28,12},{1,17},{... | collective-permute-start | bytes 614408 | tf_op jit(solution)/shard_map/ppermute | solution.py:72
  89.6 4.5 %all-to-all-start.1 = ((bf16[4,128,1280]{2,1,0:T(8,128)(2,1)}), bf16[4,128,1280]{2,1,0:T(8,128)(2,1)}, u32[]{:S(2)}, u32[]{:S(2)}) async-start(bf16[4,128,1280]{2,1,0:T(8,128)(2,1)} %get-tuple-element.87), calls=%async_computation.1 | async-start | bytes 2621440 | tf_op jit(solution)/shard_map/all_to_all | solution.py:780
  94.1 3.8 %shard_map.164 = (bf16[128,1280]{1,0:T(8,128)(2,1)S(1)}, f32[128,1280]{1,0:T(8,128)S(1)}, f32[16,128,128]{2,1,0:T(8,128)S(1)}, f32[128,128]{1,0:T(8,128)S(1)}) custom-call(s32[2,2]{1,0:T(2,128)S(1)} %bitcast.31, bf16[128,1280]{1,0:T(8,128)(2,1)S(1)} %bitcast.23, bf16[128,1280]{1,0:T(8,128)(2,1)S(1)} %bitcast.26, bf16[128,1280]{1,0:T(8,128)(2,1)S(1)} %bitcast.29, ...), custom_call_target="tpu_custom_call" | custom-call | flops 2147483648 | bytes 4194304 | tf_op jit(solution)/shard_map/pallas_call | solution.py:41
  98.0 0.0 copy-start.16
  98.0 4.3 %collective-permute-done.19.got_ref = bf16[656,320]{1,0:T(8,128)(2,1)S(1)} collective-permute-done((bf16[656,320]{1,0:T(8,128)(2,1)S(1)}, bf16[656,320]{1,0:T(8,128)(2,1)S(1)}, u32[]{:S(2)}, u32[]{:S(2)}) %collective-permute-start.19) | collective-permute-done | bytes 419872 | tf_op jit(solution)/shard_map/ppermute | solution.py:72
  102.3 0.3 shard_map.167
  102.6 0.6 collective-permute-start.21
  103.2 0.7 shard_map.168
  104.0 4.6 %all-to-all-done.1.refs_0_ = bf16[4,128,1280]{2,1,0:T(8,128)(2,1)} async-done(((bf16[4,128,1280]{2,1,0:T(8,128)(2,1)}), bf16[4,128,1280]{2,1,0:T(8,128)(2,1)}, u32[]{:S(2)}, u32[]{:S(2)}) %all-to-all-start.1) | async-done | bytes 1310752 | tf_op jit(solution)/shard_map/all_to_all | solution.py:780
  108.5 6.6 %shard_map.165 = (bf16[128,1280]{1,0:T(8,128)(2,1)}, bf16[128,1280]{1,0:T(8,128)(2,1)}, bf16[128,1280]{1,0:T(8,128)(2,1)}, bf16[128,1280]{1,0:T(8,128)(2,1)}) custom-call(bf16[4,128,1280]{2,1,0:T(8,128)(2,1)} %all-to-all-done.1.refs_0_, bf16[128,1280]{1,0:T(8,128)(2,1)} %copy-done, f32[128,1280]{1,0:T(8,128)} %copy-done.14, f32[128,128]{1,0:T(8,128)} %copy-done.16, ...), custom_call_target="tpu_custom_call" | custom-call | flops 4294967296 | bytes 4194304 | tf_op jit(solution)/shard_map/pallas_call | solution.py:41
  115.2 0.2 collective-permute-done.21.refs_1_
  115.3 0.8 shard_map.169
  116.2 0.6 reduce
  (43 shorter events, 0.1 us)
Async XLA Ops:
  6.0 15.0 %copy-start.17 = (bf16[176,640]{1,0:T(8,128)(2,1)S(1)}, bf16[176,640]{1,0:T(8,128)(2,1)}, u32[]{:S(2)}) copy-start(bf16[176,640]{1,0:T(8,128)(2,1)} %get-tuple-element.58) | copy-start | bytes 675844
  6.0 10.1 %collective-permute-start = (bf16[176,640]{1,0:T(8,128)(2,1)}, bf16[176,640]{1,0:T(8,128)(2,1)S(1)}, u32[]{:S(2)}, u32[]{:S(2)}) collective-permute-start(bf16[176,640]{1,0:T(8,128)(2,1)} %get-tuple-element.59), channel_id=1, source_target_pairs={{0,1},{1,0},{2,3},{3,2},{4,5},{5,4},{6,7},{7,6},{8,9},{9,8},{10,11... | collective-permute-start | bytes 675848 | tf_op jit(solution)/shard_map/ppermute | solution.py:68
  9.0 12.0 %collective-permute-start.1 = (bf16[176,640]{1,0:T(8,128)(2,1)}, bf16[176,640]{1,0:T(8,128)(2,1)S(1)}, u32[]{:S(2)}, u32[]{:S(2)}) collective-permute-start(bf16[176,640]{1,0:T(8,128)(2,1)} %get-tuple-element.60), channel_id=1, source_target_pairs={{0,2},{1,3},{2,0},{3,1},{4,6},{5,7},{6,4},{7,5},{8,10},{9,11},{10,... | collective-permute-start | bytes 675848 | tf_op jit(solution)/shard_map/ppermute | solution.py:68
  10.5 10.5 %collective-permute-start.2 = (bf16[176,640]{1,0:T(8,128)(2,1)}, bf16[176,640]{1,0:T(8,128)(2,1)S(1)}, u32[]{:S(2)}, u32[]{:S(2)}) collective-permute-start(bf16[176,640]{1,0:T(8,128)(2,1)} %get-tuple-element.61), channel_id=1, source_target_pairs={{0,3},{1,2},{2,1},{3,0},{4,7},{5,6},{6,5},{7,4},{8,11},{9,10},{10,... | collective-permute-start | bytes 675848 | tf_op jit(solution)/shard_map/ppermute | solution.py:68
  10.6 10.7 %copy-start.3 = (bf16[1,128,1280]{2,1,0:T(8,128)(2,1)S(1)}, bf16[1,128,1280]{2,1,0:T(8,128)(2,1)}, u32[]{:S(2)}) copy-start(bf16[1,128,1280]{2,1,0:T(8,128)(2,1)} %param.13) | copy-start | bytes 983044
  10.6 10.7 %copy-start.5 = (bf16[1,128,1280]{2,1,0:T(8,128)(2,1)S(1)}, bf16[1,128,1280]{2,1,0:T(8,128)(2,1)}, u32[]{:S(2)}) copy-start(bf16[1,128,1280]{2,1,0:T(8,128)(2,1)} %param.10) | copy-start | bytes 983044
  10.6 10.7 %copy-start.7 = (bf16[1,128,1280]{2,1,0:T(8,128)(2,1)S(1)}, bf16[1,128,1280]{2,1,0:T(8,128)(2,1)}, u32[]{:S(2)}) copy-start(bf16[1,128,1280]{2,1,0:T(8,128)(2,1)} %param.11) | copy-start | bytes 983044
  10.6 10.7 %copy-start.9 = (bf16[1,128,1280]{2,1,0:T(8,128)(2,1)S(1)}, bf16[1,128,1280]{2,1,0:T(8,128)(2,1)}, u32[]{:S(2)}) copy-start(bf16[1,128,1280]{2,1,0:T(8,128)(2,1)} %param.12) | copy-start | bytes 983044
  10.6 10.7 %copy-start.12 = (s32[1,2,2]{2,1,0:T(2,128)S(1)}, s32[1,2,2]{2,1,0:T(2,128)}, u32[]{:S(2)}) copy-start(s32[1,2,2]{2,1,0:T(2,128)} %param.16) | copy-start | bytes 52
  10.6 25.1 %all-to-all-start = ((bf16[8,32,1408]{2,1,0:T(8,128)(2,1)}), bf16[8,32,1408]{2,1,0:T(8,128)(2,1)S(1)}, u32[]{:S(2)}, u32[]{:S(2)}) async-start(bf16[8,32,1408]{2,1,0:T(8,128)(2,1)} %get-tuple-element.66), calls=%async_computation | async-start | bytes 1441792 | tf_op jit(solution)/shard_map/all_to_all | solution.py:746
  21.2 7.9 %collective-permute-start.3 = (bf16[4,176,640]{2,1,0:T(8,128)(2,1)S(1)}, bf16[4,176,640]{2,1,0:T(8,128)(2,1)S(1)}, u32[]{:S(2)}, u32[]{:S(2)}) collective-permute-start(bf16[4,176,640]{2,1,0:T(8,128)(2,1)S(1)} %pad_maximum_fusion.refs_1_), channel_id=1, source_target_pairs={{0,4},{4,0},{8,12},{12,8},{16,20},{20,16},{24,28},{28,24},{1,5},{5... | collective-permute-start | bytes 2703368 | tf_op jit(solution)/shard_map/ppermute | solution.py:72
  21.3 7.8 %copy-start.1 = (s32[3]{0:T(128)S(1)}, s32[3]{0:T(128)}, u32[]{:S(2)}) copy-start(s32[3]{0:T(128)} %pad_add_fusion.refs_0_.place_ref) | copy-start | bytes 40
  25.6 13.3 %collective-permute-start.6 = (bf16[128,1280]{1,0:T(8,128)(2,1)S(1)}, bf16[128,1280]{1,0:T(8,128)(2,1)S(1)}, u32[]{:S(2)}, u32[]{:S(2)}) collective-permute-start(bf16[128,1280]{1,0:T(8,128)(2,1)S(1)} %get-tuple-element.64.refs_0_), channel_id=1, source_target_pairs={{0,3},{1,2},{2,1},{3,0},{4,7},{5,6},{6,5},{7,4},{8,11},{9,10},{10,... | collective-permute-start | bytes 983048 | tf_op jit(solution)/shard_map/ppermute | solution.py:68
  27.1 17.0 %collective-permute-start.5 = (bf16[128,1280]{1,0:T(8,128)(2,1)S(1)}, bf16[128,1280]{1,0:T(8,128)(2,1)S(1)}, u32[]{:S(2)}, u32[]{:S(2)}) collective-permute-start(bf16[128,1280]{1,0:T(8,128)(2,1)S(1)} %get-tuple-element.64.refs_0_), channel_id=1, source_target_pairs={{0,2},{1,3},{2,0},{3,1},{4,6},{5,7},{6,4},{7,5},{8,10},{9,11},{10,... | collective-permute-start | bytes 983048 | tf_op jit(solution)/shard_map/ppermute | solution.py:68
  28.3 15.9 %collective-permute-start.4 = (bf16[128,1280]{1,0:T(8,128)(2,1)S(1)}, bf16[128,1280]{1,0:T(8,128)(2,1)}, u32[]{:S(2)}, u32[]{:S(2)}) collective-permute-start(bf16[128,1280]{1,0:T(8,128)(2,1)S(1)} %get-tuple-element.64.refs_0_), channel_id=1, source_target_pairs={{0,1},{1,0},{2,3},{3,2},{4,5},{5,4},{6,7},{7,6},{8,9},{9,8},{10,11... | collective-permute-start | bytes 983048 | tf_op jit(solution)/shard_map/ppermute | solution.py:68
  30.2 16.5 %copy-start.11 = (f32[1,1280]{1,0:T(1,128)}, f32[1,1280]{1,0:T(1,128)S(1)}, u32[]{:S(2)}) copy-start(f32[1,1280]{1,0:T(1,128)S(1)} %get-tuple-element.63.gain_ref.refs_4_) | copy-start | bytes 15364
  35.9 21.9 %copy-start = (bf16[128,1280]{1,0:T(8,128)(2,1)}, bf16[128,1280]{1,0:T(8,128)(2,1)S(1)}, u32[]{:S(2)}) copy-start(bf16[128,1280]{1,0:T(8,128)(2,1)S(1)} %shard_map.157.refs_0_.refs_1_) | copy-start | bytes 983044
  35.9 15.2 %collective-permute-start.9 = (bf16[128,1280]{1,0:T(8,128)(2,1)S(1)}, bf16[128,1280]{1,0:T(8,128)(2,1)S(1)}, u32[]{:S(2)}, u32[]{:S(2)}) collective-permute-start(bf16[128,1280]{1,0:T(8,128)(2,1)S(1)} %shard_map.157.refs_0_.refs_1_), channel_id=1, source_target_pairs={{0,3},{1,2},{2,1},{3,0},{4,7},{5,6},{6,5},{7,4},{8,11},{9,10},{10,... | collective-permute-start | bytes 983048 | tf_op jit(solution)/shard_map/ppermute | solution.py:68
  38.5 19.2 %collective-permute-start.8 = (bf16[128,1280]{1,0:T(8,128)(2,1)S(1)}, bf16[128,1280]{1,0:T(8,128)(2,1)S(1)}, u32[]{:S(2)}, u32[]{:S(2)}) collective-permute-start(bf16[128,1280]{1,0:T(8,128)(2,1)S(1)} %shard_map.157.refs_0_.refs_1_), channel_id=1, source_target_pairs={{0,2},{1,3},{2,0},{3,1},{4,6},{5,7},{6,4},{7,5},{8,10},{9,11},{10,... | collective-permute-start | bytes 983048 | tf_op jit(solution)/shard_map/ppermute | solution.py:68
  39.0 18.9 %collective-permute-start.7 = (bf16[128,1280]{1,0:T(8,128)(2,1)S(1)}, bf16[128,1280]{1,0:T(8,128)(2,1)S(1)}, u32[]{:S(2)}, u32[]{:S(2)}) collective-permute-start(bf16[128,1280]{1,0:T(8,128)(2,1)S(1)} %shard_map.157.refs_0_.refs_1_), channel_id=1, source_target_pairs={{0,1},{1,0},{2,3},{3,2},{4,5},{5,4},{6,7},{7,6},{8,9},{9,8},{10,11... | collective-permute-start | bytes 983048 | tf_op jit(solution)/shard_map/ppermute | solution.py:68
  57.8 2.4 %copy-start.2 = (bf16[640,1280]{1,0:T(8,128)(2,1)S(1)}, bf16[640,1280]{1,0:T(8,128)(2,1)}, u32[]{:S(2)}) copy-start(bf16[640,1280]{1,0:T(8,128)(2,1)} %down_ref.1) | copy-start | bytes 4915204
  60.2 3.7 %collective-permute-start.10 = (bf16[4,320,320]{2,1,0:T(8,128)(2,1)S(1)}, bf16[4,320,320]{2,1,0:T(8,128)(2,1)S(1)}, u32[]{:S(2)}, u32[]{:S(2)}) collective-permute-start(bf16[4,320,320]{2,1,0:T(8,128)(2,1)S(1)} %get-tuple-element.74), channel_id=1, source_target_pairs={{0,4},{4,0},{8,12},{12,8},{16,20},{20,16},{24,28},{28,24},{1,5},{5... | collective-permute-start | bytes 2457608 | tf_op jit(solution)/shard_map/ppermute | solution.py:72
  63.3 2.5 %collective-permute-start.14 = (bf16[4,160,640]{2,1,0:T(8,128)(2,1)S(1)}, bf16[4,160,640]{2,1,0:T(8,128)(2,1)S(1)}, u32[]{:S(2)}, u32[]{:S(2)}) collective-permute-start(bf16[4,160,640]{2,1,0:T(8,128)(2,1)S(1)} %get-tuple-element.83), channel_id=1, source_target_pairs={{0,4},{4,0},{8,12},{12,8},{16,20},{20,16},{24,28},{28,24},{1,5},{5... | collective-permute-start | bytes 2457608 | tf_op jit(solution)/shard_map/ppermute | solution.py:72
  66.6 20.3 %collective-permute-start.15 = (bf16[2,160,640]{2,1,0:T(8,128)(2,1)S(1)}, bf16[2,160,640]{2,1,0:T(8,128)(2,1)S(1)}, u32[]{:S(2)}, u32[]{:S(2)}) collective-permute-start(bf16[2,160,640]{2,1,0:T(8,128)(2,1)S(1)} %get-tuple-element.85), channel_id=1, source_target_pairs={{0,8},{4,12},{8,0},{12,4},{16,24},{20,28},{24,16},{28,20},{1,9},{5... | collective-permute-start | bytes 1228808 | tf_op jit(solution)/shard_map/ppermute | solution.py:72
  68.3 17.1 %collective-permute-start.11 = (bf16[320,320]{1,0:T(8,128)(2,1)S(1)}, bf16[320,320]{1,0:T(8,128)(2,1)S(1)}, u32[]{:S(2)}, u32[]{:S(2)}) collective-permute-start(bf16[320,320]{1,0:T(8,128)(2,1)S(1)} %get-tuple-element.78), channel_id=1, source_target_pairs={{0,1},{1,0},{2,3},{3,2},{4,5},{5,4},{6,7},{7,6},{8,9},{9,8},{10,11... | collective-permute-start | bytes 614408 | tf_op jit(solution)/shard_map/ppermute | solution.py:68
  69.3 16.0 %collective-permute-start.12 = (bf16[320,320]{1,0:T(8,128)(2,1)S(1)}, bf16[320,320]{1,0:T(8,128)(2,1)S(1)}, u32[]{:S(2)}, u32[]{:S(2)}) collective-permute-start(bf16[320,320]{1,0:T(8,128)(2,1)S(1)} %get-tuple-element.79), channel_id=1, source_target_pairs={{0,2},{1,3},{2,0},{3,1},{4,6},{5,7},{6,4},{7,5},{8,10},{9,11},{10,... | collective-permute-start | bytes 614408 | tf_op jit(solution)/shard_map/ppermute | solution.py:68
  70.2 15.2 %collective-permute-start.13 = (bf16[320,320]{1,0:T(8,128)(2,1)S(1)}, bf16[320,320]{1,0:T(8,128)(2,1)S(1)}, u32[]{:S(2)}, u32[]{:S(2)}) collective-permute-start(bf16[320,320]{1,0:T(8,128)(2,1)S(1)} %get-tuple-element.80), channel_id=1, source_target_pairs={{0,3},{1,2},{2,1},{3,0},{4,7},{5,6},{6,5},{7,4},{8,11},{9,10},{10,... | collective-permute-start | bytes 614408 | tf_op jit(solution)/shard_map/ppermute | solution.py:68
  75.1 1.2 %collective-permute-start.16 = (f32[1,1280]{1,0:T(1,128)S(1)}, f32[1,1280]{1,0:T(1,128)S(1)}, u32[]{:S(2)}, u32[]{:S(2)}) collective-permute-start(f32[1,1280]{1,0:T(1,128)S(1)} %get-tuple-element.98), channel_id=1, source_target_pairs={{0,4},{4,0},{8,12},{12,8},{16,20},{20,16},{24,28},{28,24},{1,5},{5... | collective-permute-start | bytes 15368 | tf_op jit(solution)/shard_map/ppermute | solution.py:72
  76.2 5.4 %collective-permute-start.17 = (f32[1,1280]{1,0:T(1,128)S(1)}, f32[1,1280]{1,0:T(1,128)S(1)}, u32[]{:S(2)}, u32[]{:S(2)}) collective-permute-start(f32[1,1280]{1,0:T(1,128)S(1)} %add.12), channel_id=1, source_target_pairs={{0,1},{1,0},{2,3},{3,2},{4,5},{5,4},{6,7},{7,6},{8,9},{9,8},{10,11... | collective-permute-start | bytes 15368 | tf_op jit(solution)/shard_map/ppermute | solution.py:68
  81.6 3.7 %collective-permute-start.18 = (f32[1,1280]{1,0:T(1,128)S(1)}, f32[1,1280]{1,0:T(1,128)S(1)}, u32[]{:S(2)}, u32[]{:S(2)}) collective-permute-start(f32[1,1280]{1,0:T(1,128)S(1)} %add.13.term_ref), channel_id=1, source_target_pairs={{0,2},{1,3},{2,0},{3,1},{4,6},{5,7},{6,4},{7,5},{8,10},{9,11},{10,... | collective-permute-start | bytes 15368 | tf_op jit(solution)/shard_map/ppermute | solution.py:68
  86.3 15.9 %collective-permute-start.19 = (bf16[656,320]{1,0:T(8,128)(2,1)S(1)}, bf16[656,320]{1,0:T(8,128)(2,1)S(1)}, u32[]{:S(2)}, u32[]{:S(2)}) collective-permute-start(bf16[656,320]{1,0:T(8,128)(2,1)S(1)} %get-tuple-element.100), channel_id=1, source_target_pairs={{0,8},{4,12},{8,0},{12,4},{16,24},{20,28},{24,16},{28,20},{1,9},{5... | collective-permute-start | bytes 1259528 | tf_op jit(solution)/shard_map/ppermute | solution.py:72
  87.0 16.2 %collective-permute-start.20 = (bf16[160,640]{1,0:T(8,128)(2,1)S(1)}, bf16[160,640]{1,0:T(8,128)(2,1)S(1)}, u32[]{:S(2)}, u32[]{:S(2)}) collective-permute-start(bf16[160,640]{1,0:T(8,128)(2,1)S(1)} %get-tuple-element.86), channel_id=1, source_target_pairs={{0,16},{4,20},{8,24},{12,28},{16,0},{20,4},{24,8},{28,12},{1,17},{... | collective-permute-start | bytes 614408 | tf_op jit(solution)/shard_map/ppermute | solution.py:72
  89.6 4.5 %copy-start.4 = (bf16[1,128,1280]{2,1,0:T(8,128)(2,1)S(1)}, bf16[1,128,1280]{2,1,0:T(8,128)(2,1)}, u32[]{:S(2)}) copy-start(bf16[1,128,1280]{2,1,0:T(8,128)(2,1)} %param.13) | copy-start | bytes 983044
  89.6 4.5 %copy-start.6 = (bf16[1,128,1280]{2,1,0:T(8,128)(2,1)S(1)}, bf16[1,128,1280]{2,1,0:T(8,128)(2,1)}, u32[]{:S(2)}) copy-start(bf16[1,128,1280]{2,1,0:T(8,128)(2,1)} %param.10) | copy-start | bytes 983044
  89.6 4.5 %copy-start.8 = (bf16[1,128,1280]{2,1,0:T(8,128)(2,1)S(1)}, bf16[1,128,1280]{2,1,0:T(8,128)(2,1)}, u32[]{:S(2)}) copy-start(bf16[1,128,1280]{2,1,0:T(8,128)(2,1)} %param.11) | copy-start | bytes 983044
  89.6 4.5 %copy-start.10 = (bf16[1,128,1280]{2,1,0:T(8,128)(2,1)S(1)}, bf16[1,128,1280]{2,1,0:T(8,128)(2,1)}, u32[]{:S(2)}) copy-start(bf16[1,128,1280]{2,1,0:T(8,128)(2,1)} %param.12) | copy-start | bytes 983044
  89.6 18.9 %all-to-all-start.1 = ((bf16[4,128,1280]{2,1,0:T(8,128)(2,1)}), bf16[4,128,1280]{2,1,0:T(8,128)(2,1)}, u32[]{:S(2)}, u32[]{:S(2)}) async-start(bf16[4,128,1280]{2,1,0:T(8,128)(2,1)} %get-tuple-element.87), calls=%async_computation.1 | async-start | bytes 2621440 | tf_op jit(solution)/shard_map/all_to_all | solution.py:780
  97.9 4.6 %copy-start.13 = (f32[16,128,128]{2,1,0:T(8,128)}, f32[16,128,128]{2,1,0:T(8,128)S(1)}, u32[]{:S(2)}) copy-start(f32[16,128,128]{2,1,0:T(8,128)S(1)} %get-tuple-element.91.refs_5_) | copy-start | bytes 3145732
  97.9 4.6 %copy-start.14 = (f32[128,1280]{1,0:T(8,128)}, f32[128,1280]{1,0:T(8,128)S(1)}, u32[]{:S(2)}) copy-start(f32[128,1280]{1,0:T(8,128)S(1)} %get-tuple-element.89.refs_2_) | copy-start | bytes 1966084
  97.9 4.6 %copy-start.15 = (bf16[128,1280]{1,0:T(8,128)(2,1)}, bf16[128,1280]{1,0:T(8,128)(2,1)S(1)}, u32[]{:S(2)}) copy-start(bf16[128,1280]{1,0:T(8,128)(2,1)S(1)} %get-tuple-element.92.refs_6_) | copy-start | bytes 983044
  98.0 4.6 %copy-start.16 = (f32[128,128]{1,0:T(8,128)}, f32[128,128]{1,0:T(8,128)S(1)}, u32[]{:S(2)}) copy-start(f32[128,128]{1,0:T(8,128)S(1)} %get-tuple-element.90.refs_3_) | copy-start | bytes 196612
  102.6 12.7 %collective-permute-start.21 = (bf16[336,320]{1,0:T(8,128)(2,1)S(1)}, bf16[336,320]{1,0:T(8,128)(2,1)S(1)}, u32[]{:S(2)}, u32[]{:S(2)}) collective-permute-start(bf16[336,320]{1,0:T(8,128)(2,1)S(1)} %get-tuple-element.105), channel_id=1, source_target_pairs={{0,16},{4,20},{8,24},{12,28},{16,0},{20,4},{24,8},{28,12},{1,17},{... | collective-permute-start | bytes 645128 | tf_op jit(solution)/shard_map/ppermute | solution.py:72

commit v7 on v6

--- a/solution.py
+++ b/solution.py
@@ -354,7 +354,7 @@
     rows, cols = out_refs[0].shape
     half = rows - PIECE
     own = pl.ds(pl.multiple_of(place_ref[1] * half, PIECE), half)
-    gain = gain_ref[...].astype(jnp.float32)
+    gain = gain_ref[...].astype(jnp.float32).reshape(1, -1)
     gain = jnp.concatenate([gain, jnp.zeros((1, cols - gain.shape[1]), jnp.float32)], axis=1)
     gain = jnp.broadcast_to(gain, (PIECE, cols)).astype(jnp.bfloat16)
     for k, ref in enumerate(out_refs):
@@ -384,7 +384,7 @@
         1 << 20,
         late=(4,),
         limit=MOST_BYTES,
-    )(place, slot_ids, norm_gain[None], llm_rows, w_up)
+    )(place, slot_ids, norm_gain, llm_rows, w_up)
 
 
 def join_kernel(place_ref, mine_ref, mate_ref, up_ref, gain_ref):
@@ -461,35 +461,31 @@
         give_ref[index] = value
 
 
-def down_kernel(place_ref, act_ref, *refs):
-    *rows_refs, all_ref, keep_ref, give_ref = refs
+def down_kernel(place_ref, act_ref, rows_ref, keep_ref, give_ref):
     n_dp, half, width = keep_ref.shape
-    tokens = rows_refs[0].shape[0]
-    for k, ref in enumerate(rows_refs):
-        all_ref[k * tokens : (k + 1) * tokens, :] = ref[...]
-    term = contract(act_ref[...], all_ref[...], 1, 0).astype(jnp.bfloat16)
+    term = contract(act_ref[...], rows_ref[...], 1, 0).astype(jnp.bfloat16)
     for which in range(CORES):
         for d in range(n_dp):
             piece = term[which * half : (which + 1) * half, d * width : (d + 1) * width]
             store_by_core(place_ref[1], piece, which, keep_ref, give_ref, d)
 
 
-def down_pieces(place, act_flip, rows_blocks):
-    n_dp = len(rows_blocks)
-    tokens, feat = rows_blocks[0].shape
+def down_pieces(place, act_flip, rows_all, n_dp):
+    total, feat = rows_all.shape
     cols = act_flip.shape[0]
     piece = jax.ShapeDtypeStruct((n_dp, cols // CORES, feat // n_dp), jnp.bfloat16)
     return vmem_call(
-        down_kernel,
-        (jax.ShapeDtypeStruct((n_dp * tokens, feat), jnp.bfloat16), piece, piece),
-        [pltpu.SMEM] + [pltpu.VMEM] * (1 + n_dp),
-        2 * n_dp * tokens * feat * cols,
-    )(place, act_flip, *rows_blocks)
-
-
-def up_kernel(place_ref, rows_ref, down_ref, slope_ref, flip_ref, pre_ref, keep_ref, give_ref):
+        down_kernel, (piece, piece), [pltpu.SMEM] + [pltpu.VMEM] * 2, 2 * total * feat * cols
+    )(place, act_flip, rows_all)
+
+
+def up_kernel(place_ref, down_ref, slope_ref, flip_ref, *refs):
+    *rows_refs, all_ref, pre_ref, keep_ref, give_ref = refs
     n_z, rows, cols = keep_ref.shape
-    d_act = contract(rows_ref[...], down_ref[...], 1, 1)
+    tokens = rows_refs[0].shape[0]
+    for k, ref in enumerate(rows_refs):
+        all_ref[k * tokens : (k + 1) * tokens, :] = ref[...]
+    d_act = contract(all_ref[...], down_ref[...], 1, 1)
     d_pre = (d_act * slope_ref[...]).astype(jnp.bfloat16)
     pre_ref[...] = d_pre
     term = contract(flip_ref[...], d_pre, 1, 0).astype(jnp.bfloat16)
@@ -500,16 +496,21 @@
             store_by_core(place_ref[1], piece, which, keep_ref, give_ref, z)
 
 
-def up_pieces(place, rows_all, w_down, slope, normed_flip, n_z):
+def up_pieces(place, rows_blocks, w_down, slope, normed_flip, n_z):
     total, cols = slope.shape
     feat = w_down.shape[1]
     piece = jax.ShapeDtypeStruct((n_z, feat // n_z // CORES, cols), jnp.bfloat16)
     return vmem_call(
         up_kernel,
-        (jax.ShapeDtypeStruct((total, cols), jnp.bfloat16), piece, piece),
-        [pltpu.SMEM] + [pltpu.VMEM] * 4,
+        (
+            jax.ShapeDtypeStruct((total, feat), jnp.bfloat16),
+            jax.ShapeDtypeStruct((total, cols), jnp.bfloat16),
+            piece,
+            piece,
+        ),
+        [pltpu.SMEM] + [pltpu.VMEM] * (3 + len(rows_blocks)),
         4 * total * feat * cols,
-    )(place, rows_all, w_down, slope, normed_flip)
+    )(place, w_down, slope, normed_flip, *rows_blocks)
 
 
 def part_kernel(place_ref, pre_ref, up_ref, *refs):
@@ -580,8 +581,8 @@
         ref[...] = wide_sum(keep_ref[at], mate_ref[at]).astype(jnp.bfloat16)
 
 
-def rise_kernel(place_ref, term_ref, other_ref, *refs):
-    *got_refs, keep_ref, give_ref, sum_ref = refs
+def rise_kernel(place_ref, *refs):
+    *got_refs, keep_ref, give_ref = refs
     half, width = got_refs[0].shape
     for k in range(len(got_refs)):
         ref = (keep_ref, give_ref)[k % 2]
@@ -592,10 +593,6 @@
             def _(ref=ref, at=at, got_ref=got_ref):
                 ref[at : at + half, :] = got_ref[...]
 
-    total = term_ref[...] + other_ref[...]
-    sum_ref[...] = total
-    give_ref[2 * half :, :] = to_rows(total, width)
-
 
 def from_rows(rows, count):
     rows = rows.astype(jnp.float32)
@@ -603,12 +600,12 @@
     return jnp.concatenate([rows[i : i + 1] for i in range(count)], axis=1)
 
 
-def climb_kernel(keep_ref, got_ref, term_ref, own_ref, give_ref, sum_ref):
+def climb_kernel(keep_ref, got_ref, term_ref, other_ref, own_ref, give_ref, sum_ref):
     half, width = own_ref.shape
     own_ref[...] = wide_sum(keep_ref[:half, :], got_ref[:half, :]).astype(jnp.bfloat16)
     give = wide_sum(keep_ref[half:, :], got_ref[half : 2 * half, :])
     give_ref[:half, :] = give.astype(jnp.bfloat16)
-    total = term_ref[...] + from_rows(got_ref[2 * half :, :], term_ref.shape[1] // width)
+    total = term_ref[...] + other_ref[...]
     sum_ref[...] = total
     give_ref[half:, :] = to_rows(total, width)
 
@@ -652,21 +649,20 @@
     )(place, keep, mate)
 
 
-def down_rise(place, term, other, planes):
+def down_rise(place, planes):
     half, width = planes[0].shape
     return vmem_call(
         rise_kernel,
         (
             jax.ShapeDtypeStruct((2 * half, width), jnp.bfloat16),
-            jax.ShapeDtypeStruct((2 * half + PIECE, width), jnp.bfloat16),
-            jax.ShapeDtypeStruct(term.shape, jnp.float32),
+            jax.ShapeDtypeStruct((2 * half, width), jnp.bfloat16),
         ),
-        [pltpu.SMEM] + [pltpu.VMEM] * (2 + len(planes)),
+        [pltpu.SMEM] + [pltpu.VMEM] * len(planes),
         1 << 20,
-    )(place, term, other, *planes)
-
-
-def down_climb(keep, got, term):
+    )(place, *planes)
+
+
+def down_climb(keep, got, term, other):
     half, width = keep.shape[0] // 2, keep.shape[1]
     return vmem_call(
         climb_kernel,
@@ -675,9 +671,9 @@
             jax.ShapeDtypeStruct((half + PIECE, width), jnp.bfloat16),
             jax.ShapeDtypeStruct(term.shape, jnp.float32),
         ),
-        [pltpu.VMEM] * 3,
+        [pltpu.VMEM] * 4,
         1 << 35,
-    )(keep, got, term)
+    )(keep, got, term, other)
 
 
 def down_total(own, got, term, factor):
@@ -744,8 +740,9 @@
             place, vision_slot, llm_grad[0], w_up, norm_gain, n_seq, n_dp, tokens
         )
         landing = lax.all_to_all(sent, "seq", split_axis=0, concat_axis=0, tiled=True)
-        _, unit_low = forward(window_mask[0], *attention, 1 << 31, False)
+        _, unit_low = forward(after(window_mask[0], sent), *attention, 1 << 31, False)
         unit_blocks = all_dp(unit_low)
+        others[-1] = after(others[-1], unit_low)
         mine = jnp.stack([own] + [swap_dp(block, n_dp, k + 1) for k, block in enumerate(others)])
         up_cols, gain_row = join_columns(place, mine, swap_seq(mine, n_seq, 1))
         landing = after(landing, up_cols)
@@ -760,27 +757,30 @@
     rows_blocks = all_dp(grad_rows)
     if quick:
         act_flip, slope, normed_flip, normed_all = mlp(up_cols, gain_row, unit_blocks)
-        rows_all, down_keep, down_give = down_pieces(place, act_flip, rows_blocks)
-        down_mate = swap_seq(down_give, n_seq, 1)
-        d_pre, up_keep, up_give = up_pieces(
-            place, rows_all, w_down, slope, normed_flip, n_seq // CORES
+        rows_all, d_pre, up_keep, up_give = up_pieces(
+            place, rows_blocks, w_down, slope, normed_flip, n_seq // CORES
         )
         up_mate = swap_seq(up_give, n_seq, 1)
-        own, *sends = down_planes(place, after(down_keep, d_pre), down_mate)
+        down_keep, down_give = down_pieces(place, act_flip, rows_all, n_dp)
+        down_mate = swap_seq(down_give, n_seq, 1)
+        up_keep, up_give = up_sides(place, up_keep, up_mate)
+        up_got = swap_seq(up_give, n_seq, CORES)
+        own, *sends = down_planes(place, after(down_keep, up_give), down_mate)
         planes = [own] + [swap_dp(block, n_dp, k + 1) for k, block in enumerate(sends)]
         parts, term = normed_parts(place, after(d_pre, own), up_cols, unit_blocks)
         term = term + swap_seq(term, n_seq, 1)
-        up_keep, up_give = up_sides(place, after(up_keep, own), up_mate)
-        up_got = swap_seq(up_give, n_seq, CORES)
         term = term + swap_dp(term, n_dp, 1)
-        down_keep, down_give, term = down_rise(place, term, swap_dp(term, n_dp, 2), planes)
+        down_keep, down_give = down_rise(place, planes)
         down_got = swap_seq(down_give, n_seq, CORES)
         up_keep, up_give = up_middle(up_keep, up_got)
         up_got = swap_seq(up_give, n_seq, 2 * CORES)
         d_got = lax.all_to_all(
             (after(parts, *planes, up_give)), "dp", split_axis=0, concat_axis=0, tiled=True
         )
-        own, down_give, term = down_climb(down_keep, down_got, term)
+        term = term + swap_dp(term, n_dp, 2)
+        own, down_give, term = down_climb(
+            down_keep, down_got, term, swap_seq(term, n_seq, CORES)
+        )
         down_got = swap_seq(down_give, n_seq, 2 * CORES)
         saved = forward(after(window_mask[0], up_give), *attention, 1 << 31, True)
         grads = backward_pass(d_got, saved)

time: 117 us -> 114 us (0.974)
  starting transfers between devices: 33.7 us -> 31.4 us
  local copies, waits for them, and re-layouts: 1.33 us -> 0.09 us
    ppermute x14, waiting for transfers between devices: 27.3 us -> 19.9 us  [swap_dp(): return lax.ppermute(block, 'dp', [(i, i ^ step) for i in range(count)])]
    all_to_all x1, waiting for transfers between devices: 5.39 us -> 12.2 us  [per_device(): lax.all_to_all(sent, 'seq', split_axis=0, concat_axis=0, tiled=True)]
    ppermute x8 -> x9, starting transfers between devices: 6.12 us -> 3.3 us  [swap_seq(): return lax.ppermute(block, 'seq', [(i, i ^ step) for i in range(count)])]
    broadcast_in_dim x1 -> x0, local copies, waits for them, and re-layouts: 1.24 us -> none  [send_first(): norm_gain[None]]
    ppermute x8 -> x9, waiting for transfers between devices: 6.82 us -> 7.69 us  [swap_seq(): return lax.ppermute(block, 'seq', [(i, i ^ step) for i in range(count)])]
  transfers between devices with their start and end apart: 24 -> 25, of which waited for: 14 -> 11; matrix products, arithmetic and copies ran while one was open for 0% -> 0% of each run, Pallas kernels for 24% -> 25%
where the time goes in v7:
time: 114 us
  waiting for transfers between devices  44.5 us (39%)
  Pallas kernels  35.3 us (31%)
  starting transfers between devices  31.4 us (28%)
  other arithmetic  1.43 us (1%)
    pallas_call x17, Pallas kernels, run(): pl.pallas_call(kernel if places else body, out_shape=out_shape, in_specs=...  35.3 us
    ppermute x14, waiting for transfers between devices, swap_dp(): return lax.ppermute(block, 'dp', [(i, i ^ step) for i in range(count)])  19.9 us
    ppermute x14, starting transfers between devices, swap_dp(): return lax.ppermute(block, 'dp', [(i, i ^ step) for i in range(count)])  18.3 us
    all_to_all x1, waiting for transfers between devices, per_device(): lax.all_to_all(sent, 'seq', split_axis=0, concat_axis=0, tiled=True)  12.2 us
    ppermute x9, waiting for transfers between devices, swap_seq(): return lax.ppermute(block, 'seq', [(i, i ^ step) for i in range(count)])  7.69 us
    all_to_all x1, starting transfers between devices, per_device(): lax.all_to_all(sent, 'seq', split_axis=0, concat_axis=0, tiled=True)  5.34 us
    all_to_all x1, waiting for transfers between devices, per_device(): lax.all_to_all(after(parts, *planes, up_give), 'dp', split_axis=0, concat...  4.66 us
    all_to_all x1, starting transfers between devices, per_device(): lax.all_to_all(after(parts, *planes, up_give), 'dp', split_axis=0, concat...  4.45 us
  transfers between devices with their start and end apart: 25, of which 11 were waited for; matrix products, arithmetic and copies ran while one was open for 0% of the time, Pallas kernels for 25%

profile of v7, /device:TPU:0, one launch (start us, length us, event | category | flops | bytes accessed | tf_op | source)
XLA Modules:
  0.0 113.6 jit_solution(294941672229993314)
XLA Ops:
  0.6 0.0 copy-start.12
  0.6 0.0 copy-start.3
  0.7 0.0 copy-start.9
  0.7 0.0 copy-start.7
  0.7 0.0 copy-start.5
  0.7 0.7 pad_add_fusion.refs_0_.place_ref
  1.4 3.5 %shard_map.153 = (bf16[8,32,1408]{2,1,0:T(8,128)(2,1)}, bf16[176,640]{1,0:T(8,128)(2,1)}, bf16[176,640]{1,0:T(8,128)(2,1)}, bf16[176,640]{1,0:T(8,128)(2,1)}, bf16[176,640]{1,0:T(8,128)(2,1)}) custom-call(s32[3]{0:T(128)} %pad_add_fusion.refs_0_.place_ref, s32[1,192]{1,0:T(1,128)} %refs_1_.1, bf16[320]{0:T(512)(128)(2,1)} %refs_2_.1, ...), custom_call_target="tpu_custom_call" | custom-call | flops 1048576 | bytes 4194304 | tf_op jit(solution)/shard_map/pallas_call | solution.py:41
  4.9 3.0 %collective-permute-start = (bf16[176,640]{1,0:T(8,128)(2,1)}, bf16[176,640]{1,0:T(8,128)(2,1)S(1)}, u32[]{:S(2)}, u32[]{:S(2)}) collective-permute-start(bf16[176,640]{1,0:T(8,128)(2,1)} %get-tuple-element.59), channel_id=1, source_target_pairs={{0,1},{1,0},{2,3},{3,2},{4,5},{5,4},{6,7},{7,6},{8,9},{9,8},{10,11... | collective-permute-start | bytes 675848 | tf_op jit(solution)/shard_map/ppermute | solution.py:68
  7.9 1.5 %collective-permute-start.1 = (bf16[176,640]{1,0:T(8,128)(2,1)}, bf16[176,640]{1,0:T(8,128)(2,1)S(1)}, u32[]{:S(2)}, u32[]{:S(2)}) collective-permute-start(bf16[176,640]{1,0:T(8,128)(2,1)} %get-tuple-element.60), channel_id=1, source_target_pairs={{0,2},{1,3},{2,0},{3,1},{4,6},{5,7},{6,4},{7,5},{8,10},{9,11},{10,... | collective-permute-start | bytes 675848 | tf_op jit(solution)/shard_map/ppermute | solution.py:68
  9.4 4.3 %shard_map.154 = (bf16[128,1280]{1,0:T(8,128)(2,1)}, bf16[128,1280]{1,0:T(8,128)(2,1)S(1)}) custom-call(s32[2,2]{1,0:T(2,128)S(1)} %bitcast.30, bf16[128,1280]{1,0:T(8,128)(2,1)S(1)} %bitcast.22, bf16[128,1280]{1,0:T(8,128)(2,1)S(1)} %bitcast.25, bf16[128,1280]{1,0:T(8,128)(2,1)S(1)} %bitcast.28, bf16[128,1280]{1,0:T(8,128)(2,1)S(1)} %bitcast.19), custom_call_target="tpu_custom_call" | custom-call | flops 2147483648 | bytes 4194304 | tf_op jit(solution)/shard_map/pallas_call | solution.py:41
  13.7 0.0 collective-permute-start.2
  13.8 5.3 %all-to-all-start = ((bf16[8,32,1408]{2,1,0:T(8,128)(2,1)}), bf16[8,32,1408]{2,1,0:T(8,128)(2,1)S(1)}, u32[]{:S(2)}, u32[]{:S(2)}) async-start(bf16[8,32,1408]{2,1,0:T(8,128)(2,1)} %get-tuple-element.62), calls=%async_computation | async-start | bytes 1441792 | tf_op jit(solution)/shard_map/all_to_all | solution.py:742
  19.1 2.4 %collective-permute-done.2 = bf16[176,640]{1,0:T(8,128)(2,1)S(1)} collective-permute-done((bf16[176,640]{1,0:T(8,128)(2,1)}, bf16[176,640]{1,0:T(8,128)(2,1)S(1)}, u32[]{:S(2)}, u32[]{:S(2)}) %collective-permute-start.2) | collective-permute-done | bytes 225312 | tf_op jit(solution)/shard_map/ppermute | solution.py:68
  21.6 0.1 pad_maximum_fusion.refs_1_
  21.7 0.1 collective-permute-start.3
  21.8 0.5 collective-permute-start.6
  22.3 1.5 %collective-permute-start.5 = (bf16[128,1280]{1,0:T(8,128)(2,1)S(1)}, bf16[128,1280]{1,0:T(8,128)(2,1)S(1)}, u32[]{:S(2)}, u32[]{:S(2)}) collective-permute-start(bf16[128,1280]{1,0:T(8,128)(2,1)S(1)} %get-tuple-element.64.refs_0_), channel_id=1, source_target_pairs={{0,2},{1,3},{2,0},{3,1},{4,6},{5,7},{6,4},{7,5},{8,10},{9,11},{10,... | collective-permute-start | bytes 983048 | tf_op jit(solution)/shard_map/ppermute | solution.py:68
  23.8 1.5 %collective-permute-start.4 = (bf16[128,1280]{1,0:T(8,128)(2,1)S(1)}, bf16[128,1280]{1,0:T(8,128)(2,1)}, u32[]{:S(2)}, u32[]{:S(2)}) collective-permute-start(bf16[128,1280]{1,0:T(8,128)(2,1)S(1)} %get-tuple-element.64.refs_0_), channel_id=1, source_target_pairs={{0,1},{1,0},{2,3},{3,2},{4,5},{5,4},{6,7},{7,6},{8,9},{9,8},{10,11... | collective-permute-start | bytes 983048 | tf_op jit(solution)/shard_map/ppermute | solution.py:68
  25.3 1.1 shard_map.155
  26.5 0.0 copy-start.11
  26.5 12.2 %all-to-all-done = bf16[8,32,1408]{2,1,0:T(8,128)(2,1)S(1)} async-done(((bf16[8,32,1408]{2,1,0:T(8,128)(2,1)}), bf16[8,32,1408]{2,1,0:T(8,128)(2,1)S(1)}, u32[]{:S(2)}, u32[]{:S(2)}) %all-to-all-start) | async-done | bytes 720928 | tf_op jit(solution)/shard_map/all_to_all | solution.py:742
  38.7 0.3 shard_map.157.refs_0_.refs_1_
  39.0 2.5 %collective-permute-start.9 = (bf16[128,1280]{1,0:T(8,128)(2,1)S(1)}, bf16[128,1280]{1,0:T(8,128)(2,1)S(1)}, u32[]{:S(2)}, u32[]{:S(2)}) collective-permute-start(bf16[128,1280]{1,0:T(8,128)(2,1)S(1)} %shard_map.157.refs_0_.refs_1_), channel_id=1, source_target_pairs={{0,3},{1,2},{2,1},{3,0},{4,7},{5,6},{6,5},{7,4},{8,11},{9,10},{10,... | collective-permute-start | bytes 983048 | tf_op jit(solution)/shard_map/ppermute | solution.py:68
  41.5 0.5 collective-permute-start.8
  42.0 0.5 collective-permute-start.7
  42.5 2.6 %shard_map.156 = (bf16[640,512]{1,0:T(8,128)(2,1)S(1)}, f32[512,640]{1,0:T(8,128)S(1)}, bf16[1280,512]{1,0:T(8,128)(2,1)S(1)}, bf16[512,1280]{1,0:T(8,128)(2,1)}) custom-call(bf16[1280,640]{1,0:T(8,128)(2,1)S(1)} %get-tuple-element.66.up_ref, f32[1,1280]{1,0:T(1,128)S(1)} %get-tuple-element.67.gain_ref.refs_4_, ...), custom_call_target="tpu_custom_call" | custom-call | flops 838860800 | bytes 4194304 | tf_op jit(solution)/shard_map/pallas_call | solution.py:41
  45.1 5.4 %collective-permute-done.9.refs_3_ = bf16[128,1280]{1,0:T(8,128)(2,1)S(1)} collective-permute-done((bf16[128,1280]{1,0:T(8,128)(2,1)S(1)}, bf16[128,1280]{1,0:T(8,128)(2,1)S(1)}, u32[]{:S(2)}, u32[]{:S(2)}) %collective-permute-start.9) | collective-permute-done | bytes 327712 | tf_op jit(solution)/shard_map/ppermute | solution.py:68
  50.6 5.6 %collective-permute-done.8.refs_2_ = bf16[128,1280]{1,0:T(8,128)(2,1)S(1)} collective-permute-done((bf16[128,1280]{1,0:T(8,128)(2,1)S(1)}, bf16[128,1280]{1,0:T(8,128)(2,1)S(1)}, u32[]{:S(2)}, u32[]{:S(2)}) %collective-permute-start.8) | collective-permute-done | bytes 327712 | tf_op jit(solution)/shard_map/ppermute | solution.py:68
  56.2 0.1 collective-permute-done.7.refs_1_
  56.3 3.1 %shard_map.158 = (bf16[512,1280]{1,0:T(8,128)(2,1)S(1)}, bf16[512,640]{1,0:T(8,128)(2,1)S(1)}, bf16[4,160,640]{2,1,0:T(8,128)(2,1)S(1)}, bf16[4,160,640]{2,1,0:T(8,128)(2,1)S(1)}) custom-call(s32[3]{0:T(128)S(1)} %copy-done.1, bf16[640,1280]{1,0:T(8,128)(2,1)S(1)} %copy-done.2, f32[512,640]{1,0:T(8,128)S(1)} %get-tuple-element.68.slope_ref, ...), custom_call_target="tpu_custom_call" | custom-call | flops 1677721600 | bytes 4194304 | tf_op jit(solution)/shard_map/pallas_call | solution.py:41
  59.4 0.1 collective-permute-start.10
  59.5 2.3 %shard_map.159 = (bf16[4,320,320]{2,1,0:T(8,128)(2,1)S(1)}, bf16[4,320,320]{2,1,0:T(8,128)(2,1)S(1)}) custom-call(s32[3]{0:T(128)S(1)} %copy-done.1, bf16[640,512]{1,0:T(8,128)(2,1)S(1)} %get-tuple-element.72.act_ref, bf16[512,1280]{1,0:T(8,128)(2,1)S(1)} %get-tuple-element.73.rows_ref), custom_call_target="tpu_custom_call" | custom-call | flops 838860800 | bytes 4194304 | tf_op jit(solution)/shard_map/pallas_call | solution.py:41
  61.8 0.6 collective-permute-start.11
  62.3 0.7 shard_map.160
  63.1 0.1 collective-permute-start.15
  63.2 1.4 %collective-permute-done.11.mate_ref = bf16[4,320,320]{2,1,0:T(8,128)(2,1)S(1)} collective-permute-done((bf16[4,320,320]{2,1,0:T(8,128)(2,1)S(1)}, bf16[4,320,320]{2,1,0:T(8,128)(2,1)S(1)}, u32[]{:S(2)}, u32[]{:S(2)}) %collective-permute-start.11) | collective-permute-done | bytes 819232 | tf_op jit(solution)/shard_map/ppermute | solution.py:72
  64.5 0.8 shard_map.161
  65.3 1.6 %collective-permute-start.12 = (bf16[320,320]{1,0:T(8,128)(2,1)S(1)}, bf16[320,320]{1,0:T(8,128)(2,1)S(1)}, u32[]{:S(2)}, u32[]{:S(2)}) collective-permute-start(bf16[320,320]{1,0:T(8,128)(2,1)S(1)} %get-tuple-element.83), channel_id=1, source_target_pairs={{0,1},{1,0},{2,3},{3,2},{4,5},{5,4},{6,7},{7,6},{8,9},{9,8},{10,11... | collective-permute-start | bytes 614408 | tf_op jit(solution)/shard_map/ppermute | solution.py:68
  66.9 0.7 collective-permute-start.13
  67.6 1.3 %collective-permute-start.14 = (bf16[320,320]{1,0:T(8,128)(2,1)S(1)}, bf16[320,320]{1,0:T(8,128)(2,1)S(1)}, u32[]{:S(2)}, u32[]{:S(2)}) collective-permute-start(bf16[320,320]{1,0:T(8,128)(2,1)S(1)} %get-tuple-element.85), channel_id=1, source_target_pairs={{0,3},{1,2},{2,1},{3,0},{4,7},{5,6},{6,5},{7,4},{8,11},{9,10},{10,... | collective-permute-start | bytes 614408 | tf_op jit(solution)/shard_map/ppermute | solution.py:68
  68.9 3.3 %shard_map.162 = (bf16[4,128,1280]{2,1,0:T(8,128)(2,1)}, f32[1,1280]{1,0:T(1,128)S(1)}) custom-call(s32[3]{0:T(128)S(1)} %copy-done.1, bf16[512,640]{1,0:T(8,128)(2,1)S(1)} %get-tuple-element.81.pre_ref, bf16[1280,640]{1,0:T(8,128)(2,1)S(1)} %get-tuple-element.66.up_ref, bf16[128,1280]{1,0:T(8,128)(2,1)S(1)} %get-tuple-element.64.refs_0_, ...), custom_call_target="tpu_custom_call" | custom-call | flops 838860800 | bytes 4194304 | tf_op jit(solution)/shard_map/pallas_call | solution.py:41
  72.2 1.2 %collective-permute-done.17 = f32[1,1280]{1,0:T(1,128)S(1)} collective-permute-done((f32[1,1280]{1,0:T(1,128)S(1)}, f32[1,1280]{1,0:T(1,128)S(1)}, u32[]{:S(2)}, u32[]{:S(2)}) %collective-permute-start.17) | collective-permute-done | bytes 5152 | tf_op jit(solution)/shard_map/ppermute | solution.py:72
  73.4 1.6 %collective-permute-start.18 = (f32[1,1280]{1,0:T(1,128)S(1)}, f32[1,1280]{1,0:T(1,128)S(1)}, u32[]{:S(2)}, u32[]{:S(2)}) collective-permute-start(f32[1,1280]{1,0:T(1,128)S(1)} %add.15), channel_id=1, source_target_pairs={{0,1},{1,0},{2,3},{3,2},{4,5},{5,4},{6,7},{7,6},{8,9},{9,8},{10,11... | collective-permute-start | bytes 15368 | tf_op jit(solution)/shard_map/ppermute | solution.py:68
  74.9 4.1 %collective-permute-done.18 = f32[1,1280]{1,0:T(1,128)S(1)} collective-permute-done((f32[1,1280]{1,0:T(1,128)S(1)}, f32[1,1280]{1,0:T(1,128)S(1)}, u32[]{:S(2)}, u32[]{:S(2)}) %collective-permute-start.18) | collective-permute-done | bytes 5152 | tf_op jit(solution)/shard_map/ppermute | solution.py:68
  79.1 1.5 %collective-permute-start.19 = (f32[1,1280]{1,0:T(1,128)S(1)}, f32[1,1280]{1,0:T(1,128)S(1)}, u32[]{:S(2)}, u32[]{:S(2)}) collective-permute-start(f32[1,1280]{1,0:T(1,128)S(1)} %add.16), channel_id=1, source_target_pairs={{0,2},{1,3},{2,0},{3,1},{4,6},{5,7},{6,4},{7,5},{8,10},{9,11},{10,... | collective-permute-start | bytes 15368 | tf_op jit(solution)/shard_map/ppermute | solution.py:68
  80.5 2.2 %collective-permute-done.19 = f32[1,1280]{1,0:T(1,128)S(1)} collective-permute-done((f32[1,1280]{1,0:T(1,128)S(1)}, f32[1,1280]{1,0:T(1,128)S(1)}, u32[]{:S(2)}, u32[]{:S(2)}) %collective-permute-start.19) | collective-permute-done | bytes 5152 | tf_op jit(solution)/shard_map/ppermute | solution.py:68
  82.7 0.1 collective-permute-start.20
  82.8 0.9 shard_map.166
  83.8 2.1 %collective-permute-start.16 = (bf16[640,320]{1,0:T(8,128)(2,1)S(1)}, bf16[640,320]{1,0:T(8,128)(2,1)S(1)}, u32[]{:S(2)}, u32[]{:S(2)}) collective-permute-start(bf16[640,320]{1,0:T(8,128)(2,1)S(1)} %get-tuple-element.100), channel_id=1, source_target_pairs={{0,8},{4,12},{8,0},{12,4},{16,24},{20,28},{24,16},{28,20},{1,9},{5... | collective-permute-start | bytes 1228808 | tf_op jit(solution)/shard_map/ppermute | solution.py:72
  85.8 0.1 shard_map.163
  86.0 0.3 collective-permute-start.21
  86.3 0.0 copy-start.13
  86.3 4.5 %all-to-all-start.1 = ((bf16[4,128,1280]{2,1,0:T(8,128)(2,1)}), bf16[4,128,1280]{2,1,0:T(8,128)(2,1)}, u32[]{:S(2)}, u32[]{:S(2)}) async-start(bf16[4,128,1280]{2,1,0:T(8,128)(2,1)} %get-tuple-element.88), calls=%async_computation.1 | async-start | bytes 2621440 | tf_op jit(solution)/shard_map/all_to_all | solution.py:777
  90.8 3.8 %shard_map.164 = (bf16[128,1280]{1,0:T(8,128)(2,1)S(1)}, f32[128,1280]{1,0:T(8,128)S(1)}, f32[16,128,128]{2,1,0:T(8,128)S(1)}, f32[128,128]{1,0:T(8,128)S(1)}) custom-call(s32[2,2]{1,0:T(2,128)S(1)} %bitcast.31, bf16[128,1280]{1,0:T(8,128)(2,1)S(1)} %bitcast.23, bf16[128,1280]{1,0:T(8,128)(2,1)S(1)} %bitcast.26, bf16[128,1280]{1,0:T(8,128)(2,1)S(1)} %bitcast.29, ...), custom_call_target="tpu_custom_call" | custom-call | flops 2147483648 | bytes 4194304 | tf_op jit(solution)/shard_map/pallas_call | solution.py:41
  94.7 0.0 copy-start.17
  94.7 5.1 %collective-permute-done.16.got_ref = bf16[640,320]{1,0:T(8,128)(2,1)S(1)} collective-permute-done((bf16[640,320]{1,0:T(8,128)(2,1)S(1)}, bf16[640,320]{1,0:T(8,128)(2,1)S(1)}, u32[]{:S(2)}, u32[]{:S(2)}) %collective-permute-start.16) | collective-permute-done | bytes 409632 | tf_op jit(solution)/shard_map/ppermute | solution.py:72
  99.8 0.2 shard_map.167
  100.1 0.1 collective-permute-start.22
  100.2 0.7 shard_map.168
  100.9 4.7 %all-to-all-done.1.refs_0_ = bf16[4,128,1280]{2,1,0:T(8,128)(2,1)} async-done(((bf16[4,128,1280]{2,1,0:T(8,128)(2,1)}), bf16[4,128,1280]{2,1,0:T(8,128)(2,1)}, u32[]{:S(2)}, u32[]{:S(2)}) %all-to-all-start.1) | async-done | bytes 1310752 | tf_op jit(solution)/shard_map/all_to_all | solution.py:777
  105.6 6.6 %shard_map.165 = (bf16[128,1280]{1,0:T(8,128)(2,1)}, bf16[128,1280]{1,0:T(8,128)(2,1)}, bf16[128,1280]{1,0:T(8,128)(2,1)}, bf16[128,1280]{1,0:T(8,128)(2,1)}) custom-call(bf16[4,128,1280]{2,1,0:T(8,128)(2,1)} %all-to-all-done.1.refs_0_, bf16[128,1280]{1,0:T(8,128)(2,1)} %copy-done, f32[128,1280]{1,0:T(8,128)} %copy-done.15, f32[128,128]{1,0:T(8,128)} %copy-done.17, ...), custom_call_target="tpu_custom_call" | custom-call | flops 4294967296 | bytes 4194304 | tf_op jit(solution)/shard_map/pallas_call | solution.py:41
  112.2 0.0 collective-permute-done.22.refs_1_
  112.2 0.8 shard_map.169
  113.0 0.6 reduce
  (47 shorter events, 0.1 us)
Async XLA Ops:
  0.6 8.8 %copy-start.12 = (s32[1,2,2]{2,1,0:T(2,128)S(1)}, s32[1,2,2]{2,1,0:T(2,128)}, u32[]{:S(2)}) copy-start(s32[1,2,2]{2,1,0:T(2,128)} %param.16) | copy-start | bytes 52
  0.6 8.8 %copy-start.3 = (bf16[1,128,1280]{2,1,0:T(8,128)(2,1)S(1)}, bf16[1,128,1280]{2,1,0:T(8,128)(2,1)}, u32[]{:S(2)}) copy-start(bf16[1,128,1280]{2,1,0:T(8,128)(2,1)} %param.13) | copy-start | bytes 983044
  0.7 8.8 %copy-start.9 = (bf16[1,128,1280]{2,1,0:T(8,128)(2,1)S(1)}, bf16[1,128,1280]{2,1,0:T(8,128)(2,1)}, u32[]{:S(2)}) copy-start(bf16[1,128,1280]{2,1,0:T(8,128)(2,1)} %param.12) | copy-start | bytes 983044
  0.7 8.8 %copy-start.7 = (bf16[1,128,1280]{2,1,0:T(8,128)(2,1)S(1)}, bf16[1,128,1280]{2,1,0:T(8,128)(2,1)}, u32[]{:S(2)}) copy-start(bf16[1,128,1280]{2,1,0:T(8,128)(2,1)} %param.11) | copy-start | bytes 983044
  0.7 8.8 %copy-start.5 = (bf16[1,128,1280]{2,1,0:T(8,128)(2,1)S(1)}, bf16[1,128,1280]{2,1,0:T(8,128)(2,1)}, u32[]{:S(2)}) copy-start(bf16[1,128,1280]{2,1,0:T(8,128)(2,1)} %param.10) | copy-start | bytes 983044
  4.9 14.2 %collective-permute-start = (bf16[176,640]{1,0:T(8,128)(2,1)}, bf16[176,640]{1,0:T(8,128)(2,1)S(1)}, u32[]{:S(2)}, u32[]{:S(2)}) collective-permute-start(bf16[176,640]{1,0:T(8,128)(2,1)} %get-tuple-element.59), channel_id=1, source_target_pairs={{0,1},{1,0},{2,3},{3,2},{4,5},{5,4},{6,7},{7,6},{8,9},{9,8},{10,11... | collective-permute-start | bytes 675848 | tf_op jit(solution)/shard_map/ppermute | solution.py:68
  7.9 11.2 %collective-permute-start.1 = (bf16[176,640]{1,0:T(8,128)(2,1)}, bf16[176,640]{1,0:T(8,128)(2,1)S(1)}, u32[]{:S(2)}, u32[]{:S(2)}) collective-permute-start(bf16[176,640]{1,0:T(8,128)(2,1)} %get-tuple-element.60), channel_id=1, source_target_pairs={{0,2},{1,3},{2,0},{3,1},{4,6},{5,7},{6,4},{7,5},{8,10},{9,11},{10,... | collective-permute-start | bytes 675848 | tf_op jit(solution)/shard_map/ppermute | solution.py:68
  13.7 7.8 %copy-start.18 = (bf16[176,640]{1,0:T(8,128)(2,1)S(1)}, bf16[176,640]{1,0:T(8,128)(2,1)}, u32[]{:S(2)}) copy-start(bf16[176,640]{1,0:T(8,128)(2,1)} %get-tuple-element.58) | copy-start | bytes 675844
  13.7 11.6 %copy-start.1 = (s32[3]{0:T(128)S(1)}, s32[3]{0:T(128)}, u32[]{:S(2)}) copy-start(s32[3]{0:T(128)} %pad_add_fusion.refs_0_.place_ref) | copy-start | bytes 40
  13.7 7.8 %collective-permute-start.2 = (bf16[176,640]{1,0:T(8,128)(2,1)}, bf16[176,640]{1,0:T(8,128)(2,1)S(1)}, u32[]{:S(2)}, u32[]{:S(2)}) collective-permute-start(bf16[176,640]{1,0:T(8,128)(2,1)} %get-tuple-element.65), channel_id=1, source_target_pairs={{0,3},{1,2},{2,1},{3,0},{4,7},{5,6},{6,5},{7,4},{8,11},{9,10},{10,... | collective-permute-start | bytes 675848 | tf_op jit(solution)/shard_map/ppermute | solution.py:68
  13.8 24.9 %all-to-all-start = ((bf16[8,32,1408]{2,1,0:T(8,128)(2,1)}), bf16[8,32,1408]{2,1,0:T(8,128)(2,1)S(1)}, u32[]{:S(2)}, u32[]{:S(2)}) async-start(bf16[8,32,1408]{2,1,0:T(8,128)(2,1)} %get-tuple-element.62), calls=%async_computation | async-start | bytes 1441792 | tf_op jit(solution)/shard_map/all_to_all | solution.py:742
  21.7 3.6 %collective-permute-start.3 = (bf16[4,176,640]{2,1,0:T(8,128)(2,1)S(1)}, bf16[4,176,640]{2,1,0:T(8,128)(2,1)S(1)}, u32[]{:S(2)}, u32[]{:S(2)}) collective-permute-start(bf16[4,176,640]{2,1,0:T(8,128)(2,1)S(1)} %pad_maximum_fusion.refs_1_), channel_id=1, source_target_pairs={{0,4},{4,0},{8,12},{12,8},{16,20},{20,16},{24,28},{28,24},{1,5},{5... | collective-permute-start | bytes 2703368 | tf_op jit(solution)/shard_map/ppermute | solution.py:72
  21.8 20.2 %collective-permute-start.6 = (bf16[128,1280]{1,0:T(8,128)(2,1)S(1)}, bf16[128,1280]{1,0:T(8,128)(2,1)S(1)}, u32[]{:S(2)}, u32[]{:S(2)}) collective-permute-start(bf16[128,1280]{1,0:T(8,128)(2,1)S(1)} %get-tuple-element.64.refs_0_), channel_id=1, source_target_pairs={{0,3},{1,2},{2,1},{3,0},{4,7},{5,6},{6,5},{7,4},{8,11},{9,10},{10,... | collective-permute-start | bytes 983048 | tf_op jit(solution)/shard_map/ppermute | solution.py:68
  22.3 20.2 %collective-permute-start.5 = (bf16[128,1280]{1,0:T(8,128)(2,1)S(1)}, bf16[128,1280]{1,0:T(8,128)(2,1)S(1)}, u32[]{:S(2)}, u32[]{:S(2)}) collective-permute-start(bf16[128,1280]{1,0:T(8,128)(2,1)S(1)} %get-tuple-element.64.refs_0_), channel_id=1, source_target_pairs={{0,2},{1,3},{2,0},{3,1},{4,6},{5,7},{6,4},{7,5},{8,10},{9,11},{10,... | collective-permute-start | bytes 983048 | tf_op jit(solution)/shard_map/ppermute | solution.py:68
  23.8 18.7 %collective-permute-start.4 = (bf16[128,1280]{1,0:T(8,128)(2,1)S(1)}, bf16[128,1280]{1,0:T(8,128)(2,1)}, u32[]{:S(2)}, u32[]{:S(2)}) collective-permute-start(bf16[128,1280]{1,0:T(8,128)(2,1)S(1)} %get-tuple-element.64.refs_0_), channel_id=1, source_target_pairs={{0,1},{1,0},{2,3},{3,2},{4,5},{5,4},{6,7},{7,6},{8,9},{9,8},{10,11... | collective-permute-start | bytes 983048 | tf_op jit(solution)/shard_map/ppermute | solution.py:68
  26.5 18.7 %copy-start.11 = (f32[1,1280]{1,0:T(1,128)}, f32[1,1280]{1,0:T(1,128)S(1)}, u32[]{:S(2)}) copy-start(f32[1,1280]{1,0:T(1,128)S(1)} %get-tuple-element.67.gain_ref.refs_4_) | copy-start | bytes 15364
  38.9 17.4 %copy-start = (bf16[128,1280]{1,0:T(8,128)(2,1)}, bf16[128,1280]{1,0:T(8,128)(2,1)S(1)}, u32[]{:S(2)}) copy-start(bf16[128,1280]{1,0:T(8,128)(2,1)S(1)} %shard_map.157.refs_0_.refs_1_) | copy-start | bytes 983044
  39.0 11.6 %collective-permute-start.9 = (bf16[128,1280]{1,0:T(8,128)(2,1)S(1)}, bf16[128,1280]{1,0:T(8,128)(2,1)S(1)}, u32[]{:S(2)}, u32[]{:S(2)}) collective-permute-start(bf16[128,1280]{1,0:T(8,128)(2,1)S(1)} %shard_map.157.refs_0_.refs_1_), channel_id=1, source_target_pairs={{0,3},{1,2},{2,1},{3,0},{4,7},{5,6},{6,5},{7,4},{8,11},{9,10},{10,... | collective-permute-start | bytes 983048 | tf_op jit(solution)/shard_map/ppermute | solution.py:68
  41.5 14.7 %collective-permute-start.8 = (bf16[128,1280]{1,0:T(8,128)(2,1)S(1)}, bf16[128,1280]{1,0:T(8,128)(2,1)S(1)}, u32[]{:S(2)}, u32[]{:S(2)}) collective-permute-start(bf16[128,1280]{1,0:T(8,128)(2,1)S(1)} %shard_map.157.refs_0_.refs_1_), channel_id=1, source_target_pairs={{0,2},{1,3},{2,0},{3,1},{4,6},{5,7},{6,4},{7,5},{8,10},{9,11},{10,... | collective-permute-start | bytes 983048 | tf_op jit(solution)/shard_map/ppermute | solution.py:68
  42.0 14.3 %collective-permute-start.7 = (bf16[128,1280]{1,0:T(8,128)(2,1)S(1)}, bf16[128,1280]{1,0:T(8,128)(2,1)S(1)}, u32[]{:S(2)}, u32[]{:S(2)}) collective-permute-start(bf16[128,1280]{1,0:T(8,128)(2,1)S(1)} %shard_map.157.refs_0_.refs_1_), channel_id=1, source_target_pairs={{0,1},{1,0},{2,3},{3,2},{4,5},{5,4},{6,7},{7,6},{8,9},{9,8},{10,11... | collective-permute-start | bytes 983048 | tf_op jit(solution)/shard_map/ppermute | solution.py:68
  42.5 13.8 %copy-start.2 = (bf16[640,1280]{1,0:T(8,128)(2,1)S(1)}, bf16[640,1280]{1,0:T(8,128)(2,1)}, u32[]{:S(2)}) copy-start(bf16[640,1280]{1,0:T(8,128)(2,1)} %down_ref.1) | copy-start | bytes 4915204
  59.4 3.0 %collective-permute-start.10 = (bf16[4,160,640]{2,1,0:T(8,128)(2,1)S(1)}, bf16[4,160,640]{2,1,0:T(8,128)(2,1)S(1)}, u32[]{:S(2)}, u32[]{:S(2)}) collective-permute-start(bf16[4,160,640]{2,1,0:T(8,128)(2,1)S(1)} %get-tuple-element.76), channel_id=1, source_target_pairs={{0,4},{4,0},{8,12},{12,8},{16,20},{20,16},{24,28},{28,24},{1,5},{5... | collective-permute-start | bytes 2457608 | tf_op jit(solution)/shard_map/ppermute | solution.py:72
  61.8 2.7 %collective-permute-start.11 = (bf16[4,320,320]{2,1,0:T(8,128)(2,1)S(1)}, bf16[4,320,320]{2,1,0:T(8,128)(2,1)S(1)}, u32[]{:S(2)}, u32[]{:S(2)}) collective-permute-start(bf16[4,320,320]{2,1,0:T(8,128)(2,1)S(1)} %get-tuple-element.79), channel_id=1, source_target_pairs={{0,4},{4,0},{8,12},{12,8},{16,20},{20,16},{24,28},{28,24},{1,5},{5... | collective-permute-start | bytes 2457608 | tf_op jit(solution)/shard_map/ppermute | solution.py:72
  63.1 22.8 %collective-permute-start.15 = (bf16[2,160,640]{2,1,0:T(8,128)(2,1)S(1)}, bf16[2,160,640]{2,1,0:T(8,128)(2,1)S(1)}, u32[]{:S(2)}, u32[]{:S(2)}) collective-permute-start(bf16[2,160,640]{2,1,0:T(8,128)(2,1)S(1)} %get-tuple-element.77), channel_id=1, source_target_pairs={{0,8},{4,12},{8,0},{12,4},{16,24},{20,28},{24,16},{28,20},{1,9},{5... | collective-permute-start | bytes 1228808 | tf_op jit(solution)/shard_map/ppermute | solution.py:72
  65.3 17.5 %collective-permute-start.12 = (bf16[320,320]{1,0:T(8,128)(2,1)S(1)}, bf16[320,320]{1,0:T(8,128)(2,1)S(1)}, u32[]{:S(2)}, u32[]{:S(2)}) collective-permute-start(bf16[320,320]{1,0:T(8,128)(2,1)S(1)} %get-tuple-element.83), channel_id=1, source_target_pairs={{0,1},{1,0},{2,3},{3,2},{4,5},{5,4},{6,7},{7,6},{8,9},{9,8},{10,11... | collective-permute-start | bytes 614408 | tf_op jit(solution)/shard_map/ppermute | solution.py:68
  66.9 15.9 %collective-permute-start.13 = (bf16[320,320]{1,0:T(8,128)(2,1)S(1)}, bf16[320,320]{1,0:T(8,128)(2,1)S(1)}, u32[]{:S(2)}, u32[]{:S(2)}) collective-permute-start(bf16[320,320]{1,0:T(8,128)(2,1)S(1)} %get-tuple-element.84), channel_id=1, source_target_pairs={{0,2},{1,3},{2,0},{3,1},{4,6},{5,7},{6,4},{7,5},{8,10},{9,11},{10,... | collective-permute-start | bytes 614408 | tf_op jit(solution)/shard_map/ppermute | solution.py:68
  67.6 15.2 %collective-permute-start.14 = (bf16[320,320]{1,0:T(8,128)(2,1)S(1)}, bf16[320,320]{1,0:T(8,128)(2,1)S(1)}, u32[]{:S(2)}, u32[]{:S(2)}) collective-permute-start(bf16[320,320]{1,0:T(8,128)(2,1)S(1)} %get-tuple-element.85), channel_id=1, source_target_pairs={{0,3},{1,2},{2,1},{3,0},{4,7},{5,6},{6,5},{7,4},{8,11},{9,10},{10,... | collective-permute-start | bytes 614408 | tf_op jit(solution)/shard_map/ppermute | solution.py:68
  72.2 1.2 %collective-permute-start.17 = (f32[1,1280]{1,0:T(1,128)S(1)}, f32[1,1280]{1,0:T(1,128)S(1)}, u32[]{:S(2)}, u32[]{:S(2)}) collective-permute-start(f32[1,1280]{1,0:T(1,128)S(1)} %get-tuple-element.101), channel_id=1, source_target_pairs={{0,4},{4,0},{8,12},{12,8},{16,20},{20,16},{24,28},{28,24},{1,5},{5... | collective-permute-start | bytes 15368 | tf_op jit(solution)/shard_map/ppermute | solution.py:72
  73.4 5.7 %collective-permute-start.18 = (f32[1,1280]{1,0:T(1,128)S(1)}, f32[1,1280]{1,0:T(1,128)S(1)}, u32[]{:S(2)}, u32[]{:S(2)}) collective-permute-start(f32[1,1280]{1,0:T(1,128)S(1)} %add.15), channel_id=1, source_target_pairs={{0,1},{1,0},{2,3},{3,2},{4,5},{5,4},{6,7},{7,6},{8,9},{9,8},{10,11... | collective-permute-start | bytes 15368 | tf_op jit(solution)/shard_map/ppermute | solution.py:68
  79.1 3.7 %collective-permute-start.19 = (f32[1,1280]{1,0:T(1,128)S(1)}, f32[1,1280]{1,0:T(1,128)S(1)}, u32[]{:S(2)}, u32[]{:S(2)}) collective-permute-start(f32[1,1280]{1,0:T(1,128)S(1)} %add.16), channel_id=1, source_target_pairs={{0,2},{1,3},{2,0},{3,1},{4,6},{5,7},{6,4},{7,5},{8,10},{9,11},{10,... | collective-permute-start | bytes 15368 | tf_op jit(solution)/shard_map/ppermute | solution.py:68
  82.7 11.9 %collective-permute-start.20 = (f32[1,1280]{1,0:T(1,128)S(1)}, f32[1,1280]{1,0:T(1,128)S(1)}, u32[]{:S(2)}, u32[]{:S(2)}) collective-permute-start(f32[1,1280]{1,0:T(1,128)S(1)} %add.17.term_ref), channel_id=1, source_target_pairs={{0,8},{4,12},{8,0},{12,4},{16,24},{20,28},{24,16},{28,20},{1,9},{5... | collective-permute-start | bytes 15368 | tf_op jit(solution)/shard_map/ppermute | solution.py:72
  83.8 16.0 %collective-permute-start.16 = (bf16[640,320]{1,0:T(8,128)(2,1)S(1)}, bf16[640,320]{1,0:T(8,128)(2,1)S(1)}, u32[]{:S(2)}, u32[]{:S(2)}) collective-permute-start(bf16[640,320]{1,0:T(8,128)(2,1)S(1)} %get-tuple-element.100), channel_id=1, source_target_pairs={{0,8},{4,12},{8,0},{12,4},{16,24},{20,28},{24,16},{28,20},{1,9},{5... | collective-permute-start | bytes 1228808 | tf_op jit(solution)/shard_map/ppermute | solution.py:72
  86.0 14.2 %collective-permute-start.21 = (bf16[160,640]{1,0:T(8,128)(2,1)S(1)}, bf16[160,640]{1,0:T(8,128)(2,1)S(1)}, u32[]{:S(2)}, u32[]{:S(2)}) collective-permute-start(bf16[160,640]{1,0:T(8,128)(2,1)S(1)} %get-tuple-element.87), channel_id=1, source_target_pairs={{0,16},{4,20},{8,24},{12,28},{16,0},{20,4},{24,8},{28,12},{1,17},{... | collective-permute-start | bytes 614408 | tf_op jit(solution)/shard_map/ppermute | solution.py:72
  86.3 4.5 %copy-start.4 = (bf16[1,128,1280]{2,1,0:T(8,128)(2,1)S(1)}, bf16[1,128,1280]{2,1,0:T(8,128)(2,1)}, u32[]{:S(2)}) copy-start(bf16[1,128,1280]{2,1,0:T(8,128)(2,1)} %param.13) | copy-start | bytes 983044
  86.3 4.5 %copy-start.6 = (bf16[1,128,1280]{2,1,0:T(8,128)(2,1)S(1)}, bf16[1,128,1280]{2,1,0:T(8,128)(2,1)}, u32[]{:S(2)}) copy-start(bf16[1,128,1280]{2,1,0:T(8,128)(2,1)} %param.10) | copy-start | bytes 983044
  86.3 4.5 %copy-start.8 = (bf16[1,128,1280]{2,1,0:T(8,128)(2,1)S(1)}, bf16[1,128,1280]{2,1,0:T(8,128)(2,1)}, u32[]{:S(2)}) copy-start(bf16[1,128,1280]{2,1,0:T(8,128)(2,1)} %param.11) | copy-start | bytes 983044
  86.3 4.5 %copy-start.10 = (bf16[1,128,1280]{2,1,0:T(8,128)(2,1)S(1)}, bf16[1,128,1280]{2,1,0:T(8,128)(2,1)}, u32[]{:S(2)}) copy-start(bf16[1,128,1280]{2,1,0:T(8,128)(2,1)} %param.12) | copy-start | bytes 983044
  86.3 4.5 %copy-start.13 = (s32[1,2,2]{2,1,0:T(2,128)S(1)}, s32[1,2,2]{2,1,0:T(2,128)}, u32[]{:S(2)}) copy-start(s32[1,2,2]{2,1,0:T(2,128)} %param.16) | copy-start | bytes 52
  86.3 19.3 %all-to-all-start.1 = ((bf16[4,128,1280]{2,1,0:T(8,128)(2,1)}), bf16[4,128,1280]{2,1,0:T(8,128)(2,1)}, u32[]{:S(2)}, u32[]{:S(2)}) async-start(bf16[4,128,1280]{2,1,0:T(8,128)(2,1)} %get-tuple-element.88), calls=%async_computation.1 | async-start | bytes 2621440 | tf_op jit(solution)/shard_map/all_to_all | solution.py:777
  94.6 5.4 %copy-start.14 = (f32[16,128,128]{2,1,0:T(8,128)}, f32[16,128,128]{2,1,0:T(8,128)S(1)}, u32[]{:S(2)}) copy-start(f32[16,128,128]{2,1,0:T(8,128)S(1)} %get-tuple-element.92.refs_5_) | copy-start | bytes 3145732
  94.6 5.4 %copy-start.15 = (f32[128,1280]{1,0:T(8,128)}, f32[128,1280]{1,0:T(8,128)S(1)}, u32[]{:S(2)}) copy-start(f32[128,1280]{1,0:T(8,128)S(1)} %get-tuple-element.90.refs_2_) | copy-start | bytes 1966084
  94.7 5.4 %copy-start.16 = (bf16[128,1280]{1,0:T(8,128)(2,1)}, bf16[128,1280]{1,0:T(8,128)(2,1)S(1)}, u32[]{:S(2)}) copy-start(bf16[128,1280]{1,0:T(8,128)(2,1)S(1)} %get-tuple-element.93.refs_6_) | copy-start | bytes 983044
  94.7 5.4 %copy-start.17 = (f32[128,128]{1,0:T(8,128)}, f32[128,128]{1,0:T(8,128)S(1)}, u32[]{:S(2)}) copy-start(f32[128,128]{1,0:T(8,128)S(1)} %get-tuple-element.91.refs_3_) | copy-start | bytes 196612
  100.1 12.1 %collective-permute-start.22 = (bf16[336,320]{1,0:T(8,128)(2,1)S(1)}, bf16[336,320]{1,0:T(8,128)(2,1)S(1)}, u32[]{:S(2)}, u32[]{:S(2)}) collective-permute-start(bf16[336,320]{1,0:T(8,128)(2,1)S(1)} %get-tuple-element.105), channel_id=1, source_target_pairs={{0,16},{4,20},{8,24},{12,28},{16,0},{20,4},{24,8},{28,12},{1,17},{... | collective-permute-start | bytes 645128 | tf_op jit(solution)/shard_map/ppermute | solution.py:72

commit v8 on v7

--- a/solution.py
+++ b/solution.py
@@ -363,7 +363,7 @@
         ref[half:, :] = gain
 
 
-def send_first(place, slot_ids, llm_rows, w_up, norm_gain, n_seq, n_dp, tokens):
+def send_first(slot_ids, llm_rows, w_up, norm_gain, n_seq, n_dp, tokens):
     rows, ff = w_up.shape
     per_owner = tokens // PIECE
     capacity = 1 + (per_owner + n_seq - 2) // n_seq
@@ -372,7 +372,8 @@
         (n_seq, capacity * PIECE, llm_rows.shape[1] + LANES), jnp.bfloat16
     )
 
-    def body(wait_up, place_ref, slot_ref, gain_ref, rows_ref, up_ref, tiles_ref, *piece_refs):
+    def body(wait_up, slot_ref, gain_ref, rows_ref, up_ref, tiles_ref, *piece_refs):
+        place_ref = (lax.axis_index("dp"), lax.axis_index("seq") % CORES)
         send_kernel(n_seq, capacity, per_owner, slot_ref, rows_ref, tiles_ref)
         wait_up()
         fetch_kernel(place_ref, up_ref, gain_ref, *piece_refs)
@@ -380,11 +381,11 @@
     return vmem_call(
         body,
         (tiles,) + (piece,) * n_dp,
-        [pltpu.SMEM, pltpu.SMEM, pltpu.VMEM, pl.ANY, pl.ANY],
+        [pltpu.SMEM, pltpu.VMEM, pl.ANY, pl.ANY],
         1 << 20,
-        late=(4,),
+        late=(3,),
         limit=MOST_BYTES,
-    )(place, slot_ids, norm_gain, llm_rows, w_up)
+    )(slot_ids, norm_gain, llm_rows, w_up)
 
 
 def join_kernel(place_ref, mine_ref, mate_ref, up_ref, gain_ref):
@@ -619,7 +620,7 @@
     half, width = own_ref.shape
     down_ref[...] = (wide_sum(own_ref[...], got_ref[:half, :]) * factor).astype(jnp.bfloat16)
     rest = from_rows(got_ref[half:, :], term_ref.shape[1] // width)
-    gain_ref[...] = (term_ref[...] + rest) * factor
+    gain_ref[...] = ((term_ref[...] + rest) * factor).reshape(-1)
 
 
 def up_sides(place, keep, mate):
@@ -681,12 +682,12 @@
         lambda *refs: last_kernel(factor, *refs),
         (
             jax.ShapeDtypeStruct(own.shape, jnp.bfloat16),
-            jax.ShapeDtypeStruct(term.shape, jnp.float32),
+            jax.ShapeDtypeStruct((term.size,), jnp.float32),
         ),
         [pltpu.VMEM] * 3,
         1 << 20,
     )(own, got, term)
-    return down, gain.reshape(-1)
+    return down, gain
 
 
 def after(value, *others):
@@ -737,7 +738,7 @@
     attention = (queries[0], key_rows[0], value_rows[0], resid_in[0])
     if quick:
         sent, own, *others = send_first(
-            place, vision_slot, llm_grad[0], w_up, norm_gain, n_seq, n_dp, tokens
+            vision_slot, llm_grad[0], w_up, norm_gain, n_seq, n_dp, tokens
         )
         landing = lax.all_to_all(sent, "seq", split_axis=0, concat_axis=0, tiled=True)
         _, unit_low = forward(after(window_mask[0], sent), *attention, 1 << 31, False)

time: 114 us -> 113 us (level)
  waiting for transfers between devices: 44.5 us -> 41.6 us
  local copies, waits for them, and re-layouts: 0.09 us -> 2.22 us
  other arithmetic: 1.43 us -> 0.23 us
    unnamed x38 -> x42, local copies, waits for them, and re-layouts: 0.09 us -> 2.22 us
    all_to_all x1, waiting for transfers between devices: 12.2 us -> 10.2 us  [per_device(): lax.all_to_all(sent, 'seq', split_axis=0, concat_axis=0, tiled=True)]
  transfers between devices with their start and end apart: 25 -> 25, of which waited for: 11 -> 11; matrix products, arithmetic and copies ran while one was open for 0% -> 0% of each run, Pallas kernels for 25% -> 26%
where the time goes in v8:
time: 113 us
  waiting for transfers between devices  41.6 us (37%)
  Pallas kernels  36.3 us (32%)
  starting transfers between devices  31.3 us (28%)
  local copies, waits for them, and re-layouts  2.22 us (2%)
    pallas_call x17, Pallas kernels, run(): pl.pallas_call(kernel if places else body, out_shape=out_shape, in_specs=...  36.3 us
    ppermute x14, waiting for transfers between devices, swap_dp(): return lax.ppermute(block, 'dp', [(i, i ^ step) for i in range(count)])  19.1 us
    ppermute x14, starting transfers between devices, swap_dp(): return lax.ppermute(block, 'dp', [(i, i ^ step) for i in range(count)])  18.3 us
    all_to_all x1, waiting for transfers between devices, per_device(): lax.all_to_all(sent, 'seq', split_axis=0, concat_axis=0, tiled=True)  10.2 us
    ppermute x9, waiting for transfers between devices, swap_seq(): return lax.ppermute(block, 'seq', [(i, i ^ step) for i in range(count)])  7.72 us
    all_to_all x1, starting transfers between devices, per_device(): lax.all_to_all(sent, 'seq', split_axis=0, concat_axis=0, tiled=True)  5.34 us
    all_to_all x1, waiting for transfers between devices, per_device(): lax.all_to_all(after(parts, *planes, up_give), 'dp', split_axis=0, concat...  4.64 us
    all_to_all x1, starting transfers between devices, per_device(): lax.all_to_all(after(parts, *planes, up_give), 'dp', split_axis=0, concat...  4.44 us
  transfers between devices with their start and end apart: 25, of which 11 were waited for; matrix products, arithmetic and copies ran while one was open for 0% of the time, Pallas kernels for 26%

profile of v8, /device:TPU:0, one launch (start us, length us, event | category | flops | bytes accessed | tf_op | source)
XLA Modules:
  0.0 112.7 jit_solution(9811211975134294414)
XLA Ops:
  0.6 0.0 copy-start.13
  0.6 0.0 copy-start.4
  0.7 0.0 copy-start.10
  0.7 0.0 copy-start.8
  0.7 0.0 copy-start.6
  0.7 3.7 %shard_map.153 = (bf16[8,32,1408]{2,1,0:T(8,128)(2,1)}, bf16[176,640]{1,0:T(8,128)(2,1)}, bf16[176,640]{1,0:T(8,128)(2,1)}, bf16[176,640]{1,0:T(8,128)(2,1)}, bf16[176,640]{1,0:T(8,128)(2,1)}) custom-call(s32[1,192]{1,0:T(1,128)} %refs_0_.1, bf16[320]{0:T(512)(128)(2,1)} %refs_1_.1, bf16[192,1280]{1,0:T(8,128)(2,1)} %bitcast.32, bf16[320,2560]{1,0:T(8,128)(2,1)} %refs_3_.1), custom_call_target="tpu_custom_call" | custom-call | flops 1048576 | bytes 4194304 | tf_op jit(solution)/shard_map/pallas_call | solution.py:41
  4.4 3.0 %collective-permute-start = (bf16[176,640]{1,0:T(8,128)(2,1)}, bf16[176,640]{1,0:T(8,128)(2,1)S(1)}, u32[]{:S(2)}, u32[]{:S(2)}) collective-permute-start(bf16[176,640]{1,0:T(8,128)(2,1)} %get-tuple-element.59), channel_id=1, source_target_pairs={{0,1},{1,0},{2,3},{3,2},{4,5},{5,4},{6,7},{7,6},{8,9},{9,8},{10,11... | collective-permute-start | bytes 675848 | tf_op jit(solution)/shard_map/ppermute | solution.py:68
  7.4 1.5 %collective-permute-start.1 = (bf16[176,640]{1,0:T(8,128)(2,1)}, bf16[176,640]{1,0:T(8,128)(2,1)S(1)}, u32[]{:S(2)}, u32[]{:S(2)}) collective-permute-start(bf16[176,640]{1,0:T(8,128)(2,1)} %get-tuple-element.60), channel_id=1, source_target_pairs={{0,2},{1,3},{2,0},{3,1},{4,6},{5,7},{6,4},{7,5},{8,10},{9,11},{10,... | collective-permute-start | bytes 675848 | tf_op jit(solution)/shard_map/ppermute | solution.py:68
  8.9 4.5 %shard_map.154 = (bf16[128,1280]{1,0:T(8,128)(2,1)}, bf16[128,1280]{1,0:T(8,128)(2,1)}) custom-call(s32[2,2]{1,0:T(2,128)S(1)} %bitcast.30, bf16[128,1280]{1,0:T(8,128)(2,1)S(1)} %bitcast.22, bf16[128,1280]{1,0:T(8,128)(2,1)S(1)} %bitcast.25, bf16[128,1280]{1,0:T(8,128)(2,1)S(1)} %bitcast.28, bf16[128,1280]{1,0:T(8,128)(2,1)S(1)} %bitcast.19), custom_call_target="tpu_custom_call" | custom-call | flops 2147483648 | bytes 4194304 | tf_op jit(solution)/shard_map/pallas_call | solution.py:41
  13.5 0.0 collective-permute-start.2
  13.5 5.3 %all-to-all-start = ((bf16[8,32,1408]{2,1,0:T(8,128)(2,1)}), bf16[8,32,1408]{2,1,0:T(8,128)(2,1)S(1)}, u32[]{:S(2)}, u32[]{:S(2)}) async-start(bf16[8,32,1408]{2,1,0:T(8,128)(2,1)} %get-tuple-element.62), calls=%async_computation | async-start | bytes 1441792 | tf_op jit(solution)/shard_map/all_to_all | solution.py:743
  18.8 2.2 %collective-permute-done.2 = bf16[176,640]{1,0:T(8,128)(2,1)S(1)} collective-permute-done((bf16[176,640]{1,0:T(8,128)(2,1)S(1)}, bf16[176,640]{1,0:T(8,128)(2,1)S(1)}, u32[]{:S(2)}, u32[]{:S(2)}) %collective-permute-start.2) | collective-permute-done | bytes 225312 | tf_op jit(solution)/shard_map/ppermute | solution.py:68
  21.1 0.1 pad_maximum_fusion.refs_1_
  21.2 0.1 collective-permute-start.3
  21.3 0.7 collective-permute-start.6
  22.0 1.3 %collective-permute-start.5 = (bf16[128,1280]{1,0:T(8,128)(2,1)}, bf16[128,1280]{1,0:T(8,128)(2,1)}, u32[]{:S(2)}, u32[]{:S(2)}) collective-permute-start(bf16[128,1280]{1,0:T(8,128)(2,1)} %get-tuple-element.64.refs_0_), channel_id=1, source_target_pairs={{0,2},{1,3},{2,0},{3,1},{4,6},{5,7},{6,4},{7,5},{8,10},{9,11},{10,... | collective-permute-start | bytes 983048 | tf_op jit(solution)/shard_map/ppermute | solution.py:68
  23.3 1.5 %collective-permute-start.4 = (bf16[128,1280]{1,0:T(8,128)(2,1)}, bf16[128,1280]{1,0:T(8,128)(2,1)}, u32[]{:S(2)}, u32[]{:S(2)}) collective-permute-start(bf16[128,1280]{1,0:T(8,128)(2,1)} %get-tuple-element.64.refs_0_), channel_id=1, source_target_pairs={{0,1},{1,0},{2,3},{3,2},{4,5},{5,4},{6,7},{7,6},{8,9},{9,8},{10,11... | collective-permute-start | bytes 983048 | tf_op jit(solution)/shard_map/ppermute | solution.py:68
  24.8 0.1 pad_add_fusion.refs_0_.place_ref
  24.9 0.9 copy-done
  25.9 1.2 %copy-done.1 = bf16[4,176,640]{2,1,0:T(8,128)(2,1)S(1)} copy-done((bf16[4,176,640]{2,1,0:T(8,128)(2,1)S(1)}, bf16[4,176,640]{2,1,0:T(8,128)(2,1)}, u32[]{:S(2)}) %copy-start.1) | copy-done | bytes 901144
  27.0 1.1 shard_map.155
  28.2 0.0 copy-start.12
  28.2 10.2 %all-to-all-done = bf16[8,32,1408]{2,1,0:T(8,128)(2,1)S(1)} async-done(((bf16[8,32,1408]{2,1,0:T(8,128)(2,1)}), bf16[8,32,1408]{2,1,0:T(8,128)(2,1)S(1)}, u32[]{:S(2)}, u32[]{:S(2)}) %all-to-all-start) | async-done | bytes 720928 | tf_op jit(solution)/shard_map/all_to_all | solution.py:743
  38.4 0.3 shard_map.157.refs_0_.refs_1_
  38.7 2.5 %collective-permute-start.9 = (bf16[128,1280]{1,0:T(8,128)(2,1)S(1)}, bf16[128,1280]{1,0:T(8,128)(2,1)S(1)}, u32[]{:S(2)}, u32[]{:S(2)}) collective-permute-start(bf16[128,1280]{1,0:T(8,128)(2,1)S(1)} %shard_map.157.refs_0_.refs_1_), channel_id=1, source_target_pairs={{0,3},{1,2},{2,1},{3,0},{4,7},{5,6},{6,5},{7,4},{8,11},{9,10},{10,... | collective-permute-start | bytes 983048 | tf_op jit(solution)/shard_map/ppermute | solution.py:68
  41.2 0.5 collective-permute-start.8
  41.7 0.5 collective-permute-start.7
  42.3 2.9 %shard_map.156 = (bf16[640,512]{1,0:T(8,128)(2,1)S(1)}, f32[512,640]{1,0:T(8,128)S(1)}, bf16[1280,512]{1,0:T(8,128)(2,1)S(1)}, bf16[512,1280]{1,0:T(8,128)(2,1)}) custom-call(bf16[1280,640]{1,0:T(8,128)(2,1)S(1)} %get-tuple-element.66.up_ref, f32[1,1280]{1,0:T(1,128)S(1)} %get-tuple-element.67.gain_ref.refs_4_, bf16[128,1280]{1,0:T(8,128)(2,1)} %get-tuple-element.64.refs_0_, ...), custom_call_target="tpu_custom_call" | custom-call | flops 838860800 | bytes 4194304 | tf_op jit(solution)/shard_map/pallas_call | solution.py:41
  45.2 5.2 %collective-permute-done.9.refs_3_ = bf16[128,1280]{1,0:T(8,128)(2,1)S(1)} collective-permute-done((bf16[128,1280]{1,0:T(8,128)(2,1)S(1)}, bf16[128,1280]{1,0:T(8,128)(2,1)S(1)}, u32[]{:S(2)}, u32[]{:S(2)}) %collective-permute-start.9) | collective-permute-done | bytes 327712 | tf_op jit(solution)/shard_map/ppermute | solution.py:68
  50.3 5.6 %collective-permute-done.8.refs_2_ = bf16[128,1280]{1,0:T(8,128)(2,1)S(1)} collective-permute-done((bf16[128,1280]{1,0:T(8,128)(2,1)S(1)}, bf16[128,1280]{1,0:T(8,128)(2,1)S(1)}, u32[]{:S(2)}, u32[]{:S(2)}) %collective-permute-start.8) | collective-permute-done | bytes 327712 | tf_op jit(solution)/shard_map/ppermute | solution.py:68
  55.9 0.1 collective-permute-done.7.refs_1_
  56.0 3.1 %shard_map.158 = (bf16[512,1280]{1,0:T(8,128)(2,1)S(1)}, bf16[512,640]{1,0:T(8,128)(2,1)S(1)}, bf16[4,160,640]{2,1,0:T(8,128)(2,1)S(1)}, bf16[4,160,640]{2,1,0:T(8,128)(2,1)S(1)}) custom-call(s32[3]{0:T(128)S(1)} %pad_add_fusion.refs_0_.place_ref, bf16[640,1280]{1,0:T(8,128)(2,1)S(1)} %copy-done.3, f32[512,640]{1,0:T(8,128)S(1)} %get-tuple-element.68.slope_ref, ...), custom_call_target="tpu_custom_call" | custom-call | flops 1677721600 | bytes 4194304 | tf_op jit(solution)/shard_map/pallas_call | solution.py:41
  59.1 0.1 collective-permute-start.10
  59.2 2.3 %shard_map.159 = (bf16[4,320,320]{2,1,0:T(8,128)(2,1)S(1)}, bf16[4,320,320]{2,1,0:T(8,128)(2,1)S(1)}) custom-call(s32[3]{0:T(128)S(1)} %pad_add_fusion.refs_0_.place_ref, bf16[640,512]{1,0:T(8,128)(2,1)S(1)} %get-tuple-element.72.act_ref, bf16[512,1280]{1,0:T(8,128)(2,1)S(1)} %get-tuple-element.73.rows_ref), custom_call_target="tpu_custom_call" | custom-call | flops 838860800 | bytes 4194304 | tf_op jit(solution)/shard_map/pallas_call | solution.py:41
  61.5 0.6 collective-permute-start.11
  62.1 0.7 shard_map.160
  62.8 0.1 collective-permute-start.15
  62.9 1.4 %collective-permute-done.11.mate_ref = bf16[4,320,320]{2,1,0:T(8,128)(2,1)S(1)} collective-permute-done((bf16[4,320,320]{2,1,0:T(8,128)(2,1)S(1)}, bf16[4,320,320]{2,1,0:T(8,128)(2,1)S(1)}, u32[]{:S(2)}, u32[]{:S(2)}) %collective-permute-start.11) | collective-permute-done | bytes 819232 | tf_op jit(solution)/shard_map/ppermute | solution.py:72
  64.3 0.8 shard_map.161
  65.0 1.6 %collective-permute-start.12 = (bf16[320,320]{1,0:T(8,128)(2,1)S(1)}, bf16[320,320]{1,0:T(8,128)(2,1)S(1)}, u32[]{:S(2)}, u32[]{:S(2)}) collective-permute-start(bf16[320,320]{1,0:T(8,128)(2,1)S(1)} %get-tuple-element.83), channel_id=1, source_target_pairs={{0,1},{1,0},{2,3},{3,2},{4,5},{5,4},{6,7},{7,6},{8,9},{9,8},{10,11... | collective-permute-start | bytes 614408 | tf_op jit(solution)/shard_map/ppermute | solution.py:68
  66.6 0.7 collective-permute-start.13
  67.3 1.3 %collective-permute-start.14 = (bf16[320,320]{1,0:T(8,128)(2,1)S(1)}, bf16[320,320]{1,0:T(8,128)(2,1)S(1)}, u32[]{:S(2)}, u32[]{:S(2)}) collective-permute-start(bf16[320,320]{1,0:T(8,128)(2,1)S(1)} %get-tuple-element.85), channel_id=1, source_target_pairs={{0,3},{1,2},{2,1},{3,0},{4,7},{5,6},{6,5},{7,4},{8,11},{9,10},{10,... | collective-permute-start | bytes 614408 | tf_op jit(solution)/shard_map/ppermute | solution.py:68
  68.6 3.7 %shard_map.162 = (bf16[4,128,1280]{2,1,0:T(8,128)(2,1)}, f32[1,1280]{1,0:T(1,128)S(1)}) custom-call(s32[3]{0:T(128)S(1)} %pad_add_fusion.refs_0_.place_ref, bf16[512,640]{1,0:T(8,128)(2,1)S(1)} %get-tuple-element.81.pre_ref, bf16[1280,640]{1,0:T(8,128)(2,1)S(1)} %get-tuple-element.66.up_ref, bf16[128,1280]{1,0:T(8,128)(2,1)} %get-tuple-element.64.refs_0_, ...), custom_call_target="tpu_custom_call" | custom-call | flops 838860800 | bytes 4194304 | tf_op jit(solution)/shard_map/pallas_call | solution.py:41
  72.3 1.2 %collective-permute-done.17 = f32[1,1280]{1,0:T(1,128)S(1)} collective-permute-done((f32[1,1280]{1,0:T(1,128)S(1)}, f32[1,1280]{1,0:T(1,128)S(1)}, u32[]{:S(2)}, u32[]{:S(2)}) %collective-permute-start.17) | collective-permute-done | bytes 5152 | tf_op jit(solution)/shard_map/ppermute | solution.py:72
  73.5 1.6 %collective-permute-start.18 = (f32[1,1280]{1,0:T(1,128)S(1)}, f32[1,1280]{1,0:T(1,128)S(1)}, u32[]{:S(2)}, u32[]{:S(2)}) collective-permute-start(f32[1,1280]{1,0:T(1,128)S(1)} %add.15), channel_id=1, source_target_pairs={{0,1},{1,0},{2,3},{3,2},{4,5},{5,4},{6,7},{7,6},{8,9},{9,8},{10,11... | collective-permute-start | bytes 15368 | tf_op jit(solution)/shard_map/ppermute | solution.py:68
  75.0 3.8 %collective-permute-done.18 = f32[1,1280]{1,0:T(1,128)S(1)} collective-permute-done((f32[1,1280]{1,0:T(1,128)S(1)}, f32[1,1280]{1,0:T(1,128)S(1)}, u32[]{:S(2)}, u32[]{:S(2)}) %collective-permute-start.18) | collective-permute-done | bytes 5152 | tf_op jit(solution)/shard_map/ppermute | solution.py:68
  78.8 1.5 %collective-permute-start.19 = (f32[1,1280]{1,0:T(1,128)S(1)}, f32[1,1280]{1,0:T(1,128)S(1)}, u32[]{:S(2)}, u32[]{:S(2)}) collective-permute-start(f32[1,1280]{1,0:T(1,128)S(1)} %add.16), channel_id=1, source_target_pairs={{0,2},{1,3},{2,0},{3,1},{4,6},{5,7},{6,4},{7,5},{8,10},{9,11},{10,... | collective-permute-start | bytes 15368 | tf_op jit(solution)/shard_map/ppermute | solution.py:68
  80.3 2.2 %collective-permute-done.19 = f32[1,1280]{1,0:T(1,128)S(1)} collective-permute-done((f32[1,1280]{1,0:T(1,128)S(1)}, f32[1,1280]{1,0:T(1,128)S(1)}, u32[]{:S(2)}, u32[]{:S(2)}) %collective-permute-start.19) | collective-permute-done | bytes 5152 | tf_op jit(solution)/shard_map/ppermute | solution.py:68
  82.5 0.1 collective-permute-start.20
  82.6 0.9 shard_map.166
  83.5 2.1 %collective-permute-start.16 = (bf16[640,320]{1,0:T(8,128)(2,1)S(1)}, bf16[640,320]{1,0:T(8,128)(2,1)S(1)}, u32[]{:S(2)}, u32[]{:S(2)}) collective-permute-start(bf16[640,320]{1,0:T(8,128)(2,1)S(1)} %get-tuple-element.100), channel_id=1, source_target_pairs={{0,8},{4,12},{8,0},{12,4},{16,24},{20,28},{24,16},{28,20},{1,9},{5... | collective-permute-start | bytes 1228808 | tf_op jit(solution)/shard_map/ppermute | solution.py:72
  85.6 0.1 shard_map.163
  85.7 0.3 collective-permute-start.21
  86.0 0.0 copy-start.14
  86.0 4.4 %all-to-all-start.1 = ((bf16[4,128,1280]{2,1,0:T(8,128)(2,1)}), bf16[4,128,1280]{2,1,0:T(8,128)(2,1)}, u32[]{:S(2)}, u32[]{:S(2)}) async-start(bf16[4,128,1280]{2,1,0:T(8,128)(2,1)} %get-tuple-element.88), calls=%async_computation.1 | async-start | bytes 2621440 | tf_op jit(solution)/shard_map/all_to_all | solution.py:778
  90.5 3.8 %shard_map.164 = (bf16[128,1280]{1,0:T(8,128)(2,1)S(1)}, f32[128,1280]{1,0:T(8,128)S(1)}, f32[16,128,128]{2,1,0:T(8,128)S(1)}, f32[128,128]{1,0:T(8,128)S(1)}) custom-call(s32[2,2]{1,0:T(2,128)S(1)} %bitcast.31, bf16[128,1280]{1,0:T(8,128)(2,1)S(1)} %bitcast.23, bf16[128,1280]{1,0:T(8,128)(2,1)S(1)} %bitcast.26, bf16[128,1280]{1,0:T(8,128)(2,1)S(1)} %bitcast.29, ...), custom_call_target="tpu_custom_call" | custom-call | flops 2147483648 | bytes 4194304 | tf_op jit(solution)/shard_map/pallas_call | solution.py:41
  94.4 5.2 %collective-permute-done.16.got_ref = bf16[640,320]{1,0:T(8,128)(2,1)S(1)} collective-permute-done((bf16[640,320]{1,0:T(8,128)(2,1)S(1)}, bf16[640,320]{1,0:T(8,128)(2,1)S(1)}, u32[]{:S(2)}, u32[]{:S(2)}) %collective-permute-start.16) | collective-permute-done | bytes 409632 | tf_op jit(solution)/shard_map/ppermute | solution.py:72
  99.5 0.2 shard_map.167
  99.8 0.1 collective-permute-start.22
  99.9 0.7 shard_map.168
  100.6 4.6 %all-to-all-done.1.refs_0_ = bf16[4,128,1280]{2,1,0:T(8,128)(2,1)} async-done(((bf16[4,128,1280]{2,1,0:T(8,128)(2,1)}), bf16[4,128,1280]{2,1,0:T(8,128)(2,1)}, u32[]{:S(2)}, u32[]{:S(2)}) %all-to-all-start.1) | async-done | bytes 1310752 | tf_op jit(solution)/shard_map/all_to_all | solution.py:778
  105.3 6.6 %shard_map.165 = (bf16[128,1280]{1,0:T(8,128)(2,1)}, bf16[128,1280]{1,0:T(8,128)(2,1)}, bf16[128,1280]{1,0:T(8,128)(2,1)}, bf16[128,1280]{1,0:T(8,128)(2,1)}) custom-call(bf16[4,128,1280]{2,1,0:T(8,128)(2,1)} %all-to-all-done.1.refs_0_, bf16[128,1280]{1,0:T(8,128)(2,1)} %copy-done.2, f32[128,1280]{1,0:T(8,128)} %copy-done.16, f32[128,128]{1,0:T(8,128)} %copy-done.18, ...), custom_call_target="tpu_custom_call" | custom-call | flops 4294967296 | bytes 4194304 | tf_op jit(solution)/shard_map/pallas_call | solution.py:41
  111.9 0.0 collective-permute-done.22.refs_1_
  111.9 0.8 shard_map.169
  (50 shorter events, 0.1 us)
Async XLA Ops:
  0.6 8.3 %copy-start.13 = (s32[1,2,2]{2,1,0:T(2,128)S(1)}, s32[1,2,2]{2,1,0:T(2,128)}, u32[]{:S(2)}) copy-start(s32[1,2,2]{2,1,0:T(2,128)} %param.16) | copy-start | bytes 52
  0.6 8.3 %copy-start.4 = (bf16[1,128,1280]{2,1,0:T(8,128)(2,1)S(1)}, bf16[1,128,1280]{2,1,0:T(8,128)(2,1)}, u32[]{:S(2)}) copy-start(bf16[1,128,1280]{2,1,0:T(8,128)(2,1)} %param.13) | copy-start | bytes 983044
  0.7 8.2 %copy-start.10 = (bf16[1,128,1280]{2,1,0:T(8,128)(2,1)S(1)}, bf16[1,128,1280]{2,1,0:T(8,128)(2,1)}, u32[]{:S(2)}) copy-start(bf16[1,128,1280]{2,1,0:T(8,128)(2,1)} %param.12) | copy-start | bytes 983044
  0.7 8.2 %copy-start.8 = (bf16[1,128,1280]{2,1,0:T(8,128)(2,1)S(1)}, bf16[1,128,1280]{2,1,0:T(8,128)(2,1)}, u32[]{:S(2)}) copy-start(bf16[1,128,1280]{2,1,0:T(8,128)(2,1)} %param.11) | copy-start | bytes 983044
  0.7 8.2 %copy-start.6 = (bf16[1,128,1280]{2,1,0:T(8,128)(2,1)S(1)}, bf16[1,128,1280]{2,1,0:T(8,128)(2,1)}, u32[]{:S(2)}) copy-start(bf16[1,128,1280]{2,1,0:T(8,128)(2,1)} %param.10) | copy-start | bytes 983044
  4.4 14.5 %collective-permute-start = (bf16[176,640]{1,0:T(8,128)(2,1)}, bf16[176,640]{1,0:T(8,128)(2,1)S(1)}, u32[]{:S(2)}, u32[]{:S(2)}) collective-permute-start(bf16[176,640]{1,0:T(8,128)(2,1)} %get-tuple-element.59), channel_id=1, source_target_pairs={{0,1},{1,0},{2,3},{3,2},{4,5},{5,4},{6,7},{7,6},{8,9},{9,8},{10,11... | collective-permute-start | bytes 675848 | tf_op jit(solution)/shard_map/ppermute | solution.py:68
  7.4 11.5 %collective-permute-start.1 = (bf16[176,640]{1,0:T(8,128)(2,1)}, bf16[176,640]{1,0:T(8,128)(2,1)S(1)}, u32[]{:S(2)}, u32[]{:S(2)}) collective-permute-start(bf16[176,640]{1,0:T(8,128)(2,1)} %get-tuple-element.60), channel_id=1, source_target_pairs={{0,2},{1,3},{2,0},{3,1},{4,6},{5,7},{6,4},{7,5},{8,10},{9,11},{10,... | collective-permute-start | bytes 675848 | tf_op jit(solution)/shard_map/ppermute | solution.py:68
  8.9 4.5 %copy-start.20 = (bf16[176,640]{1,0:T(8,128)(2,1)S(1)}, bf16[176,640]{1,0:T(8,128)(2,1)}, u32[]{:S(2)}) copy-start(bf16[176,640]{1,0:T(8,128)(2,1)} %get-tuple-element.65) | copy-start | bytes 675844
  13.5 7.6 %copy-start.19 = (bf16[176,640]{1,0:T(8,128)(2,1)S(1)}, bf16[176,640]{1,0:T(8,128)(2,1)}, u32[]{:S(2)}) copy-start(bf16[176,640]{1,0:T(8,128)(2,1)} %get-tuple-element.58) | copy-start | bytes 675844
  13.5 7.6 %collective-permute-start.2 = (bf16[176,640]{1,0:T(8,128)(2,1)S(1)}, bf16[176,640]{1,0:T(8,128)(2,1)S(1)}, u32[]{:S(2)}, u32[]{:S(2)}) collective-permute-start(bf16[176,640]{1,0:T(8,128)(2,1)S(1)} %copy-done.20), channel_id=1, source_target_pairs={{0,3},{1,2},{2,1},{3,0},{4,7},{5,6},{6,5},{7,4},{8,11},{9,10},{10,... | collective-permute-start | bytes 675848 | tf_op jit(solution)/shard_map/ppermute | solution.py:68
  13.5 24.9 %all-to-all-start = ((bf16[8,32,1408]{2,1,0:T(8,128)(2,1)}), bf16[8,32,1408]{2,1,0:T(8,128)(2,1)S(1)}, u32[]{:S(2)}, u32[]{:S(2)}) async-start(bf16[8,32,1408]{2,1,0:T(8,128)(2,1)} %get-tuple-element.62), calls=%async_computation | async-start | bytes 1441792 | tf_op jit(solution)/shard_map/all_to_all | solution.py:743
  21.2 3.7 %collective-permute-start.3 = (bf16[4,176,640]{2,1,0:T(8,128)(2,1)S(1)}, bf16[4,176,640]{2,1,0:T(8,128)(2,1)S(1)}, u32[]{:S(2)}, u32[]{:S(2)}) collective-permute-start(bf16[4,176,640]{2,1,0:T(8,128)(2,1)S(1)} %pad_maximum_fusion.refs_1_), channel_id=1, source_target_pairs={{0,4},{4,0},{8,12},{12,8},{16,20},{20,16},{24,28},{28,24},{1,5},{5... | collective-permute-start | bytes 2703368 | tf_op jit(solution)/shard_map/ppermute | solution.py:72
  21.3 20.4 %collective-permute-start.6 = (bf16[128,1280]{1,0:T(8,128)(2,1)}, bf16[128,1280]{1,0:T(8,128)(2,1)}, u32[]{:S(2)}, u32[]{:S(2)}) collective-permute-start(bf16[128,1280]{1,0:T(8,128)(2,1)} %get-tuple-element.64.refs_0_), channel_id=1, source_target_pairs={{0,3},{1,2},{2,1},{3,0},{4,7},{5,6},{6,5},{7,4},{8,11},{9,10},{10,... | collective-permute-start | bytes 983048 | tf_op jit(solution)/shard_map/ppermute | solution.py:68
  22.0 20.2 %collective-permute-start.5 = (bf16[128,1280]{1,0:T(8,128)(2,1)}, bf16[128,1280]{1,0:T(8,128)(2,1)}, u32[]{:S(2)}, u32[]{:S(2)}) collective-permute-start(bf16[128,1280]{1,0:T(8,128)(2,1)} %get-tuple-element.64.refs_0_), channel_id=1, source_target_pairs={{0,2},{1,3},{2,0},{3,1},{4,6},{5,7},{6,4},{7,5},{8,10},{9,11},{10,... | collective-permute-start | bytes 983048 | tf_op jit(solution)/shard_map/ppermute | solution.py:68
  23.3 18.9 %collective-permute-start.4 = (bf16[128,1280]{1,0:T(8,128)(2,1)}, bf16[128,1280]{1,0:T(8,128)(2,1)}, u32[]{:S(2)}, u32[]{:S(2)}) collective-permute-start(bf16[128,1280]{1,0:T(8,128)(2,1)} %get-tuple-element.64.refs_0_), channel_id=1, source_target_pairs={{0,1},{1,0},{2,3},{3,2},{4,5},{5,4},{6,7},{7,6},{8,9},{9,8},{10,11... | collective-permute-start | bytes 983048 | tf_op jit(solution)/shard_map/ppermute | solution.py:68
  24.9 1.0 copy-start
  25.9 1.2 %copy-start.1 = (bf16[4,176,640]{2,1,0:T(8,128)(2,1)S(1)}, bf16[4,176,640]{2,1,0:T(8,128)(2,1)}, u32[]{:S(2)}) copy-start(bf16[4,176,640]{2,1,0:T(8,128)(2,1)} %copy-done) | copy-start | bytes 2703364
  28.2 17.0 %copy-start.12 = (f32[1,1280]{1,0:T(1,128)}, f32[1,1280]{1,0:T(1,128)S(1)}, u32[]{:S(2)}) copy-start(f32[1,1280]{1,0:T(1,128)S(1)} %get-tuple-element.67.gain_ref.refs_4_) | copy-start | bytes 15364
  38.7 17.4 %copy-start.2 = (bf16[128,1280]{1,0:T(8,128)(2,1)}, bf16[128,1280]{1,0:T(8,128)(2,1)S(1)}, u32[]{:S(2)}) copy-start(bf16[128,1280]{1,0:T(8,128)(2,1)S(1)} %shard_map.157.refs_0_.refs_1_) | copy-start | bytes 983044
  38.7 11.6 %collective-permute-start.9 = (bf16[128,1280]{1,0:T(8,128)(2,1)S(1)}, bf16[128,1280]{1,0:T(8,128)(2,1)S(1)}, u32[]{:S(2)}, u32[]{:S(2)}) collective-permute-start(bf16[128,1280]{1,0:T(8,128)(2,1)S(1)} %shard_map.157.refs_0_.refs_1_), channel_id=1, source_target_pairs={{0,3},{1,2},{2,1},{3,0},{4,7},{5,6},{6,5},{7,4},{8,11},{9,10},{10,... | collective-permute-start | bytes 983048 | tf_op jit(solution)/shard_map/ppermute | solution.py:68
  41.2 14.7 %collective-permute-start.8 = (bf16[128,1280]{1,0:T(8,128)(2,1)S(1)}, bf16[128,1280]{1,0:T(8,128)(2,1)S(1)}, u32[]{:S(2)}, u32[]{:S(2)}) collective-permute-start(bf16[128,1280]{1,0:T(8,128)(2,1)S(1)} %shard_map.157.refs_0_.refs_1_), channel_id=1, source_target_pairs={{0,2},{1,3},{2,0},{3,1},{4,6},{5,7},{6,4},{7,5},{8,10},{9,11},{10,... | collective-permute-start | bytes 983048 | tf_op jit(solution)/shard_map/ppermute | solution.py:68
  41.7 14.3 %collective-permute-start.7 = (bf16[128,1280]{1,0:T(8,128)(2,1)S(1)}, bf16[128,1280]{1,0:T(8,128)(2,1)S(1)}, u32[]{:S(2)}, u32[]{:S(2)}) collective-permute-start(bf16[128,1280]{1,0:T(8,128)(2,1)S(1)} %shard_map.157.refs_0_.refs_1_), channel_id=1, source_target_pairs={{0,1},{1,0},{2,3},{3,2},{4,5},{5,4},{6,7},{7,6},{8,9},{9,8},{10,11... | collective-permute-start | bytes 983048 | tf_op jit(solution)/shard_map/ppermute | solution.py:68
  42.2 13.8 %copy-start.3 = (bf16[640,1280]{1,0:T(8,128)(2,1)S(1)}, bf16[640,1280]{1,0:T(8,128)(2,1)}, u32[]{:S(2)}) copy-start(bf16[640,1280]{1,0:T(8,128)(2,1)} %down_ref.1) | copy-start | bytes 4915204
  59.1 3.0 %collective-permute-start.10 = (bf16[4,160,640]{2,1,0:T(8,128)(2,1)S(1)}, bf16[4,160,640]{2,1,0:T(8,128)(2,1)S(1)}, u32[]{:S(2)}, u32[]{:S(2)}) collective-permute-start(bf16[4,160,640]{2,1,0:T(8,128)(2,1)S(1)} %get-tuple-element.76), channel_id=1, source_target_pairs={{0,4},{4,0},{8,12},{12,8},{16,20},{20,16},{24,28},{28,24},{1,5},{5... | collective-permute-start | bytes 2457608 | tf_op jit(solution)/shard_map/ppermute | solution.py:72
  61.5 2.7 %collective-permute-start.11 = (bf16[4,320,320]{2,1,0:T(8,128)(2,1)S(1)}, bf16[4,320,320]{2,1,0:T(8,128)(2,1)S(1)}, u32[]{:S(2)}, u32[]{:S(2)}) collective-permute-start(bf16[4,320,320]{2,1,0:T(8,128)(2,1)S(1)} %get-tuple-element.79), channel_id=1, source_target_pairs={{0,4},{4,0},{8,12},{12,8},{16,20},{20,16},{24,28},{28,24},{1,5},{5... | collective-permute-start | bytes 2457608 | tf_op jit(solution)/shard_map/ppermute | solution.py:72
  62.8 22.8 %collective-permute-start.15 = (bf16[2,160,640]{2,1,0:T(8,128)(2,1)S(1)}, bf16[2,160,640]{2,1,0:T(8,128)(2,1)S(1)}, u32[]{:S(2)}, u32[]{:S(2)}) collective-permute-start(bf16[2,160,640]{2,1,0:T(8,128)(2,1)S(1)} %get-tuple-element.77), channel_id=1, source_target_pairs={{0,8},{4,12},{8,0},{12,4},{16,24},{20,28},{24,16},{28,20},{1,9},{5... | collective-permute-start | bytes 1228808 | tf_op jit(solution)/shard_map/ppermute | solution.py:72
  65.0 17.5 %collective-permute-start.12 = (bf16[320,320]{1,0:T(8,128)(2,1)S(1)}, bf16[320,320]{1,0:T(8,128)(2,1)S(1)}, u32[]{:S(2)}, u32[]{:S(2)}) collective-permute-start(bf16[320,320]{1,0:T(8,128)(2,1)S(1)} %get-tuple-element.83), channel_id=1, source_target_pairs={{0,1},{1,0},{2,3},{3,2},{4,5},{5,4},{6,7},{7,6},{8,9},{9,8},{10,11... | collective-permute-start | bytes 614408 | tf_op jit(solution)/shard_map/ppermute | solution.py:68
  66.6 15.9 %collective-permute-start.13 = (bf16[320,320]{1,0:T(8,128)(2,1)S(1)}, bf16[320,320]{1,0:T(8,128)(2,1)S(1)}, u32[]{:S(2)}, u32[]{:S(2)}) collective-permute-start(bf16[320,320]{1,0:T(8,128)(2,1)S(1)} %get-tuple-element.84), channel_id=1, source_target_pairs={{0,2},{1,3},{2,0},{3,1},{4,6},{5,7},{6,4},{7,5},{8,10},{9,11},{10,... | collective-permute-start | bytes 614408 | tf_op jit(solution)/shard_map/ppermute | solution.py:68
  67.3 15.2 %collective-permute-start.14 = (bf16[320,320]{1,0:T(8,128)(2,1)S(1)}, bf16[320,320]{1,0:T(8,128)(2,1)S(1)}, u32[]{:S(2)}, u32[]{:S(2)}) collective-permute-start(bf16[320,320]{1,0:T(8,128)(2,1)S(1)} %get-tuple-element.85), channel_id=1, source_target_pairs={{0,3},{1,2},{2,1},{3,0},{4,7},{5,6},{6,5},{7,4},{8,11},{9,10},{10,... | collective-permute-start | bytes 614408 | tf_op jit(solution)/shard_map/ppermute | solution.py:68
  72.3 1.2 %collective-permute-start.17 = (f32[1,1280]{1,0:T(1,128)S(1)}, f32[1,1280]{1,0:T(1,128)S(1)}, u32[]{:S(2)}, u32[]{:S(2)}) collective-permute-start(f32[1,1280]{1,0:T(1,128)S(1)} %get-tuple-element.101), channel_id=1, source_target_pairs={{0,4},{4,0},{8,12},{12,8},{16,20},{20,16},{24,28},{28,24},{1,5},{5... | collective-permute-start | bytes 15368 | tf_op jit(solution)/shard_map/ppermute | solution.py:72
  73.5 5.3 %collective-permute-start.18 = (f32[1,1280]{1,0:T(1,128)S(1)}, f32[1,1280]{1,0:T(1,128)S(1)}, u32[]{:S(2)}, u32[]{:S(2)}) collective-permute-start(f32[1,1280]{1,0:T(1,128)S(1)} %add.15), channel_id=1, source_target_pairs={{0,1},{1,0},{2,3},{3,2},{4,5},{5,4},{6,7},{7,6},{8,9},{9,8},{10,11... | collective-permute-start | bytes 15368 | tf_op jit(solution)/shard_map/ppermute | solution.py:68
  78.8 3.7 %collective-permute-start.19 = (f32[1,1280]{1,0:T(1,128)S(1)}, f32[1,1280]{1,0:T(1,128)S(1)}, u32[]{:S(2)}, u32[]{:S(2)}) collective-permute-start(f32[1,1280]{1,0:T(1,128)S(1)} %add.16), channel_id=1, source_target_pairs={{0,2},{1,3},{2,0},{3,1},{4,6},{5,7},{6,4},{7,5},{8,10},{9,11},{10,... | collective-permute-start | bytes 15368 | tf_op jit(solution)/shard_map/ppermute | solution.py:68
  82.5 11.9 %collective-permute-start.20 = (f32[1,1280]{1,0:T(1,128)S(1)}, f32[1,1280]{1,0:T(1,128)S(1)}, u32[]{:S(2)}, u32[]{:S(2)}) collective-permute-start(f32[1,1280]{1,0:T(1,128)S(1)} %add.17.term_ref), channel_id=1, source_target_pairs={{0,8},{4,12},{8,0},{12,4},{16,24},{20,28},{24,16},{28,20},{1,9},{5... | collective-permute-start | bytes 15368 | tf_op jit(solution)/shard_map/ppermute | solution.py:72
  83.5 16.0 %collective-permute-start.16 = (bf16[640,320]{1,0:T(8,128)(2,1)S(1)}, bf16[640,320]{1,0:T(8,128)(2,1)S(1)}, u32[]{:S(2)}, u32[]{:S(2)}) collective-permute-start(bf16[640,320]{1,0:T(8,128)(2,1)S(1)} %get-tuple-element.100), channel_id=1, source_target_pairs={{0,8},{4,12},{8,0},{12,4},{16,24},{20,28},{24,16},{28,20},{1,9},{5... | collective-permute-start | bytes 1228808 | tf_op jit(solution)/shard_map/ppermute | solution.py:72
  85.7 14.2 %collective-permute-start.21 = (bf16[160,640]{1,0:T(8,128)(2,1)S(1)}, bf16[160,640]{1,0:T(8,128)(2,1)S(1)}, u32[]{:S(2)}, u32[]{:S(2)}) collective-permute-start(bf16[160,640]{1,0:T(8,128)(2,1)S(1)} %get-tuple-element.87), channel_id=1, source_target_pairs={{0,16},{4,20},{8,24},{12,28},{16,0},{20,4},{24,8},{28,12},{1,17},{... | collective-permute-start | bytes 614408 | tf_op jit(solution)/shard_map/ppermute | solution.py:72
  86.0 4.5 %copy-start.5 = (bf16[1,128,1280]{2,1,0:T(8,128)(2,1)S(1)}, bf16[1,128,1280]{2,1,0:T(8,128)(2,1)}, u32[]{:S(2)}) copy-start(bf16[1,128,1280]{2,1,0:T(8,128)(2,1)} %param.13) | copy-start | bytes 983044
  86.0 4.5 %copy-start.7 = (bf16[1,128,1280]{2,1,0:T(8,128)(2,1)S(1)}, bf16[1,128,1280]{2,1,0:T(8,128)(2,1)}, u32[]{:S(2)}) copy-start(bf16[1,128,1280]{2,1,0:T(8,128)(2,1)} %param.10) | copy-start | bytes 983044
  86.0 4.5 %copy-start.9 = (bf16[1,128,1280]{2,1,0:T(8,128)(2,1)S(1)}, bf16[1,128,1280]{2,1,0:T(8,128)(2,1)}, u32[]{:S(2)}) copy-start(bf16[1,128,1280]{2,1,0:T(8,128)(2,1)} %param.11) | copy-start | bytes 983044
  86.0 4.5 %copy-start.11 = (bf16[1,128,1280]{2,1,0:T(8,128)(2,1)S(1)}, bf16[1,128,1280]{2,1,0:T(8,128)(2,1)}, u32[]{:S(2)}) copy-start(bf16[1,128,1280]{2,1,0:T(8,128)(2,1)} %param.12) | copy-start | bytes 983044
  86.0 4.5 %copy-start.14 = (s32[1,2,2]{2,1,0:T(2,128)S(1)}, s32[1,2,2]{2,1,0:T(2,128)}, u32[]{:S(2)}) copy-start(s32[1,2,2]{2,1,0:T(2,128)} %param.16) | copy-start | bytes 52
  86.0 19.2 %all-to-all-start.1 = ((bf16[4,128,1280]{2,1,0:T(8,128)(2,1)}), bf16[4,128,1280]{2,1,0:T(8,128)(2,1)}, u32[]{:S(2)}, u32[]{:S(2)}) async-start(bf16[4,128,1280]{2,1,0:T(8,128)(2,1)} %get-tuple-element.88), calls=%async_computation.1 | async-start | bytes 2621440 | tf_op jit(solution)/shard_map/all_to_all | solution.py:778
  94.3 5.4 %copy-start.15 = (f32[16,128,128]{2,1,0:T(8,128)}, f32[16,128,128]{2,1,0:T(8,128)S(1)}, u32[]{:S(2)}) copy-start(f32[16,128,128]{2,1,0:T(8,128)S(1)} %get-tuple-element.92.refs_5_) | copy-start | bytes 3145732
  94.3 5.4 %copy-start.16 = (f32[128,1280]{1,0:T(8,128)}, f32[128,1280]{1,0:T(8,128)S(1)}, u32[]{:S(2)}) copy-start(f32[128,1280]{1,0:T(8,128)S(1)} %get-tuple-element.90.refs_2_) | copy-start | bytes 1966084
  94.4 5.4 %copy-start.17 = (bf16[128,1280]{1,0:T(8,128)(2,1)}, bf16[128,1280]{1,0:T(8,128)(2,1)S(1)}, u32[]{:S(2)}) copy-start(bf16[128,1280]{1,0:T(8,128)(2,1)S(1)} %get-tuple-element.93.refs_6_) | copy-start | bytes 983044
  94.4 5.4 %copy-start.18 = (f32[128,128]{1,0:T(8,128)}, f32[128,128]{1,0:T(8,128)S(1)}, u32[]{:S(2)}) copy-start(f32[128,128]{1,0:T(8,128)S(1)} %get-tuple-element.91.refs_3_) | copy-start | bytes 196612
  99.8 12.1 %collective-permute-start.22 = (bf16[336,320]{1,0:T(8,128)(2,1)S(1)}, bf16[336,320]{1,0:T(8,128)(2,1)S(1)}, u32[]{:S(2)}, u32[]{:S(2)}) collective-permute-start(bf16[336,320]{1,0:T(8,128)(2,1)S(1)} %get-tuple-element.105), channel_id=1, source_target_pairs={{0,16},{4,20},{8,24},{12,28},{16,0},{20,4},{24,8},{28,12},{1,17},{... | collective-permute-start | bytes 645128 | tf_op jit(solution)/shard_map/ppermute | solution.py:72

commit v9 on v8

--- a/solution.py
+++ b/solution.py
@@ -13,7 +13,7 @@
 PIECE = 16
 CORES = 2
 LANES = 128
-VMEM_BYTES = 16 * 1024 * 1024
+VMEM_BYTES = 8 * 1024 * 1024
 MOST_BYTES = 60 * 1024 * 1024
 
 
@@ -766,7 +766,7 @@
         down_mate = swap_seq(down_give, n_seq, 1)
         up_keep, up_give = up_sides(place, up_keep, up_mate)
         up_got = swap_seq(up_give, n_seq, CORES)
-        own, *sends = down_planes(place, after(down_keep, up_give), down_mate)
+        own, *sends = down_planes(place, after(down_keep, d_pre), down_mate)
         planes = [own] + [swap_dp(block, n_dp, k + 1) for k, block in enumerate(sends)]
         parts, term = normed_parts(place, after(d_pre, own), up_cols, unit_blocks)
         term = term + swap_seq(term, n_seq, 1)

time: 113 us -> 113 us (level)
  transfers between devices with their start and end apart: 25 -> 25, of which waited for: 11 -> 11; matrix products, arithmetic and copies ran while one was open for 0% -> 0% of each run, Pallas kernels for 26% -> 25%
where the time goes in v9:
time: 113 us
  waiting for transfers between devices  41.7 us (37%)
  Pallas kernels  36.3 us (32%)
  starting transfers between devices  31.3 us (28%)
  local copies, waits for them, and re-layouts  2.22 us (2%)
    pallas_call x17, Pallas kernels, run(): pl.pallas_call(kernel if places else body, out_shape=out_shape, in_specs=...  36.3 us
    ppermute x14, waiting for transfers between devices, swap_dp(): return lax.ppermute(block, 'dp', [(i, i ^ step) for i in range(count)])  19.1 us
    ppermute x14, starting transfers between devices, swap_dp(): return lax.ppermute(block, 'dp', [(i, i ^ step) for i in range(count)])  18.3 us
    all_to_all x1, waiting for transfers between devices, per_device(): lax.all_to_all(sent, 'seq', split_axis=0, concat_axis=0, tiled=True)  10.2 us
    ppermute x9, waiting for transfers between devices, swap_seq(): return lax.ppermute(block, 'seq', [(i, i ^ step) for i in range(count)])  7.76 us
    all_to_all x1, starting transfers between devices, per_device(): lax.all_to_all(sent, 'seq', split_axis=0, concat_axis=0, tiled=True)  5.34 us
    all_to_all x1, waiting for transfers between devices, per_device(): lax.all_to_all(after(parts, *planes, up_give), 'dp', split_axis=0, concat...  4.62 us
    all_to_all x1, starting transfers between devices, per_device(): lax.all_to_all(after(parts, *planes, up_give), 'dp', split_axis=0, concat...  4.44 us
  transfers between devices with their start and end apart: 25, of which 11 were waited for; matrix products, arithmetic and copies ran while one was open for 0% of the time, Pallas kernels for 25%

profile of v9, /device:TPU:0, one launch (start us, length us, event | category | flops | bytes accessed | tf_op | source)
XLA Modules:
  0.0 112.7 jit_solution(5541224950843380257)
XLA Ops:
  0.6 0.0 copy-start.13
  0.6 0.0 copy-start.4
  0.7 0.0 copy-start.10
  0.7 0.0 copy-start.8
  0.7 3.7 %shard_map.153 = (bf16[8,32,1408]{2,1,0:T(8,128)(2,1)}, bf16[176,640]{1,0:T(8,128)(2,1)}, bf16[176,640]{1,0:T(8,128)(2,1)}, bf16[176,640]{1,0:T(8,128)(2,1)}, bf16[176,640]{1,0:T(8,128)(2,1)}) custom-call(s32[1,192]{1,0:T(1,128)} %refs_0_.1, bf16[320]{0:T(512)(128)(2,1)} %refs_1_.1, bf16[192,1280]{1,0:T(8,128)(2,1)} %bitcast.32, bf16[320,2560]{1,0:T(8,128)(2,1)} %refs_3_.1), custom_call_target="tpu_custom_call" | custom-call | flops 1048576 | bytes 4194304 | tf_op jit(solution)/shard_map/pallas_call | solution.py:41
  4.4 3.0 %collective-permute-start = (bf16[176,640]{1,0:T(8,128)(2,1)}, bf16[176,640]{1,0:T(8,128)(2,1)S(1)}, u32[]{:S(2)}, u32[]{:S(2)}) collective-permute-start(bf16[176,640]{1,0:T(8,128)(2,1)} %get-tuple-element.59), channel_id=1, source_target_pairs={{0,1},{1,0},{2,3},{3,2},{4,5},{5,4},{6,7},{7,6},{8,9},{9,8},{10,11... | collective-permute-start | bytes 675848 | tf_op jit(solution)/shard_map/ppermute | solution.py:68
  7.4 1.5 %collective-permute-start.1 = (bf16[176,640]{1,0:T(8,128)(2,1)}, bf16[176,640]{1,0:T(8,128)(2,1)S(1)}, u32[]{:S(2)}, u32[]{:S(2)}) collective-permute-start(bf16[176,640]{1,0:T(8,128)(2,1)} %get-tuple-element.60), channel_id=1, source_target_pairs={{0,2},{1,3},{2,0},{3,1},{4,6},{5,7},{6,4},{7,5},{8,10},{9,11},{10,... | collective-permute-start | bytes 675848 | tf_op jit(solution)/shard_map/ppermute | solution.py:68
  8.9 4.5 %shard_map.154 = (bf16[128,1280]{1,0:T(8,128)(2,1)}, bf16[128,1280]{1,0:T(8,128)(2,1)}) custom-call(s32[2,2]{1,0:T(2,128)S(1)} %bitcast.30, bf16[128,1280]{1,0:T(8,128)(2,1)S(1)} %bitcast.22, bf16[128,1280]{1,0:T(8,128)(2,1)S(1)} %bitcast.25, bf16[128,1280]{1,0:T(8,128)(2,1)S(1)} %bitcast.28, bf16[128,1280]{1,0:T(8,128)(2,1)S(1)} %bitcast.19), custom_call_target="tpu_custom_call" | custom-call | flops 2147483648 | bytes 4194304 | tf_op jit(solution)/shard_map/pallas_call | solution.py:41
  13.5 0.0 collective-permute-start.2
  13.5 5.3 %all-to-all-start = ((bf16[8,32,1408]{2,1,0:T(8,128)(2,1)}), bf16[8,32,1408]{2,1,0:T(8,128)(2,1)S(1)}, u32[]{:S(2)}, u32[]{:S(2)}) async-start(bf16[8,32,1408]{2,1,0:T(8,128)(2,1)} %get-tuple-element.62), calls=%async_computation | async-start | bytes 1441792 | tf_op jit(solution)/shard_map/all_to_all | solution.py:743
  18.8 2.2 %collective-permute-done.2 = bf16[176,640]{1,0:T(8,128)(2,1)S(1)} collective-permute-done((bf16[176,640]{1,0:T(8,128)(2,1)S(1)}, bf16[176,640]{1,0:T(8,128)(2,1)S(1)}, u32[]{:S(2)}, u32[]{:S(2)}) %collective-permute-start.2) | collective-permute-done | bytes 225312 | tf_op jit(solution)/shard_map/ppermute | solution.py:68
  21.1 0.1 pad_maximum_fusion.refs_1_
  21.2 0.1 collective-permute-start.3
  21.3 0.7 collective-permute-start.6
  22.0 1.3 %collective-permute-start.5 = (bf16[128,1280]{1,0:T(8,128)(2,1)}, bf16[128,1280]{1,0:T(8,128)(2,1)}, u32[]{:S(2)}, u32[]{:S(2)}) collective-permute-start(bf16[128,1280]{1,0:T(8,128)(2,1)} %get-tuple-element.64.refs_0_), channel_id=1, source_target_pairs={{0,2},{1,3},{2,0},{3,1},{4,6},{5,7},{6,4},{7,5},{8,10},{9,11},{10,... | collective-permute-start | bytes 983048 | tf_op jit(solution)/shard_map/ppermute | solution.py:68
  23.3 1.5 %collective-permute-start.4 = (bf16[128,1280]{1,0:T(8,128)(2,1)}, bf16[128,1280]{1,0:T(8,128)(2,1)}, u32[]{:S(2)}, u32[]{:S(2)}) collective-permute-start(bf16[128,1280]{1,0:T(8,128)(2,1)} %get-tuple-element.64.refs_0_), channel_id=1, source_target_pairs={{0,1},{1,0},{2,3},{3,2},{4,5},{5,4},{6,7},{7,6},{8,9},{9,8},{10,11... | collective-permute-start | bytes 983048 | tf_op jit(solution)/shard_map/ppermute | solution.py:68
  24.8 0.1 pad_add_fusion.refs_0_.place_ref
  24.9 0.9 copy-done
  25.9 1.2 %copy-done.1 = bf16[4,176,640]{2,1,0:T(8,128)(2,1)S(1)} copy-done((bf16[4,176,640]{2,1,0:T(8,128)(2,1)S(1)}, bf16[4,176,640]{2,1,0:T(8,128)(2,1)}, u32[]{:S(2)}) %copy-start.1) | copy-done | bytes 901144
  27.0 1.1 shard_map.155
  28.2 0.0 copy-start.12
  28.2 10.2 %all-to-all-done = bf16[8,32,1408]{2,1,0:T(8,128)(2,1)S(1)} async-done(((bf16[8,32,1408]{2,1,0:T(8,128)(2,1)}), bf16[8,32,1408]{2,1,0:T(8,128)(2,1)S(1)}, u32[]{:S(2)}, u32[]{:S(2)}) %all-to-all-start) | async-done | bytes 720928 | tf_op jit(solution)/shard_map/all_to_all | solution.py:743
  38.4 0.3 shard_map.157.refs_0_.refs_1_
  38.7 2.5 %collective-permute-start.9 = (bf16[128,1280]{1,0:T(8,128)(2,1)S(1)}, bf16[128,1280]{1,0:T(8,128)(2,1)S(1)}, u32[]{:S(2)}, u32[]{:S(2)}) collective-permute-start(bf16[128,1280]{1,0:T(8,128)(2,1)S(1)} %shard_map.157.refs_0_.refs_1_), channel_id=1, source_target_pairs={{0,3},{1,2},{2,1},{3,0},{4,7},{5,6},{6,5},{7,4},{8,11},{9,10},{10,... | collective-permute-start | bytes 983048 | tf_op jit(solution)/shard_map/ppermute | solution.py:68
  41.2 0.5 collective-permute-start.8
  41.7 0.5 collective-permute-start.7
  42.3 2.9 %shard_map.156 = (bf16[640,512]{1,0:T(8,128)(2,1)S(1)}, f32[512,640]{1,0:T(8,128)S(1)}, bf16[1280,512]{1,0:T(8,128)(2,1)S(1)}, bf16[512,1280]{1,0:T(8,128)(2,1)}) custom-call(bf16[1280,640]{1,0:T(8,128)(2,1)S(1)} %get-tuple-element.66.up_ref, f32[1,1280]{1,0:T(1,128)S(1)} %get-tuple-element.67.gain_ref.refs_4_, bf16[128,1280]{1,0:T(8,128)(2,1)} %get-tuple-element.64.refs_0_, ...), custom_call_target="tpu_custom_call" | custom-call | flops 838860800 | bytes 4194304 | tf_op jit(solution)/shard_map/pallas_call | solution.py:41
  45.2 5.2 %collective-permute-done.9.refs_3_ = bf16[128,1280]{1,0:T(8,128)(2,1)S(1)} collective-permute-done((bf16[128,1280]{1,0:T(8,128)(2,1)S(1)}, bf16[128,1280]{1,0:T(8,128)(2,1)S(1)}, u32[]{:S(2)}, u32[]{:S(2)}) %collective-permute-start.9) | collective-permute-done | bytes 327712 | tf_op jit(solution)/shard_map/ppermute | solution.py:68
  50.3 5.6 %collective-permute-done.8.refs_2_ = bf16[128,1280]{1,0:T(8,128)(2,1)S(1)} collective-permute-done((bf16[128,1280]{1,0:T(8,128)(2,1)S(1)}, bf16[128,1280]{1,0:T(8,128)(2,1)S(1)}, u32[]{:S(2)}, u32[]{:S(2)}) %collective-permute-start.8) | collective-permute-done | bytes 327712 | tf_op jit(solution)/shard_map/ppermute | solution.py:68
  55.9 0.1 collective-permute-done.7.refs_1_
  56.0 3.1 %shard_map.158 = (bf16[512,1280]{1,0:T(8,128)(2,1)S(1)}, bf16[512,640]{1,0:T(8,128)(2,1)S(1)}, bf16[4,160,640]{2,1,0:T(8,128)(2,1)S(1)}, bf16[4,160,640]{2,1,0:T(8,128)(2,1)S(1)}) custom-call(s32[3]{0:T(128)S(1)} %pad_add_fusion.refs_0_.place_ref, bf16[640,1280]{1,0:T(8,128)(2,1)S(1)} %copy-done.3, f32[512,640]{1,0:T(8,128)S(1)} %get-tuple-element.68.slope_ref, ...), custom_call_target="tpu_custom_call" | custom-call | flops 1677721600 | bytes 4194304 | tf_op jit(solution)/shard_map/pallas_call | solution.py:41
  59.1 0.1 collective-permute-start.14
  59.2 2.3 %shard_map.159 = (bf16[4,320,320]{2,1,0:T(8,128)(2,1)S(1)}, bf16[4,320,320]{2,1,0:T(8,128)(2,1)S(1)}) custom-call(s32[3]{0:T(128)S(1)} %pad_add_fusion.refs_0_.place_ref, bf16[640,512]{1,0:T(8,128)(2,1)S(1)} %get-tuple-element.72.act_ref, bf16[512,1280]{1,0:T(8,128)(2,1)S(1)} %get-tuple-element.73.rows_ref), custom_call_target="tpu_custom_call" | custom-call | flops 838860800 | bytes 4194304 | tf_op jit(solution)/shard_map/pallas_call | solution.py:41
  61.5 0.6 collective-permute-start.10
  62.1 0.7 shard_map.162
  62.8 0.1 collective-permute-start.15
  62.9 1.4 %collective-permute-done.10.mate_ref = bf16[4,320,320]{2,1,0:T(8,128)(2,1)S(1)} collective-permute-done((bf16[4,320,320]{2,1,0:T(8,128)(2,1)S(1)}, bf16[4,320,320]{2,1,0:T(8,128)(2,1)S(1)}, u32[]{:S(2)}, u32[]{:S(2)}) %collective-permute-start.10) | collective-permute-done | bytes 819232 | tf_op jit(solution)/shard_map/ppermute | solution.py:72
  64.3 0.8 shard_map.160
  65.0 1.6 %collective-permute-start.11 = (bf16[320,320]{1,0:T(8,128)(2,1)S(1)}, bf16[320,320]{1,0:T(8,128)(2,1)S(1)}, u32[]{:S(2)}, u32[]{:S(2)}) collective-permute-start(bf16[320,320]{1,0:T(8,128)(2,1)S(1)} %get-tuple-element.80), channel_id=1, source_target_pairs={{0,1},{1,0},{2,3},{3,2},{4,5},{5,4},{6,7},{7,6},{8,9},{9,8},{10,11... | collective-permute-start | bytes 614408 | tf_op jit(solution)/shard_map/ppermute | solution.py:68
  66.6 0.7 collective-permute-start.12
  67.3 1.3 %collective-permute-start.13 = (bf16[320,320]{1,0:T(8,128)(2,1)S(1)}, bf16[320,320]{1,0:T(8,128)(2,1)S(1)}, u32[]{:S(2)}, u32[]{:S(2)}) collective-permute-start(bf16[320,320]{1,0:T(8,128)(2,1)S(1)} %get-tuple-element.82), channel_id=1, source_target_pairs={{0,3},{1,2},{2,1},{3,0},{4,7},{5,6},{6,5},{7,4},{8,11},{9,10},{10,... | collective-permute-start | bytes 614408 | tf_op jit(solution)/shard_map/ppermute | solution.py:68
  68.6 3.7 %shard_map.161 = (bf16[4,128,1280]{2,1,0:T(8,128)(2,1)}, f32[1,1280]{1,0:T(1,128)S(1)}) custom-call(s32[3]{0:T(128)S(1)} %pad_add_fusion.refs_0_.place_ref, bf16[512,640]{1,0:T(8,128)(2,1)S(1)} %get-tuple-element.78.pre_ref, bf16[1280,640]{1,0:T(8,128)(2,1)S(1)} %get-tuple-element.66.up_ref, bf16[128,1280]{1,0:T(8,128)(2,1)} %get-tuple-element.64.refs_0_, ...), custom_call_target="tpu_custom_call" | custom-call | flops 838860800 | bytes 4194304 | tf_op jit(solution)/shard_map/pallas_call | solution.py:41
  72.3 1.2 %collective-permute-done.17 = f32[1,1280]{1,0:T(1,128)S(1)} collective-permute-done((f32[1,1280]{1,0:T(1,128)S(1)}, f32[1,1280]{1,0:T(1,128)S(1)}, u32[]{:S(2)}, u32[]{:S(2)}) %collective-permute-start.17) | collective-permute-done | bytes 5152 | tf_op jit(solution)/shard_map/ppermute | solution.py:72
  73.5 1.6 %collective-permute-start.18 = (f32[1,1280]{1,0:T(1,128)S(1)}, f32[1,1280]{1,0:T(1,128)S(1)}, u32[]{:S(2)}, u32[]{:S(2)}) collective-permute-start(f32[1,1280]{1,0:T(1,128)S(1)} %add.15), channel_id=1, source_target_pairs={{0,1},{1,0},{2,3},{3,2},{4,5},{5,4},{6,7},{7,6},{8,9},{9,8},{10,11... | collective-permute-start | bytes 15368 | tf_op jit(solution)/shard_map/ppermute | solution.py:68
  75.0 3.8 %collective-permute-done.18 = f32[1,1280]{1,0:T(1,128)S(1)} collective-permute-done((f32[1,1280]{1,0:T(1,128)S(1)}, f32[1,1280]{1,0:T(1,128)S(1)}, u32[]{:S(2)}, u32[]{:S(2)}) %collective-permute-start.18) | collective-permute-done | bytes 5152 | tf_op jit(solution)/shard_map/ppermute | solution.py:68
  78.8 1.5 %collective-permute-start.19 = (f32[1,1280]{1,0:T(1,128)S(1)}, f32[1,1280]{1,0:T(1,128)S(1)}, u32[]{:S(2)}, u32[]{:S(2)}) collective-permute-start(f32[1,1280]{1,0:T(1,128)S(1)} %add.16), channel_id=1, source_target_pairs={{0,2},{1,3},{2,0},{3,1},{4,6},{5,7},{6,4},{7,5},{8,10},{9,11},{10,... | collective-permute-start | bytes 15368 | tf_op jit(solution)/shard_map/ppermute | solution.py:68
  80.3 2.2 %collective-permute-done.19 = f32[1,1280]{1,0:T(1,128)S(1)} collective-permute-done((f32[1,1280]{1,0:T(1,128)S(1)}, f32[1,1280]{1,0:T(1,128)S(1)}, u32[]{:S(2)}, u32[]{:S(2)}) %collective-permute-start.19) | collective-permute-done | bytes 5152 | tf_op jit(solution)/shard_map/ppermute | solution.py:68
  82.5 0.1 collective-permute-start.20
  82.6 0.9 shard_map.166
  83.5 2.1 %collective-permute-start.16 = (bf16[640,320]{1,0:T(8,128)(2,1)S(1)}, bf16[640,320]{1,0:T(8,128)(2,1)S(1)}, u32[]{:S(2)}, u32[]{:S(2)}) collective-permute-start(bf16[640,320]{1,0:T(8,128)(2,1)S(1)} %get-tuple-element.100), channel_id=1, source_target_pairs={{0,8},{4,12},{8,0},{12,4},{16,24},{20,28},{24,16},{28,20},{1,9},{5... | collective-permute-start | bytes 1228808 | tf_op jit(solution)/shard_map/ppermute | solution.py:72
  85.6 0.1 shard_map.163
  85.7 0.3 collective-permute-start.21
  86.0 0.0 copy-start.14
  86.0 4.4 %all-to-all-start.1 = ((bf16[4,128,1280]{2,1,0:T(8,128)(2,1)}), bf16[4,128,1280]{2,1,0:T(8,128)(2,1)}, u32[]{:S(2)}, u32[]{:S(2)}) async-start(bf16[4,128,1280]{2,1,0:T(8,128)(2,1)} %get-tuple-element.88), calls=%async_computation.1 | async-start | bytes 2621440 | tf_op jit(solution)/shard_map/all_to_all | solution.py:778
  90.5 3.8 %shard_map.164 = (bf16[128,1280]{1,0:T(8,128)(2,1)S(1)}, f32[128,1280]{1,0:T(8,128)S(1)}, f32[16,128,128]{2,1,0:T(8,128)S(1)}, f32[128,128]{1,0:T(8,128)S(1)}) custom-call(s32[2,2]{1,0:T(2,128)S(1)} %bitcast.31, bf16[128,1280]{1,0:T(8,128)(2,1)S(1)} %bitcast.23, bf16[128,1280]{1,0:T(8,128)(2,1)S(1)} %bitcast.26, bf16[128,1280]{1,0:T(8,128)(2,1)S(1)} %bitcast.29, ...), custom_call_target="tpu_custom_call" | custom-call | flops 2147483648 | bytes 4194304 | tf_op jit(solution)/shard_map/pallas_call | solution.py:41
  94.3 0.0 copy-start.18
  94.4 5.2 %collective-permute-done.16.got_ref = bf16[640,320]{1,0:T(8,128)(2,1)S(1)} collective-permute-done((bf16[640,320]{1,0:T(8,128)(2,1)S(1)}, bf16[640,320]{1,0:T(8,128)(2,1)S(1)}, u32[]{:S(2)}, u32[]{:S(2)}) %collective-permute-start.16) | collective-permute-done | bytes 409632 | tf_op jit(solution)/shard_map/ppermute | solution.py:72
  99.5 0.2 shard_map.167
  99.8 0.1 collective-permute-start.22
  99.9 0.7 shard_map.168
  100.6 4.6 %all-to-all-done.1.refs_0_ = bf16[4,128,1280]{2,1,0:T(8,128)(2,1)} async-done(((bf16[4,128,1280]{2,1,0:T(8,128)(2,1)}), bf16[4,128,1280]{2,1,0:T(8,128)(2,1)}, u32[]{:S(2)}, u32[]{:S(2)}) %all-to-all-start.1) | async-done | bytes 1310752 | tf_op jit(solution)/shard_map/all_to_all | solution.py:778
  105.3 6.6 %shard_map.165 = (bf16[128,1280]{1,0:T(8,128)(2,1)}, bf16[128,1280]{1,0:T(8,128)(2,1)}, bf16[128,1280]{1,0:T(8,128)(2,1)}, bf16[128,1280]{1,0:T(8,128)(2,1)}) custom-call(bf16[4,128,1280]{2,1,0:T(8,128)(2,1)} %all-to-all-done.1.refs_0_, bf16[128,1280]{1,0:T(8,128)(2,1)} %copy-done.2, f32[128,1280]{1,0:T(8,128)} %copy-done.16, f32[128,128]{1,0:T(8,128)} %copy-done.18, ...), custom_call_target="tpu_custom_call" | custom-call | flops 4294967296 | bytes 4194304 | tf_op jit(solution)/shard_map/pallas_call | solution.py:41
  111.9 0.0 collective-permute-done.22.refs_1_
  111.9 0.8 shard_map.169
  (50 shorter events, 0.1 us)
Async XLA Ops:
  0.6 8.3 %copy-start.13 = (s32[1,2,2]{2,1,0:T(2,128)S(1)}, s32[1,2,2]{2,1,0:T(2,128)}, u32[]{:S(2)}) copy-start(s32[1,2,2]{2,1,0:T(2,128)} %param.16) | copy-start | bytes 52
  0.6 8.3 %copy-start.4 = (bf16[1,128,1280]{2,1,0:T(8,128)(2,1)S(1)}, bf16[1,128,1280]{2,1,0:T(8,128)(2,1)}, u32[]{:S(2)}) copy-start(bf16[1,128,1280]{2,1,0:T(8,128)(2,1)} %param.13) | copy-start | bytes 983044
  0.7 8.2 %copy-start.10 = (bf16[1,128,1280]{2,1,0:T(8,128)(2,1)S(1)}, bf16[1,128,1280]{2,1,0:T(8,128)(2,1)}, u32[]{:S(2)}) copy-start(bf16[1,128,1280]{2,1,0:T(8,128)(2,1)} %param.12) | copy-start | bytes 983044
  0.7 8.2 %copy-start.8 = (bf16[1,128,1280]{2,1,0:T(8,128)(2,1)S(1)}, bf16[1,128,1280]{2,1,0:T(8,128)(2,1)}, u32[]{:S(2)}) copy-start(bf16[1,128,1280]{2,1,0:T(8,128)(2,1)} %param.11) | copy-start | bytes 983044
  0.7 8.2 %copy-start.6 = (bf16[1,128,1280]{2,1,0:T(8,128)(2,1)S(1)}, bf16[1,128,1280]{2,1,0:T(8,128)(2,1)}, u32[]{:S(2)}) copy-start(bf16[1,128,1280]{2,1,0:T(8,128)(2,1)} %param.10) | copy-start | bytes 983044
  4.4 14.5 %collective-permute-start = (bf16[176,640]{1,0:T(8,128)(2,1)}, bf16[176,640]{1,0:T(8,128)(2,1)S(1)}, u32[]{:S(2)}, u32[]{:S(2)}) collective-permute-start(bf16[176,640]{1,0:T(8,128)(2,1)} %get-tuple-element.59), channel_id=1, source_target_pairs={{0,1},{1,0},{2,3},{3,2},{4,5},{5,4},{6,7},{7,6},{8,9},{9,8},{10,11... | collective-permute-start | bytes 675848 | tf_op jit(solution)/shard_map/ppermute | solution.py:68
  7.4 11.5 %collective-permute-start.1 = (bf16[176,640]{1,0:T(8,128)(2,1)}, bf16[176,640]{1,0:T(8,128)(2,1)S(1)}, u32[]{:S(2)}, u32[]{:S(2)}) collective-permute-start(bf16[176,640]{1,0:T(8,128)(2,1)} %get-tuple-element.60), channel_id=1, source_target_pairs={{0,2},{1,3},{2,0},{3,1},{4,6},{5,7},{6,4},{7,5},{8,10},{9,11},{10,... | collective-permute-start | bytes 675848 | tf_op jit(solution)/shard_map/ppermute | solution.py:68
  8.9 4.5 %copy-start.20 = (bf16[176,640]{1,0:T(8,128)(2,1)S(1)}, bf16[176,640]{1,0:T(8,128)(2,1)}, u32[]{:S(2)}) copy-start(bf16[176,640]{1,0:T(8,128)(2,1)} %get-tuple-element.65) | copy-start | bytes 675844
  13.5 7.6 %copy-start.19 = (bf16[176,640]{1,0:T(8,128)(2,1)S(1)}, bf16[176,640]{1,0:T(8,128)(2,1)}, u32[]{:S(2)}) copy-start(bf16[176,640]{1,0:T(8,128)(2,1)} %get-tuple-element.58) | copy-start | bytes 675844
  13.5 7.6 %collective-permute-start.2 = (bf16[176,640]{1,0:T(8,128)(2,1)S(1)}, bf16[176,640]{1,0:T(8,128)(2,1)S(1)}, u32[]{:S(2)}, u32[]{:S(2)}) collective-permute-start(bf16[176,640]{1,0:T(8,128)(2,1)S(1)} %copy-done.20), channel_id=1, source_target_pairs={{0,3},{1,2},{2,1},{3,0},{4,7},{5,6},{6,5},{7,4},{8,11},{9,10},{10,... | collective-permute-start | bytes 675848 | tf_op jit(solution)/shard_map/ppermute | solution.py:68
  13.5 24.9 %all-to-all-start = ((bf16[8,32,1408]{2,1,0:T(8,128)(2,1)}), bf16[8,32,1408]{2,1,0:T(8,128)(2,1)S(1)}, u32[]{:S(2)}, u32[]{:S(2)}) async-start(bf16[8,32,1408]{2,1,0:T(8,128)(2,1)} %get-tuple-element.62), calls=%async_computation | async-start | bytes 1441792 | tf_op jit(solution)/shard_map/all_to_all | solution.py:743
  21.2 3.7 %collective-permute-start.3 = (bf16[4,176,640]{2,1,0:T(8,128)(2,1)S(1)}, bf16[4,176,640]{2,1,0:T(8,128)(2,1)S(1)}, u32[]{:S(2)}, u32[]{:S(2)}) collective-permute-start(bf16[4,176,640]{2,1,0:T(8,128)(2,1)S(1)} %pad_maximum_fusion.refs_1_), channel_id=1, source_target_pairs={{0,4},{4,0},{8,12},{12,8},{16,20},{20,16},{24,28},{28,24},{1,5},{5... | collective-permute-start | bytes 2703368 | tf_op jit(solution)/shard_map/ppermute | solution.py:72
  21.3 20.4 %collective-permute-start.6 = (bf16[128,1280]{1,0:T(8,128)(2,1)}, bf16[128,1280]{1,0:T(8,128)(2,1)}, u32[]{:S(2)}, u32[]{:S(2)}) collective-permute-start(bf16[128,1280]{1,0:T(8,128)(2,1)} %get-tuple-element.64.refs_0_), channel_id=1, source_target_pairs={{0,3},{1,2},{2,1},{3,0},{4,7},{5,6},{6,5},{7,4},{8,11},{9,10},{10,... | collective-permute-start | bytes 983048 | tf_op jit(solution)/shard_map/ppermute | solution.py:68
  22.0 20.2 %collective-permute-start.5 = (bf16[128,1280]{1,0:T(8,128)(2,1)}, bf16[128,1280]{1,0:T(8,128)(2,1)}, u32[]{:S(2)}, u32[]{:S(2)}) collective-permute-start(bf16[128,1280]{1,0:T(8,128)(2,1)} %get-tuple-element.64.refs_0_), channel_id=1, source_target_pairs={{0,2},{1,3},{2,0},{3,1},{4,6},{5,7},{6,4},{7,5},{8,10},{9,11},{10,... | collective-permute-start | bytes 983048 | tf_op jit(solution)/shard_map/ppermute | solution.py:68
  23.3 18.9 %collective-permute-start.4 = (bf16[128,1280]{1,0:T(8,128)(2,1)}, bf16[128,1280]{1,0:T(8,128)(2,1)}, u32[]{:S(2)}, u32[]{:S(2)}) collective-permute-start(bf16[128,1280]{1,0:T(8,128)(2,1)} %get-tuple-element.64.refs_0_), channel_id=1, source_target_pairs={{0,1},{1,0},{2,3},{3,2},{4,5},{5,4},{6,7},{7,6},{8,9},{9,8},{10,11... | collective-permute-start | bytes 983048 | tf_op jit(solution)/shard_map/ppermute | solution.py:68
  24.9 1.0 copy-start
  25.9 1.2 %copy-start.1 = (bf16[4,176,640]{2,1,0:T(8,128)(2,1)S(1)}, bf16[4,176,640]{2,1,0:T(8,128)(2,1)}, u32[]{:S(2)}) copy-start(bf16[4,176,640]{2,1,0:T(8,128)(2,1)} %copy-done) | copy-start | bytes 2703364
  28.2 17.0 %copy-start.12 = (f32[1,1280]{1,0:T(1,128)}, f32[1,1280]{1,0:T(1,128)S(1)}, u32[]{:S(2)}) copy-start(f32[1,1280]{1,0:T(1,128)S(1)} %get-tuple-element.67.gain_ref.refs_4_) | copy-start | bytes 15364
  38.7 17.4 %copy-start.2 = (bf16[128,1280]{1,0:T(8,128)(2,1)}, bf16[128,1280]{1,0:T(8,128)(2,1)S(1)}, u32[]{:S(2)}) copy-start(bf16[128,1280]{1,0:T(8,128)(2,1)S(1)} %shard_map.157.refs_0_.refs_1_) | copy-start | bytes 983044
  38.7 11.6 %collective-permute-start.9 = (bf16[128,1280]{1,0:T(8,128)(2,1)S(1)}, bf16[128,1280]{1,0:T(8,128)(2,1)S(1)}, u32[]{:S(2)}, u32[]{:S(2)}) collective-permute-start(bf16[128,1280]{1,0:T(8,128)(2,1)S(1)} %shard_map.157.refs_0_.refs_1_), channel_id=1, source_target_pairs={{0,3},{1,2},{2,1},{3,0},{4,7},{5,6},{6,5},{7,4},{8,11},{9,10},{10,... | collective-permute-start | bytes 983048 | tf_op jit(solution)/shard_map/ppermute | solution.py:68
  41.2 14.7 %collective-permute-start.8 = (bf16[128,1280]{1,0:T(8,128)(2,1)S(1)}, bf16[128,1280]{1,0:T(8,128)(2,1)S(1)}, u32[]{:S(2)}, u32[]{:S(2)}) collective-permute-start(bf16[128,1280]{1,0:T(8,128)(2,1)S(1)} %shard_map.157.refs_0_.refs_1_), channel_id=1, source_target_pairs={{0,2},{1,3},{2,0},{3,1},{4,6},{5,7},{6,4},{7,5},{8,10},{9,11},{10,... | collective-permute-start | bytes 983048 | tf_op jit(solution)/shard_map/ppermute | solution.py:68
  41.7 14.3 %collective-permute-start.7 = (bf16[128,1280]{1,0:T(8,128)(2,1)S(1)}, bf16[128,1280]{1,0:T(8,128)(2,1)S(1)}, u32[]{:S(2)}, u32[]{:S(2)}) collective-permute-start(bf16[128,1280]{1,0:T(8,128)(2,1)S(1)} %shard_map.157.refs_0_.refs_1_), channel_id=1, source_target_pairs={{0,1},{1,0},{2,3},{3,2},{4,5},{5,4},{6,7},{7,6},{8,9},{9,8},{10,11... | collective-permute-start | bytes 983048 | tf_op jit(solution)/shard_map/ppermute | solution.py:68
  42.2 13.8 %copy-start.3 = (bf16[640,1280]{1,0:T(8,128)(2,1)S(1)}, bf16[640,1280]{1,0:T(8,128)(2,1)}, u32[]{:S(2)}) copy-start(bf16[640,1280]{1,0:T(8,128)(2,1)} %down_ref.1) | copy-start | bytes 4915204
  59.1 3.0 %collective-permute-start.14 = (bf16[4,160,640]{2,1,0:T(8,128)(2,1)S(1)}, bf16[4,160,640]{2,1,0:T(8,128)(2,1)S(1)}, u32[]{:S(2)}, u32[]{:S(2)}) collective-permute-start(bf16[4,160,640]{2,1,0:T(8,128)(2,1)S(1)} %get-tuple-element.84), channel_id=1, source_target_pairs={{0,4},{4,0},{8,12},{12,8},{16,20},{20,16},{24,28},{28,24},{1,5},{5... | collective-permute-start | bytes 2457608 | tf_op jit(solution)/shard_map/ppermute | solution.py:72
  61.5 2.7 %collective-permute-start.10 = (bf16[4,320,320]{2,1,0:T(8,128)(2,1)S(1)}, bf16[4,320,320]{2,1,0:T(8,128)(2,1)S(1)}, u32[]{:S(2)}, u32[]{:S(2)}) collective-permute-start(bf16[4,320,320]{2,1,0:T(8,128)(2,1)S(1)} %get-tuple-element.76), channel_id=1, source_target_pairs={{0,4},{4,0},{8,12},{12,8},{16,20},{20,16},{24,28},{28,24},{1,5},{5... | collective-permute-start | bytes 2457608 | tf_op jit(solution)/shard_map/ppermute | solution.py:72
  62.8 22.8 %collective-permute-start.15 = (bf16[2,160,640]{2,1,0:T(8,128)(2,1)S(1)}, bf16[2,160,640]{2,1,0:T(8,128)(2,1)S(1)}, u32[]{:S(2)}, u32[]{:S(2)}) collective-permute-start(bf16[2,160,640]{2,1,0:T(8,128)(2,1)S(1)} %get-tuple-element.86), channel_id=1, source_target_pairs={{0,8},{4,12},{8,0},{12,4},{16,24},{20,28},{24,16},{28,20},{1,9},{5... | collective-permute-start | bytes 1228808 | tf_op jit(solution)/shard_map/ppermute | solution.py:72
  65.0 17.5 %collective-permute-start.11 = (bf16[320,320]{1,0:T(8,128)(2,1)S(1)}, bf16[320,320]{1,0:T(8,128)(2,1)S(1)}, u32[]{:S(2)}, u32[]{:S(2)}) collective-permute-start(bf16[320,320]{1,0:T(8,128)(2,1)S(1)} %get-tuple-element.80), channel_id=1, source_target_pairs={{0,1},{1,0},{2,3},{3,2},{4,5},{5,4},{6,7},{7,6},{8,9},{9,8},{10,11... | collective-permute-start | bytes 614408 | tf_op jit(solution)/shard_map/ppermute | solution.py:68
  66.6 15.9 %collective-permute-start.12 = (bf16[320,320]{1,0:T(8,128)(2,1)S(1)}, bf16[320,320]{1,0:T(8,128)(2,1)S(1)}, u32[]{:S(2)}, u32[]{:S(2)}) collective-permute-start(bf16[320,320]{1,0:T(8,128)(2,1)S(1)} %get-tuple-element.81), channel_id=1, source_target_pairs={{0,2},{1,3},{2,0},{3,1},{4,6},{5,7},{6,4},{7,5},{8,10},{9,11},{10,... | collective-permute-start | bytes 614408 | tf_op jit(solution)/shard_map/ppermute | solution.py:68
  67.3 15.2 %collective-permute-start.13 = (bf16[320,320]{1,0:T(8,128)(2,1)S(1)}, bf16[320,320]{1,0:T(8,128)(2,1)S(1)}, u32[]{:S(2)}, u32[]{:S(2)}) collective-permute-start(bf16[320,320]{1,0:T(8,128)(2,1)S(1)} %get-tuple-element.82), channel_id=1, source_target_pairs={{0,3},{1,2},{2,1},{3,0},{4,7},{5,6},{6,5},{7,4},{8,11},{9,10},{10,... | collective-permute-start | bytes 614408 | tf_op jit(solution)/shard_map/ppermute | solution.py:68
  72.3 1.2 %collective-permute-start.17 = (f32[1,1280]{1,0:T(1,128)S(1)}, f32[1,1280]{1,0:T(1,128)S(1)}, u32[]{:S(2)}, u32[]{:S(2)}) collective-permute-start(f32[1,1280]{1,0:T(1,128)S(1)} %get-tuple-element.101), channel_id=1, source_target_pairs={{0,4},{4,0},{8,12},{12,8},{16,20},{20,16},{24,28},{28,24},{1,5},{5... | collective-permute-start | bytes 15368 | tf_op jit(solution)/shard_map/ppermute | solution.py:72
  73.5 5.3 %collective-permute-start.18 = (f32[1,1280]{1,0:T(1,128)S(1)}, f32[1,1280]{1,0:T(1,128)S(1)}, u32[]{:S(2)}, u32[]{:S(2)}) collective-permute-start(f32[1,1280]{1,0:T(1,128)S(1)} %add.15), channel_id=1, source_target_pairs={{0,1},{1,0},{2,3},{3,2},{4,5},{5,4},{6,7},{7,6},{8,9},{9,8},{10,11... | collective-permute-start | bytes 15368 | tf_op jit(solution)/shard_map/ppermute | solution.py:68
  78.8 3.7 %collective-permute-start.19 = (f32[1,1280]{1,0:T(1,128)S(1)}, f32[1,1280]{1,0:T(1,128)S(1)}, u32[]{:S(2)}, u32[]{:S(2)}) collective-permute-start(f32[1,1280]{1,0:T(1,128)S(1)} %add.16), channel_id=1, source_target_pairs={{0,2},{1,3},{2,0},{3,1},{4,6},{5,7},{6,4},{7,5},{8,10},{9,11},{10,... | collective-permute-start | bytes 15368 | tf_op jit(solution)/shard_map/ppermute | solution.py:68
  82.5 11.9 %collective-permute-start.20 = (f32[1,1280]{1,0:T(1,128)S(1)}, f32[1,1280]{1,0:T(1,128)S(1)}, u32[]{:S(2)}, u32[]{:S(2)}) collective-permute-start(f32[1,1280]{1,0:T(1,128)S(1)} %add.17.term_ref), channel_id=1, source_target_pairs={{0,8},{4,12},{8,0},{12,4},{16,24},{20,28},{24,16},{28,20},{1,9},{5... | collective-permute-start | bytes 15368 | tf_op jit(solution)/shard_map/ppermute | solution.py:72
  83.5 16.0 %collective-permute-start.16 = (bf16[640,320]{1,0:T(8,128)(2,1)S(1)}, bf16[640,320]{1,0:T(8,128)(2,1)S(1)}, u32[]{:S(2)}, u32[]{:S(2)}) collective-permute-start(bf16[640,320]{1,0:T(8,128)(2,1)S(1)} %get-tuple-element.100), channel_id=1, source_target_pairs={{0,8},{4,12},{8,0},{12,4},{16,24},{20,28},{24,16},{28,20},{1,9},{5... | collective-permute-start | bytes 1228808 | tf_op jit(solution)/shard_map/ppermute | solution.py:72
  85.7 14.2 %collective-permute-start.21 = (bf16[160,640]{1,0:T(8,128)(2,1)S(1)}, bf16[160,640]{1,0:T(8,128)(2,1)S(1)}, u32[]{:S(2)}, u32[]{:S(2)}) collective-permute-start(bf16[160,640]{1,0:T(8,128)(2,1)S(1)} %get-tuple-element.87), channel_id=1, source_target_pairs={{0,16},{4,20},{8,24},{12,28},{16,0},{20,4},{24,8},{28,12},{1,17},{... | collective-permute-start | bytes 614408 | tf_op jit(solution)/shard_map/ppermute | solution.py:72
  86.0 4.5 %copy-start.5 = (bf16[1,128,1280]{2,1,0:T(8,128)(2,1)S(1)}, bf16[1,128,1280]{2,1,0:T(8,128)(2,1)}, u32[]{:S(2)}) copy-start(bf16[1,128,1280]{2,1,0:T(8,128)(2,1)} %param.13) | copy-start | bytes 983044
  86.0 4.5 %copy-start.7 = (bf16[1,128,1280]{2,1,0:T(8,128)(2,1)S(1)}, bf16[1,128,1280]{2,1,0:T(8,128)(2,1)}, u32[]{:S(2)}) copy-start(bf16[1,128,1280]{2,1,0:T(8,128)(2,1)} %param.10) | copy-start | bytes 983044
  86.0 4.5 %copy-start.9 = (bf16[1,128,1280]{2,1,0:T(8,128)(2,1)S(1)}, bf16[1,128,1280]{2,1,0:T(8,128)(2,1)}, u32[]{:S(2)}) copy-start(bf16[1,128,1280]{2,1,0:T(8,128)(2,1)} %param.11) | copy-start | bytes 983044
  86.0 4.5 %copy-start.11 = (bf16[1,128,1280]{2,1,0:T(8,128)(2,1)S(1)}, bf16[1,128,1280]{2,1,0:T(8,128)(2,1)}, u32[]{:S(2)}) copy-start(bf16[1,128,1280]{2,1,0:T(8,128)(2,1)} %param.12) | copy-start | bytes 983044
  86.0 4.5 %copy-start.14 = (s32[1,2,2]{2,1,0:T(2,128)S(1)}, s32[1,2,2]{2,1,0:T(2,128)}, u32[]{:S(2)}) copy-start(s32[1,2,2]{2,1,0:T(2,128)} %param.16) | copy-start | bytes 52
  86.0 19.2 %all-to-all-start.1 = ((bf16[4,128,1280]{2,1,0:T(8,128)(2,1)}), bf16[4,128,1280]{2,1,0:T(8,128)(2,1)}, u32[]{:S(2)}, u32[]{:S(2)}) async-start(bf16[4,128,1280]{2,1,0:T(8,128)(2,1)} %get-tuple-element.88), calls=%async_computation.1 | async-start | bytes 2621440 | tf_op jit(solution)/shard_map/all_to_all | solution.py:778
  94.3 5.4 %copy-start.15 = (f32[16,128,128]{2,1,0:T(8,128)}, f32[16,128,128]{2,1,0:T(8,128)S(1)}, u32[]{:S(2)}) copy-start(f32[16,128,128]{2,1,0:T(8,128)S(1)} %get-tuple-element.92.refs_5_) | copy-start | bytes 3145732
  94.3 5.4 %copy-start.16 = (f32[128,1280]{1,0:T(8,128)}, f32[128,1280]{1,0:T(8,128)S(1)}, u32[]{:S(2)}) copy-start(f32[128,1280]{1,0:T(8,128)S(1)} %get-tuple-element.90.refs_2_) | copy-start | bytes 1966084
  94.3 5.4 %copy-start.17 = (bf16[128,1280]{1,0:T(8,128)(2,1)}, bf16[128,1280]{1,0:T(8,128)(2,1)S(1)}, u32[]{:S(2)}) copy-start(bf16[128,1280]{1,0:T(8,128)(2,1)S(1)} %get-tuple-element.93.refs_6_) | copy-start | bytes 983044
  94.3 5.4 %copy-start.18 = (f32[128,128]{1,0:T(8,128)}, f32[128,128]{1,0:T(8,128)S(1)}, u32[]{:S(2)}) copy-start(f32[128,128]{1,0:T(8,128)S(1)} %get-tuple-element.91.refs_3_) | copy-start | bytes 196612
  99.8 12.1 %collective-permute-start.22 = (bf16[336,320]{1,0:T(8,128)(2,1)S(1)}, bf16[336,320]{1,0:T(8,128)(2,1)S(1)}, u32[]{:S(2)}, u32[]{:S(2)}) collective-permute-start(bf16[336,320]{1,0:T(8,128)(2,1)S(1)} %get-tuple-element.105), channel_id=1, source_target_pairs={{0,16},{4,20},{8,24},{12,28},{16,0},{20,4},{24,8},{28,12},{1,17},{... | collective-permute-start | bytes 645128 | tf_op jit(solution)/shard_map/ppermute | solution.py:72
